TPU v7x, 32 devices: a whole 2x2x4 slice. The times are simulated.
32 devices in a mesh: seq: 8 (over y, x, core), dp: 4 (over z).
Axes of the slice: x: 2, y: 2, z: 4, core: 2. Of those that a mesh axis runs over, the one named last changes fastest.
Arguments:
- layer_input: bfloat16 [4, 1536, 2048], P('dp', 'seq'), may hold values from -6 to 6
- doc_lengths: int32 [4, 4], P('dp'), may hold values from 1 to 1440, 1536 in all within a row
- attention_gain: bfloat16 [2048], P(('seq', 'dp')), may hold values from 0.5 to 1.5
- query_down: bfloat16 [2048, 1024], P(('seq', 'dp')), may hold values from -0.125 to 0.125
- query_gain: bfloat16 [1024], P(('seq', 'dp')), may hold values from 0.5 to 1.5
- query_up: bfloat16 [1024, 4096], P(('seq', 'dp')), may hold values from -0.1875 to 0.1875
- keyvalue_weight: bfloat16 [2048, 512], P(('seq', 'dp')), may hold values from -0.125 to 0.125
- output_weight: bfloat16 [4096, 2048], P(('seq', 'dp')), may hold values from -0.75 to 0.75
- feedforward_gain: bfloat16 [2048], P(('seq', 'dp')), may hold values from 0.5 to 1.5
- gate_weight: bfloat16 [2048, 5632], P(('seq', 'dp')), may hold values from -0.125 to 0.125
- up_weight: bfloat16 [2048, 5632], P(('seq', 'dp')), may hold values from -0.125 to 0.125
- down_weight: bfloat16 [5632, 2048], P(('seq', 'dp')), may hold values from -0.078125 to 0.078125
- cotangent: bfloat16 [4, 1536, 2048], P('dp', 'seq'), may hold values from -6 to 6
Outputs:
- layer_output: bfloat16 [4, 1536, 2048], P('dp', 'seq')
- input_grad: float32 [4, 1536, 2048], P('dp', 'seq')
- grad_attention_gain: float32 [2048], P(('seq', 'dp'))
- grad_query_down: float32 [2048, 1024], P(('seq', 'dp'))
- grad_query_gain: float32 [1024], P(('seq', 'dp'))
- grad_query_up: float32 [1024, 4096], P(('seq', 'dp'))
- grad_keyvalue: float32 [2048, 512], P(('seq', 'dp'))
- grad_output_weight: float32 [4096, 2048], P(('seq', 'dp'))
- grad_feedforward_gain: float32 [2048], P(('seq', 'dp'))
- grad_gate: float32 [2048, 5632], P(('seq', 'dp'))
- grad_up: float32 [2048, 5632], P(('seq', 'dp'))
- grad_down: float32 [5632, 2048], P(('seq', 'dp'))
Inputs may be any that keep to these rules, and one draw needn't show every extreme that they name: `doc_lengths`: each row's 4 lengths sum to 1536; one of them, at a place drawn from the seed, is exactly 1440.
All inputs are finite; a program needn't handle non-finite values.
Results may differ from a plain program's by a relative error of at most 0.029.
Values may be sent and summed in bfloat16 or wider, within the bound.
No kernel may reach another device: no remote copies, remote signals or barrier semaphores. Data moves between devices by JAX's collectives and lax.ppermute only.
A program may use at most 384 MiB of HBM per device.

v0:
```python
import jax
import jax.numpy as jnp
from jax import lax
from jax.sharding import PartitionSpec as P

HEADS = 16
HEAD_DIM = 256


EPS = 1e-05
ROPE_BASE = 10000.0
NEGATIVE = -1e30


def shortened(array):

    def short(part):
        return part.astype(jnp.bfloat16) if part.dtype == jnp.float32 else part

    return jax.tree.map(short, array)


def rms_norm(values, norm_gain):
    return values * lax.rsqrt(jnp.mean(values * values, axis=-1, keepdims=True) + EPS) * norm_gain


def rope_tables(position, feature_width):
    half_width = feature_width // 2
    freqs = ROPE_BASE ** (-jnp.arange(half_width, dtype=jnp.float32) * 2.0 / feature_width)
    angles = position.astype(jnp.float32)[:, None] * freqs[None, :]
    return (jnp.cos(angles), jnp.sin(angles))


def rotate(values, cosine, sine_part):
    half_width = values.shape[-1] // 2
    first_half = values[..., :half_width]
    second_half = values[..., half_width:]
    return jnp.concatenate(
        [
            first_half * cosine - second_half * sine_part,
            second_half * cosine + first_half * sine_part,
        ],
        axis=-1,
    )


def document_info(lengths_row, group_len):
    doc_ends = jnp.cumsum(lengths_row)
    places = jnp.arange(group_len, dtype=jnp.int32)
    past_ends = (places[:, None] >= doc_ends[None, :]).astype(jnp.int32)
    segment = jnp.sum(past_ends, axis=1)
    starts = jnp.sum(past_ends * lengths_row[None, :], axis=1)
    return (segment, places - starts)


def gated(gate_proj, upward):
    return jax.nn.silu(gate_proj) * upward


def matmul(left_side, right_side):
    return jnp.dot(left_side, right_side, preferred_element_type=jnp.float32)


def dot_rows(left_side, right_side):
    return lax.dot_general(
        left_side, right_side, (((1,), (1,)), ((), ())), preferred_element_type=jnp.float32
    )


def dot_cols(left_side, right_side):
    return lax.dot_general(
        left_side, right_side, (((0,), (0,)), ((), ())), preferred_element_type=jnp.float32
    )


def collect(pieces):
    return jax.tree.map(
        lambda part, own: part.astype(own.dtype),
        lax.all_gather(shortened(pieces), ("seq", "dp"), axis=0, tiled=True),
        pieces,
    )


def collect_again(pieces):
    return jax.tree.map(
        lambda part, own: part.astype(own.dtype),
        lax.all_gather(shortened(pieces), ("seq", "dp"), axis=0, tiled=True),
        pieces,
    )


def reduce_grads(term_set):
    return lax.psum_scatter(term_set, ("seq", "dp"), scatter_dimension=0, tiled=True)


def local(
    layer_input,
    doc_lengths,
    attention_gain,
    query_down,
    query_gain,
    query_up,
    keyvalue_weight,
    output_weight,
    feedforward_gain,
    gate_weight,
    up_weight,
    down_weight,
    cotangent,
):
    tokens = layer_input[0].astype(jnp.float32)
    tok_count = tokens.shape[0]
    group_len = tok_count * lax.axis_size("seq")
    first_tok = lax.axis_index("seq") * tok_count
    segment_all, position_all = document_info(doc_lengths[0], group_len)
    local_segment = lax.dynamic_slice_in_dim(segment_all, first_tok, tok_count, 0)
    local_position = lax.dynamic_slice_in_dim(position_all, first_tok, tok_count, 0)
    attention_set = collect(
        (attention_gain, query_down, query_gain, query_up, keyvalue_weight, output_weight)
    )
    (
        full_attention_gain,
        full_query_down,
        full_query_gain,
        full_query_up,
        full_keyvalue,
        full_output,
    ) = attention_set
    attention_gain_f = full_attention_gain.astype(jnp.float32)
    query_gain_f = full_query_gain.astype(jnp.float32)
    normed = rms_norm(tokens, attention_gain_f)
    normed_low = normed.astype(jnp.bfloat16)
    latent = matmul(normed_low, full_query_down)
    latent_low = rms_norm(latent, query_gain_f).astype(jnp.bfloat16)
    query_raw = matmul(latent_low, full_query_up).reshape(tok_count, HEADS, HEAD_DIM)
    keyvalue = matmul(normed_low, full_keyvalue)
    cosine, sine_part = rope_tables(local_position, HEAD_DIM)
    query_scale = HEAD_DIM ** (-0.5)
    row_count = tok_count * HEADS
    query_rows = (
        (rotate(query_raw, cosine[:, None, :], sine_part[:, None, :]) * query_scale)
        .astype(jnp.bfloat16)
        .reshape(row_count, HEAD_DIM)
    )
    key_local = rotate(keyvalue[:, :HEAD_DIM], cosine, sine_part)
    local_pairs = jnp.concatenate([key_local, keyvalue[:, HEAD_DIM:]], axis=1).astype(jnp.bfloat16)
    group_pairs = lax.all_gather(local_pairs, "seq", axis=0, tiled=True)
    row_index = first_tok + jnp.arange(row_count, dtype=jnp.int32) // HEADS
    row_segment = jnp.repeat(local_segment, HEADS)
    key_block = min(512, group_len)
    needed = (first_tok + tok_count + key_block - 1) // key_block

    def block_view(block_index):
        start = block_index * key_block
        kv_pairs = lax.dynamic_slice_in_dim(group_pairs, start, key_block, 0)
        key_index = start + jnp.arange(key_block, dtype=jnp.int32)
        key_segment = lax.dynamic_slice_in_dim(segment_all, start, key_block, 0)
        visible = (key_index[None, :] <= row_index[:, None]) & (
            key_segment[None, :] == row_segment[:, None]
        )
        scores = dot_rows(query_rows, kv_pairs[:, :HEAD_DIM])
        return (kv_pairs, visible, scores)

    def forward_block(block_index, running):
        running_max, running_sum, weighted_sum = running
        kv_pairs, visible, scores = block_view(block_index)
        masked_scores = jnp.where(visible, scores, NEGATIVE)
        new_max = jnp.maximum(running_max, jnp.max(masked_scores, axis=1))
        factor = jnp.exp(running_max - new_max)
        exp_terms = jnp.where(visible, jnp.exp(masked_scores - new_max[:, None]), 0.0)
        running_sum = running_sum * factor + jnp.sum(exp_terms, axis=1)
        weighted_sum = weighted_sum * factor[:, None] + matmul(
            exp_terms.astype(jnp.bfloat16), kv_pairs[:, HEAD_DIM:]
        )
        return (new_max, running_sum, weighted_sum)

    start_state = (
        jnp.full((row_count,), NEGATIVE, jnp.float32),
        jnp.zeros((row_count,), jnp.float32),
        jnp.zeros((row_count, HEAD_DIM), jnp.float32),
    )
    running_max, running_sum, weighted_sum = lax.fori_loop(0, needed, forward_block, start_state)
    attended = weighted_sum / running_sum[:, None]
    log_total = running_max + jnp.log(running_sum)
    mixed_low = attended.astype(jnp.bfloat16).reshape(tok_count, HEADS * HEAD_DIM)
    hidden = tokens + matmul(mixed_low, full_output)
    feed_set = collect((feedforward_gain, gate_weight, up_weight, down_weight))
    full_feed_gain, full_gate, full_upper, full_down = feed_set
    feed_gain_f = full_feed_gain.astype(jnp.float32)
    feed_low = rms_norm(hidden, feed_gain_f).astype(jnp.bfloat16)
    gate_proj = matmul(feed_low, full_gate)
    upward = matmul(feed_low, full_upper)
    active_low = gated(gate_proj, upward).astype(jnp.bfloat16)
    result = hidden + matmul(active_low, full_down)
    layer_output = result.astype(jnp.bfloat16)[None]
    feed_back = collect_again((feedforward_gain, gate_weight, up_weight, down_weight))
    back_gate, back_upper, back_down = (feed_back[1], feed_back[2], feed_back[3])
    d_result = cotangent[0].astype(jnp.float32)
    d_feed_low = d_result.astype(jnp.bfloat16)
    d_active = dot_rows(d_feed_low, back_down)
    d_gate, d_upward = jax.vjp(gated, gate_proj, upward)[1](d_active)
    d_gate_low = d_gate.astype(jnp.bfloat16)
    d_up_low = d_upward.astype(jnp.bfloat16)
    d_feed_normed = dot_rows(d_gate_low, back_gate) + dot_rows(d_up_low, back_upper)
    d_hidden_norm, grad_feed_gain_term = jax.vjp(rms_norm, hidden, feed_gain_f)[1](d_feed_normed)
    d_hidden = d_result + d_hidden_norm
    grad_down_term = dot_cols(active_low, d_feed_low)
    grad_gate_term = dot_cols(feed_low, d_gate_low)
    grad_up_term = dot_cols(feed_low, d_up_low)
    grad_feed_gain, grad_gate, grad_up, grad_down = reduce_grads(
        (grad_feed_gain_term, grad_gate_term, grad_up_term, grad_down_term)
    )
    attention_back = collect_again(
        (attention_gain, query_down, query_gain, query_up, keyvalue_weight, output_weight)
    )
    back_query_down, back_query_up, back_keyvalue, back_output = (
        attention_back[1],
        attention_back[3],
        attention_back[4],
        attention_back[5],
    )
    d_branch_low = d_hidden.astype(jnp.bfloat16)
    d_mixed_low = (
        dot_rows(d_branch_low, back_output).astype(jnp.bfloat16).reshape(row_count, HEAD_DIM)
    )
    row_offset = jnp.sum(d_mixed_low.astype(jnp.float32) * attended, axis=1)

    def backward_block(block_index, running):
        d_query_rows, kv_terms = running
        kv_pairs, visible, scores = block_view(block_index)
        prob_rows = jnp.where(
            visible, jnp.exp(jnp.where(visible, scores, NEGATIVE) - log_total[:, None]), 0.0
        )
        d_probs = dot_rows(d_mixed_low, kv_pairs[:, HEAD_DIM:])
        d_scores_low = (prob_rows * (d_probs - row_offset[:, None])).astype(jnp.bfloat16)
        d_query_rows = d_query_rows + matmul(d_scores_low, kv_pairs[:, :HEAD_DIM])
        d_keys = dot_cols(d_scores_low, query_rows)
        d_values = dot_cols(prob_rows.astype(jnp.bfloat16), d_mixed_low)
        kv_terms = lax.dynamic_update_slice_in_dim(
            kv_terms, jnp.concatenate([d_keys, d_values], axis=1), block_index * key_block, 0
        )
        return (d_query_rows, kv_terms)

    back_state = (
        jnp.zeros((row_count, HEAD_DIM), jnp.float32),
        jnp.zeros((group_len, 2 * HEAD_DIM), jnp.float32),
    )
    d_query_rows, kv_terms = lax.fori_loop(0, needed, backward_block, back_state)
    d_pairs = lax.psum_scatter(
        kv_terms.astype(jnp.bfloat16), "seq", scatter_dimension=0, tiled=True
    ).astype(jnp.float32)
    d_key_raw = rotate(d_pairs[:, :HEAD_DIM], cosine, -sine_part)
    d_keyvalue_low = jnp.concatenate([d_key_raw, d_pairs[:, HEAD_DIM:]], axis=1).astype(
        jnp.bfloat16
    )
    d_query_raw = rotate(
        d_query_rows.reshape(tok_count, HEADS, HEAD_DIM) * query_scale,
        cosine[:, None, :],
        -sine_part[:, None, :],
    )
    d_query_low = d_query_raw.reshape(tok_count, HEADS * HEAD_DIM).astype(jnp.bfloat16)
    grad_query_up_term = dot_cols(latent_low, d_query_low)
    d_latent_normed = dot_rows(d_query_low, back_query_up)
    d_latent, grad_query_gain_term = jax.vjp(rms_norm, latent, query_gain_f)[1](d_latent_normed)
    d_latent_low = d_latent.astype(jnp.bfloat16)
    d_normed = dot_rows(d_latent_low, back_query_down) + dot_rows(d_keyvalue_low, back_keyvalue)
    d_tokens, grad_attention_gain_term = jax.vjp(rms_norm, tokens, attention_gain_f)[1](d_normed)
    input_grad = (d_hidden + d_tokens)[None]
    grad_output_term = dot_cols(mixed_low, d_branch_low)
    grad_query_down_term = dot_cols(normed_low, d_latent_low)
    grad_keyvalue_term = dot_cols(normed_low, d_keyvalue_low)
    (
        grad_attention_gain,
        grad_query_down,
        grad_query_gain,
        grad_query_up,
        grad_keyvalue,
        grad_output_weight,
    ) = reduce_grads(
        (
            grad_attention_gain_term,
            grad_query_down_term,
            grad_query_gain_term,
            grad_query_up_term,
            grad_keyvalue_term,
            grad_output_term,
        )
    )
    return (
        layer_output,
        input_grad,
        grad_attention_gain,
        grad_query_down,
        grad_query_gain,
        grad_query_up,
        grad_keyvalue,
        grad_output_weight,
        grad_feed_gain,
        grad_gate,
        grad_up,
        grad_down,
    )


def solution(mesh):
    return jax.shard_map(
        local,
        mesh=mesh,
        in_specs=(
            P("dp", "seq", None),
            P("dp", None),
            P(("seq", "dp")),
            P(("seq", "dp"), None),
            P(("seq", "dp")),
            P(("seq", "dp"), None),
            P(("seq", "dp"), None),
            P(("seq", "dp"), None),
            P(("seq", "dp")),
            P(("seq", "dp"), None),
            P(("seq", "dp"), None),
            P(("seq", "dp"), None),
            P("dp", "seq", None),
        ),
        out_specs=(
            P("dp", "seq", None),
            P("dp", "seq", None),
            P(("seq", "dp")),
            P(("seq", "dp"), None),
            P(("seq", "dp")),
            P(("seq", "dp"), None),
            P(("seq", "dp"), None),
            P(("seq", "dp"), None),
            P(("seq", "dp")),
            P(("seq", "dp"), None),
            P(("seq", "dp"), None),
            P(("seq", "dp"), None),
        ),
        check_vma=False,
    )
```

profile of v0, /device:TPU:0, one launch (start us, length us, event | category | flops | bytes accessed | tf_op | source)
XLA Modules:
  0.0 5322.6 jit_solution(151444472365427319)
XLA Ops:
  12.0 42.1 all-reduce.7
  55.8 1.4 fusion.58
  57.2 12.9 all-gather.9.cloned.1.call-done
  70.2 2.5 fusion.99
  72.7 1.1 fusion.73
  77.3 56.9 %all-gather.13.cloned.1.call-done = bf16[2048,1024]{1,0:T(8,128)(2,1)} async-done(((bf16[64,1024]{1,0:T(8,128)(2,1)}), bf16[2048,1024]{1,0:T(8,128)(2,1)}) %all-gather.13.cloned.1.call-update) | async-done | bytes 4194320 | tf_op jit(solution)/shard_map/all_gather | solution.py:79
  134.2 3.3 multiply_reduce_fusion.6
  137.6 75.5 %all-gather.15.cloned.1.call-done = bf16[1024,4096]{1,0:T(8,128)(2,1)} async-done(((bf16[32,4096]{1,0:T(8,128)(2,1)}), bf16[1024,4096]{1,0:T(8,128)(2,1)}) %all-gather.15.cloned.1.call-update) | async-done | bytes 8388624 | tf_op jit(solution)/shard_map/all_gather | solution.py:79
  213.1 5.2 fusion.93
  218.4 1.2 copy.41
  220.1 1.5 fusion.48
  221.5 18.2 all-gather.11.cloned.1.call-done
  240.0 12.2 while.28
  240.5 3.0 fusion.169
  243.5 2.1 fusion.170
  246.1 5.7 convolution_add_fusion.7
  252.2 2.1 fusion.65
  254.5 3.8 reshape.221
  258.3 99.5 %all-gather.17.cloned.1.call-done = bf16[4096,2048]{1,0:T(8,128)(2,1)} async-done(((bf16[128,2048]{1,0:T(8,128)(2,1)}), bf16[4096,2048]{1,0:T(8,128)(2,1)}) %all-gather.17.cloned.1.call-update) | async-done | bytes 16777232 | tf_op jit(solution)/shard_map/all_gather | solution.py:79
  357.8 9.9 multiply_reduce_fusion.3
  367.9 135.3 %all-gather.19.cloned.1.call-done = bf16[2048,5632]{1,0:T(8,128)(2,1)} async-done(((bf16[64,5632]{1,0:T(8,128)(2,1)}), bf16[2048,5632]{1,0:T(8,128)(2,1)}) %all-gather.19.cloned.1.call-update) | async-done | bytes 23068688 | tf_op jit(solution)/shard_map/all_gather | solution.py:79
  503.3 12.0 fusion.102
  515.3 133.6 %all-gather.21.cloned.1.call-done = bf16[2048,5632]{1,0:T(8,128)(2,1)} async-done(((bf16[64,5632]{1,0:T(8,128)(2,1)}), bf16[2048,5632]{1,0:T(8,128)(2,1)}) %all-gather.21.cloned.1.call-update) | async-done | bytes 23068688 | tf_op jit(solution)/shard_map/all_gather | solution.py:79
  648.9 12.2 fusion.103
  661.1 133.5 %all-gather.23.cloned.1.call-done = bf16[5632,2048]{1,0:T(8,128)(2,1)} async-done(((bf16[176,2048]{1,0:T(8,128)(2,1)}), bf16[5632,2048]{1,0:T(8,128)(2,1)}) %all-gather.23.cloned.1.call-update) | async-done | bytes 23068688 | tf_op jit(solution)/shard_map/all_gather | solution.py:79
  794.6 16.1 multiply_convert_fusion
  810.6 12.8 fusion.104
  823.5 25.0 multiply_reduce_fusion.1
  848.5 2.1 fusion.55
  850.6 1.2 copy-done.6
  851.8 11.4 convolution_convert_fusion
  864.0 1.2 copy-done
  865.1 3.3 multiply_reduce_fusion
  868.7 1.3 broadcast_in_dim.46.clone
  870.0 21.5 while.29
  870.3 6.1 fusion.182
  876.3 4.5 fusion.183
  880.9 3.0 convolution_add_fusion.8
  883.9 1.1 fusion.184
  885.3 1.0 fusion.185
  887.1 2.0 copy.44
  889.2 1.9 constant_dynamic-update-slice_fusion.2
  891.6 78.9 %reduce-scatter.9.cloned.1.call-done = bf16[192,512]{1,0:T(8,128)(2,1)} async-done(((bf16[1536,512]{1,0:T(8,128)(2,1)}), bf16[192,512]{1,0:T(8,128)(2,1)}) %reduce-scatter.9.cloned.1.call-update) | async-done | bytes 196624 | tf_op jit(solution)/shard_map/reduce_scatter | solution.py:249
  973.6 4.0 fusion.84
  979.9 1.5 slice-done.3
  981.5 3.7 multiply_reduce_fusion.4
  986.3 4.8 fusion.95
  991.2 8.3 fusion.92
  999.6 1.3 copy-done.7
  1000.9 14.9 fusion.66
  1017.0 19.5 fusion.105
  1036.6 19.6 fusion.106
  1056.2 1.1 copy-done.15
  1057.3 19.5 fusion.61
  1076.9 14.3 fusion.50
  1092.2 3.0 fusion.54
  1095.2 39.9 all-reduce.6
  1136.9 3.0 fusion.57
  1139.8 173.1 %reduce-scatter.11.cloned.1.call-done = f32[64,1024]{1,0:T(8,128)} async-done(((f32[2048,1024]{1,0:T(8,128)}), f32[64,1024]{1,0:T(8,128)}) %reduce-scatter.11.cloned.1.call-update) | async-done | bytes 262160 | tf_op jit(solution)/shard_map/reduce_scatter | solution.py:93
  1312.9 364.6 %reduce-scatter.13.cloned.1.call-done = f32[32,4096]{1,0:T(8,128)} async-done(((f32[1024,4096]{1,0:T(8,128)}), f32[32,4096]{1,0:T(8,128)}) %reduce-scatter.13.cloned.1.call-update) | async-done | bytes 524304 | tf_op jit(solution)/shard_map/reduce_scatter | solution.py:93
  1677.5 712.8 %reduce-scatter.17.cloned.1.call-done = f32[128,2048]{1,0:T(8,128)} async-done(((f32[4096,2048]{1,0:T(8,128)}), f32[128,2048]{1,0:T(8,128)}) %reduce-scatter.17.cloned.1.call-update) | async-done | bytes 1048592 | tf_op jit(solution)/shard_map/reduce_scatter | solution.py:93
  2390.3 974.5 %reduce-scatter.19.cloned.1.call-done = f32[64,5632]{1,0:T(8,128)} async-done(((f32[2048,5632]{1,0:T(8,128)}), f32[64,5632]{1,0:T(8,128)}) %reduce-scatter.19.cloned.1.call-update) | async-done | bytes 1441808 | tf_op jit(solution)/shard_map/reduce_scatter | solution.py:93
  3364.8 975.5 %reduce-scatter.21.cloned.1.call-done = f32[64,5632]{1,0:T(8,128)} async-done(((f32[2048,5632]{1,0:T(8,128)}), f32[64,5632]{1,0:T(8,128)}) %reduce-scatter.21.cloned.1.call-update) | async-done | bytes 1441808 | tf_op jit(solution)/shard_map/reduce_scatter | solution.py:93
  4340.3 975.5 %reduce-scatter.23.cloned.1.call-done = f32[176,2048]{1,0:T(8,128)} async-done(((f32[5632,2048]{1,0:T(8,128)}), f32[176,2048]{1,0:T(8,128)}) %reduce-scatter.23.cloned.1.call-update) | async-done | bytes 1441808 | tf_op jit(solution)/shard_map/reduce_scatter | solution.py:93
  (190 shorter events, 24.8 us)
Async XLA Ops:
  7.2 63.0 %all-gather.9.cloned.1.call-start = ((), (), s32[]{:S(2)}) async-start(), calls=%async_computation.8 | async-start | bytes 2162688 | tf_op jit(solution)/shard_map/all_gather | solution.py:79
  7.9 126.3 %all-gather.13.cloned.1.call-start = ((), (), s32[]{:S(2)}) async-start(), calls=%async_computation.10 | async-start | bytes 4325376 | tf_op jit(solution)/shard_map/all_gather | solution.py:79
  8.7 204.5 %all-gather.15.cloned.1.call-start = ((), (), s32[]{:S(2)}) async-start(), calls=%async_computation.11 | async-start | bytes 8650752 | tf_op jit(solution)/shard_map/all_gather | solution.py:79
  9.4 230.4 %all-gather.11.cloned.1.call-start = ((), (), s32[]{:S(2)}) async-start(), calls=%async_computation.9 | async-start | bytes 1769472 | tf_op jit(solution)/shard_map/all_gather | solution.py:147
  54.1 80.1 %copy-start.29 = (f32[2048]{0:T(1024)}, f32[2048]{0:T(1024)S(1)}, u32[]{:S(2)}) copy-start(f32[2048]{0:T(1024)S(1)} %convert_element_type.89) | copy-start | bytes 24580
  55.0 17.7 copy-start.46
  55.8 16.9 copy-start.38
  57.2 15.4 copy-start.40
  57.2 77.0 %copy-start.34 = (f32[192]{0:T(256)}, f32[192]{0:T(256)S(1)}, u32[]{:S(2)}) copy-start(f32[192]{0:T(256)S(1)} %fusion.87) | copy-start | bytes 2308
  72.6 61.6 %copy-start.4 = (bf16[1,192,2048]{2,1,0:T(8,128)(2,1)S(1)}, bf16[1,192,2048]{2,1,0:T(8,128)(2,1)}, u32[]{:S(2)}) copy-start(bf16[1,192,2048]{2,1,0:T(8,128)(2,1)} %param.17) | copy-start | bytes 2359300
  73.8 145.8 %copy-start.19 = (f32[192,128]{1,0:T(8,128)}, f32[192,128]{1,0:T(8,128)S(1)}, u32[]{:S(2)}) copy-start(f32[192,128]{1,0:T(8,128)S(1)} %get-tuple-element.269) | copy-start | bytes 294916
  74.5 283.2 %all-gather.17.cloned.1.call-start = ((), (), s32[]{:S(2)}) async-start(), calls=%async_computation.12 | async-start | bytes 17301504 | tf_op jit(solution)/shard_map/all_gather | solution.py:79
  75.1 428.2 %all-gather.19.cloned.1.call-start = ((), (), s32[]{:S(2)}) async-start(), calls=%async_computation.13 | async-start | bytes 23789568 | tf_op jit(solution)/shard_map/all_gather | solution.py:79
  75.7 573.2 %all-gather.21.cloned.1.call-start = ((), (), s32[]{:S(2)}) async-start(), calls=%async_computation.14 | async-start | bytes 23789568 | tf_op jit(solution)/shard_map/all_gather | solution.py:79
  76.4 718.1 %all-gather.23.cloned.1.call-start = ((), (), s32[]{:S(2)}) async-start(), calls=%async_computation.15 | async-start | bytes 23789568 | tf_op jit(solution)/shard_map/all_gather | solution.py:79
  77.2 893.3 %reduce-scatter.9.cloned.1.call-start = ((), (), s32[]{:S(2)}) async-start(), calls=%async_computation.16 | async-start | bytes 1769472 | tf_op jit(solution)/shard_map/reduce_scatter | solution.py:249
  77.3 135.9 %copy-start.23 = (f32[1024]{0:T(1024)}, f32[1024]{0:T(1024)S(1)}, u32[]{:S(2)}) copy-start(f32[1024]{0:T(1024)S(1)} %convert_element_type.92) | copy-start | bytes 12292
  137.5 80.8 %copy-start.8 = (f32[192,1024]{1,0:T(8,128)}, f32[192,1024]{1,0:T(8,128)S(1)}, u32[]{:S(2)}) copy-start(f32[192,1024]{1,0:T(8,128)S(1)} %get-tuple-element.271) | copy-start | bytes 2359300
  137.6 80.8 %copy-start.44 = (f32[192]{0:T(256)}, f32[192]{0:T(256)S(1)}, u32[]{:S(2)}) copy-start(f32[192]{0:T(256)S(1)} %get-tuple-element.270) | copy-start | bytes 2308
  137.6 80.8 %copy-start.32 = (f32[192]{0:T(256)}, f32[192]{0:T(256)S(1)}, u32[]{:S(2)}) copy-start(f32[192]{0:T(256)S(1)} %fusion.88) | copy-start | bytes 2308
  243.5 2.6 copy-start.2
  252.2 2.3 copy-start.3
  367.7 480.8 %copy-start.12 = (f32[192,2048]{1,0:T(8,128)}, f32[192,2048]{1,0:T(8,128)S(1)}, u32[]{:S(2)}) copy-start(f32[192,2048]{1,0:T(8,128)S(1)} %get-tuple-element.273) | copy-start | bytes 4718596
  367.9 281.0 %copy-start.10 = (bf16[192,2048]{1,0:T(8,128)(2,1)}, bf16[192,2048]{1,0:T(8,128)(2,1)S(1)}, u32[]{:S(2)}) copy-start(bf16[192,2048]{1,0:T(8,128)(2,1)S(1)} %multiply_convert_fusion.2) | copy-start | bytes 2359300
  515.3 279.3 %copy-start.14 = (bf16[1,192,2048]{2,1,0:T(8,128)(2,1)S(1)}, bf16[1,192,2048]{2,1,0:T(8,128)(2,1)}, u32[]{:S(2)}) copy-start(bf16[1,192,2048]{2,1,0:T(8,128)(2,1)} %param.29) | copy-start | bytes 2359300
  810.6 12.8 copy-start.16
  850.6 1.2 copy-start.6
  864.0 1.2 copy-start
  876.3 7.5 slice-start
  880.8 3.0 slice-start.1
  880.8 3.0 copy-start.1
  883.9 1.4 copy-start.18
  891.5 80.0 %copy-start.39 = (f32[192]{0:T(256)S(1)}, f32[192]{0:T(256)}, u32[]{:S(2)}) copy-start(f32[192]{0:T(256)} %copy-done.38) | copy-start | bytes 2308
  891.5 80.0 %copy-start.47 = (f32[128]{0:T(128)S(1)}, f32[128]{0:T(128)}, u32[]{:S(2)}) copy-start(f32[128]{0:T(128)} %copy-done.46) | copy-start | bytes 1540
  891.5 82.1 %copy-start.30 = (f32[2048]{0:T(1024)S(1)}, f32[2048]{0:T(1024)}, u32[]{:S(2)}) copy-start(f32[2048]{0:T(1024)} %copy-done.29) | copy-start | bytes 24580
  891.5 82.1 %copy-start.35 = (f32[192]{0:T(256)S(1)}, f32[192]{0:T(256)}, u32[]{:S(2)}) copy-start(f32[192]{0:T(256)} %copy-done.34) | copy-start | bytes 2308
  891.5 248.3 %reduce-scatter.15.cloned.1.call-start = ((), (), s32[]{:S(2)}) async-start(), calls=%async_computation.19 | async-start | bytes 4325376 | tf_op jit(solution)/shard_map/reduce_scatter | solution.py:93
  972.0 1.0 copy-start.25
  972.0 1.0 copy-start.27
  977.6 335.4 %reduce-scatter.11.cloned.1.call-start = ((), (), s32[]{:S(2)}) async-start(), calls=%async_computation.17 | async-start | bytes 8650752 | tf_op jit(solution)/shard_map/reduce_scatter | solution.py:93
  977.6 2.3 slice-start.2
  978.6 2.8 slice-start.3
  979.2 2.3 copy-start.9
  979.2 2.3 copy-start.24
  979.2 2.3 copy-start.33
  981.5 3.7 copy-start.45
  981.5 3.9 copy-start.36
  985.2 1.1 copy-start.5
  991.1 686.4 %reduce-scatter.13.cloned.1.call-start = ((), (), s32[]{:S(2)}) async-start(), calls=%async_computation.18 | async-start | bytes 17301504 | tf_op jit(solution)/shard_map/reduce_scatter | solution.py:93
  999.5 1.4 copy-start.7
  999.5 1390.8 %reduce-scatter.17.cloned.1.call-start = ((), (), s32[]{:S(2)}) async-start(), calls=%async_computation.20 | async-start | bytes 34603008 | tf_op jit(solution)/shard_map/reduce_scatter | solution.py:93
  1015.8 1.1 copy-start.11
  1015.8 2349.0 %reduce-scatter.19.cloned.1.call-start = ((), (), s32[]{:S(2)}) async-start(), calls=%async_computation.21 | async-start | bytes 47579136 | tf_op jit(solution)/shard_map/reduce_scatter | solution.py:93
  1036.5 3303.8 %reduce-scatter.21.cloned.1.call-start = ((), (), s32[]{:S(2)}) async-start(), calls=%async_computation.22 | async-start | bytes 47579136 | tf_op jit(solution)/shard_map/reduce_scatter | solution.py:93
  1056.2 1.1 copy-start.15
  1056.2 4259.7 %reduce-scatter.23.cloned.1.call-start = ((), (), s32[]{:S(2)}) async-start(), calls=%async_computation.23 | async-start | bytes 47579136 | tf_op jit(solution)/shard_map/reduce_scatter | solution.py:93
  1076.9 14.4 copy-start.17
  1076.9 14.4 copy-start.22
  1076.9 14.4 copy-start.26
  1076.9 14.4 copy-start.28
  1076.9 15.2 copy-start.13
  1092.1 3.0 copy-start.42
  1092.2 3.0 copy-start.43
  1092.2 44.7 copy-start.41
  (4 other events, 3.3 us)
Sparse Core Ops, SparseCore 0:
  10.9 59.1 all-gather.8
  73.1 61.0 all-gather.12
  137.1 75.9 all-gather.14
  215.4 24.2 all-gather.10
  242.6 115.1 all-gather.16
  360.5 142.7 all-gather.18
  506.1 142.7 all-gather.20
  651.8 142.7 all-gather.22
  891.6 78.8 reduce-scatter.8
  977.7 148.1 reduce-scatter.14
  1128.8 184.1 reduce-scatter.10
  1315.6 361.8 reduce-scatter.12
  1680.4 709.8 reduce-scatter.16
  2393.1 971.6 reduce-scatter.18
  3367.5 972.7 reduce-scatter.20
  4343.1 972.7 reduce-scatter.22
where the time goes:
time: 5320 us
  waiting for transfers between devices  4930 us (93%)
  matrix products  247 us (5%)
  blocking collectives  82 us (2%)
    reduce_scatter x7, waiting for transfers between devices, reduce_grads(): lax.psum_scatter(term_set, ('seq', 'dp'), scatter_dimension=0, tiled=True)  4180 us
    all_gather x7, waiting for transfers between devices, collect(): lax.all_gather(shortened(pieces), ('seq', 'dp'), axis=0, tiled=True)  647 us
  transfers between devices with their start and end apart: 16, of which 15 were waited for; matrix products, arithmetic and copies ran while one was open for 4% of the time, Pallas kernels for 0%

commit v1 on v0

v1 whole, which is shorter than its diff:
```python
import functools

import jax
import jax.numpy as jnp
from jax import lax
from jax.experimental import pallas as pl
from jax.experimental.pallas import tpu as pltpu
from jax.sharding import PartitionSpec as P

HEADS = 16
HEAD_DIM = 256


EPS = 1e-05
ROPE_BASE = 10000.0
NEGATIVE = -1e30
BF = jnp.bfloat16
F32 = jnp.float32


def rms_norm(values, norm_gain):
    return values * lax.rsqrt(jnp.mean(values * values, axis=-1, keepdims=True) + EPS) * norm_gain


def rope_tables(position, feature_width):
    half_width = feature_width // 2
    freqs = ROPE_BASE ** (-jnp.arange(half_width, dtype=F32) * 2.0 / feature_width)
    angles = position.astype(F32)[:, None] * freqs[None, :]
    return (jnp.cos(angles), jnp.sin(angles))


def rotate(values, cosine, sine_part):
    half_width = values.shape[-1] // 2
    first_half = values[..., :half_width]
    second_half = values[..., half_width:]
    return jnp.concatenate(
        [
            first_half * cosine - second_half * sine_part,
            second_half * cosine + first_half * sine_part,
        ],
        axis=-1,
    )


def document_starts(lengths_row, group_len):
    doc_ends = jnp.cumsum(lengths_row)
    places = jnp.arange(group_len, dtype=jnp.int32)
    past_ends = (places[:, None] >= doc_ends[None, :]).astype(jnp.int32)
    starts = jnp.sum(past_ends * lengths_row[None, :], axis=1)
    return (starts, places - starts)


def gated(gate_proj, upward):
    return jax.nn.silu(gate_proj) * upward


def matmul(left_side, right_side):
    return jnp.dot(left_side, right_side, preferred_element_type=F32)


def dot_rows(left_side, right_side):
    return lax.dot_general(
        left_side, right_side, (((1,), (1,)), ((), ())), preferred_element_type=F32
    )


def dot_cols(left_side, right_side):
    return lax.dot_general(
        left_side, right_side, (((0,), (0,)), ((), ())), preferred_element_type=F32
    )


def visible_block(key_at, query_at, starts_row, shape):
    keys = key_at + lax.broadcasted_iota(jnp.int32, shape, 0)
    queries = query_at + lax.broadcasted_iota(jnp.int32, shape, 1)
    return (keys <= queries) & (keys >= starts_row)


def attend_kernel(heads, block, starts_ref, q_ref, k_ref, vt_ref, out_ref, lse_ref):
    at = pl.program_id(0)
    starts_row = starts_ref[...]
    query_at = at * block
    for head in range(heads):
        q = q_ref[:, head * HEAD_DIM : (head + 1) * HEAD_DIM]

        def step(b, running, q=q):
            running_max, running_sum, total = running
            here = pl.ds(pl.multiple_of(b * block, block), block)
            scores = dot_rows(k_ref[here, :], q)
            visible = visible_block(b * block, query_at, starts_row, scores.shape)
            scores = jnp.where(visible, scores, NEGATIVE)
            new_max = jnp.maximum(running_max, jnp.max(scores, axis=0, keepdims=True))
            factor = jnp.exp(running_max - new_max)
            terms = jnp.where(visible, jnp.exp(scores - new_max), 0.0)
            running_sum = running_sum * factor + jnp.sum(terms, axis=0, keepdims=True)
            total = total * factor + matmul(vt_ref[:, here], terms.astype(BF))
            return (new_max, running_sum, total)

        start = (
            jnp.full((1, block), NEGATIVE, F32),
            jnp.zeros((1, block), F32),
            jnp.zeros((HEAD_DIM, block), F32),
        )
        running_max, running_sum, total = lax.fori_loop(0, at + 1, step, start)
        out_ref[:, head * HEAD_DIM : (head + 1) * HEAD_DIM] = (total / running_sum).T
        lse_ref[head : head + 1, :] = running_max + jnp.log(running_sum)


def attend(starts, queries, keys, values):
    group_len, width = queries.shape
    heads = width // HEAD_DIM
    block = 256
    return pl.pallas_call(
        functools.partial(attend_kernel, heads, block),
        grid=(group_len // block,),
        in_specs=[
            pl.BlockSpec((1, block), lambda i: (0, i)),
            pl.BlockSpec((block, width), lambda i: (i, 0)),
            pl.BlockSpec((group_len, HEAD_DIM), lambda i: (0, 0)),
            pl.BlockSpec((HEAD_DIM, group_len), lambda i: (0, 0)),
        ],
        out_specs=[
            pl.BlockSpec((block, width), lambda i: (i, 0)),
            pl.BlockSpec((heads, block), lambda i: (0, i)),
        ],
        out_shape=[
            jax.ShapeDtypeStruct((group_len, width), F32),
            jax.ShapeDtypeStruct((heads, group_len), F32),
        ],
        compiler_params=pltpu.CompilerParams(vmem_limit_bytes=32 * 2**20),
        cost_estimate=pl.CostEstimate(
            flops=2 * group_len * group_len * width,
            bytes_accessed=group_len * width * 8,
            transcendentals=heads * group_len * group_len // 2,
        ),
        name="attend",
    )(starts.reshape(1, group_len), queries, keys, values.T)


def attend_back_kernel(
    heads, block, starts_ref, q_ref, dm_ref, lse_ref, off_ref, k_ref, v_ref, dq_ref, dk_ref, dv_ref
):
    at = pl.program_id(0)

    @pl.when(at == 0)
    def _():
        dk_ref[...] = jnp.zeros_like(dk_ref)
        dv_ref[...] = jnp.zeros_like(dv_ref)

    starts_row = starts_ref[...]
    query_at = at * block
    for head in range(heads):
        columns = slice(head * HEAD_DIM, (head + 1) * HEAD_DIM)
        q = q_ref[:, columns]
        dm = dm_ref[:, columns]
        lse = lse_ref[head : head + 1, :]
        off = off_ref[head : head + 1, :]

        def step(b, dq, q=q, dm=dm, lse=lse, off=off):
            here = pl.ds(pl.multiple_of(b * block, block), block)
            keys = k_ref[here, :]
            scores = dot_rows(keys, q)
            visible = visible_block(b * block, query_at, starts_row, scores.shape)
            probs = jnp.where(visible, jnp.exp(jnp.where(visible, scores, NEGATIVE) - lse), 0.0)
            d_probs = dot_rows(v_ref[here, :], dm)
            d_scores = (probs * (d_probs - off)).astype(BF)
            dv_ref[here, :] += matmul(probs.astype(BF), dm)
            dk_ref[here, :] += matmul(d_scores, q)
            return dq + dot_cols(d_scores, keys)

        dq_ref[:, columns] = lax.fori_loop(0, at + 1, step, jnp.zeros((block, HEAD_DIM), F32))


def attend_back(starts, queries, d_mixed, lse, offset, keys, values):
    group_len, width = queries.shape
    heads = width // HEAD_DIM
    block = 256
    whole = pl.BlockSpec((group_len, HEAD_DIM), lambda i: (0, 0))
    rows = pl.BlockSpec((block, width), lambda i: (i, 0))
    lanes = pl.BlockSpec((heads, block), lambda i: (0, i))
    return pl.pallas_call(
        functools.partial(attend_back_kernel, heads, block),
        grid=(group_len // block,),
        in_specs=[pl.BlockSpec((1, block), lambda i: (0, i)), rows, rows, lanes, lanes, whole, whole],
        out_specs=[rows, whole, whole],
        out_shape=[
            jax.ShapeDtypeStruct((group_len, width), F32),
            jax.ShapeDtypeStruct((group_len, HEAD_DIM), F32),
            jax.ShapeDtypeStruct((group_len, HEAD_DIM), F32),
        ],
        compiler_params=pltpu.CompilerParams(vmem_limit_bytes=32 * 2**20),
        cost_estimate=pl.CostEstimate(
            flops=5 * group_len * group_len * width,
            bytes_accessed=group_len * width * 12,
            transcendentals=heads * group_len * group_len // 2,
        ),
        name="attend_back",
    )(starts.reshape(1, group_len), queries, d_mixed, lse, offset, keys, values)


def gather_seq(rows):
    return lax.all_gather(rows, "seq", axis=0, tiled=True)


def scatter_seq(terms):
    return lax.psum_scatter(terms.astype(BF), "seq", scatter_dimension=0, tiled=True).astype(F32)


def gather_dp(rows):
    return lax.all_gather(rows, "dp", axis=0, tiled=True)


def scatter_dp(terms):
    return lax.psum_scatter(terms.astype(BF), "dp", scatter_dimension=0, tiled=True)


def columns_of(shard):
    n_seq, n_dp = lax.axis_size("seq"), lax.axis_size("dp")
    rows, width = shard.shape
    mine = lax.all_to_all(shard, "seq", split_axis=1, concat_axis=0, tiled=True)
    everyone = gather_dp(mine).reshape(n_dp, n_seq, rows, width // n_seq)
    return everyone.transpose(1, 0, 2, 3).reshape(n_seq * n_dp * rows, width // n_seq)


def columns_grad(terms):
    n_seq, n_dp = lax.axis_size("seq"), lax.axis_size("dp")
    total, width = terms.shape
    rows = total // (n_seq * n_dp)
    ordered = terms.astype(BF).reshape(n_seq, n_dp, rows, width).transpose(1, 0, 2, 3)
    summed = scatter_dp(ordered.reshape(total, width))
    mine = lax.all_to_all(summed, "seq", split_axis=0, concat_axis=1, tiled=True)
    return mine.astype(F32)


def local(
    layer_input,
    doc_lengths,
    attention_gain,
    query_down,
    query_gain,
    query_up,
    keyvalue_weight,
    output_weight,
    feedforward_gain,
    gate_weight,
    up_weight,
    down_weight,
    cotangent,
):
    n_seq, n_dp = lax.axis_size("seq"), lax.axis_size("dp")
    n_all = n_seq * n_dp
    tokens = layer_input[0].astype(F32)
    tok_count, width = tokens.shape
    latent_width = query_down.shape[1]
    group_len = tok_count * n_seq
    heads = HEADS // n_seq
    first_tok = lax.axis_index("seq") * tok_count
    starts_all, position_all = document_starts(doc_lengths[0], group_len)
    local_position = lax.dynamic_slice_in_dim(position_all, first_tok, tok_count, 0)
    cosine_all, sine_all = rope_tables(position_all, HEAD_DIM)
    cosine = lax.dynamic_slice_in_dim(cosine_all, first_tok, tok_count, 0)
    sine_part = lax.dynamic_slice_in_dim(sine_all, first_tok, tok_count, 0)

    own_rows = query_down.shape[0]
    gains = jnp.zeros((own_rows, 128), BF)
    gains = gains.at[:, 0].set(attention_gain).at[:, 1].set(feedforward_gain)
    gains = gains.at[: query_gain.shape[0], 2].set(query_gain)
    first_set = jnp.concatenate([query_down, keyvalue_weight, gains], axis=1)
    first_all = lax.all_gather(first_set, ("seq", "dp"), axis=0, tiled=True)
    first_width = latent_width + 2 * HEAD_DIM
    gain_rows = first_all[:, first_width:].T[:8]
    attention_gain_f = gain_rows[0].astype(F32)
    feed_gain_f = gain_rows[1].astype(F32)
    query_gain_f = gain_rows[2].reshape(n_all, own_rows)[:, : query_gain.shape[0]].reshape(-1).astype(F32)

    full_output = gather_dp(output_weight)
    full_query_up = columns_of(query_up)
    full_gate = columns_of(gate_weight)
    full_upper = columns_of(up_weight)
    full_down = gather_dp(down_weight)

    normed_low = rms_norm(tokens, attention_gain_f).astype(BF)
    first_out = matmul(normed_low, first_all)
    latent = first_out[:, :latent_width]
    keyvalue = first_out[:, latent_width:first_width]
    latent_low = rms_norm(latent, query_gain_f).astype(BF)
    key_local = rotate(keyvalue[:, :HEAD_DIM], cosine, sine_part)
    pack = jnp.concatenate([latent_low, key_local.astype(BF), keyvalue[:, HEAD_DIM:].astype(BF)], axis=1)
    pack_all = gather_seq(pack)
    latent_all = pack_all[:, :latent_width]
    keys = pack_all[:, latent_width : latent_width + HEAD_DIM]
    values = pack_all[:, latent_width + HEAD_DIM :]

    query_raw = matmul(latent_all, full_query_up).reshape(group_len, heads, HEAD_DIM)
    query_scale = HEAD_DIM ** (-0.5)
    queries = (
        (rotate(query_raw, cosine_all[:, None, :], sine_all[:, None, :]) * query_scale)
        .astype(BF)
        .reshape(group_len, heads * HEAD_DIM)
    )
    attended, lse = attend(starts_all, queries, keys, values)
    mixed_low = attended.astype(BF)
    hidden = tokens + scatter_seq(matmul(mixed_low, full_output))

    feed_low = rms_norm(hidden, feed_gain_f).astype(BF)
    feed_all = gather_seq(feed_low)
    gate_proj = matmul(feed_all, full_gate)
    upward = matmul(feed_all, full_upper)
    active_low = gated(gate_proj, upward).astype(BF)
    result = hidden + scatter_seq(matmul(active_low, full_down))
    layer_output = result.astype(BF)[None]

    d_result = cotangent[0].astype(F32)
    d_feed_all = gather_seq(cotangent[0])
    d_active = dot_rows(d_feed_all, full_down)
    d_gate, d_upward = jax.vjp(gated, gate_proj, upward)[1](d_active)
    d_gate_low = d_gate.astype(BF)
    d_up_low = d_upward.astype(BF)
    d_feed_normed = scatter_seq(dot_rows(d_gate_low, full_gate) + dot_rows(d_up_low, full_upper))
    d_hidden_norm, grad_feed_gain_term = jax.vjp(rms_norm, hidden, feed_gain_f)[1](d_feed_normed)
    d_hidden = d_result + d_hidden_norm
    grad_down = scatter_dp(dot_cols(active_low, d_feed_all)).astype(F32)
    grad_gate = columns_grad(dot_cols(feed_all, d_gate_low))
    grad_up = columns_grad(dot_cols(feed_all, d_up_low))

    d_branch_all = gather_seq(d_hidden.astype(BF))
    d_mixed = dot_rows(d_branch_all, full_output)
    d_mixed_low = d_mixed.astype(BF)
    offset = jnp.sum(
        (d_mixed_low.astype(F32) * attended).reshape(group_len, heads, HEAD_DIM), axis=2
    ).T
    grad_output_weight = scatter_dp(dot_cols(mixed_low, d_branch_all)).astype(F32)
    d_queries, d_keys, d_values = attend_back(
        starts_all, queries, d_mixed_low, lse, offset, keys, values
    )
    d_query_raw = rotate(
        d_queries.reshape(group_len, heads, HEAD_DIM) * query_scale,
        cosine_all[:, None, :],
        -sine_all[:, None, :],
    )
    d_query_low = d_query_raw.reshape(group_len, heads * HEAD_DIM).astype(BF)
    back_pack = jnp.concatenate([dot_rows(d_query_low, full_query_up), d_keys, d_values], axis=1)
    back_local = scatter_seq(back_pack)
    grad_query_up = columns_grad(dot_cols(latent_all, d_query_low))
    d_latent_normed = back_local[:, :latent_width]
    d_pairs = back_local[:, latent_width:]
    d_key_raw = rotate(d_pairs[:, :HEAD_DIM], cosine, -sine_part)
    d_keyvalue_low = jnp.concatenate([d_key_raw, d_pairs[:, HEAD_DIM:]], axis=1).astype(BF)
    d_latent, grad_query_gain_term = jax.vjp(rms_norm, latent, query_gain_f)[1](d_latent_normed)
    d_first_low = jnp.concatenate(
        [d_latent.astype(BF), d_keyvalue_low, jnp.zeros((tok_count, 128), BF)], axis=1
    )
    d_normed = dot_rows(d_first_low, first_all)
    d_tokens, grad_attention_gain_term = jax.vjp(rms_norm, tokens, attention_gain_f)[1](d_normed)
    input_grad = (d_hidden + d_tokens)[None]

    grad_first_term = dot_cols(normed_low, d_first_low)
    query_gain_column = jnp.zeros((n_all, own_rows), F32)
    query_gain_column = query_gain_column.at[:, : query_gain.shape[0]].set(
        grad_query_gain_term.reshape(n_all, -1)
    )
    gain_columns = jnp.stack(
        [grad_attention_gain_term, grad_feed_gain_term, query_gain_column.reshape(-1)], axis=1
    )
    grad_first_term = grad_first_term.at[:, first_width : first_width + 3].set(gain_columns)
    grad_first = scatter_dp(scatter_seq(grad_first_term)).astype(F32)
    return (
        layer_output,
        input_grad,
        grad_first[:, first_width],
        grad_first[:, :latent_width],
        grad_first[: query_gain.shape[0], first_width + 2],
        grad_query_up,
        grad_first[:, latent_width:first_width],
        grad_output_weight,
        grad_first[:, first_width + 1],
        grad_gate,
        grad_up,
        grad_down,
    )


def solution(mesh):
    shards = P(("seq", "dp"))
    tokens = P("dp", "seq", None)
    weight = P(("seq", "dp"), None)
    return jax.shard_map(
        local,
        mesh=mesh,
        in_specs=(
            tokens,
            P("dp", None),
            shards,
            weight,
            shards,
            weight,
            weight,
            weight,
            shards,
            weight,
            weight,
            weight,
            tokens,
        ),
        out_specs=(
            tokens,
            tokens,
            shards,
            weight,
            shards,
            weight,
            weight,
            weight,
            shards,
            weight,
            weight,
            weight,
        ),
        check_vma=False,
    )
```

time: 5320 us -> 1260 us (0.24)
  waiting for transfers between devices: 4930 us -> 869 us
  matrix products: 247 us -> 134 us
    reduce_scatter x8 -> x10, waiting for transfers between devices: 4250 us -> 417 us  [the longest x5 235 us: scatter_seq(): lax.psum_scatter(terms.astype(BF), 'seq', scatter_dimension=0, tiled=True)]
    all_gather x8 -> x10, waiting for transfers between devices: 665 us -> 423 us  [the longest x5 192 us: gather_dp(): return lax.all_gather(rows, 'dp', axis=0, tiled=True)]
    unnamed x2 -> x0, blocking collectives: 82 us -> none
    dot_general x9 -> x6, matrix products: 92.7 us -> 39.4 us  [dot_cols(): lax.dot_general(left_side, right_side, (((0,), (0,)), ((), ())), preferre...]
  transfers between devices with their start and end apart: 16 -> 25, of which waited for: 15 -> 23; matrix products, arithmetic and copies ran while one was open for 4% -> 12% of each run, Pallas kernels for 0% -> 2%
where the time goes in v1:
time: 1260 us; the launch traced here: 1250 us
  waiting for transfers between devices  869 us (69%)
  matrix products  134 us (11%)
  local copies, waits for them, and re-layouts  80.6 us (6%)
  other arithmetic  49.9 us (4%)
  Pallas kernels  47.9 us (4%)
  blocking collectives  40.4 us (3%)
  starting transfers between devices  17.7 us (1%)
  between operations  15.4 us (1%)
    reduce_scatter x5, waiting for transfers between devices, scatter_seq(): lax.psum_scatter(terms.astype(BF), 'seq', scatter_dimension=0, tiled=True)  235 us
    all_gather x5, waiting for transfers between devices, gather_dp(): return lax.all_gather(rows, 'dp', axis=0, tiled=True)  192 us
    reduce_scatter x5, waiting for transfers between devices, scatter_dp(): lax.psum_scatter(terms.astype(BF), 'dp', scatter_dimension=0, tiled=True)  182 us
    all_gather x4, waiting for transfers between devices, gather_seq(): return lax.all_gather(rows, 'seq', axis=0, tiled=True)  171 us
    all_gather x1, waiting for transfers between devices, local(): first_all = lax.all_gather(first_set, ('seq', 'dp'), axis=0, tiled=True)  59.9 us
    dot_general x6, matrix products, dot_rows(): lax.dot_general(left_side, right_side, (((1,), (1,)), ((), ())), preferre...  50.1 us
    dot_general x6, matrix products, matmul(): return jnp.dot(left_side, right_side, preferred_element_type=F32)  44 us
    all_to_all x2, blocking collectives, columns_of(): mine = lax.all_to_all(shard, 'seq', split_axis=1, concat_axis=0, tiled=True)  40.4 us
  transfers between devices with their start and end apart: 25, of which 23 were waited for; matrix products, arithmetic and copies ran while one was open for 12% of the time, Pallas kernels for 2%

profile of v1, /device:TPU:0, one launch (start us, length us, event | category | flops | bytes accessed | tf_op | source)
XLA Modules:
  0.0 1254.6 jit_solution(6273798243834863849)
XLA Ops:
  13.1 2.7 broadcast_select_fusion.1
  20.6 5.2 all-to-all-start
  27.5 4.2 fusion.38
  33.5 59.9 %all-gather.12.cloned.1.call-done = bf16[2048,1664]{1,0:T(8,128)(2,1)} async-done(((bf16[64,1664]{1,0:T(8,128)(2,1)}), bf16[2048,1664]{1,0:T(8,128)(2,1)}) %all-gather.12.cloned.1.call-update) | async-done | bytes 6815760 | tf_op jit(solution)/shard_map/all_gather | solution.py:269
  95.6 4.6 fusion.41
  104.1 18.1 %all-gather.16.cloned.1.call-done = bf16[1024,512]{1,0:T(8,128)(2,1)} async-done(((bf16[256,512]{1,0:T(8,128)(2,1)}), bf16[1024,512]{1,0:T(8,128)(2,1)}) %all-gather.16.cloned.1.call-update) | async-done | bytes 1048592 | tf_op jit(solution)/shard_map/all_gather | solution.py:210
  124.8 38.2 %all-gather.14.cloned.1.call-done = bf16[1536,1536]{1,0:T(8,128)(2,1)} async-done(((bf16[192,1536]{1,0:T(8,128)(2,1)}), bf16[1536,1536]{1,0:T(8,128)(2,1)}) %all-gather.14.cloned.1.call-update) | async-done | bytes 4718608 | tf_op jit(solution)/shard_map/all_gather | solution.py:202
  163.0 4.0 fusion.12
  168.6 2.7 fusion.51
  173.0 24.7 %attend.1 = (f32[1536,512]{1,0:T(8,128)S(1)}, f32[2,1536]{1,0:T(2,128)S(1)}) custom-call(s32[1,1536]{1,0:T(1,128)S(1)} %reshape.429.starts_ref, bf16[1536,512]{1,0:T(8,128)(2,1)S(1)} %copy.145.q_ref, bf16[1536,256]{1,0:T(8,128)(2,1)S(1)} %get-tuple-element.157.k_ref, bf16[256,1536]{1,0:T(8,128)(2,1)S(1)} %copy.122.vt_ref), custom_call_target="tpu_custom_call" | custom-call | flops 2415919104 | bytes 6291456 | tf_op jit(solution)/shard_map/attend/pallas_call | solution.py:113
  199.2 11.1 all-gather.18.cloned.1.call-done
  210.4 8.7 convolution_convert_fusion.1
  221.0 16.2 %all_to_all.96 = bf16[64,8,704]{2,0,1:T(8,128)(2,1)} all-to-all(bf16[64,8,704]{2,0,1:T(8,128)(2,1)S(1)} %copy.123), channel_id=1, replica_groups=mesh['seq'=8,'dp'=4] {'seq'}, dimensions={1} | all-to-all | bytes 1441792 | tf_op jit(solution)/shard_map/all_to_all | solution.py:220
  238.2 24.2 %all_to_all.97 = bf16[64,8,704]{2,0,1:T(8,128)(2,1)} all-to-all(bf16[64,8,704]{2,0,1:T(8,128)(2,1)S(1)} %copy.125), channel_id=1, replica_groups=mesh['seq'=8,'dp'=4] {'seq'}, dimensions={1} | all-to-all | bytes 1441792 | tf_op jit(solution)/shard_map/all_to_all | solution.py:220
  262.5 24.1 %reduce-scatter.14.cloned.1.call-done = bf16[192,2048]{1,0:T(8,128)(2,1)} async-done(((bf16[1536,2048]{1,0:T(8,128)(2,1)}), bf16[192,2048]{1,0:T(8,128)(2,1)}) %reduce-scatter.14.cloned.1.call-update) | async-done | bytes 786448 | tf_op jit(solution)/shard_map/reduce_scatter | solution.py:206
  288.0 2.3 multiply_convert_fusion.2
  291.9 59.6 %all-gather.22.cloned.1.call-done = bf16[2048,704]{1,0:T(8,128)(2,1)} async-done(((bf16[512,704]{1,0:T(8,128)(2,1)}), bf16[2048,704]{1,0:T(8,128)(2,1)}) %all-gather.22.cloned.1.call-update) | async-done | bytes 2883600 | tf_op jit(solution)/shard_map/all_gather | solution.py:210
  351.6 3.9 copy.124
  355.5 59.9 %all-gather.24.cloned.1.call-done = bf16[2048,704]{1,0:T(8,128)(2,1)} async-done(((bf16[512,704]{1,0:T(8,128)(2,1)}), bf16[2048,704]{1,0:T(8,128)(2,1)}) %all-gather.24.cloned.1.call-update) | async-done | bytes 2883600 | tf_op jit(solution)/shard_map/all_gather | solution.py:210
  415.4 3.8 copy.126
  419.2 43.0 %all-gather.20.cloned.1.call-done = bf16[1536,2048]{1,0:T(8,128)(2,1)} async-done(((bf16[192,2048]{1,0:T(8,128)(2,1)}), bf16[1536,2048]{1,0:T(8,128)(2,1)}) %all-gather.20.cloned.1.call-update) | async-done | bytes 6291472 | tf_op jit(solution)/shard_map/all_gather | solution.py:202
  462.2 10.5 fusion.54
  472.7 6.8 fusion.53
  479.5 43.5 %all-gather.26.cloned.1.call-done = bf16[704,2048]{1,0:T(8,128)(2,1)} async-done(((bf16[176,2048]{1,0:T(8,128)(2,1)}), bf16[704,2048]{1,0:T(8,128)(2,1)}) %all-gather.26.cloned.1.call-update) | async-done | bytes 2883600 | tf_op jit(solution)/shard_map/all_gather | solution.py:210
  523.1 46.1 %all-gather.30.cloned.1.call-done = bf16[1,1536,2048]{2,1,0:T(8,128)(2,1)} async-done(((bf16[1,192,2048]{2,1,0:T(8,128)(2,1)}), bf16[1,1536,2048]{2,1,0:T(8,128)(2,1)}) %all-gather.30.cloned.1.call-update) | async-done | bytes 6291472 | tf_op jit(solution)/shard_map/all_gather | solution.py:202
  569.2 14.5 %multiply_convert_fusion = (bf16[1536,704]{0,1:T(8,128)(2,1)}, bf16[1536,704]{0,1:T(8,128)(2,1)S(1)}, bf16[1536,704]{0,1:T(8,128)(2,1)}) fusion(f32[1536,704]{0,1:T(8,128)} %fusion.53, f32[1536,704]{0,1:T(8,128)} %fusion.54, bf16[704,2048]{1,0:T(8,128)(2,1)} %all-gather.26.cloned.1.call-done, bf16[1,1536,2048]{2,1,0:T(8,128)(2,1)} %all-gather.30.cloned.1.call-done), kind=kOutput, calls=%fused_computation.12 | convolution fusion | flops 4446486528 | bytes 24313856 | tf_op jit(solution)/shard_map/dot_general | solution.py:62
  583.7 5.2 fusion.55
  588.9 9.5 add_convert_fusion
  598.5 61.8 %reduce-scatter.18.cloned.1.call-done = bf16[192,2048]{1,0:T(8,128)(2,1)} async-done(((bf16[1536,2048]{1,0:T(8,128)(2,1)}), bf16[192,2048]{1,0:T(8,128)(2,1)}) %reduce-scatter.18.cloned.1.call-update) | async-done | bytes 786448 | tf_op jit(solution)/shard_map/reduce_scatter | solution.py:206
  664.2 2.3 copy.131
  666.5 43.3 %all-gather.28.cloned.1.call-done = bf16[1536,2048]{1,0:T(8,128)(2,1)} async-done(((bf16[192,2048]{1,0:T(8,128)(2,1)}), bf16[1536,2048]{1,0:T(8,128)(2,1)}) %all-gather.28.cloned.1.call-update) | async-done | bytes 6291472 | tf_op jit(solution)/shard_map/all_gather | solution.py:202
  709.8 9.9 convert_multiply_fusion.4
  719.7 5.3 reshape.441
  725.1 4.3 reduce_sum.105
  733.3 23.3 %attend_back.1 = (f32[1536,512]{1,0:T(8,128)S(1)}, f32[1536,256]{1,0:T(8,128)S(1)}, f32[1536,256]{1,0:T(8,128)S(1)}) custom-call(s32[1,1536]{1,0:T(1,128)S(1)} %reshape.429.starts_ref, bf16[1536,512]{1,0:T(8,128)(2,1)S(1)} %copy.145.q_ref, bf16[1536,512]{1,0:T(8,128)(2,1)S(1)} %copy-done.7, f32[2,1536]{1,0:T(2,128)S(1)} %get-tuple-element.78.lse_ref, ...), custom_call_target="tpu_custom_call" | custom-call | flops 6039797760 | bytes 9437184 | tf_op jit(solution)/shard_map/attend_back/pallas_call | solution.py:181
  759.7 3.7 copy.148
  769.9 2.3 pad_maximum_fusion
  773.8 8.8 convolution_convert_fusion.3
  782.6 3.3 copy.138
  789.4 8.7 convolution_convert_fusion.4
  798.1 3.1 copy.135
  804.0 22.3 %reduce-scatter.20.cloned.1.call-done = bf16[192,1536]{1,0:T(8,128)(2,1)} async-done(((bf16[1536,1536]{1,0:T(8,128)(2,1)}), bf16[192,1536]{1,0:T(8,128)(2,1)}) %reduce-scatter.20.cloned.1.call-update) | async-done | bytes 589840 | tf_op jit(solution)/shard_map/reduce_scatter | solution.py:206
  831.7 2.1 fusion.39
  833.9 9.1 fusion.22
  846.7 8.7 fusion.8
  856.8 3.7 fusion.30
  862.8 7.5 convolution_convert_fusion.5
  870.4 9.4 convolution_convert_fusion
  879.8 9.1 reduce-scatter.30.cloned.1.call-done
  888.8 3.7 all-to-all-start.5
  892.5 58.9 %reduce-scatter.28.cloned.1.call-done = bf16[512,704]{1,0:T(8,128)(2,1)} async-done(((bf16[2048,704]{1,0:T(8,128)(2,1)}), bf16[512,704]{1,0:T(8,128)(2,1)}) %reduce-scatter.28.cloned.1.call-update) | async-done | bytes 720912 | tf_op jit(solution)/shard_map/reduce_scatter | solution.py:214
  951.4 3.7 all-to-all-start.4
  955.1 64.3 %reduce-scatter.22.cloned.1.call-done = bf16[256,1664]{0,1:T(8,128)(2,1)} async-done(((bf16[2048,1664]{0,1:T(8,128)(2,1)}), bf16[256,1664]{0,1:T(8,128)(2,1)}) %reduce-scatter.22.cloned.1.call-update) | async-done | bytes 851984 | tf_op jit(solution)/shard_map/reduce_scatter | solution.py:206
  1019.4 2.2 copy.146
  1021.6 56.1 %reduce-scatter.32.cloned.1.call-done = bf16[176,2048]{1,0:T(8,128)(2,1)} async-done(((bf16[704,2048]{1,0:T(8,128)(2,1)}), bf16[176,2048]{1,0:T(8,128)(2,1)}) %reduce-scatter.32.cloned.1.call-update) | async-done | bytes 720912 | tf_op jit(solution)/shard_map/reduce_scatter | solution.py:214
  1077.8 2.4 convert_element_type.214
  1082.9 24.7 %reduce-scatter.24.cloned.1.call-done = bf16[256,512]{1,0:T(8,128)(2,1)} async-done(((bf16[1024,512]{1,0:T(8,128)(2,1)}), bf16[256,512]{1,0:T(8,128)(2,1)}) %reduce-scatter.24.cloned.1.call-update) | async-done | bytes 262160 | tf_op jit(solution)/shard_map/reduce_scatter | solution.py:214
  1107.5 3.6 all-to-all-start.3
  1113.9 4.2 all-to-all-done.3
  1119.0 33.5 %reduce-scatter.26.cloned.1.call-done = bf16[128,2048]{1,0:T(8,128)(2,1)} async-done(((bf16[512,2048]{1,0:T(8,128)(2,1)}), bf16[128,2048]{1,0:T(8,128)(2,1)}) %reduce-scatter.26.cloned.1.call-update) | async-done | bytes 524304 | tf_op jit(solution)/shard_map/reduce_scatter | solution.py:214
  1152.4 2.1 convert_element_type.204
  1154.6 62.2 %reduce-scatter.16.cloned.1.call-done = bf16[192,2048]{1,0:T(8,128)(2,1)} async-done(((bf16[1536,2048]{1,0:T(8,128)(2,1)}), bf16[192,2048]{1,0:T(8,128)(2,1)}) %reduce-scatter.16.cloned.1.call-update) | async-done | bytes 786448 | tf_op jit(solution)/shard_map/reduce_scatter | solution.py:206
  1216.8 4.2 fusion.27
  1221.0 22.4 %reduce-scatter.34.cloned.1.call-done = bf16[64,1664]{1,0:T(8,128)(2,1)} async-done(((bf16[256,1664]{1,0:T(8,128)(2,1)}), bf16[64,1664]{1,0:T(8,128)(2,1)}) %reduce-scatter.34.cloned.1.call-update) | async-done | bytes 213008
  (244 shorter events, 81.9 us)
Async XLA Ops:
  7.2 24.5 %copy-start.8 = (bf16[1,192,2048]{2,1,0:T(8,128)(2,1)S(1)}, bf16[1,192,2048]{2,1,0:T(8,128)(2,1)}, u32[]{:S(2)}) copy-start(bf16[1,192,2048]{2,1,0:T(8,128)(2,1)} %param.23) | copy-start | bytes 2359300
  7.2 86.2 %all-gather.12.cloned.1.call-start = ((), (), s32[]{:S(2)}) async-start(), calls=%async_computation.17 | async-start | bytes 7028736 | tf_op jit(solution)/shard_map/all_gather | solution.py:269
  20.6 12.1 all-to-all-start
  25.8 96.3 %all-gather.16.cloned.1.call-start = ((), (), s32[]{:S(2)}) async-start(), calls=%async_computation.19 | async-start | bytes 1310720 | tf_op jit(solution)/shard_map/all_gather | solution.py:210
  31.6 71.8 %copy-start.25 = (f32[1536,128]{1,0:T(8,128)}, f32[1536,128]{1,0:T(8,128)S(1)}, u32[]{:S(2)}) copy-start(f32[1536,128]{1,0:T(8,128)S(1)} %get-tuple-element.168) | copy-start | bytes 2359300
  31.6 72.1 %copy-start.24 = (f32[1536,128]{1,0:T(8,128)}, f32[1536,128]{1,0:T(8,128)S(1)}, u32[]{:S(2)}) copy-start(f32[1536,128]{1,0:T(8,128)S(1)} %get-tuple-element.167) | copy-start | bytes 2359300
  31.9 62.6 %copy-start.45 = (f32[192]{0:T(256)}, f32[192]{0:T(256)S(1)}, u32[]{:S(2)}) copy-start(f32[192]{0:T(256)S(1)} %fusion.28) | copy-start | bytes 2308
  31.9 68.3 %copy-start.43 = (f32[192]{0:T(256)}, f32[192]{0:T(256)S(1)}, u32[]{:S(2)}) copy-start(f32[192]{0:T(256)S(1)} %fusion.45) | copy-start | bytes 2308
  33.5 129.5 %all-gather.14.cloned.1.call-start = ((), (), s32[]{:S(2)}) async-start(), calls=%async_computation.18 | async-start | bytes 5308416 | tf_op jit(solution)/shard_map/all_gather | solution.py:202
  95.4 4.8 copy-start.37
  95.6 5.5 copy-start.39
  100.4 3.1 copy-start.41
  102.3 108.1 %all-gather.18.cloned.1.call-start = ((), (), s32[]{:S(2)}) async-start(), calls=%async_computation.20 | async-start | bytes 2621440 | tf_op jit(solution)/shard_map/all_gather | solution.py:210
  102.9 183.6 %reduce-scatter.14.cloned.1.call-start = ((), (), s32[]{:S(2)}) async-start(), calls=%async_computation.21 | async-start | bytes 7077888 | tf_op jit(solution)/shard_map/reduce_scatter | solution.py:206
  103.8 63.2 %copy-start.22 = (f32[1536,128]{0,1:T(8,128)}, f32[1536,128]{0,1:T(8,128)S(1)}, u32[]{:S(2)}) copy-start(f32[1536,128]{0,1:T(8,128)S(1)} %copy.119) | copy-start | bytes 2359300
  123.5 43.5 %copy-start.26 = (bf16[8,4,32,512]{3,2,1,0:T(8,128)(2,1)}, bf16[8,4,32,512]{3,2,1,0:T(8,128)(2,1)S(1)}, u32[]{:S(2)}) copy-start(bf16[8,4,32,512]{3,2,1,0:T(8,128)(2,1)S(1)} %copy.117) | copy-start | bytes 3145732
  171.2 26.4 %copy-start.3 = (bf16[1536,256]{1,0:T(8,128)(2,1)}, bf16[1536,256]{1,0:T(8,128)(2,1)S(1)}, u32[]{:S(2)}) copy-start(bf16[1536,256]{1,0:T(8,128)(2,1)S(1)} %get-tuple-element.157.k_ref) | copy-start | bytes 2359300
  219.1 132.5 %all-gather.22.cloned.1.call-start = ((), (), s32[]{:S(2)}) async-start(), calls=%async_computation.23 | async-start | bytes 3932160 | tf_op jit(solution)/shard_map/all_gather | solution.py:210
  221.0 16.3 %copy-start.36 = (bf16[64,5632]{1,0:T(8,128)(2,1)S(1)}, bf16[64,5632]{1,0:T(8,128)(2,1)}, u32[]{:S(2)}) copy-start(bf16[64,5632]{1,0:T(8,128)(2,1)} %param.33) | copy-start | bytes 2162692
  237.3 178.1 %all-gather.24.cloned.1.call-start = ((), (), s32[]{:S(2)}) async-start(), calls=%async_computation.24 | async-start | bytes 3932160 | tf_op jit(solution)/shard_map/all_gather | solution.py:210
  238.0 48.5 %copy-start.9 = (bf16[1,192,2048]{2,1,0:T(8,128)(2,1)S(1)}, bf16[1,192,2048]{2,1,0:T(8,128)(2,1)}, u32[]{:S(2)}) copy-start(bf16[1,192,2048]{2,1,0:T(8,128)(2,1)} %param.23) | copy-start | bytes 2359300
  262.4 199.8 %all-gather.20.cloned.1.call-start = ((), (), s32[]{:S(2)}) async-start(), calls=%async_computation.22 | async-start | bytes 7077888 | tf_op jit(solution)/shard_map/all_gather | solution.py:202
  290.4 232.7 %all-gather.26.cloned.1.call-start = ((), (), s32[]{:S(2)}) async-start(), calls=%async_computation.25 | async-start | bytes 3604480 | tf_op jit(solution)/shard_map/all_gather | solution.py:210
  291.1 278.1 %all-gather.30.cloned.1.call-start = ((), (), s32[]{:S(2)}) async-start(), calls=%async_computation.36 | async-start | bytes 7077888 | tf_op jit(solution)/shard_map/all_gather | solution.py:202
  291.7 368.7 %reduce-scatter.18.cloned.1.call-start = ((), (), s32[]{:S(2)}) async-start(), calls=%async_computation.27 | async-start | bytes 7077888 | tf_op jit(solution)/shard_map/reduce_scatter | solution.py:206
  462.2 10.5 copy-start.29
  462.2 10.5 copy-start.49
  569.2 14.5 %copy-start.30 = (bf16[4,8,64,704]{3,2,0,1:T(8,128)(2,1)S(1)}, bf16[4,8,64,704]{3,2,0,1:T(8,128)(2,1)}, u32[]{:S(2)}) copy-start(bf16[4,8,64,704]{3,2,0,1:T(8,128)(2,1)} %copy.124) | copy-start | bytes 8650756
  583.7 5.2 copy-start.50
  583.7 5.2 copy-start.31
  598.5 61.9 %copy-start.13 = (bf16[192,2048]{1,0:T(8,128)(2,1)S(1)}, bf16[192,2048]{1,0:T(8,128)(2,1)}, u32[]{:S(2)}) copy-start(bf16[192,2048]{1,0:T(8,128)(2,1)} %reduce-scatter.14.cloned.1.call-done) | copy-start | bytes 2359300
  598.5 111.3 %all-gather.28.cloned.1.call-start = ((), (), s32[]{:S(2)}) async-start(), calls=%async_computation.28 | async-start | bytes 7077888 | tf_op jit(solution)/shard_map/all_gather | solution.py:202
  660.4 2.0 copy-start.18
  660.4 2.0 copy-start.20
  664.1 162.2 %reduce-scatter.20.cloned.1.call-start = ((), (), s32[]{:S(2)}) async-start(), calls=%async_computation.29 | async-start | bytes 5308416 | tf_op jit(solution)/shard_map/reduce_scatter | solution.py:206
  759.7 3.7 copy-start.1
  763.4 2.1 copy-start.23
  763.4 2.3 copy-start.28
  766.4 3.4 copy-start.32
  772.2 116.6 %reduce-scatter.30.cloned.1.call-start = ((), (), s32[]{:S(2)}) async-start(), calls=%async_computation.34 | async-start | bytes 3932160 | tf_op jit(solution)/shard_map/reduce_scatter | solution.py:214
  787.9 163.5 %reduce-scatter.28.cloned.1.call-start = ((), (), s32[]{:S(2)}) async-start(), calls=%async_computation.33 | async-start | bytes 3932160 | tf_op jit(solution)/shard_map/reduce_scatter | solution.py:214
  803.1 24.4 %copy-start.17 = (f32[192,1664]{1,0:T(8,128)S(1)}, f32[192,1664]{1,0:T(8,128)}, u32[]{:S(2)}) copy-start(f32[192,1664]{1,0:T(8,128)} %copy-done.16) | copy-start | bytes 3833860
  803.1 24.4 %copy-start.40 = (f32[1024]{0:T(1024)S(1)}, f32[1024]{0:T(1024)}, u32[]{:S(2)}) copy-start(f32[1024]{0:T(1024)} %copy-done.39) | copy-start | bytes 12292
  803.1 24.4 %copy-start.42 = (f32[192]{0:T(256)S(1)}, f32[192]{0:T(256)}, u32[]{:S(2)}) copy-start(f32[192]{0:T(256)} %copy-done.41) | copy-start | bytes 2308
  803.1 25.5 %copy-start.48 = (f32[192]{0:T(256)S(1)}, f32[192]{0:T(256)}, u32[]{:S(2)}) copy-start(f32[192]{0:T(256)} %copy-done.47) | copy-start | bytes 2308
  803.1 216.3 %reduce-scatter.22.cloned.1.call-start = ((), (), s32[]{:S(2)}) async-start(), calls=%async_computation.30 | async-start | bytes 7667712 | tf_op jit(solution)/shard_map/reduce_scatter | solution.py:206
  827.5 4.2 copy-start.10
  827.5 4.2 copy-start.38
  827.5 4.2 copy-start.44
  833.8 9.1 copy-start.12
  845.1 232.7 %reduce-scatter.32.cloned.1.call-start = ((), (), s32[]{:S(2)}) async-start(), calls=%async_computation.35 | async-start | bytes 3604480 | tf_op jit(solution)/shard_map/reduce_scatter | solution.py:214
  855.4 252.1 %reduce-scatter.24.cloned.1.call-start = ((), (), s32[]{:S(2)}) async-start(), calls=%async_computation.31 | async-start | bytes 1310720 | tf_op jit(solution)/shard_map/reduce_scatter | solution.py:214
  860.5 2.3 copy-start.6
  861.6 290.8 %reduce-scatter.26.cloned.1.call-start = ((), (), s32[]{:S(2)}) async-start(), calls=%async_computation.32 | async-start | bytes 2621440 | tf_op jit(solution)/shard_map/reduce_scatter | solution.py:214
  870.3 346.5 %reduce-scatter.16.cloned.1.call-start = ((), (), s32[]{:S(2)}) async-start(), calls=%async_computation.26 | async-start | bytes 7077888 | tf_op jit(solution)/shard_map/reduce_scatter | solution.py:206
  888.8 62.6 %all-to-all-start.5 = ((bf16[8,64,704]{2,1,0:T(8,128)(2,1)}), bf16[8,64,704]{2,1,0:T(8,128)(2,1)S(1)}, u32[]{:S(2)}, u32[]{:S(2)}) async-start(bf16[8,64,704]{2,1,0:T(8,128)(2,1)} %bitcast.174), calls=%async_computation.14 | async-start | bytes 1572864 | tf_op jit(solution)/shard_map/all_to_all | solution.py:231
  951.4 131.5 %all-to-all-start.4 = ((bf16[8,64,704]{2,1,0:T(8,128)(2,1)}), bf16[8,64,704]{2,1,0:T(8,128)(2,1)S(1)}, u32[]{:S(2)}, u32[]{:S(2)}) async-start(bf16[8,64,704]{2,1,0:T(8,128)(2,1)} %bitcast.173), calls=%async_computation.12 | async-start | bytes 1572864 | tf_op jit(solution)/shard_map/all_to_all | solution.py:231
  955.1 288.4 %reduce-scatter.34.cloned.1.call-start = ((), (), s32[]{:S(2)}) async-start(), calls=%async_computation.37 | async-start | bytes 1064960
  1107.5 10.6 all-to-all-start.3
  1113.9 40.7 %copy-start.46 = (f32[192]{0:T(256)S(1)}, f32[192]{0:T(256)}, u32[]{:S(2)}) copy-start(f32[192]{0:T(256)} %copy-done.45) | copy-start | bytes 2308
  1113.9 102.9 %copy-start.11 = (bf16[1,192,2048]{2,1,0:T(8,128)(2,1)S(1)}, bf16[1,192,2048]{2,1,0:T(8,128)(2,1)}, u32[]{:S(2)}) copy-start(bf16[1,192,2048]{2,1,0:T(8,128)(2,1)} %param.23) | copy-start | bytes 2359300
  1113.9 102.9 %copy-start.14 = (bf16[192,2048]{1,0:T(8,128)(2,1)S(1)}, bf16[192,2048]{1,0:T(8,128)(2,1)}, u32[]{:S(2)}) copy-start(bf16[192,2048]{1,0:T(8,128)(2,1)} %reduce-scatter.14.cloned.1.call-done) | copy-start | bytes 2359300
  1113.9 102.9 %copy-start.19 = (bf16[1,192,2048]{2,1,0:T(8,128)(2,1)S(1)}, bf16[1,192,2048]{2,1,0:T(8,128)(2,1)}, u32[]{:S(2)}) copy-start(bf16[1,192,2048]{2,1,0:T(8,128)(2,1)} %param.35) | copy-start | bytes 2359300
  1113.9 102.9 %copy-start.21 = (bf16[192,2048]{1,0:T(8,128)(2,1)S(1)}, bf16[192,2048]{1,0:T(8,128)(2,1)}, u32[]{:S(2)}) copy-start(bf16[192,2048]{1,0:T(8,128)(2,1)} %reduce-scatter.18.cloned.1.call-done) | copy-start | bytes 2359300
  (15 other events, 19.9 us)
Sparse Core Ops, SparseCore 0:
  19.1 74.2 all-gather.11
  95.6 26.5 all-gather.15
  124.6 38.3 all-gather.13
  164.4 45.9 all-gather.17
  219.2 67.2 reduce-scatter.13
  288.0 63.4 all-gather.21
  353.2 62.1 all-gather.23
  418.0 44.1 all-gather.19
  463.9 59.1 all-gather.25
  525.0 44.1 all-gather.29
  598.6 61.7 reduce-scatter.17
  664.2 45.5 all-gather.27
  772.4 53.8 reduce-scatter.19
  828.5 60.2 reduce-scatter.29
  891.1 60.2 reduce-scatter.27
  955.1 64.2 reduce-scatter.21
  1021.5 56.1 reduce-scatter.31
  1080.5 26.9 reduce-scatter.23
  1109.9 42.4 reduce-scatter.25
  1155.7 61.0 reduce-scatter.15
  1219.2 24.1 reduce-scatter.33

commit v2 on v1

v2 whole, which is shorter than its diff:
```python
import functools

import jax
import jax.numpy as jnp
from jax import lax
from jax.experimental import pallas as pl
from jax.experimental.pallas import tpu as pltpu
from jax.sharding import PartitionSpec as P

HEADS = 16
HEAD_DIM = 256


EPS = 1e-05
ROPE_BASE = 10000.0
NEGATIVE = -1e30
BF = jnp.bfloat16
F32 = jnp.float32


def rms_norm(values, norm_gain):
    return values * lax.rsqrt(jnp.mean(values * values, axis=-1, keepdims=True) + EPS) * norm_gain


def rope_tables(position, feature_width):
    half_width = feature_width // 2
    freqs = ROPE_BASE ** (-jnp.arange(half_width, dtype=F32) * 2.0 / feature_width)
    angles = position.astype(F32)[:, None] * freqs[None, :]
    return (jnp.cos(angles), jnp.sin(angles))


def rotate(values, cosine, sine_part):
    half_width = values.shape[-1] // 2
    first_half = values[..., :half_width]
    second_half = values[..., half_width:]
    return jnp.concatenate(
        [
            first_half * cosine - second_half * sine_part,
            second_half * cosine + first_half * sine_part,
        ],
        axis=-1,
    )


def document_starts(lengths_row, group_len):
    doc_ends = jnp.cumsum(lengths_row)
    places = jnp.arange(group_len, dtype=jnp.int32)
    past_ends = (places[:, None] >= doc_ends[None, :]).astype(jnp.int32)
    starts = jnp.sum(past_ends * lengths_row[None, :], axis=1)
    return (starts, places - starts)


def gated(gate_proj, upward):
    return jax.nn.silu(gate_proj) * upward


def matmul(left_side, right_side):
    return jnp.dot(left_side, right_side, preferred_element_type=F32)


def dot_rows(left_side, right_side):
    return lax.dot_general(
        left_side, right_side, (((1,), (1,)), ((), ())), preferred_element_type=F32
    )


def dot_cols(left_side, right_side):
    return lax.dot_general(
        left_side, right_side, (((0,), (0,)), ((), ())), preferred_element_type=F32
    )


def flip(block, bits):
    n_seq = lax.axis_size("seq")
    return lax.ppermute(block, "seq", [(i, i ^ bits) for i in range(n_seq)])


def gather_blocks(rows):
    n_seq = lax.axis_size("seq")
    blocks = {0: rows}
    if n_seq == 8:
        half = rows.shape[0] // 2
        blocks[2] = flip(rows, 2)
        blocks[4] = flip(rows, 4)
        blocks[6] = jnp.concatenate([flip(blocks[4][:half], 2), flip(blocks[2][half:], 4)], axis=0)
    else:
        for bits in range(2, n_seq, 2):
            blocks[bits] = flip(rows, bits)
    for bits in range(0, n_seq, 2):
        blocks[bits + 1] = flip(blocks[bits], 1)
    return [blocks[k] for k in range(n_seq)]


def gather_chips(rows):
    blocks = gather_blocks(rows)
    return [
        jnp.concatenate([blocks[k], blocks[k + 1]], axis=0) for k in range(0, len(blocks), 2)
    ]


def plus(first, second):
    return (first.astype(F32) + second.astype(F32)).astype(BF)


def scatter_blocks(terms):
    n_seq = lax.axis_size("seq")
    sums = {}
    for bits in range(n_seq - 2, -1, -2):
        sums[bits] = plus(terms[bits], flip(terms[bits + 1], 1))
    if n_seq == 8:
        half = terms[0].shape[0] // 2
        far_x = flip(sums[6][:half], 2)
        far_y = flip(sums[6][half:], 4)
        from_x = [flip(sums[2][:half], 2), flip(plus(sums[2][half:], far_y), 2)]
        from_y = [flip(plus(sums[4][:half], far_x), 4), flip(sums[4][half:], 4)]
        return sums[0].astype(F32) + jnp.concatenate(
            [x.astype(F32) + y.astype(F32) for x, y in zip(from_x, from_y, strict=True)], axis=0
        )
    total = sums[0].astype(F32)
    for bits in range(2, n_seq, 2):
        total = total + flip(sums[bits], bits).astype(F32)
    return total


def scatter_chips(terms):
    rows = terms[0].shape[0] // 2
    return scatter_blocks([part for term in terms for part in (term[:rows], term[rows:])])


def relative(values, axis):
    n_seq, me = lax.axis_size("seq"), lax.axis_index("seq")
    size = values.shape[axis] // n_seq
    parts = [
        lax.dynamic_slice_in_dim(values, (me ^ k) * size, size, axis) for k in range(n_seq)
    ]
    return jnp.concatenate(parts, axis=axis)


def gather_dp(rows):
    return lax.all_gather(rows, "dp", axis=0, tiled=True)


def scatter_dp(terms):
    return lax.psum_scatter(terms, "dp", scatter_dimension=0, tiled=True)


def split_columns(shard):
    n_seq = lax.axis_size("seq")
    rows, width = shard.shape
    parts = shard.reshape(rows, n_seq, width // n_seq).transpose(1, 0, 2)
    return lax.all_to_all(parts, "seq", 0, 0).reshape(n_seq * rows, width // n_seq)


def join_columns(parts):
    n_seq = lax.axis_size("seq")
    rows, width = parts.shape
    back = lax.all_to_all(parts.reshape(n_seq, rows // n_seq, width), "seq", 0, 0)
    return back.transpose(1, 0, 2)


def rows_in_order(gathered, rows):
    n_seq, n_dp = lax.axis_size("seq"), lax.axis_size("dp")
    width = gathered.shape[1]
    return (
        gathered.reshape(n_dp, n_seq, rows, width).transpose(1, 0, 2, 3).reshape(-1, width)
    )


def rows_by_dp(terms):
    n_seq, n_dp = lax.axis_size("seq"), lax.axis_size("dp")
    total, width = terms.shape
    rows = total // (n_seq * n_dp)
    return terms.reshape(n_seq, n_dp, rows, width).transpose(1, 0, 2, 3).reshape(total, width)


def block_places(shape, axis, core):
    rows = lax.broadcasted_iota(jnp.int32, shape, axis)
    half = shape[axis] // 2
    return rows + core * jnp.where(rows < half, half, -half)


def attend_kernel(heads, block, me_ref, starts_ref, q_ref, k_ref, vt_ref, out_ref, lse_ref):
    me = me_ref[0]
    chip, core = me >> 1, me & 1
    at = pl.program_id(0) ^ chip
    starts_row = starts_ref[...]
    key_place = block_places((block, 1), 0, core)
    query_place = at * block + block_places((1, block), 1, core)
    columns = [slice(h * HEAD_DIM, (h + 1) * HEAD_DIM) for h in range(heads)]

    def step(b, running):
        here = pl.ds(pl.multiple_of((b ^ chip) * block, block), block)
        keys_here = b * block + key_place
        visible = (keys_here <= query_place) & (keys_here >= starts_row)
        result = []
        for head in range(heads):
            running_max, running_sum, total = running[head]
            scores = dot_rows(k_ref[here, :], q_ref[:, columns[head]])
            scores = jnp.where(visible, scores, NEGATIVE)
            new_max = jnp.maximum(running_max, jnp.max(scores, axis=0, keepdims=True))
            factor = jnp.exp(running_max - new_max)
            terms = jnp.where(visible, jnp.exp(scores - new_max), 0.0)
            running_sum = running_sum * factor + jnp.sum(terms, axis=0, keepdims=True)
            total = total * factor + matmul(vt_ref[:, here], terms.astype(BF))
            result.append((new_max, running_sum, total))
        return tuple(result)

    start = (
        jnp.full((1, block), NEGATIVE, F32),
        jnp.zeros((1, block), F32),
        jnp.zeros((HEAD_DIM, block), F32),
    )
    running = lax.fori_loop(0, at + 1, step, (start,) * heads)
    for head in range(heads):
        running_max, running_sum, total = running[head]
        out_ref[:, columns[head]] = (total / running_sum).T
        lse_ref[head : head + 1, :] = running_max + jnp.log(running_sum)


def attend(me, starts, queries, keys, values, block):
    group_len, width = queries.shape
    heads = width // HEAD_DIM
    return pl.pallas_call(
        functools.partial(attend_kernel, heads, block),
        grid_spec=pltpu.PrefetchScalarGridSpec(
            num_scalar_prefetch=1,
            grid=(group_len // block,),
            in_specs=[
                pl.BlockSpec((1, block), lambda i, me: (0, i)),
                pl.BlockSpec((block, width), lambda i, me: (i, 0)),
                pl.BlockSpec((group_len, HEAD_DIM), lambda i, me: (0, 0)),
                pl.BlockSpec((HEAD_DIM, group_len), lambda i, me: (0, 0)),
            ],
            out_specs=[
                pl.BlockSpec((block, width), lambda i, me: (i, 0)),
                pl.BlockSpec((heads, block), lambda i, me: (0, i)),
            ],
        ),
        out_shape=[
            jax.ShapeDtypeStruct((group_len, width), F32),
            jax.ShapeDtypeStruct((heads, group_len), F32),
        ],
        compiler_params=pltpu.CompilerParams(vmem_limit_bytes=32 * 2**20),
        cost_estimate=pl.CostEstimate(
            flops=2 * group_len * group_len * width,
            bytes_accessed=group_len * width * 8,
            transcendentals=heads * group_len * group_len // 2,
        ),
        name="attend",
    )(me, starts.reshape(1, group_len), queries, keys, values.T)


def attend_back_kernel(
    heads,
    block,
    me_ref,
    starts_ref,
    q_ref,
    dm_ref,
    lse_ref,
    off_ref,
    k_ref,
    v_ref,
    dq_ref,
    dk_ref,
    dv_ref,
):
    me = me_ref[0]
    chip, core = me >> 1, me & 1
    at = pl.program_id(0) ^ chip

    @pl.when(pl.program_id(0) == 0)
    def _():
        dk_ref[...] = jnp.zeros_like(dk_ref)
        dv_ref[...] = jnp.zeros_like(dv_ref)

    starts_row = starts_ref[...]
    key_place = block_places((block, 1), 0, core)
    query_place = at * block + block_places((1, block), 1, core)
    columns = [slice(h * HEAD_DIM, (h + 1) * HEAD_DIM) for h in range(heads)]

    def step(b, running):
        here = pl.ds(pl.multiple_of((b ^ chip) * block, block), block)
        keys_here = b * block + key_place
        visible = (keys_here <= query_place) & (keys_here >= starts_row)
        keys, values = k_ref[here, :], v_ref[here, :]
        result = []
        for head in range(heads):
            q, dm = q_ref[:, columns[head]], dm_ref[:, columns[head]]
            scores = dot_rows(keys, q)
            scores = jnp.where(visible, scores, NEGATIVE)
            probs = jnp.where(visible, jnp.exp(scores - lse_ref[head : head + 1, :]), 0.0)
            d_probs = dot_rows(values, dm)
            d_scores = (probs * (d_probs - off_ref[head : head + 1, :])).astype(BF)
            dv_ref[here, :] += matmul(probs.astype(BF), dm)
            dk_ref[here, :] += matmul(d_scores, q)
            result.append(running[head] + dot_cols(d_scores, keys))
        return tuple(result)

    start = (jnp.zeros((block, HEAD_DIM), F32),) * heads
    d_queries = lax.fori_loop(0, at + 1, step, start)
    for head in range(heads):
        dq_ref[:, columns[head]] = d_queries[head]


def attend_back(me, starts, queries, d_mixed, lse, offset, keys, values, block):
    group_len, width = queries.shape
    heads = width // HEAD_DIM
    whole = pl.BlockSpec((group_len, HEAD_DIM), lambda i, me: (0, 0))
    rows = pl.BlockSpec((block, width), lambda i, me: (i, 0))
    lanes = pl.BlockSpec((heads, block), lambda i, me: (0, i))
    first = pl.BlockSpec((1, block), lambda i, me: (0, i))
    return pl.pallas_call(
        functools.partial(attend_back_kernel, heads, block),
        grid_spec=pltpu.PrefetchScalarGridSpec(
            num_scalar_prefetch=1,
            grid=(group_len // block,),
            in_specs=[first, rows, rows, lanes, lanes, whole, whole],
            out_specs=[rows, whole, whole],
        ),
        out_shape=[
            jax.ShapeDtypeStruct((group_len, width), F32),
            jax.ShapeDtypeStruct((group_len, HEAD_DIM), F32),
            jax.ShapeDtypeStruct((group_len, HEAD_DIM), F32),
        ],
        compiler_params=pltpu.CompilerParams(vmem_limit_bytes=32 * 2**20),
        cost_estimate=pl.CostEstimate(
            flops=5 * group_len * group_len * width,
            bytes_accessed=group_len * width * 12,
            transcendentals=heads * group_len * group_len // 2,
        ),
        name="attend_back",
    )(me, starts.reshape(1, group_len), queries, d_mixed, lse, offset, keys, values)


def local(
    layer_input,
    doc_lengths,
    attention_gain,
    query_down,
    query_gain,
    query_up,
    keyvalue_weight,
    output_weight,
    feedforward_gain,
    gate_weight,
    up_weight,
    down_weight,
    cotangent,
):
    n_seq, n_dp = lax.axis_size("seq"), lax.axis_size("dp")
    me = lax.axis_index("seq")
    chips = range(n_seq // 2)
    input_low = layer_input[0]
    tokens = input_low.astype(F32)
    tok_count, width = tokens.shape
    latent_width = query_down.shape[1]
    group_len = tok_count * n_seq
    heads = HEADS // n_seq
    hidden_units = gate_weight.shape[1] // n_seq

    starts_all, position_all = document_starts(doc_lengths[0], group_len)
    starts_all = relative(starts_all, 0)
    position_all = relative(position_all, 0)
    cosine_all, sine_all = rope_tables(position_all, HEAD_DIM)
    cosine, sine_part = cosine_all[:tok_count], sine_all[:tok_count]
    me_array = me.astype(jnp.int32).reshape(1)

    own_rows = query_down.shape[0]
    query_rows = query_gain.shape[0]
    gains = jnp.stack(
        [attention_gain, feedforward_gain, jnp.pad(query_gain, (0, own_rows - query_rows))], axis=1
    )
    first_set = jnp.concatenate(
        [query_down, keyvalue_weight, jnp.pad(gains, ((0, 0), (0, 125)))], axis=1
    )
    first_part = gather_dp(first_set)

    query_part = split_columns(query_up)
    fold = query_part.shape[0] * query_part.shape[1] // width
    attention_part = gather_dp(
        jnp.concatenate([output_weight, query_part.reshape(fold, width)], axis=0)
    ).reshape(n_dp, -1, width)
    out_rows = output_weight.shape[0]
    full_output = attention_part[:, :out_rows].reshape(-1, width)
    full_query_up = rows_in_order(
        attention_part[:, out_rows:].reshape(-1, query_part.shape[1]), query_up.shape[0]
    )
    gate_up = jnp.concatenate(
        [gate_weight.reshape(own_rows, n_seq, -1), up_weight.reshape(own_rows, n_seq, -1)], axis=2
    )
    full_gate_up = rows_in_order(
        gather_dp(split_columns(gate_up.reshape(own_rows, -1))), own_rows
    )
    full_down = gather_dp(down_weight)

    first_all = jnp.concatenate(gather_blocks(first_part), axis=0)
    first_width = latent_width + 2 * HEAD_DIM
    gain_rows = first_all[:, first_width:].T[:8].astype(F32)
    attention_gain_rel = gain_rows[0]
    feed_gain_f = relative(gain_rows[1], 0)
    query_gain_f = relative(gain_rows[2], 0).reshape(-1, own_rows)[:, :query_rows].reshape(-1)

    tokens_rel = relative(input_low, 1).astype(F32)
    normed_rel = rms_norm(tokens_rel, attention_gain_rel).astype(BF)
    first_out = matmul(normed_rel, first_all)
    latent = first_out[:, :latent_width]
    keyvalue = first_out[:, latent_width:first_width]
    latent_low = rms_norm(latent, query_gain_f).astype(BF)
    key_local = rotate(keyvalue[:, :HEAD_DIM], cosine, sine_part)
    pack = jnp.concatenate(
        [latent_low, key_local.astype(BF), keyvalue[:, HEAD_DIM:].astype(BF)], axis=1
    )
    pack_all = jnp.concatenate(gather_blocks(pack), axis=0)
    latent_all = pack_all[:, :latent_width]
    keys = pack_all[:, latent_width : latent_width + HEAD_DIM]
    values = pack_all[:, latent_width + HEAD_DIM :]

    query_raw = matmul(latent_all, full_query_up)
    query_scale = HEAD_DIM ** (-0.5)
    queries = jnp.concatenate(
        [
            rotate(query_raw[:, h * HEAD_DIM : (h + 1) * HEAD_DIM], cosine_all, sine_all)
            * query_scale
            for h in range(heads)
        ],
        axis=1,
    ).astype(BF)
    block = 2 * tok_count
    attended, lse = attend(me_array, starts_all, queries, keys, values, block)
    mixed_low = attended.astype(BF)
    spans = [slice(j * block, (j + 1) * block) for j in chips]
    hidden = tokens + scatter_chips(
        [matmul(mixed_low[span], full_output).astype(BF) for span in spans]
    )

    cotangent_low = lax.optimization_barrier((cotangent[0], pack_all))[0]
    d_feed = gather_chips(cotangent_low)
    d_result = cotangent_low.astype(F32)

    feed_low = rms_norm(hidden, feed_gain_f).astype(BF)
    feed = gather_chips(feed_low)
    gate_proj, upward, active_low = [], [], []
    for j in chips:
        both = matmul(feed[j], full_gate_up)
        gate_proj.append(both[:, :hidden_units])
        upward.append(both[:, hidden_units:])
        active_low.append(gated(gate_proj[j], upward[j]).astype(BF))
    d_gate_up = []
    for j in chips:
        d_active = dot_rows(d_feed[j], full_down)
        pair = jax.vjp(gated, gate_proj[j], upward[j])[1](d_active)
        d_gate_up.append(jnp.concatenate(pair, axis=1).astype(BF))
    d_feed_normed = scatter_chips(
        [dot_rows(d_gate_up[j], full_gate_up).astype(BF) for j in chips]
    )
    feed_all = jnp.concatenate(feed, axis=0)
    d_feed_all = jnp.concatenate(d_feed, axis=0)
    active_all = jnp.concatenate(active_low, axis=0)
    d_gate_up_all = jnp.concatenate(d_gate_up, axis=0)
    grad_down = scatter_dp(dot_cols(active_all, d_feed_all).astype(BF)).astype(F32)
    grad_gate_up = scatter_dp(rows_by_dp(dot_cols(feed_all, d_gate_up_all).astype(BF)))

    d_hidden_norm, grad_feed_gain_term = jax.vjp(rms_norm, hidden, feed_gain_f)[1](d_feed_normed)
    d_hidden = d_result + d_hidden_norm
    d_branch = gather_chips(d_hidden.astype(BF))
    result = hidden + scatter_chips(
        [
            matmul(lax.optimization_barrier((active_low[j], d_branch[j]))[0], full_down).astype(BF)
            for j in chips
        ]
    )
    layer_output = result.astype(BF)[None]

    d_mixed_low = jnp.concatenate(
        [dot_rows(d_branch[j], full_output).astype(BF) for j in chips], axis=0
    )
    offset = jnp.stack(
        [
            jnp.sum(
                d_mixed_low[:, h * HEAD_DIM : (h + 1) * HEAD_DIM].astype(F32)
                * attended[:, h * HEAD_DIM : (h + 1) * HEAD_DIM],
                axis=1,
            )
            for h in range(heads)
        ]
    )
    d_queries, d_keys, d_values = attend_back(
        me_array, starts_all, queries, d_mixed_low, lse, offset, keys, values, block
    )
    d_query_low = jnp.concatenate(
        [
            rotate(d_queries[:, h * HEAD_DIM : (h + 1) * HEAD_DIM], cosine_all, -sine_all)
            * query_scale
            for h in range(heads)
        ],
        axis=1,
    ).astype(BF)
    back_local = scatter_chips(
        [
            jnp.concatenate(
                [
                    dot_rows(d_query_low[span], full_query_up).astype(BF),
                    d_keys[span].astype(BF),
                    d_values[span].astype(BF),
                ],
                axis=1,
            )
            for span in spans
        ]
    )
    d_branch_all = jnp.concatenate(d_branch, axis=0)
    grad_output_term = dot_cols(mixed_low, d_branch_all).astype(BF)
    grad_query_term = rows_by_dp(dot_cols(latent_all, d_query_low).astype(BF))
    grad_attention = scatter_dp(
        jnp.concatenate(
            [
                grad_output_term.reshape(n_dp, out_rows, width),
                grad_query_term.reshape(n_dp, fold, width),
            ],
            axis=1,
        ).reshape(-1, width)
    )
    grad_output_weight = grad_attention[:out_rows].astype(F32)
    grad_query_up = join_columns(grad_attention[out_rows:].reshape(query_part.shape))
    grad_query_up = grad_query_up.astype(F32).reshape(query_rows, -1)

    d_latent_normed = back_local[:, :latent_width]
    d_pairs = back_local[:, latent_width:]
    d_key_raw = rotate(d_pairs[:, :HEAD_DIM], cosine, -sine_part)
    d_keyvalue_low = jnp.concatenate([d_key_raw, d_pairs[:, HEAD_DIM:]], axis=1).astype(BF)
    d_latent, grad_query_gain_term = jax.vjp(rms_norm, latent, query_gain_f)[1](d_latent_normed)
    d_first_low = jnp.concatenate(
        [d_latent.astype(BF), d_keyvalue_low, jnp.zeros((tok_count, 128), BF)], axis=1
    )
    d_normed_rel = dot_rows(d_first_low, first_all)
    d_tokens_rel, attention_gain_term = jax.vjp(rms_norm, tokens_rel, attention_gain_rel)[1](
        d_normed_rel
    )
    input_grad = (d_hidden + relative(d_tokens_rel, 1))[None]

    query_gain_term = jnp.pad(
        grad_query_gain_term.reshape(-1, query_rows), ((0, 0), (0, own_rows - query_rows))
    ).reshape(-1)
    gain_terms = jnp.stack(
        [attention_gain_term, relative(grad_feed_gain_term, 0), relative(query_gain_term, 0)],
        axis=1,
    )
    first_terms = jnp.concatenate(
        [
            dot_cols(normed_rel, d_first_low[:, :first_width]).astype(BF),
            jnp.pad(gain_terms, ((0, 0), (0, 125))).astype(BF),
        ],
        axis=1,
    )
    first_rows = first_terms.shape[0] // n_seq
    grad_first = scatter_dp(
        scatter_blocks(
            [first_terms[k * first_rows : (k + 1) * first_rows] for k in range(n_seq)]
        ).astype(BF)
    ).astype(F32)

    gate_up_rows = join_columns(grad_gate_up).astype(F32)
    return (
        layer_output,
        input_grad,
        grad_first[:, first_width],
        grad_first[:, :latent_width],
        grad_first[:query_rows, first_width + 2],
        grad_query_up,
        grad_first[:, latent_width:first_width],
        grad_output_weight,
        grad_first[:, first_width + 1],
        gate_up_rows[:, :, :hidden_units].reshape(own_rows, -1),
        gate_up_rows[:, :, hidden_units:].reshape(own_rows, -1),
        grad_down,
    )


def solution(mesh):
    shards = P(("seq", "dp"))
    tokens = P("dp", "seq", None)
    weight = P(("seq", "dp"), None)
    return jax.shard_map(
        local,
        mesh=mesh,
        in_specs=(
            tokens,
            P("dp", None),
            shards,
            weight,
            shards,
            weight,
            weight,
            weight,
            shards,
            weight,
            weight,
            weight,
            tokens,
        ),
        out_specs=(
            tokens,
            tokens,
            shards,
            weight,
            shards,
            weight,
            weight,
            weight,
            shards,
            weight,
            weight,
            weight,
        ),
        check_vma=False,
    )
```

time: 1260 us -> 731 us (0.58)
  waiting for transfers between devices: 869 us -> 243 us
  starting transfers between devices: 17.7 us -> 72.7 us
  local copies, waits for them, and re-layouts: 80.6 us -> 126 us
  blocking collectives: 40.4 us -> 67.2 us
  matrix products: 134 us -> 110 us
  Pallas kernels: 47.9 us -> 30.6 us
    reduce_scatter x10 -> x3, waiting for transfers between devices: 417 us -> 0.01 us  [scatter_dp(): return lax.psum_scatter(terms, 'dp', scatter_dimension=0, tiled=True)]
    all_gather x5 -> x0, waiting for transfers between devices: 230 us -> none  [the longest x4 171 us: gather_seq(): return lax.all_gather(rows, 'seq', axis=0, tiled=True)]
    ppermute x0 -> x90, waiting for transfers between devices: none -> 230 us  [flip(): return lax.ppermute(block, 'seq', [(i, i ^ bits) for i in range(n_seq)])]
    all_gather x5 -> x3, waiting for transfers between devices: 192 us -> 0.01 us  [gather_dp(): return lax.all_gather(rows, 'dp', axis=0, tiled=True)]
    ppermute x0 -> x90, starting transfers between devices: none -> 64.2 us  [flip(): return lax.ppermute(block, 'seq', [(i, i ^ bits) for i in range(n_seq)])]
    unnamed x113 -> x267, local copies, waits for them, and re-layouts: 25.9 us -> 67.5 us
    all_gather x0 -> x1, blocking collectives: none -> 32.4 us  [gather_dp(): return lax.all_gather(rows, 'dp', axis=0, tiled=True)]
    slice x1 -> x50, local copies, waits for them, and re-layouts: 0.39 us -> 18.8 us  [the longest x1 3.15 us: local(): full_output = attention_part[:, :out_rows].reshape(-1, width)]
  transfers between devices with their start and end apart: 25 -> 99, of which waited for: 23 -> 38; matrix products, arithmetic and copies ran while one was open for 12% -> 34% of each run, Pallas kernels for 2% -> 2%
where the time goes in v2:
time: 731 us; the launch traced here: 725 us
  waiting for transfers between devices  243 us (33%)
  local copies, waits for them, and re-layouts  126 us (17%)
  matrix products  110 us (15%)
  starting transfers between devices  72.7 us (10%)
  blocking collectives  67.2 us (9%)
  other arithmetic  58.4 us (8%)
  Pallas kernels  30.6 us (4%)
  between operations  17.6 us (2%)
    ppermute x90, waiting for transfers between devices, flip(): return lax.ppermute(block, 'seq', [(i, i ^ bits) for i in range(n_seq)])  230 us
    unnamed x267, local copies, waits for them, and re-layouts  67.5 us
    ppermute x90, starting transfers between devices, flip(): return lax.ppermute(block, 'seq', [(i, i ^ bits) for i in range(n_seq)])  64.2 us
    dot_general x17, matrix products, dot_rows(): lax.dot_general(left_side, right_side, (((1,), (1,)), ((), ())), preferre...  41 us
    dot_general x14, matrix products, matmul(): return jnp.dot(left_side, right_side, preferred_element_type=F32)  38.4 us
    all_to_all x2, blocking collectives, split_columns(): lax.all_to_all(parts, 'seq', 0, 0).reshape(n_seq * rows, width // n_seq)  34.7 us
    all_gather x1, blocking collectives, gather_dp(): return lax.all_gather(rows, 'dp', axis=0, tiled=True)  32.4 us
    dot_general x5, matrix products, dot_cols(): lax.dot_general(left_side, right_side, (((0,), (0,)), ((), ())), preferre...  30.2 us
  transfers between devices with their start and end apart: 99, of which 38 were waited for; matrix products, arithmetic and copies ran while one was open for 34% of the time, Pallas kernels for 2%

profile of v2, /device:TPU:0, one launch (start us, length us, event | category | flops | bytes accessed | tf_op | source)
XLA Modules:
  0.0 725.3 jit_solution(1017025238535685500)
XLA Ops:
  8.3 11.9 %all_to_all.20 = bf16[8,32,512]{2,1,0:T(8,128)(2,1)S(1)} all-to-all(bf16[8,32,512]{2,1,0:T(8,128)(2,1)S(1)} %bitcast.160), channel_id=1, replica_groups=mesh['seq'=8,'dp'=4] {'seq'}, dimensions={0} | all-to-all | bytes 524288 | tf_op jit(solution)/shard_map/all_to_all | solution.py:151
  23.4 22.8 %all_to_all.21 = bf16[8,64,1408]{2,1,0:T(8,128)(2,1)} all-to-all(bf16[8,64,1408]{2,1,0:T(8,128)(2,1)S(1)} %copy.123), channel_id=1, replica_groups=mesh['seq'=8,'dp'=4] {'seq'}, dimensions={0} | all-to-all | bytes 2883584 | tf_op jit(solution)/shard_map/all_to_all | solution.py:151
  46.5 32.4 %all_gather.12 = bf16[256,1664]{1,0:T(8,128)(2,1)S(1)} all-gather(bf16[64,1664]{1,0:T(8,128)(2,1)S(1)} %fusion.150), channel_id=1, replica_groups=mesh['seq'=8,'dp'=4] {'dp'}, dimensions={0}, use_global_device_ids=true | all-gather | bytes 1064960 | tf_op jit(solution)/shard_map/all_gather | solution.py:140
  82.5 4.5 multiply_cosine_fusion
  87.0 12.4 %collective-permute-done.1 = bf16[256,1664]{1,0:T(8,128)(2,1)} collective-permute-done((bf16[256,1664]{1,0:T(8,128)(2,1)S(1)}, bf16[256,1664]{1,0:T(8,128)(2,1)}, u32[]{:S(2)}, u32[]{:S(2)}) %collective-permute-start.1) | collective-permute-done | bytes 852000 | tf_op jit(solution)/shard_map/ppermute | solution.py:75
  107.1 4.7 collective-permute-done.5
  111.8 2.6 collective-permute-done.6
  131.9 13.9 %collective-permute-done.9 = bf16[192,1536]{1,0:T(8,128)(2,1)S(1)} collective-permute-done((bf16[192,1536]{1,0:T(8,128)(2,1)S(1)}, bf16[192,1536]{1,0:T(8,128)(2,1)S(1)}, u32[]{:S(2)}, u32[]{:S(2)}) %collective-permute-start.9) | collective-permute-done | bytes 589856 | tf_op jit(solution)/shard_map/ppermute | solution.py:75
  148.6 6.0 collective-permute-done.14
  163.0 3.1 slice.644
  166.9 4.1 fusion.9
  171.0 3.6 fusion.119
  176.7 15.3 %attend.1 = (f32[1536,512]{1,0:T(8,128)S(1)}, f32[2,1536]{1,0:T(2,128)S(1)}) custom-call(s32[1]{0:T(128)} %bitcast.1.me_ref, s32[1,1536]{1,0:T(1,128)S(1)} %reshape.292.starts_ref, bf16[1536,512]{1,0:T(8,128)(2,1)S(1)} %pad_maximum_fusion.3.q_ref, bf16[1536,256]{1,0:T(8,128)(2,1)S(1)} %copy-done.4, bf16[256,1536]{1,0:T(8,128)(2,1)S(1)} %copy-done.2), custom_call_target="tpu_custom_call" | custom-call | flops 2415919104 | bytes 6291456 | tf_op jit(solution)/shard_map/attend/pallas_call | solution.py:223
  204.9 7.1 collective-permute-done.21
  214.5 6.0 collective-permute-done.18
  220.5 9.1 %collective-permute-done.22 = bf16[96,2048]{1,0:T(8,128)(2,1)S(1)} collective-permute-done((bf16[96,2048]{1,0:T(8,128)(2,1)S(1)}, bf16[96,2048]{1,0:T(8,128)(2,1)S(1)}, u32[]{:S(2)}, u32[]{:S(2)}) %collective-permute-start.22) | collective-permute-done | bytes 393248 | tf_op jit(solution)/shard_map/ppermute | solution.py:75
  236.2 16.7 %collective-permute-done.37 = bf16[192,2048]{1,0:T(8,128)(2,1)} collective-permute-done((bf16[192,2048]{1,0:T(8,128)(2,1)}, bf16[192,2048]{1,0:T(8,128)(2,1)}, u32[]{:S(2)}, u32[]{:S(2)}) %collective-permute-start.37) | collective-permute-done | bytes 786464 | tf_op jit(solution)/shard_map/ppermute | solution.py:75
  257.1 19.2 %collective-permute-done.43 = bf16[96,2048]{1,0:T(8,128)(2,1)S(1)} collective-permute-done((bf16[96,2048]{1,0:T(8,128)(2,1)S(1)}, bf16[96,2048]{1,0:T(8,128)(2,1)S(1)}, u32[]{:S(2)}, u32[]{:S(2)}) %collective-permute-start.43) | collective-permute-done | bytes 393248 | tf_op jit(solution)/shard_map/ppermute | solution.py:75
  282.1 7.8 %collective-permute-done.40 = bf16[96,2048]{1,0:T(8,128)(2,1)S(1)} collective-permute-done((bf16[96,2048]{1,0:T(8,128)(2,1)S(1)}, bf16[96,2048]{1,0:T(8,128)(2,1)S(1)}, u32[]{:S(2)}, u32[]{:S(2)}) %collective-permute-start.40) | collective-permute-done | bytes 393248 | tf_op jit(solution)/shard_map/ppermute | solution.py:75
  294.0 3.2 copy.124
  297.4 5.7 fusion.59
  303.5 5.3 fusion.41
  308.9 5.8 fusion.77
  315.1 2.6 convolution_convert_fusion.10
  318.2 3.7 fusion.83
  322.2 2.6 convolution_convert_fusion.8
  325.7 4.0 fusion.49
  329.7 4.0 fusion.29
  333.7 4.0 fusion.74
  338.1 2.8 convolution_convert_fusion.11
  341.0 4.0 fusion.80
  345.3 2.6 convolution_convert_fusion.9
  354.0 14.9 %collective-permute-done.47 = bf16[96,2048]{1,0:T(8,128)(2,1)S(1)} collective-permute-done((bf16[96,2048]{1,0:T(8,128)(2,1)S(1)}, bf16[96,2048]{1,0:T(8,128)(2,1)S(1)}, u32[]{:S(2)}, u32[]{:S(2)}) %collective-permute-start.47) | collective-permute-done | bytes 393248 | tf_op jit(solution)/shard_map/ppermute | solution.py:75
  369.6 2.6 collective-permute-done.49
  372.9 7.3 %collective-permute-done.48 = bf16[96,2048]{1,0:T(8,128)(2,1)S(1)} collective-permute-done((bf16[96,2048]{1,0:T(8,128)(2,1)S(1)}, bf16[96,2048]{1,0:T(8,128)(2,1)S(1)}, u32[]{:S(2)}, u32[]{:S(2)}) %collective-permute-start.48) | collective-permute-done | bytes 393248 | tf_op jit(solution)/shard_map/ppermute | solution.py:75
  383.4 3.4 constant_dynamic-update-slice_fusion.47
  388.9 15.6 %collective-permute-done.58 = bf16[192,2048]{1,0:T(8,128)(2,1)S(1)} collective-permute-done((bf16[192,2048]{1,0:T(8,128)(2,1)S(1)}, bf16[192,2048]{1,0:T(8,128)(2,1)S(1)}, u32[]{:S(2)}, u32[]{:S(2)}) %collective-permute-start.58) | collective-permute-done | bytes 786464 | tf_op jit(solution)/shard_map/ppermute | solution.py:75
  409.2 4.0 collective-permute-done.61
  417.8 4.7 convolution_convert_fusion.3
  424.4 15.3 %attend_back.1 = (f32[1536,512]{1,0:T(8,128)S(1)}, f32[1536,256]{1,0:T(8,128)S(1)}, f32[1536,256]{1,0:T(8,128)S(1)}) custom-call(s32[1]{0:T(128)} %bitcast.1.me_ref, s32[1,1536]{1,0:T(1,128)S(1)} %reshape.292.starts_ref, bf16[1536,512]{1,0:T(8,128)(2,1)S(1)} %copy-done.1, bf16[1536,512]{1,0:T(8,128)(2,1)S(1)} %pad_maximum_fusion.5.dm_ref, ...), custom_call_target="tpu_custom_call" | custom-call | flops 6039797760 | bytes 9437184 | tf_op jit(solution)/shard_map/attend_back/pallas_call | solution.py:313
  439.8 3.6 fusion.117
  449.0 4.0 pad_maximum_fusion
  467.8 12.5 %convolution_convert_fusion.1 = bf16[2048,1408]{1,0:T(8,128)(2,1)S(1)} fusion(bf16[1536,2048]{1,0:T(8,128)(2,1)} %constant_dynamic-update-slice_fusion.48, bf16[384,1408]{1,0:T(8,128)(2,1)S(1)} %copy-done.47, bf16[384,1408]{1,0:T(8,128)(2,1)S(1)} %copy-done.51, bf16[384,1408]{1,0:T(8,128)(2,1)S(1)} %copy-done.45, bf16[384,1408]{1,0:T(8,128)(2,1)S(1)} %copy-done.49), kind=kOutput, calls=%fused_computation.8 | convolution fusion | flops 8878555136 | bytes 16384000 | tf_op jit(solution)/shard_map/dot_general | solution.py:68
  480.3 3.0 copy.135
  483.4 3.4 convolution_convert_fusion.7
  506.2 9.2 %convolution_convert_fusion.2 = bf16[704,2048]{1,0:T(8,128)(2,1)} fusion(bf16[1536,2048]{1,0:T(8,128)(2,1)} %constant_dynamic-update-slice_fusion.57, bf16[384,704]{1,0:T(8,128)(2,1)S(1)} %copy-done.86, bf16[384,704]{1,0:T(8,128)(2,1)S(1)} %copy-done.89, bf16[384,704]{1,0:T(8,128)(2,1)S(1)} %copy-done.88, bf16[384,704]{1,0:T(8,128)(2,1)S(1)} %copy-done.91), kind=kOutput, calls=%fused_computation.23 | convolution fusion | flops 4439277568 | bytes 11337728 | tf_op jit(solution)/shard_map/dot_general | solution.py:68
  515.7 3.5 convolution_convert_fusion.6
  536.7 5.4 collective-permute-done.75
  542.6 6.3 collective-permute-done.77
  551.2 7.6 %collective-permute-done.76 = bf16[96,1536]{1,0:T(8,128)(2,1)S(1)} collective-permute-done((bf16[96,1536]{1,0:T(8,128)(2,1)S(1)}, bf16[96,1536]{1,0:T(8,128)(2,1)S(1)}, u32[]{:S(2)}, u32[]{:S(2)}) %collective-permute-start.76) | collective-permute-done | bytes 294944 | tf_op jit(solution)/shard_map/ppermute | solution.py:75
  560.8 3.3 collective-permute-done.79
  591.4 5.7 fusion.22
  607.7 6.8 collective-permute-done.65
  616.3 7.3 %collective-permute-done.85 = bf16[128,1664]{0,1:T(8,128)(2,1)S(1)} collective-permute-done((bf16[128,1664]{0,1:T(8,128)(2,1)S(1)}, bf16[128,1664]{0,1:T(8,128)(2,1)S(1)}, u32[]{:S(2)}, u32[]{:S(2)}) %collective-permute-start.85) | collective-permute-done | bytes 426016 | tf_op jit(solution)/shard_map/ppermute | solution.py:75
  625.2 8.7 %collective-permute-done.87 = bf16[128,1664]{0,1:T(8,128)(2,1)S(1)} collective-permute-done((bf16[128,1664]{0,1:T(8,128)(2,1)S(1)}, bf16[128,1664]{0,1:T(8,128)(2,1)S(1)}, u32[]{:S(2)}, u32[]{:S(2)}) %collective-permute-start.87) | collective-permute-done | bytes 426016 | tf_op jit(solution)/shard_map/ppermute | solution.py:75
  636.1 10.5 %collective-permute-done.86 = bf16[128,1664]{0,1:T(8,128)(2,1)S(1)} collective-permute-done((bf16[128,1664]{0,1:T(8,128)(2,1)S(1)}, bf16[128,1664]{0,1:T(8,128)(2,1)S(1)}, u32[]{:S(2)}, u32[]{:S(2)}) %collective-permute-start.86) | collective-permute-done | bytes 426016 | tf_op jit(solution)/shard_map/ppermute | solution.py:75
  648.3 4.1 collective-permute-done.89
  654.2 3.3 collective-permute-done.88
  661.5 4.4 collective-permute-done.67
  673.9 3.4 all-to-all-start.2
  679.6 4.6 all-to-all-done.2
  684.2 4.6 all-to-all-start.3
  688.9 5.0 add_bitcast_fusion
  696.2 8.4 %reduce-scatter.13.cloned.1.call-done = bf16[64,1664]{1,0:T(8,128)(2,1)} async-done(((bf16[256,1664]{1,0:T(8,128)(2,1)}), bf16[64,1664]{1,0:T(8,128)(2,1)}) %reduce-scatter.13.cloned.1.call-update) | async-done | bytes 213008
  (664 shorter events, 247.3 us)
Async XLA Ops:
  7.2 154.5 %all-gather.4.cloned.1.call-start = ((), (), s32[]{:S(2)}) async-start(), calls=%async_computation.8 | async-start | bytes 3932160 | tf_op jit(solution)/shard_map/all_gather | solution.py:140
  21.3 272.7 %all-gather.6.cloned.1.call-start = ((), (), s32[]{:S(2)}) async-start(), calls=%async_computation.9 | async-start | bytes 7208960 | tf_op jit(solution)/shard_map/all_gather | solution.py:140
  46.2 262.6 %all-gather.8.cloned.1.call-start = ((), (), s32[]{:S(2)}) async-start(), calls=%async_computation.10 | async-start | bytes 3604480 | tf_op jit(solution)/shard_map/all_gather | solution.py:140
  79.0 20.5 %collective-permute-start.3 = (bf16[256,1664]{1,0:T(8,128)(2,1)S(1)}, bf16[256,1664]{1,0:T(8,128)(2,1)S(1)}, u32[]{:S(2)}, u32[]{:S(2)}) collective-permute-start(bf16[256,1664]{1,0:T(8,128)(2,1)S(1)} %all_gather.12), channel_id=1, source_target_pairs={{0,16},{4,20},{8,24},{12,28},{16,0},{20,4},{24,8},{28,12},{1,17},{... | collective-permute-start | bytes 2555912 | tf_op jit(solution)/shard_map/ppermute | solution.py:75
  79.6 19.8 %collective-permute-start.1 = (bf16[256,1664]{1,0:T(8,128)(2,1)S(1)}, bf16[256,1664]{1,0:T(8,128)(2,1)}, u32[]{:S(2)}, u32[]{:S(2)}) collective-permute-start(bf16[256,1664]{1,0:T(8,128)(2,1)S(1)} %all_gather.12), channel_id=1, source_target_pairs={{0,8},{4,12},{8,0},{12,4},{16,24},{20,28},{24,16},{28,20},{1,9},{5... | collective-permute-start | bytes 2555912 | tf_op jit(solution)/shard_map/ppermute | solution.py:75
  80.2 22.5 %collective-permute-start = (bf16[256,1664]{1,0:T(8,128)(2,1)S(1)}, bf16[256,1664]{1,0:T(8,128)(2,1)}, u32[]{:S(2)}, u32[]{:S(2)}) collective-permute-start(bf16[256,1664]{1,0:T(8,128)(2,1)S(1)} %all_gather.12), channel_id=1, source_target_pairs={{0,4},{4,0},{8,12},{12,8},{16,20},{20,16},{24,28},{28,24},{1,5},{5... | collective-permute-start | bytes 2555912 | tf_op jit(solution)/shard_map/ppermute | solution.py:75
  80.3 591.8 %reduce-scatter.7.cloned.1.call-start = ((), (), s32[]{:S(2)}) async-start(), calls=%async_computation.11 | async-start | bytes 3932160 | tf_op jit(solution)/shard_map/reduce_scatter | solution.py:144
  99.4 15.2 %collective-permute-start.2 = (bf16[256,1664]{1,0:T(8,128)(2,1)}, bf16[256,1664]{1,0:T(8,128)(2,1)}, u32[]{:S(2)}, u32[]{:S(2)}) collective-permute-start(bf16[256,1664]{1,0:T(8,128)(2,1)} %collective-permute-done.1), channel_id=1, source_target_pairs={{0,4},{4,0},{8,12},{12,8},{16,20},{20,16},{24,28},{28,24},{1,5},{5... | collective-permute-start | bytes 2555912 | tf_op jit(solution)/shard_map/ppermute | solution.py:75
  99.5 12.3 %collective-permute-start.5 = (bf16[128,1664]{1,0:T(8,128)(2,1)S(1)}, bf16[128,1664]{1,0:T(8,128)(2,1)S(1)}, u32[]{:S(2)}, u32[]{:S(2)}) collective-permute-start(bf16[128,1664]{1,0:T(8,128)(2,1)S(1)} %slice.620), channel_id=1, source_target_pairs={{0,8},{4,12},{8,0},{12,4},{16,24},{20,28},{24,16},{28,20},{1,9},{5... | collective-permute-start | bytes 1277960 | tf_op jit(solution)/shard_map/ppermute | solution.py:75
  102.4 12.0 %collective-permute-start.6 = (bf16[128,1664]{1,0:T(8,128)(2,1)S(1)}, bf16[128,1664]{1,0:T(8,128)(2,1)S(1)}, u32[]{:S(2)}, u32[]{:S(2)}) collective-permute-start(bf16[128,1664]{1,0:T(8,128)(2,1)S(1)} %slice.621), channel_id=1, source_target_pairs={{0,16},{4,20},{8,24},{12,28},{16,0},{20,4},{24,8},{28,12},{1,17},{... | collective-permute-start | bytes 1277960 | tf_op jit(solution)/shard_map/ppermute | solution.py:75
  102.8 15.0 %collective-permute-start.4 = (bf16[256,1664]{1,0:T(8,128)(2,1)S(1)}, bf16[256,1664]{1,0:T(8,128)(2,1)S(1)}, u32[]{:S(2)}, u32[]{:S(2)}) collective-permute-start(bf16[256,1664]{1,0:T(8,128)(2,1)S(1)} %collective-permute-done.3), channel_id=1, source_target_pairs={{0,4},{4,0},{8,12},{12,8},{16,20},{20,16},{24,28},{28,24},{1,5},{5... | collective-permute-start | bytes 2555912 | tf_op jit(solution)/shard_map/ppermute | solution.py:75
  130.1 15.8 %collective-permute-start.9 = (bf16[192,1536]{1,0:T(8,128)(2,1)S(1)}, bf16[192,1536]{1,0:T(8,128)(2,1)S(1)}, u32[]{:S(2)}, u32[]{:S(2)}) collective-permute-start(bf16[192,1536]{1,0:T(8,128)(2,1)S(1)} %get-tuple-element.201), channel_id=1, source_target_pairs={{0,8},{4,12},{8,0},{12,4},{16,24},{20,28},{24,16},{28,20},{1,9},{5... | collective-permute-start | bytes 1769480 | tf_op jit(solution)/shard_map/ppermute | solution.py:75
  130.4 18.1 %collective-permute-start.8 = (bf16[192,1536]{1,0:T(8,128)(2,1)S(1)}, bf16[192,1536]{1,0:T(8,128)(2,1)S(1)}, u32[]{:S(2)}, u32[]{:S(2)}) collective-permute-start(bf16[192,1536]{1,0:T(8,128)(2,1)S(1)} %get-tuple-element.201), channel_id=1, source_target_pairs={{0,4},{4,0},{8,12},{12,8},{16,20},{20,16},{24,28},{28,24},{1,5},{5... | collective-permute-start | bytes 1769480 | tf_op jit(solution)/shard_map/ppermute | solution.py:75
  130.7 15.6 %collective-permute-start.11 = (bf16[192,1536]{1,0:T(8,128)(2,1)S(1)}, bf16[192,1536]{1,0:T(8,128)(2,1)S(1)}, u32[]{:S(2)}, u32[]{:S(2)}) collective-permute-start(bf16[192,1536]{1,0:T(8,128)(2,1)S(1)} %get-tuple-element.201), channel_id=1, source_target_pairs={{0,16},{4,20},{8,24},{12,28},{16,0},{20,4},{24,8},{28,12},{1,17},{... | collective-permute-start | bytes 1769480 | tf_op jit(solution)/shard_map/ppermute | solution.py:75
  199.3 30.5 %collective-permute-start.16 = (bf16[192,2048]{1,0:T(8,128)(2,1)S(1)}, bf16[192,2048]{1,0:T(8,128)(2,1)S(1)}, u32[]{:S(2)}, u32[]{:S(2)}) collective-permute-start(bf16[192,2048]{1,0:T(8,128)(2,1)S(1)} %slice.646), channel_id=1, source_target_pairs={{0,4},{4,0},{8,12},{12,8},{16,20},{20,16},{24,28},{28,24},{1,5},{5... | collective-permute-start | bytes 2359304 | tf_op jit(solution)/shard_map/ppermute | solution.py:75
  200.0 12.0 %collective-permute-start.21 = (bf16[96,2048]{1,0:T(8,128)(2,1)S(1)}, bf16[96,2048]{1,0:T(8,128)(2,1)S(1)}, u32[]{:S(2)}, u32[]{:S(2)}) collective-permute-start(bf16[96,2048]{1,0:T(8,128)(2,1)S(1)} %get-tuple-element.197), channel_id=1, source_target_pairs={{0,8},{4,12},{8,0},{12,4},{16,24},{20,28},{24,16},{28,20},{1,9},{5... | collective-permute-start | bytes 1179656 | tf_op jit(solution)/shard_map/ppermute | solution.py:75
  201.8 12.1 %collective-permute-start.23 = (bf16[96,2048]{1,0:T(8,128)(2,1)S(1)}, bf16[96,2048]{1,0:T(8,128)(2,1)S(1)}, u32[]{:S(2)}, u32[]{:S(2)}) collective-permute-start(bf16[96,2048]{1,0:T(8,128)(2,1)S(1)} %get-tuple-element.198), channel_id=1, source_target_pairs={{0,16},{4,20},{8,24},{12,28},{16,0},{20,4},{24,8},{28,12},{1,17},{... | collective-permute-start | bytes 1179656 | tf_op jit(solution)/shard_map/ppermute | solution.py:75
  202.5 27.2 %collective-permute-start.25 = (bf16[96,2048]{1,0:T(8,128)(2,1)S(1)}, bf16[96,2048]{1,0:T(8,128)(2,1)S(1)}, u32[]{:S(2)}, u32[]{:S(2)}) collective-permute-start(bf16[96,2048]{1,0:T(8,128)(2,1)S(1)} %slice.661), channel_id=1, source_target_pairs={{0,16},{4,20},{8,24},{12,28},{16,0},{20,4},{24,8},{28,12},{1,17},{... | collective-permute-start | bytes 1179656 | tf_op jit(solution)/shard_map/ppermute | solution.py:75
  204.6 15.9 %collective-permute-start.18 = (bf16[96,2048]{1,0:T(8,128)(2,1)S(1)}, bf16[96,2048]{1,0:T(8,128)(2,1)S(1)}, u32[]{:S(2)}, u32[]{:S(2)}) collective-permute-start(bf16[96,2048]{1,0:T(8,128)(2,1)S(1)} %slice.650), channel_id=1, source_target_pairs={{0,8},{4,12},{8,0},{12,4},{16,24},{20,28},{24,16},{28,20},{1,9},{5... | collective-permute-start | bytes 1179656 | tf_op jit(solution)/shard_map/ppermute | solution.py:75
  212.2 17.4 %collective-permute-start.22 = (bf16[96,2048]{1,0:T(8,128)(2,1)S(1)}, bf16[96,2048]{1,0:T(8,128)(2,1)S(1)}, u32[]{:S(2)}, u32[]{:S(2)}) collective-permute-start(bf16[96,2048]{1,0:T(8,128)(2,1)S(1)} %add_convert_fusion.27), channel_id=1, source_target_pairs={{0,16},{4,20},{8,24},{12,28},{16,0},{20,4},{24,8},{28,12},{1,17},{... | collective-permute-start | bytes 1179656 | tf_op jit(solution)/shard_map/ppermute | solution.py:75
  214.0 15.7 %collective-permute-start.24 = (bf16[96,2048]{1,0:T(8,128)(2,1)S(1)}, bf16[96,2048]{1,0:T(8,128)(2,1)S(1)}, u32[]{:S(2)}, u32[]{:S(2)}) collective-permute-start(bf16[96,2048]{1,0:T(8,128)(2,1)S(1)} %add_convert_fusion.26), channel_id=1, source_target_pairs={{0,8},{4,12},{8,0},{12,4},{16,24},{20,28},{24,16},{28,20},{1,9},{5... | collective-permute-start | bytes 1179656 | tf_op jit(solution)/shard_map/ppermute | solution.py:75
  232.1 20.8 %collective-permute-start.37 = (bf16[192,2048]{1,0:T(8,128)(2,1)}, bf16[192,2048]{1,0:T(8,128)(2,1)}, u32[]{:S(2)}, u32[]{:S(2)}) collective-permute-start(bf16[192,2048]{1,0:T(8,128)(2,1)} %get-tuple-element.117), channel_id=1, source_target_pairs={{0,16},{4,20},{8,24},{12,28},{16,0},{20,4},{24,8},{28,12},{1,17},{... | collective-permute-start | bytes 2359304 | tf_op jit(solution)/shard_map/ppermute | solution.py:75
  232.4 21.9 %collective-permute-start.31 = (bf16[192,2048]{1,0:T(8,128)(2,1)}, bf16[192,2048]{1,0:T(8,128)(2,1)}, u32[]{:S(2)}, u32[]{:S(2)}) collective-permute-start(bf16[192,2048]{1,0:T(8,128)(2,1)} %get-tuple-element.117), channel_id=1, source_target_pairs={{0,8},{4,12},{8,0},{12,4},{16,24},{20,28},{24,16},{28,20},{1,9},{5... | collective-permute-start | bytes 2359304 | tf_op jit(solution)/shard_map/ppermute | solution.py:75
  234.1 43.3 %collective-permute-start.35 = (bf16[192,2048]{1,0:T(8,128)(2,1)}, bf16[192,2048]{1,0:T(8,128)(2,1)}, u32[]{:S(2)}, u32[]{:S(2)}) collective-permute-start(bf16[192,2048]{1,0:T(8,128)(2,1)} %bitcast.28), channel_id=1, source_target_pairs={{0,16},{4,20},{8,24},{12,28},{16,0},{20,4},{24,8},{28,12},{1,17},{... | collective-permute-start | bytes 2359304 | tf_op jit(solution)/shard_map/ppermute | solution.py:75
  234.5 45.5 %collective-permute-start.29 = (bf16[192,2048]{1,0:T(8,128)(2,1)}, bf16[192,2048]{1,0:T(8,128)(2,1)}, u32[]{:S(2)}, u32[]{:S(2)}) collective-permute-start(bf16[192,2048]{1,0:T(8,128)(2,1)} %bitcast.28), channel_id=1, source_target_pairs={{0,8},{4,12},{8,0},{12,4},{16,24},{20,28},{24,16},{28,20},{1,9},{5... | collective-permute-start | bytes 2359304 | tf_op jit(solution)/shard_map/ppermute | solution.py:75
  253.9 22.4 %collective-permute-start.43 = (bf16[96,2048]{1,0:T(8,128)(2,1)S(1)}, bf16[96,2048]{1,0:T(8,128)(2,1)S(1)}, u32[]{:S(2)}, u32[]{:S(2)}) collective-permute-start(bf16[96,2048]{1,0:T(8,128)(2,1)S(1)} %slice.679), channel_id=1, source_target_pairs={{0,8},{4,12},{8,0},{12,4},{16,24},{20,28},{24,16},{28,20},{1,9},{5... | collective-permute-start | bytes 1179656 | tf_op jit(solution)/shard_map/ppermute | solution.py:75
  255.4 20.9 %collective-permute-start.44 = (bf16[96,2048]{1,0:T(8,128)(2,1)S(1)}, bf16[96,2048]{1,0:T(8,128)(2,1)S(1)}, u32[]{:S(2)}, u32[]{:S(2)}) collective-permute-start(bf16[96,2048]{1,0:T(8,128)(2,1)S(1)} %slice.680), channel_id=1, source_target_pairs={{0,16},{4,20},{8,24},{12,28},{16,0},{20,4},{24,8},{28,12},{1,17},{... | collective-permute-start | bytes 1179656 | tf_op jit(solution)/shard_map/ppermute | solution.py:75
  277.3 19.9 %collective-permute-start.45 = (bf16[192,2048]{1,0:T(8,128)(2,1)}, bf16[192,2048]{1,0:T(8,128)(2,1)}, u32[]{:S(2)}, u32[]{:S(2)}) collective-permute-start(bf16[192,2048]{1,0:T(8,128)(2,1)} %pad_maximum_fusion.20), channel_id=1, source_target_pairs={{0,4},{4,0},{8,12},{12,8},{16,20},{20,16},{24,28},{28,24},{1,5},{5... | collective-permute-start | bytes 2359304 | tf_op jit(solution)/shard_map/ppermute | solution.py:75
  278.4 11.6 %collective-permute-start.40 = (bf16[96,2048]{1,0:T(8,128)(2,1)S(1)}, bf16[96,2048]{1,0:T(8,128)(2,1)S(1)}, u32[]{:S(2)}, u32[]{:S(2)}) collective-permute-start(bf16[96,2048]{1,0:T(8,128)(2,1)S(1)} %slice.677), channel_id=1, source_target_pairs={{0,8},{4,12},{8,0},{12,4},{16,24},{20,28},{24,16},{28,20},{1,9},{5... | collective-permute-start | bytes 1179656 | tf_op jit(solution)/shard_map/ppermute | solution.py:75
  281.0 11.3 %collective-permute-start.41 = (bf16[96,2048]{1,0:T(8,128)(2,1)S(1)}, bf16[96,2048]{1,0:T(8,128)(2,1)S(1)}, u32[]{:S(2)}, u32[]{:S(2)}) collective-permute-start(bf16[96,2048]{1,0:T(8,128)(2,1)S(1)} %slice.678), channel_id=1, source_target_pairs={{0,16},{4,20},{8,24},{12,28},{16,0},{20,4},{24,8},{28,12},{1,17},{... | collective-permute-start | bytes 1179656 | tf_op jit(solution)/shard_map/ppermute | solution.py:75
  281.6 52.1 %collective-permute-start.27 = (bf16[192,2048]{1,0:T(8,128)(2,1)}, bf16[192,2048]{1,0:T(8,128)(2,1)}, u32[]{:S(2)}, u32[]{:S(2)}) collective-permute-start(bf16[192,2048]{1,0:T(8,128)(2,1)} %bitcast.28), channel_id=1, source_target_pairs={{0,4},{4,0},{8,12},{12,8},{16,20},{20,16},{24,28},{28,24},{1,5},{5... | collective-permute-start | bytes 2359304 | tf_op jit(solution)/shard_map/ppermute | solution.py:75
  281.6 59.3 %collective-permute-start.36 = (bf16[192,2048]{1,0:T(8,128)(2,1)}, bf16[192,2048]{1,0:T(8,128)(2,1)}, u32[]{:S(2)}, u32[]{:S(2)}) collective-permute-start(bf16[192,2048]{1,0:T(8,128)(2,1)} %collective-permute-done.35), channel_id=1, source_target_pairs={{0,4},{4,0},{8,12},{12,8},{16,20},{20,16},{24,28},{28,24},{1,5},{5... | collective-permute-start | bytes 2359304 | tf_op jit(solution)/shard_map/ppermute | solution.py:75
  290.0 18.9 %collective-permute-start.30 = (bf16[192,2048]{1,0:T(8,128)(2,1)}, bf16[192,2048]{1,0:T(8,128)(2,1)}, u32[]{:S(2)}, u32[]{:S(2)}) collective-permute-start(bf16[192,2048]{1,0:T(8,128)(2,1)} %collective-permute-done.29), channel_id=1, source_target_pairs={{0,4},{4,0},{8,12},{12,8},{16,20},{20,16},{24,28},{28,24},{1,5},{5... | collective-permute-start | bytes 2359304 | tf_op jit(solution)/shard_map/ppermute | solution.py:75
  297.3 20.5 %collective-permute-start.42 = (bf16[192,2048]{1,0:T(8,128)(2,1)}, bf16[192,2048]{1,0:T(8,128)(2,1)}, u32[]{:S(2)}, u32[]{:S(2)}) collective-permute-start(bf16[192,2048]{1,0:T(8,128)(2,1)} %pad_maximum_fusion.19), channel_id=1, source_target_pairs={{0,4},{4,0},{8,12},{12,8},{16,20},{20,16},{24,28},{28,24},{1,5},{5... | collective-permute-start | bytes 2359304 | tf_op jit(solution)/shard_map/ppermute | solution.py:75
  303.0 26.7 %collective-permute-start.26 = (bf16[192,2048]{1,0:T(8,128)(2,1)}, bf16[192,2048]{1,0:T(8,128)(2,1)}, u32[]{:S(2)}, u32[]{:S(2)}) collective-permute-start(bf16[192,2048]{1,0:T(8,128)(2,1)} %get-tuple-element.117), channel_id=1, source_target_pairs={{0,4},{4,0},{8,12},{12,8},{16,20},{20,16},{24,28},{28,24},{1,5},{5... | collective-permute-start | bytes 2359304 | tf_op jit(solution)/shard_map/ppermute | solution.py:75
  308.9 16.7 %collective-permute-start.38 = (bf16[192,2048]{1,0:T(8,128)(2,1)}, bf16[192,2048]{1,0:T(8,128)(2,1)}, u32[]{:S(2)}, u32[]{:S(2)}) collective-permute-start(bf16[192,2048]{1,0:T(8,128)(2,1)} %collective-permute-done.37), channel_id=1, source_target_pairs={{0,4},{4,0},{8,12},{12,8},{16,20},{20,16},{24,28},{28,24},{1,5},{5... | collective-permute-start | bytes 2359304 | tf_op jit(solution)/shard_map/ppermute | solution.py:75
  325.0 23.6 %collective-permute-start.33 = (bf16[192,2048]{1,0:T(8,128)(2,1)S(1)}, bf16[192,2048]{1,0:T(8,128)(2,1)S(1)}, u32[]{:S(2)}, u32[]{:S(2)}) collective-permute-start(bf16[192,2048]{1,0:T(8,128)(2,1)S(1)} %slice.670), channel_id=1, source_target_pairs={{0,4},{4,0},{8,12},{12,8},{16,20},{20,16},{24,28},{28,24},{1,5},{5... | collective-permute-start | bytes 2359304 | tf_op jit(solution)/shard_map/ppermute | solution.py:75
  325.6 24.0 %collective-permute-start.46 = (bf16[192,2048]{1,0:T(8,128)(2,1)S(1)}, bf16[192,2048]{1,0:T(8,128)(2,1)S(1)}, u32[]{:S(2)}, u32[]{:S(2)}) collective-permute-start(bf16[192,2048]{1,0:T(8,128)(2,1)S(1)} %slice.684), channel_id=1, source_target_pairs={{0,4},{4,0},{8,12},{12,8},{16,20},{20,16},{24,28},{28,24},{1,5},{5... | collective-permute-start | bytes 2359304 | tf_op jit(solution)/shard_map/ppermute | solution.py:75
  348.1 34.6 %collective-permute-start.28 = (bf16[192,2048]{1,0:T(8,128)(2,1)S(1)}, bf16[192,2048]{1,0:T(8,128)(2,1)S(1)}, u32[]{:S(2)}, u32[]{:S(2)}) collective-permute-start(bf16[192,2048]{1,0:T(8,128)(2,1)S(1)} %slice.666), channel_id=1, source_target_pairs={{0,4},{4,0},{8,12},{12,8},{16,20},{20,16},{24,28},{28,24},{1,5},{5... | collective-permute-start | bytes 2359304 | tf_op jit(solution)/shard_map/ppermute | solution.py:75
  349.0 23.9 %collective-permute-start.34 = (bf16[96,2048]{1,0:T(8,128)(2,1)S(1)}, bf16[96,2048]{1,0:T(8,128)(2,1)S(1)}, u32[]{:S(2)}, u32[]{:S(2)}) collective-permute-start(bf16[96,2048]{1,0:T(8,128)(2,1)S(1)} %slice.671), channel_id=1, source_target_pairs={{0,8},{4,12},{8,0},{12,4},{16,24},{20,28},{24,16},{28,20},{1,9},{5... | collective-permute-start | bytes 1179656 | tf_op jit(solution)/shard_map/ppermute | solution.py:75
  349.9 19.0 %collective-permute-start.47 = (bf16[96,2048]{1,0:T(8,128)(2,1)S(1)}, bf16[96,2048]{1,0:T(8,128)(2,1)S(1)}, u32[]{:S(2)}, u32[]{:S(2)}) collective-permute-start(bf16[96,2048]{1,0:T(8,128)(2,1)S(1)} %get-tuple-element.195), channel_id=1, source_target_pairs={{0,8},{4,12},{8,0},{12,4},{16,24},{20,28},{24,16},{28,20},{1,9},{5... | collective-permute-start | bytes 1179656 | tf_op jit(solution)/shard_map/ppermute | solution.py:75
  351.9 28.4 %collective-permute-start.51 = (bf16[96,2048]{1,0:T(8,128)(2,1)S(1)}, bf16[96,2048]{1,0:T(8,128)(2,1)S(1)}, u32[]{:S(2)}, u32[]{:S(2)}) collective-permute-start(bf16[96,2048]{1,0:T(8,128)(2,1)S(1)} %slice.688), channel_id=1, source_target_pairs={{0,16},{4,20},{8,24},{12,28},{16,0},{20,4},{24,8},{28,12},{1,17},{... | collective-permute-start | bytes 1179656 | tf_op jit(solution)/shard_map/ppermute | solution.py:75
  352.5 19.7 %collective-permute-start.49 = (bf16[96,2048]{1,0:T(8,128)(2,1)S(1)}, bf16[96,2048]{1,0:T(8,128)(2,1)S(1)}, u32[]{:S(2)}, u32[]{:S(2)}) collective-permute-start(bf16[96,2048]{1,0:T(8,128)(2,1)S(1)} %get-tuple-element.196), channel_id=1, source_target_pairs={{0,16},{4,20},{8,24},{12,28},{16,0},{20,4},{24,8},{28,12},{1,17},{... | collective-permute-start | bytes 1179656 | tf_op jit(solution)/shard_map/ppermute | solution.py:75
  369.0 11.2 %collective-permute-start.48 = (bf16[96,2048]{1,0:T(8,128)(2,1)S(1)}, bf16[96,2048]{1,0:T(8,128)(2,1)S(1)}, u32[]{:S(2)}, u32[]{:S(2)}) collective-permute-start(bf16[96,2048]{1,0:T(8,128)(2,1)S(1)} %add_convert_fusion.25), channel_id=1, source_target_pairs={{0,16},{4,20},{8,24},{12,28},{16,0},{20,4},{24,8},{28,12},{1,17},{... | collective-permute-start | bytes 1179656 | tf_op jit(solution)/shard_map/ppermute | solution.py:75
  386.8 17.7 %collective-permute-start.58 = (bf16[192,2048]{1,0:T(8,128)(2,1)S(1)}, bf16[192,2048]{1,0:T(8,128)(2,1)S(1)}, u32[]{:S(2)}, u32[]{:S(2)}) collective-permute-start(bf16[192,2048]{1,0:T(8,128)(2,1)S(1)} %get-tuple-element.119), channel_id=1, source_target_pairs={{0,16},{4,20},{8,24},{12,28},{16,0},{20,4},{24,8},{28,12},{1,17},{... | collective-permute-start | bytes 2359304 | tf_op jit(solution)/shard_map/ppermute | solution.py:75
  387.3 17.7 %collective-permute-start.54 = (bf16[192,2048]{1,0:T(8,128)(2,1)S(1)}, bf16[192,2048]{1,0:T(8,128)(2,1)S(1)}, u32[]{:S(2)}, u32[]{:S(2)}) collective-permute-start(bf16[192,2048]{1,0:T(8,128)(2,1)S(1)} %get-tuple-element.119), channel_id=1, source_target_pairs={{0,8},{4,12},{8,0},{12,4},{16,24},{20,28},{24,16},{28,20},{1,9},{5... | collective-permute-start | bytes 2359304 | tf_op jit(solution)/shard_map/ppermute | solution.py:75
  388.9 19.0 %collective-permute-start.52 = (bf16[192,2048]{1,0:T(8,128)(2,1)S(1)}, bf16[192,2048]{1,0:T(8,128)(2,1)S(1)}, u32[]{:S(2)}, u32[]{:S(2)}) collective-permute-start(bf16[192,2048]{1,0:T(8,128)(2,1)S(1)} %get-tuple-element.119), channel_id=1, source_target_pairs={{0,4},{4,0},{8,12},{12,8},{16,20},{20,16},{24,28},{28,24},{1,5},{5... | collective-permute-start | bytes 2359304 | tf_op jit(solution)/shard_map/ppermute | solution.py:75
  453.0 231.2 %reduce-scatter.9.cloned.1.call-start = ((), (), s32[]{:S(2)}) async-start(), calls=%async_computation.12 | async-start | bytes 7208960 | tf_op jit(solution)/shard_map/reduce_scatter | solution.py:144
  483.4 210.4 %reduce-scatter.11.cloned.1.call-start = ((), (), s32[]{:S(2)}) async-start(), calls=%async_computation.13 | async-start | bytes 3604480 | tf_op jit(solution)/shard_map/reduce_scatter | solution.py:144
  489.0 199.8 %collective-permute-start.53 = (bf16[192,2048]{1,0:T(8,128)(2,1)}, bf16[192,2048]{1,0:T(8,128)(2,1)}, u32[]{:S(2)}, u32[]{:S(2)}) collective-permute-start(bf16[192,2048]{1,0:T(8,128)(2,1)} %slice.690), channel_id=1, source_target_pairs={{0,4},{4,0},{8,12},{12,8},{16,20},{20,16},{24,28},{28,24},{1,5},{5... | collective-permute-start | bytes 2359304 | tf_op jit(solution)/shard_map/ppermute | solution.py:75
  515.4 189.1 %reduce-scatter.13.cloned.1.call-start = ((), (), s32[]{:S(2)}) async-start(), calls=%async_computation.14 | async-start | bytes 1064960
  525.3 40.7 %collective-permute-start.70 = (bf16[192,1536]{1,0:T(8,128)(2,1)S(1)}, bf16[192,1536]{1,0:T(8,128)(2,1)S(1)}, u32[]{:S(2)}, u32[]{:S(2)}) collective-permute-start(bf16[192,1536]{1,0:T(8,128)(2,1)S(1)} %slice.712), channel_id=1, source_target_pairs={{0,4},{4,0},{8,12},{12,8},{16,20},{20,16},{24,28},{28,24},{1,5},{5... | collective-permute-start | bytes 1769480 | tf_op jit(solution)/shard_map/ppermute | solution.py:75
  530.7 146.7 %collective-permute-start.69 = (bf16[96,2048]{1,0:T(8,128)(2,1)}, bf16[96,2048]{1,0:T(8,128)(2,1)}, u32[]{:S(2)}, u32[]{:S(2)}) collective-permute-start(bf16[96,2048]{1,0:T(8,128)(2,1)} %slice.704), channel_id=1, source_target_pairs={{0,16},{4,20},{8,24},{12,28},{16,0},{20,4},{24,8},{28,12},{1,17},{... | collective-permute-start | bytes 1179656 | tf_op jit(solution)/shard_map/ppermute | solution.py:75
  533.4 15.6 %collective-permute-start.77 = (bf16[96,1536]{1,0:T(8,128)(2,1)S(1)}, bf16[96,1536]{1,0:T(8,128)(2,1)S(1)}, u32[]{:S(2)}, u32[]{:S(2)}) collective-permute-start(bf16[96,1536]{1,0:T(8,128)(2,1)S(1)} %get-tuple-element.200), channel_id=1, source_target_pairs={{0,16},{4,20},{8,24},{12,28},{16,0},{20,4},{24,8},{28,12},{1,17},{... | collective-permute-start | bytes 884744 | tf_op jit(solution)/shard_map/ppermute | solution.py:75
  550.8 13.3 %collective-permute-start.79 = (bf16[96,1536]{1,0:T(8,128)(2,1)S(1)}, bf16[96,1536]{1,0:T(8,128)(2,1)S(1)}, u32[]{:S(2)}, u32[]{:S(2)}) collective-permute-start(bf16[96,1536]{1,0:T(8,128)(2,1)S(1)} %slice.736), channel_id=1, source_target_pairs={{0,16},{4,20},{8,24},{12,28},{16,0},{20,4},{24,8},{28,12},{1,17},{... | collective-permute-start | bytes 884744 | tf_op jit(solution)/shard_map/ppermute | solution.py:75
  602.5 12.0 %collective-permute-start.65 = (bf16[96,2048]{1,0:T(8,128)(2,1)S(1)}, bf16[96,2048]{1,0:T(8,128)(2,1)S(1)}, u32[]{:S(2)}, u32[]{:S(2)}) collective-permute-start(bf16[96,2048]{1,0:T(8,128)(2,1)S(1)} %copy-done.59), channel_id=1, source_target_pairs={{0,8},{4,12},{8,0},{12,4},{16,24},{20,28},{24,16},{28,20},{1,9},{5... | collective-permute-start | bytes 1179656 | tf_op jit(solution)/shard_map/ppermute | solution.py:75
  604.1 55.0 %collective-permute-start.80 = (bf16[256,1664]{0,1:T(8,128)(2,1)S(1)}, bf16[256,1664]{0,1:T(8,128)(2,1)S(1)}, u32[]{:S(2)}, u32[]{:S(2)}) collective-permute-start(bf16[256,1664]{0,1:T(8,128)(2,1)S(1)} %get-tuple-element.131), channel_id=1, source_target_pairs={{0,4},{4,0},{8,12},{12,8},{16,20},{20,16},{24,28},{28,24},{1,5},{5... | collective-permute-start | bytes 2555912 | tf_op jit(solution)/shard_map/ppermute | solution.py:75
  606.1 17.6 %collective-permute-start.85 = (bf16[128,1664]{0,1:T(8,128)(2,1)S(1)}, bf16[128,1664]{0,1:T(8,128)(2,1)S(1)}, u32[]{:S(2)}, u32[]{:S(2)}) collective-permute-start(bf16[128,1664]{0,1:T(8,128)(2,1)S(1)} %get-tuple-element.172), channel_id=1, source_target_pairs={{0,8},{4,12},{8,0},{12,4},{16,24},{20,28},{24,16},{28,20},{1,9},{5... | collective-permute-start | bytes 1277960 | tf_op jit(solution)/shard_map/ppermute | solution.py:75
  614.7 20.7 %collective-permute-start.82 = (bf16[128,1664]{0,1:T(8,128)(2,1)S(1)}, bf16[128,1664]{0,1:T(8,128)(2,1)S(1)}, u32[]{:S(2)}, u32[]{:S(2)}) collective-permute-start(bf16[128,1664]{0,1:T(8,128)(2,1)S(1)} %slice.749), channel_id=1, source_target_pairs={{0,8},{4,12},{8,0},{12,4},{16,24},{20,28},{24,16},{28,20},{1,9},{5... | collective-permute-start | bytes 1277960 | tf_op jit(solution)/shard_map/ppermute | solution.py:75
  633.9 12.8 %collective-permute-start.86 = (bf16[128,1664]{0,1:T(8,128)(2,1)S(1)}, bf16[128,1664]{0,1:T(8,128)(2,1)S(1)}, u32[]{:S(2)}, u32[]{:S(2)}) collective-permute-start(bf16[128,1664]{0,1:T(8,128)(2,1)S(1)} %add_convert_fusion.21), channel_id=1, source_target_pairs={{0,16},{4,20},{8,24},{12,28},{16,0},{20,4},{24,8},{28,12},{1,17},{... | collective-permute-start | bytes 1277960 | tf_op jit(solution)/shard_map/ppermute | solution.py:75
  635.4 17.0 %collective-permute-start.89 = (bf16[128,1664]{0,1:T(8,128)(2,1)S(1)}, bf16[128,1664]{0,1:T(8,128)(2,1)S(1)}, u32[]{:S(2)}, u32[]{:S(2)}) collective-permute-start(bf16[128,1664]{0,1:T(8,128)(2,1)S(1)} %slice.760), channel_id=1, source_target_pairs={{0,16},{4,20},{8,24},{12,28},{16,0},{20,4},{24,8},{28,12},{1,17},{... | collective-permute-start | bytes 1277960 | tf_op jit(solution)/shard_map/ppermute | solution.py:75
  652.4 15.8 %collective-permute-start.57 = (bf16[96,2048]{1,0:T(8,128)(2,1)S(1)}, bf16[96,2048]{1,0:T(8,128)(2,1)S(1)}, u32[]{:S(2)}, u32[]{:S(2)}) collective-permute-start(bf16[96,2048]{1,0:T(8,128)(2,1)S(1)} %copy-done.57), channel_id=1, source_target_pairs={{0,8},{4,12},{8,0},{12,4},{16,24},{20,28},{24,16},{28,20},{1,9},{5... | collective-permute-start | bytes 1179656 | tf_op jit(solution)/shard_map/ppermute | solution.py:75
  659.1 11.0 %collective-permute-start.66 = (bf16[96,2048]{1,0:T(8,128)(2,1)S(1)}, bf16[96,2048]{1,0:T(8,128)(2,1)}, u32[]{:S(2)}, u32[]{:S(2)}) collective-permute-start(bf16[96,2048]{1,0:T(8,128)(2,1)S(1)} %add_convert_fusion.23), channel_id=1, source_target_pairs={{0,16},{4,20},{8,24},{12,28},{16,0},{20,4},{24,8},{28,12},{1,17},{... | collective-permute-start | bytes 1179656 | tf_op jit(solution)/shard_map/ppermute | solution.py:75
  684.2 26.4 %all-to-all-start.3 = ((bf16[8,64,1408]{2,1,0:T(8,128)(2,1)}), bf16[8,64,1408]{2,1,0:T(8,128)(2,1)}, u32[]{:S(2)}, u32[]{:S(2)}) async-start(bf16[8,64,1408]{2,1,0:T(8,128)(2,1)} %bitcast.158), calls=%async_computation.5 | async-start | bytes 2883584 | tf_op jit(solution)/shard_map/all_to_all | solution.py:157
  (130 other events, 1133.4 us)
Sparse Core Ops, SparseCore 0:
  21.4 76.3 all-gather.3
  99.4 105.3 all-gather.5
  206.4 57.4 all-gather.7
  453.2 61.0 reduce-scatter.6
  516.4 102.2 reduce-scatter.8
  620.9 56.7 reduce-scatter.10
  680.5 23.9 reduce-scatter.12

commit v3 on v2

v3 whole, which is shorter than its diff:
```python
import functools

import jax
import jax.numpy as jnp
from jax import lax
from jax.experimental import pallas as pl
from jax.experimental.pallas import tpu as pltpu
from jax.sharding import PartitionSpec as P

HEADS = 16
HEAD_DIM = 256


EPS = 1e-05
ROPE_BASE = 10000.0
NEGATIVE = -1e30
BF = jnp.bfloat16
F32 = jnp.float32
SMALL = pl.CostEstimate(flops=1024, bytes_accessed=1024, transcendentals=0)


def rms_norm(values, norm_gain):
    return values * lax.rsqrt(jnp.mean(values * values, axis=-1, keepdims=True) + EPS) * norm_gain


def rope_tables(position, feature_width):
    half_width = feature_width // 2
    freqs = ROPE_BASE ** (-jnp.arange(half_width, dtype=F32) * 2.0 / feature_width)
    angles = position.astype(F32)[:, None] * freqs[None, :]
    return (jnp.cos(angles), jnp.sin(angles))


def rotate(values, cosine, sine_part):
    half_width = values.shape[-1] // 2
    first_half = values[..., :half_width]
    second_half = values[..., half_width:]
    return jnp.concatenate(
        [
            first_half * cosine - second_half * sine_part,
            second_half * cosine + first_half * sine_part,
        ],
        axis=-1,
    )


def document_starts(lengths_row, group_len):
    doc_ends = jnp.cumsum(lengths_row)
    places = jnp.arange(group_len, dtype=jnp.int32)
    past_ends = (places[:, None] >= doc_ends[None, :]).astype(jnp.int32)
    starts = jnp.sum(past_ends * lengths_row[None, :], axis=1)
    return (starts, places - starts)


def gated(gate_proj, upward):
    return jax.nn.silu(gate_proj) * upward


def matmul(left_side, right_side):
    return jnp.dot(left_side, right_side, preferred_element_type=F32)


def dot_rows(left_side, right_side):
    return lax.dot_general(
        left_side, right_side, (((1,), (1,)), ((), ())), preferred_element_type=F32
    )


def dot_cols(left_side, right_side):
    return lax.dot_general(
        left_side, right_side, (((0,), (0,)), ((), ())), preferred_element_type=F32
    )


def flip(block, bits):
    n_seq = lax.axis_size("seq")
    return lax.ppermute(block, "seq", [(i, i ^ bits) for i in range(n_seq)])


def gather_near(rows):
    n_seq = lax.axis_size("seq")
    hops = (2, 4) if n_seq == 8 else range(2, n_seq, 2)
    return {0: rows} | {bits: flip(rows, bits) for bits in hops}


def gather_far(blocks):
    if lax.axis_size("seq") != 8:
        return blocks
    half = blocks[0].shape[0] // 2
    far = [flip(blocks[4][:half], 2), flip(blocks[2][half:], 4)]
    return blocks | {6: jnp.concatenate(far, axis=0)}


def gather_cores(blocks):
    whole = []
    for bits in range(0, lax.axis_size("seq"), 2):
        whole += [blocks[bits], flip(blocks[bits], 1)]
    return whole


def gather_blocks(rows):
    return gather_cores(gather_far(gather_near(rows)))


def together(*values):
    flat, tree = jax.tree.flatten(values)
    return jax.tree.unflatten(tree, lax.optimization_barrier(flat))


def stack_kernel(count, *refs):
    sources, target, held, arrived, left = refs[:count], *refs[count:]
    rows = sources[0].shape[0]
    moves = []
    for k, source in enumerate(sources):
        here = pl.ds(k * rows, rows)
        moves.append(
            (
                pltpu.make_async_copy(source, held.at[here], arrived.at[k]),
                pltpu.make_async_copy(held.at[here], target.at[here], left.at[k]),
            )
        )
    for come, _ in moves:
        come.start()
    for come, go in moves:
        come.wait()
        go.start()
    for _, go in moves:
        go.wait()


def stack_blocks(blocks):
    rows, width = blocks[0].shape
    shape, dtype = (len(blocks) * rows, width), blocks[0].dtype
    size = shape[0] * width * dtype.itemsize
    return pl.pallas_call(
        functools.partial(stack_kernel, len(blocks)),
        in_specs=[pl.BlockSpec(memory_space=pl.ANY)] * len(blocks),
        out_specs=pl.BlockSpec(memory_space=pl.ANY),
        out_shape=jax.ShapeDtypeStruct(shape, dtype),
        scratch_shapes=[pltpu.VMEM(shape, dtype)]
        + [pltpu.SemaphoreType.DMA((len(blocks),))] * 2,
        compiler_params=pltpu.CompilerParams(vmem_limit_bytes=size + 4 * 2**20),
        cost_estimate=SMALL,
        name="stack_blocks",
    )(*blocks)


def gather_seq(rows):
    return stack_blocks(gather_blocks(rows))


def plus(first, second):
    return (first.astype(F32) + second.astype(F32)).astype(BF)


def chip_sums(even, odd, count):
    total = plus(even, flip(odd, 1))
    rows = total.shape[0] // count
    return [total[k * rows : (k + 1) * rows] for k in range(count)]


def scatter_relay(sums):
    n_seq = lax.axis_size("seq")
    if n_seq != 8:
        return {k: [part] for k, part in enumerate(sums)}
    half = sums[0].shape[0] // 2
    far_x = flip(sums[3][:half], 2)
    far_y = flip(sums[3][half:], 4)
    return {
        0: [sums[0]],
        1: [sums[1][:half], plus(sums[1][half:], far_y)],
        2: [sums[2][half:], plus(sums[2][:half], far_x)],
    }


def scatter_last(left):
    n_seq = lax.axis_size("seq")
    if n_seq != 8:
        return sum(
            (flip(parts[0], 2 * k) if k else parts[0]).astype(F32) for k, parts in left.items()
        )
    x_low, x_high = [flip(part, 2).astype(F32) for part in left[1]]
    y_high, y_low = [flip(part, 4).astype(F32) for part in left[2]]
    return left[0][0].astype(F32) + jnp.concatenate([x_low + y_low, x_high + y_high], axis=0)


def scatter_pairs(even, odd):
    count = lax.axis_size("seq") // 2
    return scatter_last(scatter_relay(chip_sums(even, odd, count)))


def relative(values, axis):
    n_seq, me = lax.axis_size("seq"), lax.axis_index("seq")
    size = values.shape[axis] // n_seq
    parts = [
        lax.dynamic_slice_in_dim(values, (me ^ k) * size, size, axis) for k in range(n_seq)
    ]
    return jnp.concatenate(parts, axis=axis)


def relative_vectors(values):
    n_seq, me = lax.axis_size("seq"), lax.axis_index("seq")
    count, length = values.shape
    values = values.reshape(count, n_seq, length // n_seq)
    bit = 1
    while bit < n_seq:
        pairs = values.reshape(count, n_seq // (2 * bit), 2, bit, length // n_seq)
        swapped = jnp.concatenate([pairs[:, :, 1:], pairs[:, :, :1]], axis=2)
        values = jnp.where((me & bit) != 0, swapped, pairs).reshape(values.shape)
        bit *= 2
    return values.reshape(count, length)


def gather_dp(rows):
    return lax.all_gather(rows, "dp", axis=0, tiled=True)


def gather_dp_steps(rows):
    n_dp, me = lax.axis_size("dp"), lax.axis_index("dp")
    size = rows.shape[0]
    whole = jnp.zeros((n_dp * size, rows.shape[1]), rows.dtype)
    for bits in range(n_dp):
        block = rows
        if bits:
            block = lax.ppermute(rows, "dp", [(i, i ^ bits) for i in range(n_dp)])
        whole = lax.dynamic_update_slice_in_dim(whole, block, (me ^ bits) * size, 0)
    return whole


def scatter_dp(terms):
    return lax.psum_scatter(terms, "dp", scatter_dimension=0, tiled=True)


def split_columns(shard):
    n_seq = lax.axis_size("seq")
    rows, width = shard.shape
    return shard.reshape(rows, n_seq, width // n_seq).transpose(1, 0, 2)


def exchange(parts):
    return lax.all_to_all(parts, "seq", 0, 0)


def rows_in_order(gathered, rows):
    n_seq, n_dp = lax.axis_size("seq"), lax.axis_size("dp")
    width = gathered.shape[-1]
    return gathered.reshape(n_dp, n_seq, rows, width).transpose(1, 0, 2, 3).reshape(-1, width)


def rows_by_dp(terms):
    n_seq, n_dp = lax.axis_size("seq"), lax.axis_size("dp")
    total, width = terms.shape
    rows = total // (n_seq * n_dp)
    return terms.reshape(n_seq, n_dp, rows, width).transpose(1, 0, 2, 3)


def first_kernel(count, low_width, x_ref, *refs):
    blocks, (out_ref, normed_ref, gains_ref) = refs[:count], refs[count:]
    rows = blocks[0].shape[0]
    x = x_ref[...].astype(F32)
    scale = lax.rsqrt(jnp.mean(x * x, axis=1, keepdims=True) + EPS)
    for k in range(count):
        here = slice(k * rows, (k + 1) * rows)
        gains = blocks[k][:, low_width:].astype(F32).T
        gains_ref[:, here] = gains[: gains_ref.shape[0]]
        normed = (x_ref[:, here].astype(F32) * scale * gains[:1]).astype(BF)
        normed_ref[:, here] = normed
        part = matmul(normed, blocks[k][:, :low_width])
        if k == 0:
            out_ref[...] = part
        else:
            out_ref[...] += part


def first_projections(x, blocks, low_width):
    tok_count, width = x.shape
    vmem = pl.BlockSpec(memory_space=pltpu.VMEM)
    return pl.pallas_call(
        functools.partial(first_kernel, len(blocks), low_width),
        in_specs=[vmem] * (1 + len(blocks)),
        out_specs=[vmem] * 3,
        out_shape=[
            jax.ShapeDtypeStruct((tok_count, low_width), F32),
            jax.ShapeDtypeStruct((tok_count, width), BF),
            jax.ShapeDtypeStruct((8, width), F32),
        ],
        compiler_params=pltpu.CompilerParams(vmem_limit_bytes=40 * 2**20),
        cost_estimate=SMALL,
        name="first_projections",
    )(x, *blocks)


def weights_in_order(raw_ref, gate_ref, up_ref):
    n_dp, n_seq, _, rows, _ = raw_ref.shape
    for s in range(n_seq):
        for z in range(n_dp):
            here = pl.ds((s * n_dp + z) * rows, rows)
            gate_ref[here, :] = raw_ref[z, s, 0]
            up_ref[here, :] = raw_ref[z, s, 1]


def feed_kernel(count, block, *refs):
    blocks, raw_ref = refs[:count], refs[count]
    x_ref, act_ref, silu_ref, slope_ref, gate_ref, up_ref = refs[count + 1 :]
    at = pl.program_id(0)

    @pl.when(at == 0)
    def _():
        rows = blocks[0].shape[0]
        for k, source in enumerate(blocks):
            x_ref[k * rows : (k + 1) * rows, :] = source[...]
        weights_in_order(raw_ref, gate_ref, up_ref)

    x = x_ref[pl.ds(pl.multiple_of(at * block, block), block), :]
    gate = matmul(x, gate_ref[...])
    upward = matmul(x, up_ref[...])
    sigmoid = 1.0 / (1.0 + jnp.exp(-gate))
    silu = gate * sigmoid
    act_ref[...] = (silu * upward).astype(BF)
    silu_ref[...] = silu.astype(BF)
    slope_ref[...] = (upward * (sigmoid + silu * (1.0 - sigmoid))).astype(BF)


def whole_spec(shape):
    return pl.BlockSpec(shape, lambda *_: (0,) * len(shape), pipeline_mode=pl.Buffered(1))


def feed_forward(blocks, raw, block):
    rows, width = blocks[0].shape
    group_len = rows * len(blocks)
    hidden = raw.shape[-1]
    units = pl.BlockSpec((block, hidden), lambda i: (i, 0))
    weight = jax.ShapeDtypeStruct((width, hidden), BF)
    return pl.pallas_call(
        functools.partial(feed_kernel, len(blocks), block),
        grid=(group_len // block,),
        in_specs=[whole_spec((rows, width))] * len(blocks) + [whole_spec(raw.shape)],
        out_specs=[whole_spec((group_len, width))]
        + [units] * 3
        + [whole_spec((width, hidden))] * 2,
        out_shape=[jax.ShapeDtypeStruct((group_len, width), BF)]
        + [jax.ShapeDtypeStruct((group_len, hidden), BF)] * 3
        + [weight] * 2,
        compiler_params=pltpu.CompilerParams(vmem_limit_bytes=52 * 2**20),
        cost_estimate=SMALL,
        name="feed_forward",
    )(*blocks, raw)


def feed_back_kernel(
    d_ref, silu_ref, slope_ref, gate_ref, up_ref, down_ref, dg_ref, du_ref, even_ref, odd_ref
):
    d_active = dot_rows(d_ref[...], down_ref[...])
    d_gate = (d_active * slope_ref[...].astype(F32)).astype(BF)
    d_up = (d_active * silu_ref[...].astype(F32)).astype(BF)
    dg_ref[...] = d_gate
    du_ref[...] = d_up
    terms = (dot_rows(d_gate, gate_ref[...]) + dot_rows(d_up, up_ref[...])).astype(BF)
    half = terms.shape[0] // 2
    even_ref[...] = terms[:half]
    odd_ref[...] = terms[half:]


def feed_back(d, silu, slope, gate, up, down, block, first, count):
    width, hidden = gate.shape
    tokens = pl.BlockSpec((block, width), lambda i: (i + first, 0))
    units = pl.BlockSpec((block, hidden), lambda i: (i + first, 0))
    half = pl.BlockSpec((block // 2, width), lambda i: (i, 0))
    return pl.pallas_call(
        feed_back_kernel,
        grid=(count,),
        in_specs=[tokens, units, units]
        + [whole_spec(gate.shape), whole_spec(up.shape), whole_spec(down.shape)],
        out_specs=[pl.BlockSpec((block, hidden), lambda i: (i, 0))] * 2 + [half] * 2,
        out_shape=[jax.ShapeDtypeStruct((count * block, hidden), BF)] * 2
        + [jax.ShapeDtypeStruct((count * block // 2, width), BF)] * 2,
        compiler_params=pltpu.CompilerParams(vmem_limit_bytes=44 * 2**20),
        cost_estimate=SMALL,
        name="feed_back",
    )(d, silu, slope, gate, up, down)


def gate_up_grad_kernel(x_ref, dg_low, du_low, dg_high, du_high, out_ref):
    n_dp, _, _, rows, _ = out_ref.shape
    middle = dg_low.shape[0]
    low, high = x_ref[:middle, :], x_ref[middle:, :]
    for which, (d_low, d_high) in enumerate(((dg_low, dg_high), (du_low, du_high))):
        terms = (dot_cols(low, d_low[...]) + dot_cols(high, d_high[...])).astype(BF)
        for z in range(n_dp):
            out_ref[z, 0, which] = terms[z * rows : (z + 1) * rows]


def gate_up_grad(x, low, high, n_dp, n_seq):
    group_len, width = x.shape
    hidden = low[0].shape[1]
    rows = width // (n_dp * n_seq)
    return pl.pallas_call(
        gate_up_grad_kernel,
        grid=(n_seq,),
        in_specs=[pl.BlockSpec((group_len, n_dp * rows), lambda i: (0, i))]
        + [whole_spec(part.shape) for part in (*low, *high)],
        out_specs=pl.BlockSpec((n_dp, 1, 2, rows, hidden), lambda i: (0, i, 0, 0, 0)),
        out_shape=jax.ShapeDtypeStruct((n_dp, n_seq, 2, rows, hidden), BF),
        compiler_params=pltpu.CompilerParams(vmem_limit_bytes=40 * 2**20),
        cost_estimate=SMALL,
        name="gate_up_grad",
    )(x, *low, *high)


def pair_product_kernel(left_ref, right_ref, even_ref, odd_ref):
    terms = matmul(left_ref[...], right_ref[...]).astype(BF)
    half = terms.shape[0] // 2
    even_ref[...] = terms[:half]
    odd_ref[...] = terms[half:]


def pair_product(left, right, block):
    rows, depth = left.shape
    width = right.shape[1]
    half = pl.BlockSpec((block // 2, width), lambda i: (i, 0))
    return pl.pallas_call(
        pair_product_kernel,
        grid=(rows // block,),
        in_specs=[pl.BlockSpec((block, depth), lambda i: (i, 0)), whole_spec(right.shape)],
        out_specs=[half] * 2,
        out_shape=[jax.ShapeDtypeStruct((rows // 2, width), BF)] * 2,
        compiler_params=pltpu.CompilerParams(vmem_limit_bytes=32 * 2**20),
        cost_estimate=SMALL,
        name="pair_product",
    )(left, right)


def last_kernel(
    count,
    back_ref,
    latent_ref,
    query_gain_ref,
    normed_ref,
    x_ref,
    gain_ref,
    cos_ref,
    sin_ref,
    *refs,
):
    blocks, (even_ref, odd_ref, dx_ref, query_term_ref, gain_term_ref) = refs[:count], refs[count:]
    latent_width = latent_ref.shape[1]
    first_width = back_ref.shape[1]
    rows = blocks[0].shape[0]

    def norm_back(v, e, gain):
        r = lax.rsqrt(jnp.mean(v * v, axis=1, keepdims=True) + EPS)
        u = v * r
        eg = e * gain
        grad = r * (eg - u * jnp.mean(eg * u, axis=1, keepdims=True))
        return grad, jnp.sum(e * u, axis=0, keepdims=True)

    d_latent, query_term_ref[...] = norm_back(
        latent_ref[...], back_ref[:, :latent_width], query_gain_ref[...]
    )
    half = HEAD_DIM // 2
    first_half = back_ref[:, latent_width : latent_width + half]
    second_half = back_ref[:, latent_width + half : latent_width + HEAD_DIM]
    cosine, sine_part = cos_ref[...], sin_ref[...]
    d_first = jnp.concatenate(
        [
            d_latent,
            first_half * cosine + second_half * sine_part,
            second_half * cosine - first_half * sine_part,
            back_ref[:, latent_width + HEAD_DIM :],
        ],
        axis=1,
    ).astype(BF)
    for k in range(count):
        here = slice(k * rows, (k + 1) * rows)
        target = odd_ref if k % 2 else even_ref
        at = slice(k // 2 * rows, (k // 2 + 1) * rows)
        target[at, :first_width] = dot_cols(normed_ref[:, here], d_first).astype(BF)
        dx_ref[:, here] = dot_rows(d_first, blocks[k][:, :first_width])
    dx_ref[...], gain_term_ref[...] = norm_back(
        x_ref[...].astype(F32), dx_ref[...], gain_ref[...]
    )


def last_products(back, latent, query_gain, normed, x, gain, cosine, sine_part, blocks):
    tok_count, width = x.shape
    rows, first_width = blocks[0].shape
    vmem = pl.BlockSpec(memory_space=pltpu.VMEM)
    half = jax.ShapeDtypeStruct((len(blocks) // 2 * rows, first_width), BF)
    return pl.pallas_call(
        functools.partial(last_kernel, len(blocks)),
        in_specs=[vmem] * (8 + len(blocks)),
        out_specs=[vmem] * 5,
        out_shape=[
            half,
            half,
            jax.ShapeDtypeStruct((tok_count, width), F32),
            jax.ShapeDtypeStruct((1, latent.shape[1]), F32),
            jax.ShapeDtypeStruct((1, width), F32),
        ],
        compiler_params=pltpu.CompilerParams(vmem_limit_bytes=44 * 2**20),
        cost_estimate=SMALL,
        name="last_products",
    )(back, latent, query_gain, normed, x, gain, cosine, sine_part, *blocks)


def block_places(shape, axis, core):
    rows = lax.broadcasted_iota(jnp.int32, shape, axis)
    half = shape[axis] // 2
    return rows + core * jnp.where(rows < half, half, -half)


def rotate_heads(values, cosine, sine_part, scale):
    half = HEAD_DIM // 2
    parts = []
    for at in range(0, values.shape[1], HEAD_DIM):
        first_half = values[:, at : at + half]
        second_half = values[:, at + half : at + HEAD_DIM]
        parts.append((first_half * cosine - second_half * sine_part) * scale)
        parts.append((second_half * cosine + first_half * sine_part) * scale)
    return jnp.concatenate(parts, axis=1)


def attend_kernel(
    count,
    heads,
    block,
    me_ref,
    starts_ref,
    cos_ref,
    sin_ref,
    wq_ref,
    wo_ref,
    *refs,
):
    packs = refs[:count]
    lat_ref, k_ref, v_ref, q_ref, mixed_ref, lse_ref, even_ref, odd_ref, vt_ref = refs[count:]
    me = me_ref[0]
    chip, core = me >> 1, me & 1
    index = pl.program_id(0)
    at = index ^ chip
    latent_width = lat_ref.shape[1]

    @pl.when(index == 0)
    def _():
        rows = packs[0].shape[0]
        for k, pack in enumerate(packs):
            here = slice(k * rows, (k + 1) * rows)
            lat_ref[here, :] = pack[:, :latent_width]
            k_ref[here, :] = pack[:, latent_width : latent_width + HEAD_DIM]
            v_ref[here, :] = pack[:, latent_width + HEAD_DIM :]
        for j in range(count // 2):
            here = slice(j * block, (j + 1) * block)
            vt_ref[:, here] = v_ref[here, :].T

    own = pl.ds(pl.multiple_of(index * block, block), block)
    query_raw = matmul(lat_ref[own, :], wq_ref[...])
    q_ref[...] = rotate_heads(
        query_raw, cos_ref[...], sin_ref[...], HEAD_DIM ** (-0.5)
    ).astype(BF)
    starts_row = starts_ref[...]
    key_place = block_places((block, 1), 0, core)
    query_place = at * block + block_places((1, block), 1, core)
    columns = [slice(h * HEAD_DIM, (h + 1) * HEAD_DIM) for h in range(heads)]

    def step(b, running):
        here = pl.ds(pl.multiple_of((b ^ chip) * block, block), block)
        keys_here = b * block + key_place
        visible = (keys_here <= query_place) & (keys_here >= starts_row)
        result = []
        for head in range(heads):
            running_max, running_sum, total = running[head]
            scores = dot_rows(k_ref[here, :], q_ref[:, columns[head]])
            scores = jnp.where(visible, scores, NEGATIVE)
            new_max = jnp.maximum(running_max, jnp.max(scores, axis=0, keepdims=True))
            factor = jnp.exp(running_max - new_max)
            terms = jnp.where(visible, jnp.exp(scores - new_max), 0.0)
            running_sum = running_sum * factor + jnp.sum(terms, axis=0, keepdims=True)
            total = total * factor + matmul(vt_ref[:, here], terms.astype(BF))
            result.append((new_max, running_sum, total))
        return tuple(result)

    start = (
        jnp.full((1, block), NEGATIVE, F32),
        jnp.zeros((1, block), F32),
        jnp.zeros((HEAD_DIM, block), F32),
    )
    running = lax.fori_loop(0, at + 1, step, (start,) * heads)
    for head in range(heads):
        running_max, running_sum, total = running[head]
        mixed_ref[:, columns[head]] = (total / running_sum).T.astype(BF)
        lse_ref[head : head + 1, :] = running_max + jnp.log(running_sum)
    terms = matmul(mixed_ref[...], wo_ref[...]).astype(BF)
    even_ref[...] = terms[: block // 2]
    odd_ref[...] = terms[block // 2 :]


def attend(me, starts, cosine, sine_part, query_up, output, packs, latent_width, block):
    rows, pack_width = packs[0].shape
    group_len = rows * len(packs)
    width = query_up.shape[1]
    heads = width // HEAD_DIM
    out_width = output.shape[1]
    tokens = pl.BlockSpec((block, width), lambda i, me: (i, 0))
    half = pl.BlockSpec((block // 2, out_width), lambda i, me: (i, 0))
    angle = pl.BlockSpec((block, HEAD_DIM // 2), lambda i, me: (i, 0))
    lanes = pl.BlockSpec((heads, block), lambda i, me: (0, i))
    shape = jax.ShapeDtypeStruct
    return pl.pallas_call(
        functools.partial(attend_kernel, len(packs), heads, block),
        grid_spec=pltpu.PrefetchScalarGridSpec(
            num_scalar_prefetch=1,
            grid=(group_len // block,),
            in_specs=[
                pl.BlockSpec((1, block), lambda i, me: (0, i)),
                angle,
                angle,
                whole_spec(query_up.shape),
                whole_spec(output.shape),
            ]
            + [whole_spec((rows, pack_width))] * len(packs),
            out_specs=[
                whole_spec((group_len, latent_width)),
                whole_spec((group_len, HEAD_DIM)),
                whole_spec((group_len, HEAD_DIM)),
                tokens,
                tokens,
                lanes,
                half,
                half,
            ],
            scratch_shapes=[pltpu.VMEM((HEAD_DIM, group_len), BF)],
        ),
        out_shape=[
            shape((group_len, latent_width), BF),
            shape((group_len, HEAD_DIM), BF),
            shape((group_len, HEAD_DIM), BF),
            shape((group_len, width), BF),
            shape((group_len, width), BF),
            shape((heads, group_len), F32),
            shape((group_len // 2, out_width), BF),
            shape((group_len // 2, out_width), BF),
        ],
        compiler_params=pltpu.CompilerParams(vmem_limit_bytes=44 * 2**20),
        cost_estimate=SMALL,
        name="attend",
    )(me, starts.reshape(1, group_len), cosine, sine_part, query_up, output, *packs)


def attend_back_kernel(
    count,
    heads,
    block,
    me_ref,
    starts_ref,
    cos_ref,
    sin_ref,
    q_ref,
    mixed_ref,
    lse_ref,
    k_ref,
    v_ref,
    wq_ref,
    wo_ref,
    *refs,
):
    blocks = refs[:count]
    d_ref, dq_ref, even_ref, odd_ref, dk_ref, dv_ref = refs[count:]
    me = me_ref[0]
    chip, core = me >> 1, me & 1
    index = pl.program_id(0)
    at = index ^ chip
    half = block // 2
    latent_width = wq_ref.shape[0]

    @pl.when(index == 0)
    def _():
        rows = blocks[0].shape[0]
        for k, source in enumerate(blocks):
            d_ref[k * rows : (k + 1) * rows, :] = source[...]
        dk_ref[...] = jnp.zeros_like(dk_ref)
        dv_ref[...] = jnp.zeros_like(dv_ref)

    own = pl.ds(pl.multiple_of(index * block, block), block)
    d_mixed = dot_rows(d_ref[own, :], wo_ref[...]).astype(BF)
    starts_row = starts_ref[...]
    key_place = block_places((block, 1), 0, core)
    query_place = at * block + block_places((1, block), 1, core)
    columns = [slice(h * HEAD_DIM, (h + 1) * HEAD_DIM) for h in range(heads)]
    offsets = [
        jnp.sum(
            (d_mixed[:, cols].astype(F32) * mixed_ref[:, cols].astype(F32)).T,
            axis=0,
            keepdims=True,
        )
        for cols in columns
    ]

    def step(b, running):
        here = pl.ds(pl.multiple_of((b ^ chip) * block, block), block)
        keys_here = b * block + key_place
        visible = (keys_here <= query_place) & (keys_here >= starts_row)
        keys, values = k_ref[here, :], v_ref[here, :]
        result = []
        for head in range(heads):
            q, dm = q_ref[:, columns[head]], d_mixed[:, columns[head]]
            scores = dot_rows(keys, q)
            scores = jnp.where(visible, scores, NEGATIVE)
            probs = jnp.where(visible, jnp.exp(scores - lse_ref[head : head + 1, :]), 0.0)
            d_probs = dot_rows(values, dm)
            d_scores = (probs * (d_probs - offsets[head])).astype(BF)
            dv_ref[here, :] += matmul(probs.astype(BF), dm)
            dk_ref[here, :] += matmul(d_scores, q)
            result.append(running[head] + dot_cols(d_scores, keys))
        return tuple(result)

    start = (jnp.zeros((block, HEAD_DIM), F32),) * heads
    d_queries = jnp.concatenate(lax.fori_loop(0, at + 1, step, start), axis=1)
    dq_ref[...] = rotate_heads(
        d_queries, cos_ref[...], -sin_ref[...], HEAD_DIM ** (-0.5)
    ).astype(BF)
    terms = dot_rows(dq_ref[...], wq_ref[...]).astype(BF)
    rows_here = pl.ds(pl.multiple_of(index * half, half), half)
    even_ref[rows_here, :latent_width] = terms[:half]
    odd_ref[rows_here, :latent_width] = terms[half:]

    @pl.when(index == pl.num_programs(0) - 1)
    def _():
        for j in range(count // 2):
            to = slice(j * half, (j + 1) * half)
            for target, first in ((even_ref, j * block), (odd_ref, j * block + half)):
                rows = slice(first, first + half)
                target[to, latent_width : latent_width + HEAD_DIM] = dk_ref[rows, :].astype(BF)
                target[to, latent_width + HEAD_DIM :] = dv_ref[rows, :].astype(BF)


def attend_back(
    me, starts, cosine, sine_part, queries, mixed, lse, keys, values, query_up, output, blocks, block
):
    group_len, width = queries.shape
    heads = width // HEAD_DIM
    rows, out_width = blocks[0].shape
    latent_width = query_up.shape[0]
    pack_width = latent_width + 2 * HEAD_DIM
    tokens = pl.BlockSpec((block, width), lambda i, me: (i, 0))
    angle = pl.BlockSpec((block, HEAD_DIM // 2), lambda i, me: (i, 0))
    lanes = pl.BlockSpec((heads, block), lambda i, me: (0, i))
    half = (group_len // 2, pack_width)
    shape = jax.ShapeDtypeStruct
    return pl.pallas_call(
        functools.partial(attend_back_kernel, len(blocks), heads, block),
        grid_spec=pltpu.PrefetchScalarGridSpec(
            num_scalar_prefetch=1,
            grid=(group_len // block,),
            in_specs=[
                pl.BlockSpec((1, block), lambda i, me: (0, i)),
                angle,
                angle,
                tokens,
                tokens,
                lanes,
                whole_spec(keys.shape),
                whole_spec(values.shape),
                whole_spec(query_up.shape),
                whole_spec(output.shape),
            ]
            + [whole_spec((rows, out_width))] * len(blocks),
            out_specs=[
                whole_spec((group_len, out_width)),
                tokens,
                whole_spec(half),
                whole_spec(half),
            ],
            scratch_shapes=[pltpu.VMEM((group_len, HEAD_DIM), F32)] * 2,
        ),
        out_shape=[
            shape((group_len, out_width), BF),
            shape((group_len, width), BF),
            shape(half, BF),
            shape(half, BF),
        ],
        compiler_params=pltpu.CompilerParams(vmem_limit_bytes=48 * 2**20),
        cost_estimate=SMALL,
        name="attend_back",
    )(
        me,
        starts.reshape(1, group_len),
        cosine,
        sine_part,
        queries,
        mixed,
        lse,
        keys,
        values,
        query_up,
        output,
        *blocks,
    )


def local(
    layer_input,
    doc_lengths,
    attention_gain,
    query_down,
    query_gain,
    query_up,
    keyvalue_weight,
    output_weight,
    feedforward_gain,
    gate_weight,
    up_weight,
    down_weight,
    cotangent,
):
    n_seq, n_dp = lax.axis_size("seq"), lax.axis_size("dp")
    me = lax.axis_index("seq")
    input_low = layer_input[0]
    tokens = input_low.astype(F32)
    tok_count, width = tokens.shape
    latent_width = query_down.shape[1]
    group_len = tok_count * n_seq
    heads = HEADS // n_seq
    hidden_units = gate_weight.shape[1] // n_seq

    starts_all, position_all = document_starts(doc_lengths[0], group_len)
    starts_all = relative(starts_all, 0)
    position_all = relative(position_all, 0)
    cosine_all, sine_all = rope_tables(position_all, HEAD_DIM)
    me_array = me.astype(jnp.int32).reshape(1)

    own_rows = query_down.shape[0]
    query_rows = query_gain.shape[0]
    gains = jnp.stack(
        [attention_gain, feedforward_gain, jnp.pad(query_gain, (0, own_rows - query_rows))], axis=1
    )
    first_set = jnp.concatenate(
        [query_down, keyvalue_weight, jnp.pad(gains, ((0, 0), (0, 125)))], axis=1
    )
    first_set, query_up = together(first_set, query_up)
    first_part = gather_dp_steps(first_set)
    d_feed_blocks = gather_near(cotangent[0])
    query_part = exchange(split_columns(query_up)).reshape(-1, query_up.shape[1] // n_seq)
    fold = query_part.shape[0] * query_part.shape[1] // width
    attention_set = jnp.concatenate([output_weight, query_part.reshape(fold, width)], axis=0)
    first_part, d_feed_blocks, cosine_all, sine_all, attention_set = together(
        first_part, d_feed_blocks, cosine_all, sine_all, attention_set
    )
    cosine, sine_part = cosine_all[:tok_count], sine_all[:tok_count]
    attention_part = gather_dp(attention_set)
    gate_weight, up_weight, first_part = together(gate_weight, up_weight, first_part)
    gate_up = exchange(jnp.stack([split_columns(gate_weight), split_columns(up_weight)], axis=1))
    first_blocks, gate_up, d_feed_blocks = together(
        gather_blocks(first_part), gate_up, d_feed_blocks
    )
    full_gate_up = gather_dp(gate_up.reshape(-1, hidden_units)).reshape(n_dp, *gate_up.shape)
    full_down = gather_dp(down_weight)
    d_feed_blocks = gather_far(d_feed_blocks)
    tokens_low_rel = relative(input_low, 1)
    first_width = latent_width + 2 * HEAD_DIM
    first_out, normed_rel, gain_rows = first_projections(
        tokens_low_rel, first_blocks, first_width
    )
    tokens_rel = tokens_low_rel.astype(F32)
    attention_gain_rel = gain_rows[0]
    other_gains = relative_vectors(gain_rows[1:3])
    feed_gain_f = other_gains[0]
    query_gain_f = other_gains[1].reshape(-1, own_rows)[:, :query_rows].reshape(-1)

    latent = first_out[:, :latent_width]
    keyvalue = first_out[:, latent_width:first_width]
    latent_low = rms_norm(latent, query_gain_f).astype(BF)
    key_local = rotate(keyvalue[:, :HEAD_DIM], cosine, sine_part)
    pack = jnp.concatenate(
        [latent_low, key_local.astype(BF), keyvalue[:, HEAD_DIM:].astype(BF)], axis=1
    )
    pack, attention_part = together(pack, attention_part)
    out_rows = output_weight.shape[0]
    attention_part = attention_part.reshape(n_dp, -1, width)
    full_output = attention_part[:, :out_rows].reshape(-1, width)
    full_query_up = rows_in_order(
        attention_part[:, out_rows:].reshape(-1, query_part.shape[1]), query_up.shape[0]
    )
    packs = gather_blocks(pack)
    d_feed = stack_blocks(gather_cores(d_feed_blocks))
    packs, full_query_up, full_output, d_feed = together(
        packs, full_query_up, full_output, d_feed
    )
    block = 2 * tok_count
    latent_all, keys, values, queries, mixed_low, lse, out_even, out_odd = attend(
        me_array,
        starts_all,
        cosine_all,
        sine_all,
        full_query_up,
        full_output,
        packs,
        latent_width,
        block,
    )

    d_result = cotangent[0].astype(F32)
    hidden = tokens + scatter_pairs(out_even, out_odd)
    hidden, full_gate_up = together(hidden, full_gate_up)

    feed_low = rms_norm(hidden, feed_gain_f).astype(BF)
    feed_blocks = gather_blocks(feed_low)
    feed, active_low, silu_low, slope_low, gate_ordered, up_ordered = feed_forward(
        feed_blocks, full_gate_up, block
    )
    grad_down_term = dot_cols(active_low, d_feed).astype(BF)
    silu_low, grad_down_term = lax.optimization_barrier((silu_low, grad_down_term))
    grad_down = scatter_dp(grad_down_term)
    half_chips = n_seq // 4
    dg_high, du_high, *terms_high = feed_back(
        d_feed,
        silu_low,
        slope_low,
        gate_ordered,
        up_ordered,
        full_down,
        block,
        half_chips,
        half_chips,
    )
    silu_again, terms_high = together(silu_low, terms_high)
    dg_low, du_low, *terms_low = feed_back(
        d_feed, silu_again, slope_low, gate_ordered, up_ordered, full_down, block, 0, half_chips
    )
    feed_sums = chip_sums(*terms_low, half_chips) + chip_sums(*terms_high, half_chips)
    feed_sums, feed = together(feed_sums, feed)
    d_feed_normed = scatter_last(scatter_relay(feed_sums))
    grad_gate_up_term = gate_up_grad(feed, (dg_low, du_low), (dg_high, du_high), n_dp, n_seq)
    d_feed_normed, grad_gate_up_term = together(d_feed_normed, grad_gate_up_term)
    grad_gate_up = scatter_dp(grad_gate_up_term.reshape(-1, hidden_units))

    d_hidden_norm, grad_feed_gain_term = jax.vjp(rms_norm, hidden, feed_gain_f)[1](d_feed_normed)
    d_hidden = d_result + d_hidden_norm
    d_branch_blocks = gather_blocks(d_hidden.astype(BF))
    result_terms = pair_product(active_low, full_down, block)
    result_sums = chip_sums(*result_terms, n_seq // 2)
    d_branch_blocks, result_sums = together(d_branch_blocks, result_sums)
    result_left = scatter_relay(result_sums)
    d_branch, d_query_low, back_even, back_odd = attend_back(
        me_array,
        starts_all,
        cosine_all,
        sine_all,
        queries,
        mixed_low,
        lse,
        keys,
        values,
        full_query_up,
        full_output,
        d_branch_blocks,
        block,
    )
    back_even, back_odd, grad_down, result_left = together(
        back_even, back_odd, grad_down, result_left
    )
    back_local = scatter_pairs(back_even, back_odd)
    grad_output_term = dot_cols(mixed_low, d_branch).astype(BF)
    grad_query_term = rows_by_dp(dot_cols(latent_all, d_query_low).astype(BF))
    grad_attention_term = jnp.concatenate(
        [
            grad_output_term.reshape(n_dp, out_rows, width),
            grad_query_term.reshape(n_dp, fold, width),
        ],
        axis=1,
    ).reshape(-1, width)
    back_local, grad_attention_term, grad_gate_up = together(
        back_local, grad_attention_term, grad_gate_up
    )
    grad_attention = scatter_dp(grad_attention_term)

    first_even, first_odd, d_tokens_rel, query_term, gain_term = last_products(
        back_local,
        latent,
        query_gain_f.reshape(1, -1),
        normed_rel,
        tokens_low_rel,
        gain_rows[:1],
        cosine,
        sine_part,
        first_blocks,
    )
    input_grad = (d_hidden + relative(d_tokens_rel, 1))[None]
    query_column = jnp.pad(
        query_term.reshape(-1, query_rows), ((0, 0), (0, own_rows - query_rows))
    ).reshape(1, -1)
    other_terms = relative_vectors(
        jnp.concatenate([grad_feed_gain_term.reshape(1, -1), query_column], axis=0)
    )
    gain_terms = jnp.concatenate([gain_term, other_terms], axis=0)
    columns = jnp.pad(gain_terms, ((0, 125), (0, 0))).T.astype(BF).reshape(n_seq, -1, 128)
    first_even = lax.dynamic_update_slice(
        first_even, columns[0::2].reshape(-1, 128), (0, first_width)
    )
    first_odd = lax.dynamic_update_slice(
        first_odd, columns[1::2].reshape(-1, 128), (0, first_width)
    )
    first_sum = scatter_pairs(first_even, first_odd).astype(BF)
    first_sum, grad_attention = lax.optimization_barrier((first_sum, grad_attention))
    grad_first = scatter_dp(first_sum).astype(F32)
    result_left, first_sum = together(result_left, first_sum)
    result = hidden + scatter_last(result_left)
    layer_output = result.astype(BF)[None]

    grad_output_weight = grad_attention[:out_rows].astype(F32)
    grad_query_up = exchange(grad_attention[out_rows:].reshape(n_seq, query_rows, -1))
    grad_query_up = grad_query_up.transpose(1, 0, 2).reshape(query_rows, -1).astype(F32)

    gate_up_rows = exchange(grad_gate_up.reshape(n_seq, 2, own_rows, -1)).astype(F32)
    grad_gate = gate_up_rows[:, 0].transpose(1, 0, 2).reshape(own_rows, -1)
    grad_up = gate_up_rows[:, 1].transpose(1, 0, 2).reshape(own_rows, -1)
    return (
        layer_output,
        input_grad,
        grad_first[:, first_width],
        grad_first[:, :latent_width],
        grad_first[:query_rows, first_width + 2],
        grad_query_up,
        grad_first[:, latent_width:first_width],
        grad_output_weight,
        grad_first[:, first_width + 1],
        grad_gate,
        grad_up,
        grad_down.astype(F32),
    )


def solution(mesh):
    shards = P(("seq", "dp"))
    tokens = P("dp", "seq", None)
    weight = P(("seq", "dp"), None)
    return jax.shard_map(
        local,
        mesh=mesh,
        in_specs=(
            tokens,
            P("dp", None),
            shards,
            weight,
            shards,
            weight,
            weight,
            weight,
            shards,
            weight,
            weight,
            weight,
            tokens,
        ),
        out_specs=(
            tokens,
            tokens,
            shards,
            weight,
            shards,
            weight,
            weight,
            weight,
            shards,
            weight,
            weight,
            weight,
        ),
        check_vma=False,
    )
```

time: 731 us -> 651 us (0.89)
  Pallas kernels: 30.6 us -> 139 us
  matrix products: 110 us -> 17.9 us
  blocking collectives: 67.2 us -> 0 us
  waiting for transfers between devices: 243 us -> 199 us
    pallas_call x2 -> x10, Pallas kernels: 30.6 us -> 139 us  [the longest x1 30.5 us: attend_back(): pl.pallas_call(functools.partial(attend_back_kernel, len(blocks), heads,...]
    dot_general x31 -> x0, matrix products: 79.4 us -> none  [the longest x17 41 us: dot_rows(): lax.dot_general(left_side, right_side, (((1,), (1,)), ((), ())), preferre...]
    ppermute x90 -> x76, waiting for transfers between devices: 230 us -> 186 us  [flip(): return lax.ppermute(block, 'seq', [(i, i ^ bits) for i in range(n_seq)])]
    all_to_all x2 -> x0, blocking collectives: 34.7 us -> none  [split_columns(): lax.all_to_all(parts, 'seq', 0, 0).reshape(n_seq * rows, width // n_seq)]
    all_gather x1 -> x0, blocking collectives: 32.4 us -> none  [gather_dp(): return lax.all_gather(rows, 'dp', axis=0, tiled=True)]
    convert_element_type x23 -> x13, other arithmetic: 5.85 us -> 20.5 us  [plus(): return (first.astype(F32) + second.astype(F32)).astype(BF)]
    dot_general x5 -> x3, matrix products: 30.2 us -> 17.9 us  [dot_cols(): lax.dot_general(left_side, right_side, (((0,), (0,)), ((), ())), preferre...]
    unnamed x10 -> x2, other arithmetic: 9.29 us -> 0.05 us
  transfers between devices with their start and end apart: 99 -> 90, of which waited for: 38 -> 41; matrix products, arithmetic and copies ran while one was open for 34% -> 24% of each run, Pallas kernels for 2% -> 16%
where the time goes in v3:
time: 651 us; the launch traced here: 641 us
  waiting for transfers between devices  199 us (31%)
  Pallas kernels  139 us (21%)
  local copies, waits for them, and re-layouts  128 us (20%)
  starting transfers between devices  79.7 us (12%)
  other arithmetic  61.3 us (9%)
  matrix products  17.9 us (3%)
  between operations  16.3 us (3%)
    ppermute x76, waiting for transfers between devices, flip(): return lax.ppermute(block, 'seq', [(i, i ^ bits) for i in range(n_seq)])  186 us
    unnamed x234, local copies, waits for them, and re-layouts  63.2 us
    ppermute x76, starting transfers between devices, flip(): return lax.ppermute(block, 'seq', [(i, i ^ bits) for i in range(n_seq)])  58.2 us
    pallas_call x1, Pallas kernels, attend_back(): pl.pallas_call(functools.partial(attend_back_kernel, len(blocks), heads,...  30.5 us
    pallas_call x2, Pallas kernels, feed_back(): pl.pallas_call(feed_back_kernel, grid=(count,), in_specs=[tokens, units,...  29.7 us
    pallas_call x1, Pallas kernels, attend(): pl.pallas_call(functools.partial(attend_kernel, len(packs), heads, block)...  25.6 us
    convert_element_type x13, other arithmetic, plus(): return (first.astype(F32) + second.astype(F32)).astype(BF)  20.5 us
    pallas_call x1, Pallas kernels, feed_forward(): pl.pallas_call(functools.partial(feed_kernel, len(blocks), block), grid=(...  19 us
  transfers between devices with their start and end apart: 90, of which 41 were waited for; matrix products, arithmetic and copies ran while one was open for 24% of the time, Pallas kernels for 16%

profile of v3, /device:TPU:0, one launch (start us, length us, event | category | flops | bytes accessed | tf_op | source)
XLA Modules:
  0.0 641.1 jit_solution(11840162202194491058)
XLA Ops:
  10.3 5.0 collective-permute-start.2
  20.8 3.4 all-to-all-start
  25.5 2.8 multiply_sine_fusion
  30.5 3.2 collective-permute-done.1
  35.7 3.1 all-to-all-done
  45.4 17.3 %collective-permute-done.8.refs_4_ = bf16[256,1664]{1,0:T(8,128)(2,1)S(1)} collective-permute-done((bf16[256,1664]{1,0:T(8,128)(2,1)S(1)}, bf16[256,1664]{1,0:T(8,128)(2,1)S(1)}, u32[]{:S(2)}, u32[]{:S(2)}) %collective-permute-start.8) | collective-permute-done | bytes 852000 | tf_op jit(solution)/shard_map/ppermute | solution.py:76
  68.0 2.5 reshape.421
  70.5 2.5 reshape.422
  76.0 4.3 all-to-all-start.1
  97.5 3.9 all-to-all-done.1
  103.7 3.8 first_projections.1
  112.5 2.2 fusion.24
  122.3 10.0 %collective-permute-done.16.refs_4_ = bf16[192,1536]{1,0:T(8,128)(2,1)S(1)} collective-permute-done((bf16[192,1536]{1,0:T(8,128)(2,1)S(1)}, bf16[192,1536]{1,0:T(8,128)(2,1)S(1)}, u32[]{:S(2)}, u32[]{:S(2)}) %collective-permute-start.16) | collective-permute-done | bytes 589856 | tf_op jit(solution)/shard_map/ppermute | solution.py:76
  132.4 6.3 collective-permute-done.24
  144.7 3.4 collective-permute-done.18
  148.8 2.6 collective-permute-done.19
  163.2 2.7 copy-done
  168.6 2.5 reshape_reshape.25
  172.5 25.6 %attend.1 = (bf16[1536,1024]{1,0:T(8,128)(2,1)}, bf16[1536,256]{1,0:T(8,128)(2,1)S(1)}, bf16[1536,256]{1,0:T(8,128)(2,1)S(1)}, bf16[1536,512]{1,0:T(8,128)(2,1)}...) custom-call(s32[1]{0:T(128)} %bitcast.1.me_ref, ...), custom_call_target="tpu_custom_call" | custom-call | flops 1024 | bytes 1024 | tf_op jit(solution)/shard_map/attend/pallas_call | solution.py:607
  198.2 5.8 collective-permute-done.27
  204.0 3.2 add_convert_fusion.2
  211.2 7.5 %collective-permute-done.31 = bf16[96,2048]{1,0:T(8,128)(2,1)S(1)} collective-permute-done((bf16[96,2048]{1,0:T(8,128)(2,1)S(1)}, bf16[96,2048]{1,0:T(8,128)(2,1)S(1)}, u32[]{:S(2)}, u32[]{:S(2)}) %collective-permute-start.31) | collective-permute-done | bytes 393248 | tf_op jit(solution)/shard_map/ppermute | solution.py:76
  218.6 2.5 collective-permute-done.29
  224.0 5.6 collective-permute-done.28
  229.6 4.0 collective-permute-done.30
  233.7 5.3 collective-permute-done.33
  242.6 16.0 %collective-permute-done.37.refs_4_ = bf16[192,2048]{1,0:T(8,128)(2,1)S(1)} collective-permute-done((bf16[192,2048]{1,0:T(8,128)(2,1)S(1)}, bf16[192,2048]{1,0:T(8,128)(2,1)S(1)}, u32[]{:S(2)}, u32[]{:S(2)}) %collective-permute-start.37) | collective-permute-done | bytes 786464 | tf_op jit(solution)/shard_map/ppermute | solution.py:76
  262.2 5.0 collective-permute-done.39
  268.4 2.3 collective-permute-done.41.refs_7_
  270.8 19.0 %feed_forward.1 = (bf16[1536,2048]{1,0:T(8,128)(2,1)}, bf16[1536,704]{1,0:T(8,128)(2,1)}, bf16[1536,704]{1,0:T(8,128)(2,1)}, bf16[1536,704]{1,0:T(8,128)(2,1)}, ...) custom-call(bf16[192,2048]{1,0:T(8,128)(2,1)S(1)} %multiply_convert_fusion.refs_0_, ...), custom_call_target="tpu_custom_call" | custom-call | flops 1024 | bytes 1024 | tf_op jit(solution)/shard_map/feed_forward/pallas_call | solution.py:333
  289.8 7.8 %convolution_convert_fusion = bf16[704,2048]{1,0:T(8,128)(2,1)} fusion(bf16[1536,704]{1,0:T(8,128)(2,1)} %get-tuple-element.178.left_ref, bf16[1536,2048]{1,0:T(8,128)(2,1)S(1)} %bitcast.109), kind=kOutput, calls=%fused_computation.4 | convolution fusion | flops 4430626816 | bytes 11337728 | tf_op jit(solution)/shard_map/dot_general | solution.py:69
  299.3 14.8 %feed_back.2 = (bf16[768,704]{1,0:T(8,128)(2,1)S(1)}, bf16[768,704]{1,0:T(8,128)(2,1)S(1)}, bf16[384,2048]{1,0:T(8,128)(2,1)S(1)}, bf16[384,2048]{1,0:T(8,128)(2,1)}) custom-call(bf16[1536,2048]{1,0:T(8,128)(2,1)} %copy-done, bf16[1536,704]{1,0:T(8,128)(2,1)S(1)} %copy-done.3, bf16[1536,704]{1,0:T(8,128)(2,1)S(1)} %copy-done.4, ...), custom_call_target="tpu_custom_call" | custom-call | flops 1024 | bytes 1024 | tf_op jit(solution)/shard_map/feed_back/pallas_call | solution.py:368
  316.3 14.8 %feed_back.3 = (bf16[768,704]{1,0:T(8,128)(2,1)S(1)}, bf16[768,704]{1,0:T(8,128)(2,1)S(1)}, bf16[384,2048]{1,0:T(8,128)(2,1)S(1)}, bf16[384,2048]{1,0:T(8,128)(2,1)}) custom-call(bf16[1536,2048]{1,0:T(8,128)(2,1)} %copy-done, bf16[1536,704]{1,0:T(8,128)(2,1)S(1)} %copy-done.3, bf16[1536,704]{1,0:T(8,128)(2,1)S(1)} %copy-done.4, ...), custom_call_target="tpu_custom_call" | custom-call | flops 1024 | bytes 1024 | tf_op jit(solution)/shard_map/feed_back/pallas_call | solution.py:368
  335.2 3.0 collective-permute-done.42
  342.0 2.2 add_convert_fusion.4
  346.0 6.5 %pair_product.1 = (bf16[768,2048]{1,0:T(8,128)(2,1)S(1)}, bf16[768,2048]{1,0:T(8,128)(2,1)}) custom-call(bf16[1536,704]{1,0:T(8,128)(2,1)S(1)} %copy-done.26, bf16[704,2048]{1,0:T(8,128)(2,1)S(1)} %copy-done.1), custom_call_target="tpu_custom_call" | custom-call | flops 1024 | bytes 1024 | tf_op jit(solution)/shard_map/pair_product/pallas_call | solution.py:420
  356.9 12.8 %gate_up_grad.1 = bf16[4,8,2,64,704]{4,3,2,1,0:T(8,128)(2,1)S(1)} custom-call(bf16[1536,2048]{1,0:T(8,128)(2,1)} %get-tuple-element.195.x_ref, bf16[768,704]{1,0:T(8,128)(2,1)S(1)} %copy-done.37, bf16[768,704]{1,0:T(8,128)(2,1)S(1)} %copy-done.39, bf16[768,704]{1,0:T(8,128)(2,1)S(1)} %get-tuple-element.198.dg_high, bf16[768,704]{1,0:T(8,128)(2,1)S(1)} %copy-done.35), custom_call_target="tpu_custom_call" | custom-call | flops 1024 | bytes 1024 | tf_op jit(solution)/shard_map/gate_up_grad/pallas_call | solution.py:396
  369.8 2.7 copy-done.2
  375.4 7.9 %collective-permute-done.46 = bf16[96,2048]{1,0:T(8,128)(2,1)S(1)} collective-permute-done((bf16[96,2048]{1,0:T(8,128)(2,1)S(1)}, bf16[96,2048]{1,0:T(8,128)(2,1)S(1)}, u32[]{:S(2)}, u32[]{:S(2)}) %collective-permute-start.46) | collective-permute-done | bytes 393248 | tf_op jit(solution)/shard_map/ppermute | solution.py:76
  388.1 2.5 multiply_reduce_fusion
  393.3 16.8 %collective-permute-done.53.refs_4_ = bf16[192,2048]{1,0:T(8,128)(2,1)S(1)} collective-permute-done((bf16[192,2048]{1,0:T(8,128)(2,1)S(1)}, bf16[192,2048]{1,0:T(8,128)(2,1)S(1)}, u32[]{:S(2)}, u32[]{:S(2)}) %collective-permute-start.53) | collective-permute-done | bytes 786464 | tf_op jit(solution)/shard_map/ppermute | solution.py:76
  412.6 6.8 %collective-permute-done.55 = bf16[96,2048]{1,0:T(8,128)(2,1)S(1)} collective-permute-done((bf16[96,2048]{1,0:T(8,128)(2,1)S(1)}, bf16[96,2048]{1,0:T(8,128)(2,1)S(1)}, u32[]{:S(2)}, u32[]{:S(2)}) %collective-permute-start.55) | collective-permute-done | bytes 393248 | tf_op jit(solution)/shard_map/ppermute | solution.py:76
  420.0 3.2 add_convert_fusion.1
  426.7 30.5 %attend_back.1 = (bf16[1536,2048]{1,0:T(8,128)(2,1)}, bf16[1536,512]{1,0:T(8,128)(2,1)}, bf16[768,1536]{1,0:T(8,128)(2,1)}, bf16[768,1536]{1,0:T(8,128)(2,1)}) custom-call(s32[1]{0:T(128)} %bitcast.1.me_ref, s32[1,1536]{1,0:T(1,128)S(1)} %reshape.419.starts_ref, f32[1536,128]{1,0:T(8,128)S(1)} %copy-done.9, f32[1536,128]{1,0:T(8,128)S(1)} %copy-done.7, ...), custom_call_target="tpu_custom_call" | custom-call | flops 1024 | bytes 1024 | tf_op jit(solution)/shard_map/attend_back/pallas_call | solution.py:748
  460.7 9.2 %collective-permute-done.59 = bf16[96,2048]{1,0:T(8,128)(2,1)S(1)} collective-permute-done((bf16[96,2048]{1,0:T(8,128)(2,1)S(1)}, bf16[96,2048]{1,0:T(8,128)(2,1)S(1)}, u32[]{:S(2)}, u32[]{:S(2)}) %collective-permute-start.59) | collective-permute-done | bytes 393248 | tf_op jit(solution)/shard_map/ppermute | solution.py:76
  473.5 8.2 %convolution_convert_fusion.1 = bf16[512,2048]{1,0:T(8,128)(2,1)} fusion(bf16[1536,512]{1,0:T(8,128)(2,1)} %get-tuple-element.171.mixed_ref, bf16[1536,2048]{1,0:T(8,128)(2,1)} %get-tuple-element.225), kind=kOutput, calls=%fused_computation.8 | convolution fusion | flops 3222274048 | bytes 9961472 | tf_op jit(solution)/shard_map/dot_general | solution.py:69
  481.7 2.4 add_convert_fusion.3
  490.4 2.7 reshape.430
  497.9 3.6 pad_maximum_fusion
  503.9 3.1 collective-permute-done.64
  507.1 4.6 collective-permute-done.67
  511.9 2.4 maximum_add_fusion.4.back_ref
  517.7 9.5 %last_products.1 = (bf16[1024,1664]{1,0:T(8,128)(2,1)}, bf16[1024,1664]{1,0:T(8,128)(2,1)}, f32[192,2048]{1,0:T(8,128)}, f32[1,1024]{1,0:T(1,128)S(1)}, f32[1,2048]{1,0:T(1,128)S(1)}) custom-call(f32[192,1536]{1,0:T(8,128)} %maximum_add_fusion.4.back_ref, f32[192,1024]{1,0:T(8,128)S(1)} %copy-done.23, f32[1,1024]{1,0:T(1,128)S(1)} %broadcast_in_dim_reshape.3.query_gain_ref, ...), custom_call_target="tpu_custom_call" | custom-call | flops 1024 | bytes 1024 | tf_op jit(solution)/shard_map/last_products/pallas_call | solution.py:488
  537.2 3.6 all-to-all-start.3
  547.0 3.9 add_convert_fusion
  558.8 11.1 %collective-permute-done.72 = bf16[128,1664]{1,0:T(8,128)(2,1)S(1)} collective-permute-done((bf16[128,1664]{1,0:T(8,128)(2,1)S(1)}, bf16[128,1664]{1,0:T(8,128)(2,1)S(1)}, u32[]{:S(2)}, u32[]{:S(2)}) %collective-permute-start.72) | collective-permute-done | bytes 426016 | tf_op jit(solution)/shard_map/ppermute | solution.py:76
  577.4 2.3 copy.72
  584.1 8.2 %collective-permute-done.74 = bf16[128,1664]{1,0:T(8,128)(2,1)S(1)} collective-permute-done((bf16[128,1664]{1,0:T(8,128)(2,1)}, bf16[128,1664]{1,0:T(8,128)(2,1)S(1)}, u32[]{:S(2)}, u32[]{:S(2)}) %collective-permute-start.74) | collective-permute-done | bytes 426016 | tf_op jit(solution)/shard_map/ppermute | solution.py:76
  592.6 2.2 fusion
  597.8 3.7 all-to-all-start.2
  606.6 2.2 all-to-all-done.2
  609.8 6.7 %collective-permute-done.75 = bf16[96,2048]{1,0:T(8,128)(2,1)} collective-permute-done((bf16[96,2048]{1,0:T(8,128)(2,1)S(1)}, bf16[96,2048]{1,0:T(8,128)(2,1)}, u32[]{:S(2)}, u32[]{:S(2)}) %collective-permute-start.75) | collective-permute-done | bytes 393248 | tf_op jit(solution)/shard_map/ppermute | solution.py:76
  617.7 6.6 %collective-permute-done.77 = bf16[96,2048]{1,0:T(8,128)(2,1)S(1)} collective-permute-done((bf16[96,2048]{1,0:T(8,128)(2,1)S(1)}, bf16[96,2048]{1,0:T(8,128)(2,1)S(1)}, u32[]{:S(2)}, u32[]{:S(2)}) %collective-permute-start.77) | collective-permute-done | bytes 393248 | tf_op jit(solution)/shard_map/ppermute | solution.py:76
  624.5 3.8 add_bitcast_fusion
  (538 shorter events, 209.0 us)
Async XLA Ops:
  10.3 24.4 %collective-permute-start.2 = (bf16[64,1664]{1,0:T(8,128)(2,1)}, bf16[64,1664]{1,0:T(8,128)(2,1)}, u32[]{:S(2)}, u32[]{:S(2)}) collective-permute-start(bf16[64,1664]{1,0:T(8,128)(2,1)} %fusion.11), channel_id=1, source_target_pairs={{0,3},{1,2},{2,1},{3,0},{4,7},{5,6},{6,5},{7,4},{8,11},{9,10},{10,... | collective-permute-start | bytes 638984 | tf_op jit(solution)/shard_map/ppermute | solution.py:224
  15.3 18.4 %collective-permute-start.1 = (bf16[64,1664]{1,0:T(8,128)(2,1)}, bf16[64,1664]{1,0:T(8,128)(2,1)}, u32[]{:S(2)}, u32[]{:S(2)}) collective-permute-start(bf16[64,1664]{1,0:T(8,128)(2,1)} %fusion.11), channel_id=1, source_target_pairs={{0,2},{1,3},{2,0},{3,1},{4,6},{5,7},{6,4},{7,5},{8,10},{9,11},{10,... | collective-permute-start | bytes 638984 | tf_op jit(solution)/shard_map/ppermute | solution.py:224
  15.3 14.2 %collective-permute-start = (bf16[64,1664]{1,0:T(8,128)(2,1)}, bf16[64,1664]{1,0:T(8,128)(2,1)}, u32[]{:S(2)}, u32[]{:S(2)}) collective-permute-start(bf16[64,1664]{1,0:T(8,128)(2,1)} %fusion.11), channel_id=1, source_target_pairs={{0,1},{1,0},{2,3},{3,2},{4,5},{5,4},{6,7},{7,6},{8,9},{9,8},{10,11... | collective-permute-start | bytes 638984 | tf_op jit(solution)/shard_map/ppermute | solution.py:224
  15.9 25.9 %collective-permute-start.4 = (bf16[192,2048]{1,0:T(8,128)(2,1)}, bf16[192,2048]{1,0:T(8,128)(2,1)S(1)}, u32[]{:S(2)}, u32[]{:S(2)}) collective-permute-start(bf16[192,2048]{1,0:T(8,128)(2,1)} %bitcast.113), channel_id=1, source_target_pairs={{0,16},{4,20},{8,24},{12,28},{16,0},{20,4},{24,8},{28,12},{1,17},{... | collective-permute-start | bytes 2359304 | tf_op jit(solution)/shard_map/ppermute | solution.py:76
  17.7 24.1 %collective-permute-start.3 = (bf16[192,2048]{1,0:T(8,128)(2,1)}, bf16[192,2048]{1,0:T(8,128)(2,1)}, u32[]{:S(2)}, u32[]{:S(2)}) collective-permute-start(bf16[192,2048]{1,0:T(8,128)(2,1)} %bitcast.114), channel_id=1, source_target_pairs={{0,8},{4,12},{8,0},{12,4},{16,24},{20,28},{24,16},{28,20},{1,9},{5... | collective-permute-start | bytes 2359304 | tf_op jit(solution)/shard_map/ppermute | solution.py:76
  20.8 18.0 %all-to-all-start = ((bf16[8,32,512]{2,1,0:T(8,128)(2,1)}), bf16[8,32,512]{2,1,0:T(8,128)(2,1)S(1)}, u32[]{:S(2)}, u32[]{:S(2)}) async-start(bf16[8,32,512]{2,1,0:T(8,128)(2,1)} %bitcast.102), calls=%async_computation | async-start | bytes 524288 | tf_op jit(solution)/shard_map/all_to_all | solution.py:240
  24.2 91.7 %all-gather.4.cloned.1.call-start = ((), (), s32[]{:S(2)}) async-start(), calls=%async_computation.8 | async-start | bytes 3932160 | tf_op jit(solution)/shard_map/all_gather | solution.py:214
  42.7 20.0 %collective-permute-start.8 = (bf16[256,1664]{1,0:T(8,128)(2,1)S(1)}, bf16[256,1664]{1,0:T(8,128)(2,1)S(1)}, u32[]{:S(2)}, u32[]{:S(2)}) collective-permute-start(bf16[256,1664]{1,0:T(8,128)(2,1)S(1)} %constant_dynamic-update-slice_fusion.14.refs_0_), channel_id=1, source_target_pairs={{0,16},{4,20},{8,24},{12,28},{16,0},{20,4},{24,8},{28,12},{1,17},{... | collective-permute-start | bytes 2555912 | tf_op jit(solution)/shard_map/ppermute | solution.py:76
  44.3 21.1 %collective-permute-start.6 = (bf16[256,1664]{1,0:T(8,128)(2,1)S(1)}, bf16[256,1664]{1,0:T(8,128)(2,1)S(1)}, u32[]{:S(2)}, u32[]{:S(2)}) collective-permute-start(bf16[256,1664]{1,0:T(8,128)(2,1)S(1)} %constant_dynamic-update-slice_fusion.14.refs_0_), channel_id=1, source_target_pairs={{0,8},{4,12},{8,0},{12,4},{16,24},{20,28},{24,16},{28,20},{1,9},{5... | collective-permute-start | bytes 2555912 | tf_op jit(solution)/shard_map/ppermute | solution.py:76
  63.6 17.4 %collective-permute-start.10 = (bf16[128,1664]{1,0:T(8,128)(2,1)}, bf16[128,1664]{1,0:T(8,128)(2,1)}, u32[]{:S(2)}, u32[]{:S(2)}) collective-permute-start(bf16[128,1664]{1,0:T(8,128)(2,1)} %slice.384), channel_id=1, source_target_pairs={{0,8},{4,12},{8,0},{12,4},{16,24},{20,28},{24,16},{28,20},{1,9},{5... | collective-permute-start | bytes 1277960 | tf_op jit(solution)/shard_map/ppermute | solution.py:76
  67.1 15.6 %collective-permute-start.11 = (bf16[128,1664]{1,0:T(8,128)(2,1)}, bf16[128,1664]{1,0:T(8,128)(2,1)}, u32[]{:S(2)}, u32[]{:S(2)}) collective-permute-start(bf16[128,1664]{1,0:T(8,128)(2,1)} %slice.385), channel_id=1, source_target_pairs={{0,16},{4,20},{8,24},{12,28},{16,0},{20,4},{24,8},{28,12},{1,17},{... | collective-permute-start | bytes 1277960 | tf_op jit(solution)/shard_map/ppermute | solution.py:76
  68.0 29.5 %collective-permute-start.5 = (bf16[256,1664]{1,0:T(8,128)(2,1)S(1)}, bf16[256,1664]{1,0:T(8,128)(2,1)}, u32[]{:S(2)}, u32[]{:S(2)}) collective-permute-start(bf16[256,1664]{1,0:T(8,128)(2,1)S(1)} %constant_dynamic-update-slice_fusion.14.refs_0_), channel_id=1, source_target_pairs={{0,4},{4,0},{8,12},{12,8},{16,20},{20,16},{24,28},{28,24},{1,5},{5... | collective-permute-start | bytes 2555912 | tf_op jit(solution)/shard_map/ppermute | solution.py:76
  76.0 25.3 %all-to-all-start.1 = ((bf16[8,2,64,704]{3,2,1,0:T(8,128)(2,1)}), bf16[8,2,64,704]{3,2,1,0:T(8,128)(2,1)}, u32[]{:S(2)}, u32[]{:S(2)}) async-start(bf16[8,2,64,704]{3,2,1,0:T(8,128)(2,1)} %copy.66), calls=%async_computation.1 | async-start | bytes 3145728 | tf_op jit(solution)/shard_map/all_to_all | solution.py:240
  80.3 160.2 %all-gather.6.cloned.1.call-start = ((), (), s32[]{:S(2)}) async-start(), calls=%async_computation.9 | async-start | bytes 7864320 | tf_op jit(solution)/shard_map/all_gather | solution.py:214
  80.3 21.0 %collective-permute-start.9 = (bf16[256,1664]{1,0:T(8,128)(2,1)S(1)}, bf16[256,1664]{1,0:T(8,128)(2,1)}, u32[]{:S(2)}, u32[]{:S(2)}) collective-permute-start(bf16[256,1664]{1,0:T(8,128)(2,1)S(1)} %collective-permute-done.8.refs_4_), channel_id=1, source_target_pairs={{0,4},{4,0},{8,12},{12,8},{16,20},{20,16},{24,28},{28,24},{1,5},{5... | collective-permute-start | bytes 2555912 | tf_op jit(solution)/shard_map/ppermute | solution.py:76
  80.9 20.5 %collective-permute-start.7 = (bf16[256,1664]{1,0:T(8,128)(2,1)}, bf16[256,1664]{1,0:T(8,128)(2,1)}, u32[]{:S(2)}, u32[]{:S(2)}) collective-permute-start(bf16[256,1664]{1,0:T(8,128)(2,1)} %copy-done.16), channel_id=1, source_target_pairs={{0,4},{4,0},{8,12},{12,8},{16,20},{20,16},{24,28},{28,24},{1,5},{5... | collective-permute-start | bytes 2555912 | tf_op jit(solution)/shard_map/ppermute | solution.py:76
  84.6 16.8 %collective-permute-start.12 = (bf16[256,1664]{1,0:T(8,128)(2,1)}, bf16[256,1664]{1,0:T(8,128)(2,1)}, u32[]{:S(2)}, u32[]{:S(2)}) collective-permute-start(bf16[256,1664]{1,0:T(8,128)(2,1)} %constant_dynamic-update-slice_fusion.refs_6_), channel_id=1, source_target_pairs={{0,4},{4,0},{8,12},{12,8},{16,20},{20,16},{24,28},{28,24},{1,5},{5... | collective-permute-start | bytes 2555912 | tf_op jit(solution)/shard_map/ppermute | solution.py:76
  114.8 182.9 %all-gather.8.cloned.1.call-start = ((), (), s32[]{:S(2)}) async-start(), calls=%async_computation.10 | async-start | bytes 3604480 | tf_op jit(solution)/shard_map/all_gather | solution.py:214
  116.0 16.3 %collective-permute-start.16 = (bf16[192,1536]{1,0:T(8,128)(2,1)S(1)}, bf16[192,1536]{1,0:T(8,128)(2,1)S(1)}, u32[]{:S(2)}, u32[]{:S(2)}) collective-permute-start(bf16[192,1536]{1,0:T(8,128)(2,1)S(1)} %pad_maximum_fusion.3.refs_0_), channel_id=1, source_target_pairs={{0,16},{4,20},{8,24},{12,28},{16,0},{20,4},{24,8},{28,12},{1,17},{... | collective-permute-start | bytes 1769480 | tf_op jit(solution)/shard_map/ppermute | solution.py:76
  116.6 22.0 %collective-permute-start.14 = (bf16[192,1536]{1,0:T(8,128)(2,1)S(1)}, bf16[192,1536]{1,0:T(8,128)(2,1)}, u32[]{:S(2)}, u32[]{:S(2)}) collective-permute-start(bf16[192,1536]{1,0:T(8,128)(2,1)S(1)} %pad_maximum_fusion.3.refs_0_), channel_id=1, source_target_pairs={{0,8},{4,12},{8,0},{12,4},{16,24},{20,28},{24,16},{28,20},{1,9},{5... | collective-permute-start | bytes 1769480 | tf_op jit(solution)/shard_map/ppermute | solution.py:76
  118.3 20.4 %collective-permute-start.24 = (bf16[96,2048]{1,0:T(8,128)(2,1)S(1)}, bf16[96,2048]{1,0:T(8,128)(2,1)S(1)}, u32[]{:S(2)}, u32[]{:S(2)}) collective-permute-start(bf16[96,2048]{1,0:T(8,128)(2,1)S(1)} %slice.318), channel_id=1, source_target_pairs={{0,8},{4,12},{8,0},{12,4},{16,24},{20,28},{24,16},{28,20},{1,9},{5... | collective-permute-start | bytes 1179656 | tf_op jit(solution)/shard_map/ppermute | solution.py:76
  120.8 21.4 %collective-permute-start.25 = (bf16[96,2048]{1,0:T(8,128)(2,1)S(1)}, bf16[96,2048]{1,0:T(8,128)(2,1)S(1)}, u32[]{:S(2)}, u32[]{:S(2)}) collective-permute-start(bf16[96,2048]{1,0:T(8,128)(2,1)S(1)} %slice.319), channel_id=1, source_target_pairs={{0,16},{4,20},{8,24},{12,28},{16,0},{20,4},{24,8},{28,12},{1,17},{... | collective-permute-start | bytes 1179656 | tf_op jit(solution)/shard_map/ppermute | solution.py:76
  122.3 31.2 %collective-permute-start.22 = (bf16[192,2048]{1,0:T(8,128)(2,1)}, bf16[192,2048]{1,0:T(8,128)(2,1)S(1)}, u32[]{:S(2)}, u32[]{:S(2)}) collective-permute-start(bf16[192,2048]{1,0:T(8,128)(2,1)} %collective-permute-done.3.refs_2_), channel_id=1, source_target_pairs={{0,4},{4,0},{8,12},{12,8},{16,20},{20,16},{24,28},{28,24},{1,5},{5... | collective-permute-start | bytes 2359304 | tf_op jit(solution)/shard_map/ppermute | solution.py:76
  132.3 22.1 %collective-permute-start.23 = (bf16[192,2048]{1,0:T(8,128)(2,1)S(1)}, bf16[192,2048]{1,0:T(8,128)(2,1)S(1)}, u32[]{:S(2)}, u32[]{:S(2)}) collective-permute-start(bf16[192,2048]{1,0:T(8,128)(2,1)S(1)} %copy-done.28), channel_id=1, source_target_pairs={{0,4},{4,0},{8,12},{12,8},{16,20},{20,16},{24,28},{28,24},{1,5},{5... | collective-permute-start | bytes 2359304 | tf_op jit(solution)/shard_map/ppermute | solution.py:76
  138.7 13.5 %collective-permute-start.21 = (bf16[192,2048]{1,0:T(8,128)(2,1)S(1)}, bf16[192,2048]{1,0:T(8,128)(2,1)S(1)}, u32[]{:S(2)}, u32[]{:S(2)}) collective-permute-start(bf16[192,2048]{1,0:T(8,128)(2,1)S(1)} %bitcast.115), channel_id=1, source_target_pairs={{0,4},{4,0},{8,12},{12,8},{16,20},{20,16},{24,28},{28,24},{1,5},{5... | collective-permute-start | bytes 2359304 | tf_op jit(solution)/shard_map/ppermute | solution.py:76
  151.4 21.0 %collective-permute-start.13 = (bf16[192,1536]{1,0:T(8,128)(2,1)S(1)}, bf16[192,1536]{1,0:T(8,128)(2,1)}, u32[]{:S(2)}, u32[]{:S(2)}) collective-permute-start(bf16[192,1536]{1,0:T(8,128)(2,1)S(1)} %pad_maximum_fusion.3.refs_0_), channel_id=1, source_target_pairs={{0,4},{4,0},{8,12},{12,8},{16,20},{20,16},{24,28},{28,24},{1,5},{5... | collective-permute-start | bytes 1769480 | tf_op jit(solution)/shard_map/ppermute | solution.py:76
  153.0 19.4 %collective-permute-start.17 = (bf16[192,1536]{1,0:T(8,128)(2,1)S(1)}, bf16[192,1536]{1,0:T(8,128)(2,1)}, u32[]{:S(2)}, u32[]{:S(2)}) collective-permute-start(bf16[192,1536]{1,0:T(8,128)(2,1)S(1)} %collective-permute-done.16.refs_4_), channel_id=1, source_target_pairs={{0,4},{4,0},{8,12},{12,8},{16,20},{20,16},{24,28},{28,24},{1,5},{5... | collective-permute-start | bytes 1769480 | tf_op jit(solution)/shard_map/ppermute | solution.py:76
  154.4 18.0 %collective-permute-start.15 = (bf16[192,1536]{1,0:T(8,128)(2,1)}, bf16[192,1536]{1,0:T(8,128)(2,1)}, u32[]{:S(2)}, u32[]{:S(2)}) collective-permute-start(bf16[192,1536]{1,0:T(8,128)(2,1)} %collective-permute-done.14.refs_2_), channel_id=1, source_target_pairs={{0,4},{4,0},{8,12},{12,8},{16,20},{20,16},{24,28},{28,24},{1,5},{5... | collective-permute-start | bytes 1769480 | tf_op jit(solution)/shard_map/ppermute | solution.py:76
  155.3 17.1 %collective-permute-start.20 = (bf16[192,1536]{1,0:T(8,128)(2,1)}, bf16[192,1536]{1,0:T(8,128)(2,1)}, u32[]{:S(2)}, u32[]{:S(2)}) collective-permute-start(bf16[192,1536]{1,0:T(8,128)(2,1)} %constant_dynamic-update-slice_fusion.2.refs_6_), channel_id=1, source_target_pairs={{0,4},{4,0},{8,12},{12,8},{16,20},{20,16},{24,28},{28,24},{1,5},{5... | collective-permute-start | bytes 1769480 | tf_op jit(solution)/shard_map/ppermute | solution.py:76
  207.4 11.2 %collective-permute-start.31 = (bf16[96,2048]{1,0:T(8,128)(2,1)S(1)}, bf16[96,2048]{1,0:T(8,128)(2,1)S(1)}, u32[]{:S(2)}, u32[]{:S(2)}) collective-permute-start(bf16[96,2048]{1,0:T(8,128)(2,1)S(1)} %get-tuple-element.264), channel_id=1, source_target_pairs={{0,16},{4,20},{8,24},{12,28},{16,0},{20,4},{24,8},{28,12},{1,17},{... | collective-permute-start | bytes 1179656 | tf_op jit(solution)/shard_map/ppermute | solution.py:76
  209.2 12.0 %collective-permute-start.29 = (bf16[96,2048]{1,0:T(8,128)(2,1)S(1)}, bf16[96,2048]{1,0:T(8,128)(2,1)S(1)}, u32[]{:S(2)}, u32[]{:S(2)}) collective-permute-start(bf16[96,2048]{1,0:T(8,128)(2,1)S(1)} %get-tuple-element.265), channel_id=1, source_target_pairs={{0,8},{4,12},{8,0},{12,4},{16,24},{20,28},{24,16},{28,20},{1,9},{5... | collective-permute-start | bytes 1179656 | tf_op jit(solution)/shard_map/ppermute | solution.py:76
  209.5 20.1 %collective-permute-start.28 = (bf16[96,2048]{1,0:T(8,128)(2,1)S(1)}, bf16[96,2048]{1,0:T(8,128)(2,1)S(1)}, u32[]{:S(2)}, u32[]{:S(2)}) collective-permute-start(bf16[96,2048]{1,0:T(8,128)(2,1)S(1)} %get-tuple-element.262), channel_id=1, source_target_pairs={{0,8},{4,12},{8,0},{12,4},{16,24},{20,28},{24,16},{28,20},{1,9},{5... | collective-permute-start | bytes 1179656 | tf_op jit(solution)/shard_map/ppermute | solution.py:76
  221.4 12.1 %collective-permute-start.30 = (bf16[96,2048]{1,0:T(8,128)(2,1)S(1)}, bf16[96,2048]{1,0:T(8,128)(2,1)S(1)}, u32[]{:S(2)}, u32[]{:S(2)}) collective-permute-start(bf16[96,2048]{1,0:T(8,128)(2,1)S(1)} %get-tuple-element.266), channel_id=1, source_target_pairs={{0,16},{4,20},{8,24},{12,28},{16,0},{20,4},{24,8},{28,12},{1,17},{... | collective-permute-start | bytes 1179656 | tf_op jit(solution)/shard_map/ppermute | solution.py:76
  221.9 248.9 %reduce-scatter.5.cloned.1.call-start = ((), (), s32[]{:S(2)}) async-start(), calls=%async_computation.11 | async-start | bytes 3604480 | tf_op jit(solution)/shard_map/reduce_scatter | solution.py:230
  222.0 17.0 %collective-permute-start.33 = (bf16[96,2048]{1,0:T(8,128)(2,1)S(1)}, bf16[96,2048]{1,0:T(8,128)(2,1)S(1)}, u32[]{:S(2)}, u32[]{:S(2)}) collective-permute-start(bf16[96,2048]{1,0:T(8,128)(2,1)S(1)} %get-tuple-element.263), channel_id=1, source_target_pairs={{0,16},{4,20},{8,24},{12,28},{16,0},{20,4},{24,8},{28,12},{1,17},{... | collective-permute-start | bytes 1179656 | tf_op jit(solution)/shard_map/ppermute | solution.py:76
  223.7 15.2 %collective-permute-start.32 = (bf16[96,2048]{1,0:T(8,128)(2,1)S(1)}, bf16[96,2048]{1,0:T(8,128)(2,1)S(1)}, u32[]{:S(2)}, u32[]{:S(2)}) collective-permute-start(bf16[96,2048]{1,0:T(8,128)(2,1)S(1)} %get-tuple-element.267), channel_id=1, source_target_pairs={{0,8},{4,12},{8,0},{12,4},{16,24},{20,28},{24,16},{28,20},{1,9},{5... | collective-permute-start | bytes 1179656 | tf_op jit(solution)/shard_map/ppermute | solution.py:76
  241.7 17.0 %collective-permute-start.37 = (bf16[192,2048]{1,0:T(8,128)(2,1)S(1)}, bf16[192,2048]{1,0:T(8,128)(2,1)S(1)}, u32[]{:S(2)}, u32[]{:S(2)}) collective-permute-start(bf16[192,2048]{1,0:T(8,128)(2,1)S(1)} %multiply_convert_fusion.refs_0_), channel_id=1, source_target_pairs={{0,16},{4,20},{8,24},{12,28},{16,0},{20,4},{24,8},{28,12},{1,17},{... | collective-permute-start | bytes 2359304 | tf_op jit(solution)/shard_map/ppermute | solution.py:76
  242.4 18.0 %collective-permute-start.35 = (bf16[192,2048]{1,0:T(8,128)(2,1)S(1)}, bf16[192,2048]{1,0:T(8,128)(2,1)S(1)}, u32[]{:S(2)}, u32[]{:S(2)}) collective-permute-start(bf16[192,2048]{1,0:T(8,128)(2,1)S(1)} %multiply_convert_fusion.refs_0_), channel_id=1, source_target_pairs={{0,8},{4,12},{8,0},{12,4},{16,24},{20,28},{24,16},{28,20},{1,9},{5... | collective-permute-start | bytes 2359304 | tf_op jit(solution)/shard_map/ppermute | solution.py:76
  335.0 179.3 %reduce-scatter.7.cloned.1.call-start = ((), (), s32[]{:S(2)}) async-start(), calls=%async_computation.12 | async-start | bytes 7864320 | tf_op jit(solution)/shard_map/reduce_scatter | solution.py:230
  344.4 28.1 %collective-permute-start.45 = (bf16[96,2048]{1,0:T(8,128)(2,1)S(1)}, bf16[96,2048]{1,0:T(8,128)(2,1)S(1)}, u32[]{:S(2)}, u32[]{:S(2)}) collective-permute-start(bf16[96,2048]{1,0:T(8,128)(2,1)S(1)} %get-tuple-element.288), channel_id=1, source_target_pairs={{0,8},{4,12},{8,0},{12,4},{16,24},{20,28},{24,16},{28,20},{1,9},{5... | collective-permute-start | bytes 1179656 | tf_op jit(solution)/shard_map/ppermute | solution.py:76
  354.1 65.9 %collective-permute-start.58 = (bf16[768,2048]{1,0:T(8,128)(2,1)}, bf16[768,2048]{1,0:T(8,128)(2,1)}, u32[]{:S(2)}, u32[]{:S(2)}) collective-permute-start(bf16[768,2048]{1,0:T(8,128)(2,1)} %get-tuple-element.202), channel_id=1, source_target_pairs={{0,4},{4,0},{8,12},{12,8},{16,20},{20,16},{24,28},{28,24},{1,5},{5... | collective-permute-start | bytes 9437192 | tf_op jit(solution)/shard_map/ppermute | solution.py:76
  354.3 29.1 %collective-permute-start.49 = (bf16[96,2048]{1,0:T(8,128)(2,1)S(1)}, bf16[96,2048]{1,0:T(8,128)(2,1)S(1)}, u32[]{:S(2)}, u32[]{:S(2)}) collective-permute-start(bf16[96,2048]{1,0:T(8,128)(2,1)S(1)} %slice.339), channel_id=1, source_target_pairs={{0,16},{4,20},{8,24},{12,28},{16,0},{20,4},{24,8},{28,12},{1,17},{... | collective-permute-start | bytes 1179656 | tf_op jit(solution)/shard_map/ppermute | solution.py:76
  355.4 20.0 %collective-permute-start.44 = (bf16[96,2048]{1,0:T(8,128)(2,1)S(1)}, bf16[96,2048]{1,0:T(8,128)(2,1)S(1)}, u32[]{:S(2)}, u32[]{:S(2)}) collective-permute-start(bf16[96,2048]{1,0:T(8,128)(2,1)S(1)} %slice.334), channel_id=1, source_target_pairs={{0,8},{4,12},{8,0},{12,4},{16,24},{20,28},{24,16},{28,20},{1,9},{5... | collective-permute-start | bytes 1179656 | tf_op jit(solution)/shard_map/ppermute | solution.py:76
  356.0 18.3 %collective-permute-start.47 = (bf16[96,2048]{1,0:T(8,128)(2,1)S(1)}, bf16[96,2048]{1,0:T(8,128)(2,1)S(1)}, u32[]{:S(2)}, u32[]{:S(2)}) collective-permute-start(bf16[96,2048]{1,0:T(8,128)(2,1)S(1)} %get-tuple-element.289), channel_id=1, source_target_pairs={{0,16},{4,20},{8,24},{12,28},{16,0},{20,4},{24,8},{28,12},{1,17},{... | collective-permute-start | bytes 1179656 | tf_op jit(solution)/shard_map/ppermute | solution.py:76
  386.7 209.1 %reduce-scatter.9.cloned.1.call-start = ((), (), s32[]{:S(2)}) async-start(), calls=%async_computation.13 | async-start | bytes 3932160 | tf_op jit(solution)/shard_map/reduce_scatter | solution.py:230
  391.7 18.4 %collective-permute-start.53 = (bf16[192,2048]{1,0:T(8,128)(2,1)S(1)}, bf16[192,2048]{1,0:T(8,128)(2,1)S(1)}, u32[]{:S(2)}, u32[]{:S(2)}) collective-permute-start(bf16[192,2048]{1,0:T(8,128)(2,1)S(1)} %fusion.17.refs_0_), channel_id=1, source_target_pairs={{0,16},{4,20},{8,24},{12,28},{16,0},{20,4},{24,8},{28,12},{1,17},{... | collective-permute-start | bytes 2359304 | tf_op jit(solution)/shard_map/ppermute | solution.py:76
  392.6 18.1 %collective-permute-start.51 = (bf16[192,2048]{1,0:T(8,128)(2,1)S(1)}, bf16[192,2048]{1,0:T(8,128)(2,1)S(1)}, u32[]{:S(2)}, u32[]{:S(2)}) collective-permute-start(bf16[192,2048]{1,0:T(8,128)(2,1)S(1)} %fusion.17.refs_0_), channel_id=1, source_target_pairs={{0,8},{4,12},{8,0},{12,4},{16,24},{20,28},{24,16},{28,20},{1,9},{5... | collective-permute-start | bytes 2359304 | tf_op jit(solution)/shard_map/ppermute | solution.py:76
  412.0 12.4 %collective-permute-start.50 = (bf16[192,2048]{1,0:T(8,128)(2,1)S(1)}, bf16[192,2048]{1,0:T(8,128)(2,1)S(1)}, u32[]{:S(2)}, u32[]{:S(2)}) collective-permute-start(bf16[192,2048]{1,0:T(8,128)(2,1)S(1)} %fusion.17.refs_0_), channel_id=1, source_target_pairs={{0,4},{4,0},{8,12},{12,8},{16,20},{20,16},{24,28},{28,24},{1,5},{5... | collective-permute-start | bytes 2359304 | tf_op jit(solution)/shard_map/ppermute | solution.py:76
  412.0 12.4 %collective-permute-start.54 = (bf16[192,2048]{1,0:T(8,128)(2,1)S(1)}, bf16[192,2048]{1,0:T(8,128)(2,1)S(1)}, u32[]{:S(2)}, u32[]{:S(2)}) collective-permute-start(bf16[192,2048]{1,0:T(8,128)(2,1)S(1)} %collective-permute-done.53.refs_4_), channel_id=1, source_target_pairs={{0,4},{4,0},{8,12},{12,8},{16,20},{20,16},{24,28},{28,24},{1,5},{5... | collective-permute-start | bytes 2359304 | tf_op jit(solution)/shard_map/ppermute | solution.py:76
  424.5 35.3 %collective-permute-start.60 = (bf16[96,2048]{1,0:T(8,128)(2,1)S(1)}, bf16[96,2048]{1,0:T(8,128)(2,1)S(1)}, u32[]{:S(2)}, u32[]{:S(2)}) collective-permute-start(bf16[96,2048]{1,0:T(8,128)(2,1)S(1)} %get-tuple-element.286), channel_id=1, source_target_pairs={{0,8},{4,12},{8,0},{12,4},{16,24},{20,28},{24,16},{28,20},{1,9},{5... | collective-permute-start | bytes 1179656 | tf_op jit(solution)/shard_map/ppermute | solution.py:76
  458.7 11.2 %collective-permute-start.59 = (bf16[96,2048]{1,0:T(8,128)(2,1)S(1)}, bf16[96,2048]{1,0:T(8,128)(2,1)S(1)}, u32[]{:S(2)}, u32[]{:S(2)}) collective-permute-start(bf16[96,2048]{1,0:T(8,128)(2,1)S(1)} %get-tuple-element.287), channel_id=1, source_target_pairs={{0,16},{4,20},{8,24},{12,28},{16,0},{20,4},{24,8},{28,12},{1,17},{... | collective-permute-start | bytes 1179656 | tf_op jit(solution)/shard_map/ppermute | solution.py:76
  470.8 11.0 %collective-permute-start.61 = (bf16[768,1536]{1,0:T(8,128)(2,1)}, bf16[768,1536]{1,0:T(8,128)(2,1)}, u32[]{:S(2)}, u32[]{:S(2)}) collective-permute-start(bf16[768,1536]{1,0:T(8,128)(2,1)} %get-tuple-element.224), channel_id=1, source_target_pairs={{0,4},{4,0},{8,12},{12,8},{16,20},{20,16},{24,28},{28,24},{1,5},{5... | collective-permute-start | bytes 7077896 | tf_op jit(solution)/shard_map/ppermute | solution.py:76
  534.9 12.1 %collective-permute-start.68 = (bf16[1024,1664]{1,0:T(8,128)(2,1)}, bf16[1024,1664]{1,0:T(8,128)(2,1)}, u32[]{:S(2)}, u32[]{:S(2)}) collective-permute-start(bf16[1024,1664]{1,0:T(8,128)(2,1)} %constant_dynamic-update-slice_fusion.12), channel_id=1, source_target_pairs={{0,4},{4,0},{8,12},{12,8},{16,20},{20,16},{24,28},{28,24},{1,5},{5... | collective-permute-start | bytes 10223624 | tf_op jit(solution)/shard_map/ppermute | solution.py:76
  537.2 35.8 %all-to-all-start.3 = ((bf16[8,2,64,704]{3,2,1,0:T(8,128)(2,1)}), bf16[8,2,64,704]{3,2,1,0:T(8,128)(2,1)S(1)}, u32[]{:S(2)}, u32[]{:S(2)}) async-start(bf16[8,2,64,704]{3,2,1,0:T(8,128)(2,1)} %bitcast.127), calls=%async_computation.7 | async-start | bytes 3145728 | tf_op jit(solution)/shard_map/all_to_all | solution.py:240
  540.8 87.5 %reduce-scatter.11.cloned.1.call-start = ((), (), s32[]{:S(2)}) async-start(), calls=%async_computation.14 | async-start | bytes 1064960 | tf_op jit(solution)/shard_map/reduce_scatter | solution.py:230
  551.9 18.0 %collective-permute-start.72 = (bf16[128,1664]{1,0:T(8,128)(2,1)S(1)}, bf16[128,1664]{1,0:T(8,128)(2,1)S(1)}, u32[]{:S(2)}, u32[]{:S(2)}) collective-permute-start(bf16[128,1664]{1,0:T(8,128)(2,1)S(1)} %get-tuple-element.252), channel_id=1, source_target_pairs={{0,16},{4,20},{8,24},{12,28},{16,0},{20,4},{24,8},{28,12},{1,17},{... | collective-permute-start | bytes 1277960 | tf_op jit(solution)/shard_map/ppermute | solution.py:76
  553.9 16.6 %collective-permute-start.70 = (bf16[128,1664]{1,0:T(8,128)(2,1)S(1)}, bf16[128,1664]{1,0:T(8,128)(2,1)S(1)}, u32[]{:S(2)}, u32[]{:S(2)}) collective-permute-start(bf16[128,1664]{1,0:T(8,128)(2,1)S(1)} %get-tuple-element.253), channel_id=1, source_target_pairs={{0,8},{4,12},{8,0},{12,4},{16,24},{20,28},{24,16},{28,20},{1,9},{5... | collective-permute-start | bytes 1277960 | tf_op jit(solution)/shard_map/ppermute | solution.py:76
  558.3 24.6 %collective-permute-start.69 = (bf16[128,1664]{1,0:T(8,128)(2,1)}, bf16[128,1664]{1,0:T(8,128)(2,1)}, u32[]{:S(2)}, u32[]{:S(2)}) collective-permute-start(bf16[128,1664]{1,0:T(8,128)(2,1)} %get-tuple-element.250), channel_id=1, source_target_pairs={{0,8},{4,12},{8,0},{12,4},{16,24},{20,28},{24,16},{28,20},{1,9},{5... | collective-permute-start | bytes 1277960 | tf_op jit(solution)/shard_map/ppermute | solution.py:76
  570.7 12.2 %collective-permute-start.71 = (bf16[128,1664]{1,0:T(8,128)(2,1)S(1)}, bf16[128,1664]{1,0:T(8,128)(2,1)}, u32[]{:S(2)}, u32[]{:S(2)}) collective-permute-start(bf16[128,1664]{1,0:T(8,128)(2,1)S(1)} %get-tuple-element.254), channel_id=1, source_target_pairs={{0,16},{4,20},{8,24},{12,28},{16,0},{20,4},{24,8},{28,12},{1,17},{... | collective-permute-start | bytes 1277960 | tf_op jit(solution)/shard_map/ppermute | solution.py:76
  597.8 11.1 %all-to-all-start.2 = ((bf16[8,32,512]{2,1,0:T(8,128)(2,1)}), bf16[8,32,512]{2,1,0:T(8,128)(2,1)S(1)}, u32[]{:S(2)}, u32[]{:S(2)}) async-start(bf16[8,32,512]{2,1,0:T(8,128)(2,1)} %reshape.437), calls=%async_computation.6 | async-start | bytes 524288 | tf_op jit(solution)/shard_map/all_to_all | solution.py:240
  601.4 15.0 %collective-permute-start.75 = (bf16[96,2048]{1,0:T(8,128)(2,1)S(1)}, bf16[96,2048]{1,0:T(8,128)(2,1)}, u32[]{:S(2)}, u32[]{:S(2)}) collective-permute-start(bf16[96,2048]{1,0:T(8,128)(2,1)S(1)} %copy-done.85), channel_id=1, source_target_pairs={{0,8},{4,12},{8,0},{12,4},{16,24},{20,28},{24,16},{28,20},{1,9},{5... | collective-permute-start | bytes 1179656 | tf_op jit(solution)/shard_map/ppermute | solution.py:76
  603.4 13.0 %collective-permute-start.76 = (bf16[96,2048]{1,0:T(8,128)(2,1)S(1)}, bf16[96,2048]{1,0:T(8,128)(2,1)}, u32[]{:S(2)}, u32[]{:S(2)}) collective-permute-start(bf16[96,2048]{1,0:T(8,128)(2,1)S(1)} %copy-done.86), channel_id=1, source_target_pairs={{0,16},{4,20},{8,24},{12,28},{16,0},{20,4},{24,8},{28,12},{1,17},{... | collective-permute-start | bytes 1179656 | tf_op jit(solution)/shard_map/ppermute | solution.py:76
  606.0 18.3 %collective-permute-start.77 = (bf16[96,2048]{1,0:T(8,128)(2,1)S(1)}, bf16[96,2048]{1,0:T(8,128)(2,1)S(1)}, u32[]{:S(2)}, u32[]{:S(2)}) collective-permute-start(bf16[96,2048]{1,0:T(8,128)(2,1)S(1)} %copy-done.87), channel_id=1, source_target_pairs={{0,8},{4,12},{8,0},{12,4},{16,24},{20,28},{24,16},{28,20},{1,9},{5... | collective-permute-start | bytes 1179656 | tf_op jit(solution)/shard_map/ppermute | solution.py:76
  606.6 17.8 %collective-permute-start.78 = (bf16[96,2048]{1,0:T(8,128)(2,1)S(1)}, bf16[96,2048]{1,0:T(8,128)(2,1)S(1)}, u32[]{:S(2)}, u32[]{:S(2)}) collective-permute-start(bf16[96,2048]{1,0:T(8,128)(2,1)S(1)} %copy-done.84), channel_id=1, source_target_pairs={{0,16},{4,20},{8,24},{12,28},{16,0},{20,4},{24,8},{28,12},{1,17},{... | collective-permute-start | bytes 1179656 | tf_op jit(solution)/shard_map/ppermute | solution.py:76
  (132 other events, 1425.3 us)
Sparse Core Ops, SparseCore 0:
  42.8 64.3 all-gather.3
  114.9 114.6 all-gather.5
  231.2 57.3 all-gather.7
  335.1 56.0 reduce-scatter.4
  393.4 110.5 reduce-scatter.6
  535.0 60.6 reduce-scatter.8
  598.1 24.1 reduce-scatter.10

commit v4 on v3

--- a/solution.py
+++ b/solution.py
@@ -16,7 +16,123 @@
 NEGATIVE = -1e30
 BF = jnp.bfloat16
 F32 = jnp.float32
-SMALL = pl.CostEstimate(flops=1024, bytes_accessed=1024, transcendentals=0)
+KERNEL_VMEM = 60 * 2**20
+
+
+KERNEL_COST = dict(
+    stack_blocks=0.01,
+    first_projections=0.01,
+    attend=0.01,
+    feed_forward=0.01,
+    feed_back=0.01,
+    gate_up_grad=0.01,
+    pair_product=3,
+    attend_back=0.01,
+    last_products=0.01,
+    first_grads=0.01,
+    columns_back=0.01,
+    attention_grads=0.01,
+)
+(
+    FIRST_PART,
+    FIRST_NEAR,
+    FIRST_FAR,
+    FIRST_BLOCKS,
+    PACK,
+    PACK_NEAR,
+    PACKS,
+    ATTENDED,
+    OUT_LEFT,
+    HIDDEN,
+    FEED_NEAR,
+    FEED_BLOCKS,
+    ACTIVE,
+    TERMS_HIGH,
+    TERMS_LOW,
+    FEED_SUMS,
+    FEED_LEFT,
+    D_NORMED,
+    BRANCH_NEAR,
+    BRANCH_BLOCKS,
+    BRANCH_ALL,
+    BACK_TERMS,
+    BACK_SUMS,
+    BACK_LEFT,
+    BACK_LOCAL,
+    FIRST_TERMS,
+    LAST_NEAR,
+    LAST_BLOCKS,
+    FIRST_SUM,
+) = range(29)
+DUE = dict(
+    tables=FIRST_BLOCKS,
+    feed_step=FIRST_PART,
+    query_part=FIRST_PART,
+    gate_up_parts=FIRST_NEAR,
+    gate_up=PACK,
+    gate_up_all=FEED_NEAR,
+    feed_far=ATTENDED,
+    feed_stack=FEED_NEAR,
+    grad_down_term=ACTIVE,
+    down_all=TERMS_HIGH,
+    high_swap=TERMS_LOW,
+    grad_down=D_NORMED,
+    grad_gate_up_term=D_NORMED,
+    result_terms=BRANCH_NEAR,
+    result_sums=BRANCH_BLOCKS,
+    result_left=BRANCH_ALL,
+    grad_gate_up=BACK_LEFT,
+    grad_attention_term=BACK_LEFT,
+    grad_attention=FIRST_SUM,
+    attention=PACK,
+    attention_weights=PACK_NEAR,
+    normed_columns=ACTIVE,
+    result_hops=BACK_TERMS,
+)
+BEGIN = dict(
+    output=FIRST_PART,
+    gate_up=FIRST_FAR,
+    feed_far=PACKS,
+    grad_gate_up_term=FEED_LEFT,
+    result_terms=D_NORMED,
+    result_left=BRANCH_NEAR,
+    result_last=FIRST_SUM,
+    grad_attention_term=BACK_SUMS,
+    normed_columns=FEED_BLOCKS,
+    feed_stack=HIDDEN,
+    gate_up_rows=FIRST_SUM,
+)
+
+
+def takes(kernel):
+    microseconds = KERNEL_COST[kernel]
+    return pl.CostEstimate(
+        flops=int(microseconds * 1e9), bytes_accessed=int(microseconds * 2e6), transcendentals=0
+    )
+
+
+class Chain:
+    def __init__(self):
+        self.stages = {}
+        self.side = {}
+
+    def add(self, **made):
+        self.side.update(made)
+
+    def begin(self, **waiting):
+        ((name, value),) = waiting.items()
+        return after(value, self.stages[BEGIN[name]]) if name in BEGIN else value
+
+    def stage(self, at, value):
+        due = [name for name in self.side if DUE.get(name) == at]
+        if due:
+            value, there = together(value, [self.side[name] for name in due])
+            self.side.update(zip(due, there, strict=True))
+        self.stages[at] = value
+        return value
+
+    def __getattr__(self, name):
+        return self.side[name]
 
 
 def rms_norm(values, norm_gain):
@@ -86,15 +202,23 @@
     if lax.axis_size("seq") != 8:
         return blocks
     half = blocks[0].shape[0] // 2
-    far = [flip(blocks[4][:half], 2), flip(blocks[2][half:], 4)]
-    return blocks | {6: jnp.concatenate(far, axis=0)}
+    return blocks | {6: [flip(blocks[4][:half], 2), flip(blocks[2][half:], 4)]}
 
 
 def gather_cores(blocks):
     whole = []
     for bits in range(0, lax.axis_size("seq"), 2):
-        whole += [blocks[bits], flip(blocks[bits], 1)]
+        own = blocks[bits] if isinstance(blocks[bits], list) else [blocks[bits]]
+        whole += own + [flip(piece, 1) for piece in own]
     return whole
+
+
+def piece_slices(pieces):
+    slices, first = [], 0
+    for piece in pieces:
+        slices.append(slice(first, first + piece.shape[0]))
+        first += piece.shape[0]
+    return slices
 
 
 def gather_blocks(rows):
@@ -106,12 +230,15 @@
     return jax.tree.unflatten(tree, lax.optimization_barrier(flat))
 
 
+def after(values, *first):
+    return together(values, *first)[0]
+
+
 def stack_kernel(count, *refs):
     sources, target, held, arrived, left = refs[:count], *refs[count:]
-    rows = sources[0].shape[0]
     moves = []
-    for k, source in enumerate(sources):
-        here = pl.ds(k * rows, rows)
+    for k, (source, rows) in enumerate(zip(sources, piece_slices(sources), strict=True)):
+        here = pl.ds(rows.start, rows.stop - rows.start)
         moves.append(
             (
                 pltpu.make_async_copy(source, held.at[here], arrived.at[k]),
@@ -127,35 +254,33 @@
         go.wait()
 
 
-def stack_blocks(blocks):
-    rows, width = blocks[0].shape
-    shape, dtype = (len(blocks) * rows, width), blocks[0].dtype
-    size = shape[0] * width * dtype.itemsize
+def stack_blocks(pieces):
+    width, dtype = pieces[0].shape[1], pieces[0].dtype
+    shape = (sum(piece.shape[0] for piece in pieces), width)
     return pl.pallas_call(
-        functools.partial(stack_kernel, len(blocks)),
-        in_specs=[pl.BlockSpec(memory_space=pl.ANY)] * len(blocks),
+        functools.partial(stack_kernel, len(pieces)),
+        in_specs=[pl.BlockSpec(memory_space=pl.ANY)] * len(pieces),
         out_specs=pl.BlockSpec(memory_space=pl.ANY),
         out_shape=jax.ShapeDtypeStruct(shape, dtype),
         scratch_shapes=[pltpu.VMEM(shape, dtype)]
-        + [pltpu.SemaphoreType.DMA((len(blocks),))] * 2,
-        compiler_params=pltpu.CompilerParams(vmem_limit_bytes=size + 4 * 2**20),
-        cost_estimate=SMALL,
+        + [pltpu.SemaphoreType.DMA((len(pieces),))] * 2,
+        compiler_params=pltpu.CompilerParams(vmem_limit_bytes=KERNEL_VMEM),
+        cost_estimate=takes("stack_blocks"),
         name="stack_blocks",
-    )(*blocks)
-
-
-def gather_seq(rows):
-    return stack_blocks(gather_blocks(rows))
+    )(*pieces)
 
 
 def plus(first, second):
     return (first.astype(F32) + second.astype(F32)).astype(BF)
 
 
-def chip_sums(even, odd, count):
-    total = plus(even, flip(odd, 1))
+def split_chips(total, count):
     rows = total.shape[0] // count
     return [total[k * rows : (k + 1) * rows] for k in range(count)]
+
+
+def chip_sums(even, odd, count):
+    return split_chips(plus(even, flip(odd, 1)), count)
 
 
 def scatter_relay(sums):
@@ -172,15 +297,22 @@
     }
 
 
+def last_hops(left):
+    if lax.axis_size("seq") != 8:
+        return [flip(parts[0], 2 * k) for k, parts in left.items() if k]
+    return [flip(part, 2) for part in left[1]] + [flip(part, 4) for part in left[2]]
+
+
+def hops_sum(left, hops):
+    own = left[0][0].astype(F32)
+    if lax.axis_size("seq") != 8:
+        return sum((hop.astype(F32) for hop in hops), own)
+    x_low, x_high, y_high, y_low = [hop.astype(F32) for hop in hops]
+    return own + jnp.concatenate([x_low + y_low, x_high + y_high], axis=0)
+
+
 def scatter_last(left):
-    n_seq = lax.axis_size("seq")
-    if n_seq != 8:
-        return sum(
-            (flip(parts[0], 2 * k) if k else parts[0]).astype(F32) for k, parts in left.items()
-        )
-    x_low, x_high = [flip(part, 2).astype(F32) for part in left[1]]
-    y_high, y_low = [flip(part, 4).astype(F32) for part in left[2]]
-    return left[0][0].astype(F32) + jnp.concatenate([x_low + y_low, x_high + y_high], axis=0)
+    return hops_sum(left, last_hops(left))
 
 
 def scatter_pairs(even, odd):
@@ -253,40 +385,96 @@
     return terms.reshape(n_seq, n_dp, rows, width).transpose(1, 0, 2, 3)
 
 
-def first_kernel(count, low_width, x_ref, *refs):
-    blocks, (out_ref, normed_ref, gains_ref) = refs[:count], refs[count:]
-    rows = blocks[0].shape[0]
+def spread(n_dp, own, rows):
+    shape = (n_dp * own, n_dp * rows)
+    at = lax.broadcasted_iota(jnp.int32, shape, 0)
+    to = lax.broadcasted_iota(jnp.int32, shape, 1)
+    hit = to == at // own * rows + at % own
+    return jnp.where(hit, 1.0, 0.0).astype(BF)
+
+
+def exchanged_rows(rows, me):
+    count = len(rows)
+    result = []
+    for k in range(count):
+        row = rows[0]
+        for at in range(1, count):
+            row = jnp.where((me ^ k) == at, rows[at], row)
+        result.append(row)
+    return result
+
+
+def first_kernel(count, n_seq, n_dp, me_ref, x_ref, cos_ref, sin_ref, *refs):
+    pieces = refs[:count]
+    pack_ref, latent_ref, parts_ref, gain_ref, feed_gain_ref, query_gain_ref, out_ref = refs[count:]
+    me = me_ref[0]
+    latent_width = latent_ref.shape[1]
+    low_width = pack_ref.shape[1]
     x = x_ref[...].astype(F32)
     scale = lax.rsqrt(jnp.mean(x * x, axis=1, keepdims=True) + EPS)
-    for k in range(count):
-        here = slice(k * rows, (k + 1) * rows)
-        gains = blocks[k][:, low_width:].astype(F32).T
-        gains_ref[:, here] = gains[: gains_ref.shape[0]]
-        normed = (x_ref[:, here].astype(F32) * scale * gains[:1]).astype(BF)
-        normed_ref[:, here] = normed
-        part = matmul(normed, blocks[k][:, :low_width])
+    size = x_ref.shape[1] // n_seq
+    gains = []
+    for k, here in enumerate(piece_slices(pieces)):
+        gains.append(pieces[k][:, low_width:].astype(F32).T[:8])
+        owner, first = me ^ (here.start // size), here.start % size
+        rows = here.stop - here.start
+        own = pl.ds(pl.multiple_of(owner * size + first, rows), rows)
+        normed = (x_ref[:, own].astype(F32) * scale * gains[k][:1]).astype(BF)
+        parts_ref[owner, :, first : first + rows] = normed
+        gain_ref[:, own] = gains[k][:1]
+        feed_gain_ref[:, own] = gains[k][1:2]
+        part = matmul(normed, pieces[k][:, :low_width])
         if k == 0:
             out_ref[...] = part
         else:
             out_ref[...] += part
-
-
-def first_projections(x, blocks, low_width):
+    gains = jnp.concatenate(gains, axis=1)
+    own = latent_width // (n_seq * n_dp)
+    query_rows = []
+    for k in range(n_seq):
+        query_rows.append(gains[2:3, k * size : (k + 1) * size])
+    query_rows = exchanged_rows(query_rows, me)
+    query_rows = dot_rows(
+        jnp.concatenate(query_rows, axis=0).astype(BF), spread(n_dp, own, size // n_dp)
+    )
+    query_gain = jnp.concatenate([query_rows[k : k + 1] for k in range(n_seq)], axis=1)
+    query_gain_ref[...] = query_gain
+    latent = out_ref[:, :latent_width]
+    latent_ref[...] = latent
+    latent_scale = lax.rsqrt(jnp.mean(latent * latent, axis=1, keepdims=True) + EPS)
+    pack_ref[:, :latent_width] = (latent * latent_scale * query_gain).astype(BF)
+    keyvalue = out_ref[:, latent_width:]
+    pack_ref[:, latent_width : latent_width + HEAD_DIM] = rotate_heads(
+        keyvalue[:, :HEAD_DIM], cos_ref[...], sin_ref[...], 1.0
+    ).astype(BF)
+    pack_ref[:, latent_width + HEAD_DIM :] = keyvalue[:, HEAD_DIM:].astype(BF)
+
+
+def first_projections(me, x, cosine, sine_part, pieces, latent_width):
+    n_seq = lax.axis_size("seq")
     tok_count, width = x.shape
+    low_width = pieces[0].shape[1] - 128
     vmem = pl.BlockSpec(memory_space=pltpu.VMEM)
+    shape = jax.ShapeDtypeStruct
     return pl.pallas_call(
-        functools.partial(first_kernel, len(blocks), low_width),
-        in_specs=[vmem] * (1 + len(blocks)),
-        out_specs=[vmem] * 3,
+        functools.partial(
+            first_kernel, len(pieces), lax.axis_size("seq"), lax.axis_size("dp")
+        ),
+        in_specs=[pl.BlockSpec(memory_space=pltpu.SMEM)] + [vmem] * (3 + len(pieces)),
+        out_specs=[vmem] * 6,
         out_shape=[
-            jax.ShapeDtypeStruct((tok_count, low_width), F32),
-            jax.ShapeDtypeStruct((tok_count, width), BF),
-            jax.ShapeDtypeStruct((8, width), F32),
+            shape((tok_count, low_width), BF),
+            shape((tok_count, latent_width), F32),
+            shape((n_seq, tok_count, width // n_seq), BF),
+            shape((1, width), F32),
+            shape((1, width), F32),
+            shape((1, latent_width), F32),
         ],
-        compiler_params=pltpu.CompilerParams(vmem_limit_bytes=40 * 2**20),
-        cost_estimate=SMALL,
+        scratch_shapes=[pltpu.VMEM((tok_count, low_width), F32)],
+        compiler_params=pltpu.CompilerParams(vmem_limit_bytes=KERNEL_VMEM),
+        cost_estimate=takes("first_projections"),
         name="first_projections",
-    )(x, *blocks)
+    )(me, x, cosine, sine_part, *pieces)
 
 
 def weights_in_order(raw_ref, gate_ref, up_ref):
@@ -305,9 +493,8 @@
 
     @pl.when(at == 0)
     def _():
-        rows = blocks[0].shape[0]
-        for k, source in enumerate(blocks):
-            x_ref[k * rows : (k + 1) * rows, :] = source[...]
+        for source, here in zip(blocks, piece_slices(blocks), strict=True):
+            x_ref[here, :] = source[...]
         weights_in_order(raw_ref, gate_ref, up_ref)
 
     x = x_ref[pl.ds(pl.multiple_of(at * block, block), block), :]
@@ -325,23 +512,23 @@
 
 
 def feed_forward(blocks, raw, block):
-    rows, width = blocks[0].shape
-    group_len = rows * len(blocks)
+    width = blocks[0].shape[1]
+    group_len = sum(piece.shape[0] for piece in blocks)
     hidden = raw.shape[-1]
     units = pl.BlockSpec((block, hidden), lambda i: (i, 0))
     weight = jax.ShapeDtypeStruct((width, hidden), BF)
     return pl.pallas_call(
         functools.partial(feed_kernel, len(blocks), block),
         grid=(group_len // block,),
-        in_specs=[whole_spec((rows, width))] * len(blocks) + [whole_spec(raw.shape)],
+        in_specs=[whole_spec(piece.shape) for piece in blocks] + [whole_spec(raw.shape)],
         out_specs=[whole_spec((group_len, width))]
         + [units] * 3
         + [whole_spec((width, hidden))] * 2,
         out_shape=[jax.ShapeDtypeStruct((group_len, width), BF)]
         + [jax.ShapeDtypeStruct((group_len, hidden), BF)] * 3
         + [weight] * 2,
-        compiler_params=pltpu.CompilerParams(vmem_limit_bytes=52 * 2**20),
-        cost_estimate=SMALL,
+        compiler_params=pltpu.CompilerParams(vmem_limit_bytes=KERNEL_VMEM),
+        cost_estimate=takes("feed_forward"),
         name="feed_forward",
     )(*blocks, raw)
 
@@ -373,8 +560,8 @@
         out_specs=[pl.BlockSpec((block, hidden), lambda i: (i, 0))] * 2 + [half] * 2,
         out_shape=[jax.ShapeDtypeStruct((count * block, hidden), BF)] * 2
         + [jax.ShapeDtypeStruct((count * block // 2, width), BF)] * 2,
-        compiler_params=pltpu.CompilerParams(vmem_limit_bytes=44 * 2**20),
-        cost_estimate=SMALL,
+        compiler_params=pltpu.CompilerParams(vmem_limit_bytes=KERNEL_VMEM),
+        cost_estimate=takes("feed_back"),
         name="feed_back",
     )(d, silu, slope, gate, up, down)
 
@@ -400,8 +587,8 @@
         + [whole_spec(part.shape) for part in (*low, *high)],
         out_specs=pl.BlockSpec((n_dp, 1, 2, rows, hidden), lambda i: (0, i, 0, 0, 0)),
         out_shape=jax.ShapeDtypeStruct((n_dp, n_seq, 2, rows, hidden), BF),
-        compiler_params=pltpu.CompilerParams(vmem_limit_bytes=40 * 2**20),
-        cost_estimate=SMALL,
+        compiler_params=pltpu.CompilerParams(vmem_limit_bytes=KERNEL_VMEM),
+        cost_estimate=takes("gate_up_grad"),
         name="gate_up_grad",
     )(x, *low, *high)
 
@@ -423,28 +610,35 @@
         in_specs=[pl.BlockSpec((block, depth), lambda i: (i, 0)), whole_spec(right.shape)],
         out_specs=[half] * 2,
         out_shape=[jax.ShapeDtypeStruct((rows // 2, width), BF)] * 2,
-        compiler_params=pltpu.CompilerParams(vmem_limit_bytes=32 * 2**20),
-        cost_estimate=SMALL,
+        compiler_params=pltpu.CompilerParams(vmem_limit_bytes=KERNEL_VMEM),
+        cost_estimate=takes("pair_product"),
         name="pair_product",
     )(left, right)
 
 
+GAIN_ROWS = 32
+
+
 def last_kernel(
     count,
+    n_seq,
+    me_ref,
     back_ref,
     latent_ref,
     query_gain_ref,
-    normed_ref,
     x_ref,
     gain_ref,
     cos_ref,
     sin_ref,
+    feed_term_ref,
     *refs,
 ):
-    blocks, (even_ref, odd_ref, dx_ref, query_term_ref, gain_term_ref) = refs[:count], refs[count:]
+    blocks, (load_ref, dx_ref) = refs[:count], refs[count:]
+    me = me_ref[0]
     latent_width = latent_ref.shape[1]
-    first_width = back_ref.shape[1]
-    rows = blocks[0].shape[0]
+    tok_count, first_width = back_ref.shape
+    width = x_ref.shape[1]
+    size = width // n_seq
 
     def norm_back(v, e, gain):
         r = lax.rsqrt(jnp.mean(v * v, axis=1, keepdims=True) + EPS)
@@ -453,7 +647,7 @@
         grad = r * (eg - u * jnp.mean(eg * u, axis=1, keepdims=True))
         return grad, jnp.sum(e * u, axis=0, keepdims=True)
 
-    d_latent, query_term_ref[...] = norm_back(
+    d_latent, query_term = norm_back(
         latent_ref[...], back_ref[:, :latent_width], query_gain_ref[...]
     )
     half = HEAD_DIM // 2
@@ -469,37 +663,97 @@
         ],
         axis=1,
     ).astype(BF)
-    for k in range(count):
-        here = slice(k * rows, (k + 1) * rows)
-        target = odd_ref if k % 2 else even_ref
-        at = slice(k // 2 * rows, (k // 2 + 1) * rows)
-        target[at, :first_width] = dot_cols(normed_ref[:, here], d_first).astype(BF)
-        dx_ref[:, here] = dot_rows(d_first, blocks[k][:, :first_width])
-    dx_ref[...], gain_term_ref[...] = norm_back(
-        x_ref[...].astype(F32), dx_ref[...], gain_ref[...]
-    )
-
-
-def last_products(back, latent, query_gain, normed, x, gain, cosine, sine_part, blocks):
+    load_ref[:tok_count, :] = d_first
+    for piece, here in zip(blocks, piece_slices(blocks), strict=True):
+        rows = here.stop - here.start
+        place = (me ^ (here.start // size)) * size + here.start % size
+        own = pl.ds(pl.multiple_of(place, rows), rows)
+        dx_ref[:, own] = dot_rows(d_first, piece[:, :first_width])
+    dx_ref[...], gain_term = norm_back(x_ref[...].astype(F32), dx_ref[...], gain_ref[...])
+    pad = jnp.zeros((1, 2 * first_width - width), F32)
+    rows = [
+        gain_term[:, :first_width],
+        jnp.concatenate([gain_term[:, first_width:], pad], axis=1),
+        feed_term_ref[:, :first_width],
+        jnp.concatenate([feed_term_ref[:, first_width:], pad], axis=1),
+        jnp.concatenate([query_term, jnp.zeros((1, first_width - latent_width), F32)], axis=1),
+        jnp.zeros((GAIN_ROWS - 5, first_width), F32),
+    ]
+    load_ref[tok_count:, :] = jnp.concatenate(rows, axis=0).astype(BF)
+
+
+def last_products(me, back, latent, query_gain, x, gain, cosine, sine_part, feed_term, blocks):
     tok_count, width = x.shape
-    rows, first_width = blocks[0].shape
     vmem = pl.BlockSpec(memory_space=pltpu.VMEM)
-    half = jax.ShapeDtypeStruct((len(blocks) // 2 * rows, first_width), BF)
     return pl.pallas_call(
-        functools.partial(last_kernel, len(blocks)),
-        in_specs=[vmem] * (8 + len(blocks)),
-        out_specs=[vmem] * 5,
+        functools.partial(last_kernel, len(blocks), lax.axis_size("seq")),
+        in_specs=[pl.BlockSpec(memory_space=pltpu.SMEM)] + [vmem] * (8 + len(blocks)),
+        out_specs=[vmem] * 2,
         out_shape=[
-            half,
-            half,
+            jax.ShapeDtypeStruct((tok_count + GAIN_ROWS, back.shape[1]), BF),
             jax.ShapeDtypeStruct((tok_count, width), F32),
-            jax.ShapeDtypeStruct((1, latent.shape[1]), F32),
-            jax.ShapeDtypeStruct((1, width), F32),
         ],
-        compiler_params=pltpu.CompilerParams(vmem_limit_bytes=44 * 2**20),
-        cost_estimate=SMALL,
+        compiler_params=pltpu.CompilerParams(vmem_limit_bytes=KERNEL_VMEM),
+        cost_estimate=takes("last_products"),
         name="last_products",
-    )(back, latent, query_gain, normed, x, gain, cosine, sine_part, *blocks)
+    )(me, back, latent, query_gain, x, gain, cosine, sine_part, feed_term, *blocks)
+
+
+def first_grads_kernel(count, n_seq, n_dp, latent_width, me_ref, normed_ref, *refs):
+    pieces, (out_ref, d_ref, x_ref) = refs[:count], refs[count:]
+    me = me_ref[0]
+    tok_count, size = normed_ref.shape[1:]
+    first_width = d_ref.shape[1]
+    block = tok_count + GAIN_ROWS
+    terms = jnp.zeros((8, first_width), F32)
+    for piece, here in zip(pieces, piece_slices(pieces), strict=True):
+        k, first = here.start // block, here.start % block
+        tokens = min(tok_count - first, piece.shape[0])
+        d_ref[k * tok_count + first : k * tok_count + first + tokens, :] = piece[:tokens, :]
+        if tokens < piece.shape[0]:
+            terms = terms + piece[tokens : tokens + 16, :].astype(F32)[:8]
+    for k in range(n_seq):
+        x_ref[k * tok_count : (k + 1) * tok_count, :] = normed_ref[me ^ k]
+    out_ref[:, :first_width] = dot_cols(x_ref[...], d_ref[...]).astype(BF)
+    width = size * n_seq
+    rest = width - first_width
+
+    def share(row, length):
+        own = row[:, :length]
+        for k in range(1, n_seq):
+            own = jnp.where(me == k, row[:, k * length : (k + 1) * length], own)
+        return own
+
+    gain = jnp.concatenate([terms[0:1], terms[1:2, :rest]], axis=1)
+    feed = jnp.concatenate([terms[2:3], terms[3:4, :rest]], axis=1)
+    query = share(terms[4:5, :latent_width], latent_width // n_seq)
+    query = matmul(
+        jnp.concatenate([query] * 8, axis=0).astype(BF),
+        spread(n_dp, query.shape[1] // n_dp, size // n_dp),
+    )[:1]
+    rows = [share(gain, size), share(feed, size), query, jnp.zeros((125, size), F32)]
+    out_ref[:, first_width:] = jnp.concatenate(rows, axis=0).T.astype(BF)
+
+
+def first_grads(me, normed, pieces, latent_width):
+    n_seq, tok_count, size = normed.shape
+    first_width = pieces[0].shape[1]
+    vmem = pl.BlockSpec(memory_space=pltpu.VMEM)
+    return pl.pallas_call(
+        functools.partial(
+            first_grads_kernel, len(pieces), n_seq, lax.axis_size("dp"), latent_width
+        ),
+        in_specs=[pl.BlockSpec(memory_space=pltpu.SMEM)] + [vmem] * (1 + len(pieces)),
+        out_specs=vmem,
+        out_shape=jax.ShapeDtypeStruct((size, first_width + 128), BF),
+        scratch_shapes=[
+            pltpu.VMEM((n_seq * tok_count, first_width), BF),
+            pltpu.VMEM((n_seq * tok_count, size), BF),
+        ],
+        compiler_params=pltpu.CompilerParams(vmem_limit_bytes=KERNEL_VMEM),
+        cost_estimate=takes("first_grads"),
+        name="first_grads",
+    )(me, normed, *pieces)
 
 
 def block_places(shape, axis, core):
@@ -541,13 +795,11 @@
 
     @pl.when(index == 0)
     def _():
-        rows = packs[0].shape[0]
-        for k, pack in enumerate(packs):
-            here = slice(k * rows, (k + 1) * rows)
+        for pack, here in zip(packs, piece_slices(packs), strict=True):
             lat_ref[here, :] = pack[:, :latent_width]
             k_ref[here, :] = pack[:, latent_width : latent_width + HEAD_DIM]
             v_ref[here, :] = pack[:, latent_width + HEAD_DIM :]
-        for j in range(count // 2):
+        for j in range(k_ref.shape[0] // block):
             here = slice(j * block, (j + 1) * block)
             vt_ref[:, here] = v_ref[here, :].T
 
@@ -594,8 +846,8 @@
 
 
 def attend(me, starts, cosine, sine_part, query_up, output, packs, latent_width, block):
-    rows, pack_width = packs[0].shape
-    group_len = rows * len(packs)
+    pack_width = packs[0].shape[1]
+    group_len = sum(piece.shape[0] for piece in packs)
     width = query_up.shape[1]
     heads = width // HEAD_DIM
     out_width = output.shape[1]
@@ -616,7 +868,7 @@
                 whole_spec(query_up.shape),
                 whole_spec(output.shape),
             ]
-            + [whole_spec((rows, pack_width))] * len(packs),
+            + [whole_spec(piece.shape) for piece in packs],
             out_specs=[
                 whole_spec((group_len, latent_width)),
                 whole_spec((group_len, HEAD_DIM)),
@@ -639,10 +891,10 @@
             shape((group_len // 2, out_width), BF),
             shape((group_len // 2, out_width), BF),
         ],
-        compiler_params=pltpu.CompilerParams(vmem_limit_bytes=44 * 2**20),
-        cost_estimate=SMALL,
+        compiler_params=pltpu.CompilerParams(vmem_limit_bytes=KERNEL_VMEM),
+        cost_estimate=takes("attend"),
         name="attend",
-    )(me, starts.reshape(1, group_len), cosine, sine_part, query_up, output, *packs)
+    )(me, starts, cosine, sine_part, query_up, output, *packs)
 
 
 def attend_back_kernel(
@@ -673,9 +925,8 @@
 
     @pl.when(index == 0)
     def _():
-        rows = blocks[0].shape[0]
-        for k, source in enumerate(blocks):
-            d_ref[k * rows : (k + 1) * rows, :] = source[...]
+        for source, here in zip(blocks, piece_slices(blocks), strict=True):
+            d_ref[here, :] = source[...]
         dk_ref[...] = jnp.zeros_like(dk_ref)
         dv_ref[...] = jnp.zeros_like(dv_ref)
 
@@ -724,7 +975,7 @@
 
     @pl.when(index == pl.num_programs(0) - 1)
     def _():
-        for j in range(count // 2):
+        for j in range(k_ref.shape[0] // block):
             to = slice(j * half, (j + 1) * half)
             for target, first in ((even_ref, j * block), (odd_ref, j * block + half)):
                 rows = slice(first, first + half)
@@ -737,7 +988,7 @@
 ):
     group_len, width = queries.shape
     heads = width // HEAD_DIM
-    rows, out_width = blocks[0].shape
+    out_width = blocks[0].shape[1]
     latent_width = query_up.shape[0]
     pack_width = latent_width + 2 * HEAD_DIM
     tokens = pl.BlockSpec((block, width), lambda i, me: (i, 0))
@@ -762,7 +1013,7 @@
                 whole_spec(query_up.shape),
                 whole_spec(output.shape),
             ]
-            + [whole_spec((rows, out_width))] * len(blocks),
+            + [whole_spec(piece.shape) for piece in blocks],
             out_specs=[
                 whole_spec((group_len, out_width)),
                 tokens,
@@ -777,12 +1028,12 @@
             shape(half, BF),
             shape(half, BF),
         ],
-        compiler_params=pltpu.CompilerParams(vmem_limit_bytes=48 * 2**20),
-        cost_estimate=SMALL,
+        compiler_params=pltpu.CompilerParams(vmem_limit_bytes=KERNEL_VMEM),
+        cost_estimate=takes("attend_back"),
         name="attend_back",
     )(
         me,
-        starts.reshape(1, group_len),
+        starts,
         cosine,
         sine_part,
         queries,
@@ -794,6 +1045,62 @@
         output,
         *blocks,
     )
+
+
+def attention_grads_kernel(n_dp, query_rows, mixed_ref, latent_ref, dq_ref, d_ref, out_ref):
+    out_rows = mixed_ref.shape[1] // n_dp
+    output_terms = dot_cols(mixed_ref[...], d_ref[...]).astype(BF)
+    query_terms = dot_cols(latent_ref[...], dq_ref[...])
+    for z in range(n_dp):
+        out_ref[z, :out_rows, :] = output_terms[z * out_rows : (z + 1) * out_rows]
+        parts = [
+            query_terms[first : first + query_rows]
+            for first in range(z * query_rows, query_terms.shape[0], n_dp * query_rows)
+        ]
+        out_ref[z, out_rows:, :] = jnp.concatenate(parts, axis=0).astype(BF)
+
+
+def attention_grads(mixed, latent, d_query, d_branch, n_dp, query_rows):
+    group_len, width = d_branch.shape
+    heads_width = mixed.shape[1]
+    sets = width // heads_width
+    part = latent.shape[1] // sets
+    rows = heads_width // n_dp + part // n_dp
+    return pl.pallas_call(
+        functools.partial(attention_grads_kernel, n_dp, query_rows),
+        grid=(sets,),
+        in_specs=[
+            whole_spec(mixed.shape),
+            pl.BlockSpec((group_len, part), lambda j: (0, j)),
+            whole_spec(d_query.shape),
+            pl.BlockSpec((group_len, heads_width), lambda j: (0, j)),
+        ],
+        out_specs=pl.BlockSpec((n_dp, rows, heads_width), lambda j: (0, 0, j)),
+        out_shape=jax.ShapeDtypeStruct((n_dp, rows, width), BF),
+        compiler_params=pltpu.CompilerParams(vmem_limit_bytes=KERNEL_VMEM),
+        cost_estimate=takes("attention_grads"),
+        name="attention_grads",
+    )(mixed, latent, d_query, d_branch)
+
+
+def columns_back_kernel(parts_ref, *targets):
+    for which, target in enumerate(targets):
+        parts = [parts_ref[k, which].astype(F32) for k in range(parts_ref.shape[0])]
+        target[...] = jnp.concatenate(parts, axis=1)
+
+
+def columns_back(parts):
+    n_seq, kinds, rows, columns = parts.shape
+    vmem = pl.BlockSpec(memory_space=pltpu.VMEM)
+    return pl.pallas_call(
+        columns_back_kernel,
+        in_specs=[vmem],
+        out_specs=[vmem] * kinds,
+        out_shape=[jax.ShapeDtypeStruct((rows, n_seq * columns), F32)] * kinds,
+        compiler_params=pltpu.CompilerParams(vmem_limit_bytes=KERNEL_VMEM),
+        cost_estimate=takes("columns_back"),
+        name="columns_back",
+    )(parts)
 
 
 def local(
@@ -835,56 +1142,48 @@
     first_set = jnp.concatenate(
         [query_down, keyvalue_weight, jnp.pad(gains, ((0, 0), (0, 125)))], axis=1
     )
+    chain = Chain()
+    block = 2 * tok_count
+    half_chips = n_seq // 4
+    first_width = latent_width + 2 * HEAD_DIM
+    out_rows = output_weight.shape[0]
+
+    chain.add(tables=(cosine_all, sine_all, starts_all.reshape(1, group_len)))
     first_set, query_up = together(first_set, query_up)
-    first_part = gather_dp_steps(first_set)
-    d_feed_blocks = gather_near(cotangent[0])
-    query_part = exchange(split_columns(query_up)).reshape(-1, query_up.shape[1] // n_seq)
+    chain.add(query_part=exchange(split_columns(query_up)))
+    chain.add(feed_step=gather_near(cotangent[0]))
+    first_part = chain.stage(FIRST_PART, gather_dp_steps(first_set))
+    query_part = chain.query_part.reshape(-1, query_up.shape[1] // n_seq)
     fold = query_part.shape[0] * query_part.shape[1] // width
     attention_set = jnp.concatenate([output_weight, query_part.reshape(fold, width)], axis=0)
-    first_part, d_feed_blocks, cosine_all, sine_all, attention_set = together(
-        first_part, d_feed_blocks, cosine_all, sine_all, attention_set
-    )
+    chain.add(attention=gather_dp(chain.begin(attention=attention_set)))
+    chain.add(gate_up_parts=jnp.stack([split_columns(gate_weight), split_columns(up_weight)], axis=1),
+    )
+    near = chain.stage(FIRST_NEAR, gather_near(first_part))
+    far = chain.stage(FIRST_FAR, gather_far(near))
+    chain.add(gate_up=exchange(chain.begin(gate_up=chain.gate_up_parts)))
+    first_blocks = chain.stage(FIRST_BLOCKS, gather_cores(far))
+    cosine_all, sine_all, starts_all = chain.tables
     cosine, sine_part = cosine_all[:tok_count], sine_all[:tok_count]
-    attention_part = gather_dp(attention_set)
-    gate_weight, up_weight, first_part = together(gate_weight, up_weight, first_part)
-    gate_up = exchange(jnp.stack([split_columns(gate_weight), split_columns(up_weight)], axis=1))
-    first_blocks, gate_up, d_feed_blocks = together(
-        gather_blocks(first_part), gate_up, d_feed_blocks
-    )
-    full_gate_up = gather_dp(gate_up.reshape(-1, hidden_units)).reshape(n_dp, *gate_up.shape)
-    full_down = gather_dp(down_weight)
-    d_feed_blocks = gather_far(d_feed_blocks)
-    tokens_low_rel = relative(input_low, 1)
-    first_width = latent_width + 2 * HEAD_DIM
-    first_out, normed_rel, gain_rows = first_projections(
-        tokens_low_rel, first_blocks, first_width
-    )
-    tokens_rel = tokens_low_rel.astype(F32)
-    attention_gain_rel = gain_rows[0]
-    other_gains = relative_vectors(gain_rows[1:3])
-    feed_gain_f = other_gains[0]
-    query_gain_f = other_gains[1].reshape(-1, own_rows)[:, :query_rows].reshape(-1)
-
-    latent = first_out[:, :latent_width]
-    keyvalue = first_out[:, latent_width:first_width]
-    latent_low = rms_norm(latent, query_gain_f).astype(BF)
-    key_local = rotate(keyvalue[:, :HEAD_DIM], cosine, sine_part)
-    pack = jnp.concatenate(
-        [latent_low, key_local.astype(BF), keyvalue[:, HEAD_DIM:].astype(BF)], axis=1
-    )
-    pack, attention_part = together(pack, attention_part)
-    out_rows = output_weight.shape[0]
-    attention_part = attention_part.reshape(n_dp, -1, width)
+    pack, latent, normed_parts, attention_gain_row, feed_gain_row, query_gain_row = first_projections(
+        me_array, input_low, cosine, sine_part, first_blocks, latent_width
+    )
+    feed_gain_f = feed_gain_row[0]
+    pack = chain.stage(PACK, pack)
+    attention_part = chain.attention.reshape(n_dp, -1, width)
     full_output = attention_part[:, :out_rows].reshape(-1, width)
     full_query_up = rows_in_order(
         attention_part[:, out_rows:].reshape(-1, query_part.shape[1]), query_up.shape[0]
     )
-    packs = gather_blocks(pack)
-    d_feed = stack_blocks(gather_cores(d_feed_blocks))
-    packs, full_query_up, full_output, d_feed = together(
-        packs, full_query_up, full_output, d_feed
-    )
-    block = 2 * tok_count
+    chain.add(attention_weights=(full_output, full_query_up))
+    near = chain.stage(PACK_NEAR, gather_near(pack))
+    gate_up = chain.gate_up
+    chain.add(gate_up_all=gather_dp(gate_up.reshape(-1, hidden_units)).reshape(n_dp, *gate_up.shape),
+    )
+    chain.add(down_all=gather_dp(down_weight))
+    packs = chain.stage(PACKS, gather_cores(gather_far(near)))
+    full_output, full_query_up = chain.attention_weights
+    chain.add(feed_far=gather_far(chain.begin(feed_far=chain.feed_step)))
     latent_all, keys, values, queries, mixed_low, lse, out_even, out_odd = attend(
         me_array,
         starts_all,
@@ -896,49 +1195,64 @@
         latent_width,
         block,
     )
+    out_even, out_odd = chain.stage(ATTENDED, (out_even, out_odd))
+    feed_pieces = gather_cores(chain.feed_far)
+    out_left = chain.stage(OUT_LEFT, scatter_relay(chip_sums(out_even, out_odd, n_seq // 2))
+    )
+    hidden = chain.stage(HIDDEN, tokens + scatter_last(out_left))
+
+    chain.add(feed_stack=stack_blocks(chain.begin(feed_stack=feed_pieces)))
+    feed_low = rms_norm(hidden, feed_gain_f).astype(BF)
+    near = chain.stage(FEED_NEAR, gather_near(feed_low))
+    feed_blocks = chain.stage(FEED_BLOCKS, gather_cores(gather_far(near)))
+    chain.add(normed_columns=exchange(chain.begin(normed_columns=normed_parts)))
+    feed, active_low, silu_low, slope_low, gate_ordered, up_ordered = feed_forward(
+        feed_blocks, chain.gate_up_all, block
+    )
+    chain.add(grad_down_term=dot_cols(active_low, chain.feed_stack).astype(BF))
+    silu_low = chain.stage(ACTIVE, silu_low)
+    d_feed = chain.feed_stack
+    chain.add(grad_down=scatter_dp(chain.grad_down_term))
+    weights = (gate_ordered, up_ordered, chain.down_all)
+    dg_high, du_high, even_high, odd_high = feed_back(
+        d_feed, silu_low, slope_low, *weights, block, half_chips, half_chips
+    )
+    even_high, odd_high = chain.stage(TERMS_HIGH, (even_high, odd_high))
+    chain.add(high_swap=flip(odd_high, 1))
+    dg_low, du_low, *terms_low = feed_back(
+        d_feed, after(silu_low, odd_high), slope_low, *weights, block, 0, half_chips
+    )
+    terms_low = chain.stage(TERMS_LOW, terms_low)
+    feed_sums = chip_sums(*terms_low, half_chips) + split_chips(
+        plus(even_high, chain.high_swap), half_chips
+    )
+    feed_sums = chain.stage(FEED_SUMS, feed_sums)
+    feed_left = chain.stage(FEED_LEFT, scatter_relay(feed_sums))
+    chain.add(grad_gate_up_term=gate_up_grad(
+            chain.begin(grad_gate_up_term=feed),
+            (dg_low, du_low),
+            (dg_high, du_high),
+            n_dp,
+            n_seq,
+        ),
+    )
+    d_feed_normed = chain.stage(D_NORMED, scatter_last(feed_left))
+    chain.add(grad_gate_up=scatter_dp(chain.grad_gate_up_term.reshape(-1, hidden_units)))
 
     d_result = cotangent[0].astype(F32)
-    hidden = tokens + scatter_pairs(out_even, out_odd)
-    hidden, full_gate_up = together(hidden, full_gate_up)
-
-    feed_low = rms_norm(hidden, feed_gain_f).astype(BF)
-    feed_blocks = gather_blocks(feed_low)
-    feed, active_low, silu_low, slope_low, gate_ordered, up_ordered = feed_forward(
-        feed_blocks, full_gate_up, block
-    )
-    grad_down_term = dot_cols(active_low, d_feed).astype(BF)
-    silu_low, grad_down_term = lax.optimization_barrier((silu_low, grad_down_term))
-    grad_down = scatter_dp(grad_down_term)
-    half_chips = n_seq // 4
-    dg_high, du_high, *terms_high = feed_back(
-        d_feed,
-        silu_low,
-        slope_low,
-        gate_ordered,
-        up_ordered,
-        full_down,
-        block,
-        half_chips,
-        half_chips,
-    )
-    silu_again, terms_high = together(silu_low, terms_high)
-    dg_low, du_low, *terms_low = feed_back(
-        d_feed, silu_again, slope_low, gate_ordered, up_ordered, full_down, block, 0, half_chips
-    )
-    feed_sums = chip_sums(*terms_low, half_chips) + chip_sums(*terms_high, half_chips)
-    feed_sums, feed = together(feed_sums, feed)
-    d_feed_normed = scatter_last(scatter_relay(feed_sums))
-    grad_gate_up_term = gate_up_grad(feed, (dg_low, du_low), (dg_high, du_high), n_dp, n_seq)
-    d_feed_normed, grad_gate_up_term = together(d_feed_normed, grad_gate_up_term)
-    grad_gate_up = scatter_dp(grad_gate_up_term.reshape(-1, hidden_units))
-
     d_hidden_norm, grad_feed_gain_term = jax.vjp(rms_norm, hidden, feed_gain_f)[1](d_feed_normed)
     d_hidden = d_result + d_hidden_norm
-    d_branch_blocks = gather_blocks(d_hidden.astype(BF))
-    result_terms = pair_product(active_low, full_down, block)
-    result_sums = chip_sums(*result_terms, n_seq // 2)
-    d_branch_blocks, result_sums = together(d_branch_blocks, result_sums)
-    result_left = scatter_relay(result_sums)
+    chain.add(result_terms=pair_product(chain.begin(result_terms=active_low), chain.down_all, block),
+    )
+    near = chain.stage(BRANCH_NEAR, gather_near(d_hidden.astype(BF)))
+    chain.add(result_sums=chip_sums(*chain.result_terms, n_seq // 2))
+    d_branch_blocks = gather_cores(gather_far(near))
+    d_branch_blocks, feed_gain_term = chain.stage(BRANCH_BLOCKS, (d_branch_blocks, grad_feed_gain_term.reshape(1, -1))
+    )
+    chain.add(result_left=scatter_relay(chain.begin(result_left=chain.result_sums)))
+    d_branch_blocks = chain.stage(BRANCH_ALL, d_branch_blocks)
+    result_left = chain.result_left
+    chain.add(result_hops=last_hops(result_left))
     d_branch, d_query_low, back_even, back_odd = attend_back(
         me_array,
         starts_all,
@@ -954,64 +1268,49 @@
         d_branch_blocks,
         block,
     )
-    back_even, back_odd, grad_down, result_left = together(
-        back_even, back_odd, grad_down, result_left
-    )
-    back_local = scatter_pairs(back_even, back_odd)
-    grad_output_term = dot_cols(mixed_low, d_branch).astype(BF)
-    grad_query_term = rows_by_dp(dot_cols(latent_all, d_query_low).astype(BF))
-    grad_attention_term = jnp.concatenate(
-        [
-            grad_output_term.reshape(n_dp, out_rows, width),
-            grad_query_term.reshape(n_dp, fold, width),
-        ],
-        axis=1,
-    ).reshape(-1, width)
-    back_local, grad_attention_term, grad_gate_up = together(
-        back_local, grad_attention_term, grad_gate_up
-    )
-    grad_attention = scatter_dp(grad_attention_term)
-
-    first_even, first_odd, d_tokens_rel, query_term, gain_term = last_products(
+    back_even, back_odd = chain.stage(BACK_TERMS, (back_even, back_odd))
+    back_sums = chain.stage(BACK_SUMS, chip_sums(back_even, back_odd, n_seq // 2))
+    d_branch, latent_all = chain.begin(grad_attention_term=(d_branch, latent_all))
+    chain.add(grad_attention_term=attention_grads(mixed_low, latent_all, d_query_low, d_branch, n_dp, query_rows),
+    )
+    back_left = chain.stage(BACK_LEFT, scatter_relay(back_sums))
+    back_local = chain.stage(BACK_LOCAL, scatter_last(back_left))
+    chain.add(grad_attention=scatter_dp(chain.grad_attention_term.reshape(-1, width)))
+    load, d_tokens = last_products(
+        me_array,
         back_local,
         latent,
-        query_gain_f.reshape(1, -1),
-        normed_rel,
-        tokens_low_rel,
-        gain_rows[:1],
+        query_gain_row,
+        input_low,
+        attention_gain_row,
         cosine,
         sine_part,
+        feed_gain_term,
         first_blocks,
     )
-    input_grad = (d_hidden + relative(d_tokens_rel, 1))[None]
-    query_column = jnp.pad(
-        query_term.reshape(-1, query_rows), ((0, 0), (0, own_rows - query_rows))
-    ).reshape(1, -1)
-    other_terms = relative_vectors(
-        jnp.concatenate([grad_feed_gain_term.reshape(1, -1), query_column], axis=0)
-    )
-    gain_terms = jnp.concatenate([gain_term, other_terms], axis=0)
-    columns = jnp.pad(gain_terms, ((0, 125), (0, 0))).T.astype(BF).reshape(n_seq, -1, 128)
-    first_even = lax.dynamic_update_slice(
-        first_even, columns[0::2].reshape(-1, 128), (0, first_width)
-    )
-    first_odd = lax.dynamic_update_slice(
-        first_odd, columns[1::2].reshape(-1, 128), (0, first_width)
-    )
-    first_sum = scatter_pairs(first_even, first_odd).astype(BF)
-    first_sum, grad_attention = lax.optimization_barrier((first_sum, grad_attention))
+    load = chain.stage(FIRST_TERMS, load)
+    near = chain.stage(LAST_NEAR, gather_near(load))
+    d_tokens = after(d_tokens, load)
+    input_grad = (d_hidden + d_tokens)[None]
+    chain.add(input_grad=input_grad)
+    loads = chain.stage(LAST_BLOCKS, gather_cores(gather_far(near)))
+    first_sum = chain.stage(FIRST_SUM, first_grads(me_array, chain.normed_columns, loads, latent_width)
+    )
+    gate_up_rows = chain.begin(gate_up_rows=chain.grad_gate_up)
+    gate_up_rows = exchange(gate_up_rows.reshape(n_seq, 2, own_rows, -1))
     grad_first = scatter_dp(first_sum).astype(F32)
-    result_left, first_sum = together(result_left, first_sum)
-    result = hidden + scatter_last(result_left)
+    result = hidden + hops_sum(result_left, chain.begin(result_last=chain.result_hops))
     layer_output = result.astype(BF)[None]
 
+    grad_down = chain.grad_down
+    grad_attention = chain.grad_attention
     grad_output_weight = grad_attention[:out_rows].astype(F32)
-    grad_query_up = exchange(grad_attention[out_rows:].reshape(n_seq, query_rows, -1))
+    grad_query_up = grad_attention[out_rows:].reshape(fold, -1, heads * HEAD_DIM)
+    grad_query_up = grad_query_up.transpose(1, 0, 2).reshape(n_seq, query_rows, -1)
+    grad_query_up = exchange(after(grad_query_up, gate_up_rows))
     grad_query_up = grad_query_up.transpose(1, 0, 2).reshape(query_rows, -1).astype(F32)
 
-    gate_up_rows = exchange(grad_gate_up.reshape(n_seq, 2, own_rows, -1)).astype(F32)
-    grad_gate = gate_up_rows[:, 0].transpose(1, 0, 2).reshape(own_rows, -1)
-    grad_up = gate_up_rows[:, 1].transpose(1, 0, 2).reshape(own_rows, -1)
+    grad_gate, grad_up = columns_back(gate_up_rows)
     return (
         layer_output,
         input_grad,

time: 651 us -> 586 us (0.900)
  local copies, waits for them, and re-layouts: 128 us -> 42.7 us
  Pallas kernels: 139 us -> 174 us
  other arithmetic: 61.3 us -> 42.3 us
  waiting for transfers between devices: 199 us -> 210 us
  matrix products: 17.9 us -> 9.75 us
    unnamed x234 -> x122, local copies, waits for them, and re-layouts: 63.2 us -> 7.75 us
    pallas_call x3 -> x6, Pallas kernels: 15.3 us -> 38.8 us  [the longest x1 9.94 us: attention_grads(): pl.pallas_call(functools.partial(attention_grads_kernel, n_dp, query_rows...]
    ppermute x76 -> x83, waiting for transfers between devices: 186 us -> 171 us  [flip(): return lax.ppermute(block, 'seq', [(i, i ^ bits) for i in range(n_seq)])]
    all_to_all x4 -> x5, waiting for transfers between devices: 9.21 us -> 22.8 us  [exchange(): return lax.all_to_all(parts, 'seq', 0, 0)]
    dot_general x3 -> x1, matrix products: 17.9 us -> 9.75 us  [dot_cols(): lax.dot_general(left_side, right_side, (((0,), (0,)), ((), ())), preferre...]
    all_to_all x4 -> x5, starting transfers between devices: 15 us -> 19.1 us  [exchange(): return lax.all_to_all(parts, 'seq', 0, 0)]
    convert_element_type x13 -> x11, other arithmetic: 20.5 us -> 16.6 us  [plus(): return (first.astype(F32) + second.astype(F32)).astype(BF)]
    ppermute x76 -> x83, starting transfers between devices: 58.2 us -> 57.3 us  [flip(): return lax.ppermute(block, 'seq', [(i, i ^ bits) for i in range(n_seq)])]
  transfers between devices with their start and end apart: 90 -> 98, of which waited for: 41 -> 48; matrix products, arithmetic and copies ran while one was open for 24% -> 13% of each run, Pallas kernels for 16% -> 27%
where the time goes in v4:
time: 586 us; the launch traced here: 578 us
  waiting for transfers between devices  210 us (36%)
  Pallas kernels  174 us (30%)
  starting transfers between devices  83.6 us (14%)
  local copies, waits for them, and re-layouts  42.7 us (7%)
  other arithmetic  42.3 us (7%)
  between operations  15.6 us (3%)
  matrix products  9.75 us (2%)
    ppermute x83, waiting for transfers between devices, flip(): return lax.ppermute(block, 'seq', [(i, i ^ bits) for i in range(n_seq)])  171 us
    ppermute x83, starting transfers between devices, flip(): return lax.ppermute(block, 'seq', [(i, i ^ bits) for i in range(n_seq)])  57.3 us
    pallas_call x1, Pallas kernels, attend_back(): pl.pallas_call(functools.partial(attend_back_kernel, len(blocks), heads,...  32.3 us
    pallas_call x2, Pallas kernels, feed_back(): pl.pallas_call(feed_back_kernel, grid=(count,), in_specs=[tokens, units,...  31.4 us
    pallas_call x1, Pallas kernels, attend(): pl.pallas_call(functools.partial(attend_kernel, len(packs), heads, block)...  26.5 us
    all_to_all x5, waiting for transfers between devices, exchange(): return lax.all_to_all(parts, 'seq', 0, 0)  22.8 us
    pallas_call x1, Pallas kernels, feed_forward(): pl.pallas_call(functools.partial(feed_kernel, len(blocks), block), grid=(...  20.7 us
    all_to_all x5, starting transfers between devices, exchange(): return lax.all_to_all(parts, 'seq', 0, 0)  19.1 us
  transfers between devices with their start and end apart: 98, of which 48 were waited for; matrix products, arithmetic and copies ran while one was open for 13% of the time, Pallas kernels for 27%

profile of v4, /device:TPU:0, one launch (start us, length us, event | category | flops | bytes accessed | tf_op | source)
XLA Modules:
  0.0 577.7 jit_solution(8531814331606008426)
XLA Ops:
  9.6 5.1 collective-permute-start.2
  20.2 3.4 all-to-all-start
  23.8 4.6 collective-permute-done
  28.5 4.3 collective-permute-done.1
  32.9 5.4 all-to-all-done
  42.8 1.9 reshape.184
  44.8 14.6 %collective-permute-done.6.refs_4_ = bf16[256,1664]{1,0:T(8,128)(2,1)S(1)} collective-permute-done((bf16[256,1664]{1,0:T(8,128)(2,1)S(1)}, bf16[256,1664]{1,0:T(8,128)(2,1)S(1)}, u32[]{:S(2)}, u32[]{:S(2)}) %collective-permute-start.6) | collective-permute-done | bytes 852000 | tf_op jit(solution)/shard_map/ppermute | solution.py:192
  64.3 7.4 %collective-permute-done.10.refs_6_ = bf16[128,1664]{1,0:T(8,128)(2,1)} collective-permute-done((bf16[128,1664]{1,0:T(8,128)(2,1)S(1)}, bf16[128,1664]{1,0:T(8,128)(2,1)}, u32[]{:S(2)}, u32[]{:S(2)}) %collective-permute-start.10) | collective-permute-done | bytes 426016 | tf_op jit(solution)/shard_map/ppermute | solution.py:192
  74.4 4.4 all-to-all-start.1
  81.5 2.8 multiply_sine_fusion
  87.6 6.4 %first_projections.1 = (bf16[192,1536]{1,0:T(8,128)(2,1)}, f32[192,1024]{1,0:T(8,128)}, bf16[8,192,256]{2,1,0:T(8,128)(2,1)}, f32[1,2048]{1,0:T(1,128)}, f32[1,2048]{1,0:T(1,128)}, /*index=5*/f32[1,1024]{1,0:T(1,128)}) custom-call(s32[1]{0:T(128)} %bitcast.1.me_ref, bf16[192,2048]{1,0:T(8,128)(2,1)} %bitcast.60, f32[192,128]{1,0:T(8,128)} %slice.191.cos_ref, ...), custom_call_target="tpu_custom_call" | custom-call | flops 10000000 | bytes 20000 | tf_op jit(solution)/shard_map/first_projections/pallas_call | solution.py:459
  94.0 5.8 %all-to-all-done.1 = bf16[8,2,64,704]{3,2,1,0:T(8,128)(2,1)} async-done(((bf16[8,2,64,704]{3,2,1,0:T(8,128)(2,1)}), bf16[8,2,64,704]{3,2,1,0:T(8,128)(2,1)}, u32[]{:S(2)}, u32[]{:S(2)}) %all-to-all-start.1) | async-done | bytes 1441824 | tf_op jit(solution)/shard_map/all_to_all | solution.py:372
  99.8 4.0 all-gather.4.cloned.1.call-done
  108.4 3.2 slice.243
  113.3 6.1 %collective-permute-done.15.refs_4_ = bf16[192,1536]{1,0:T(8,128)(2,1)S(1)} collective-permute-done((bf16[192,1536]{1,0:T(8,128)(2,1)}, bf16[192,1536]{1,0:T(8,128)(2,1)S(1)}, u32[]{:S(2)}, u32[]{:S(2)}) %collective-permute-start.15) | collective-permute-done | bytes 589856 | tf_op jit(solution)/shard_map/ppermute | solution.py:192
  123.3 5.0 collective-permute-done.19.refs_6_
  133.2 1.8 slice.197
  136.2 26.5 %attend.1 = (bf16[1536,1024]{1,0:T(8,128)(2,1)}, bf16[1536,256]{1,0:T(8,128)(2,1)}, bf16[1536,256]{1,0:T(8,128)(2,1)}, bf16[1536,512]{1,0:T(8,128)(2,1)}, bf16[1...) custom-call(s32[1]{0:T(128)} %bitcast.1.me_ref, ...), custom_call_target="tpu_custom_call" | custom-call | flops 10000000 | bytes 20000 | tf_op jit(solution)/shard_map/attend/pallas_call | solution.py:859
  162.9 5.9 %collective-permute-done.25 = bf16[768,2048]{1,0:T(8,128)(2,1)S(1)} collective-permute-done((bf16[768,2048]{1,0:T(8,128)(2,1)}, bf16[768,2048]{1,0:T(8,128)(2,1)S(1)}, u32[]{:S(2)}, u32[]{:S(2)}) %collective-permute-start.25) | collective-permute-done | bytes 3145760 | tf_op jit(solution)/shard_map/ppermute | solution.py:192
  168.8 3.3 add_convert_fusion.1
  175.7 7.7 %collective-permute-done.29 = bf16[96,2048]{1,0:T(8,128)(2,1)S(1)} collective-permute-done((bf16[96,2048]{1,0:T(8,128)(2,1)S(1)}, bf16[96,2048]{1,0:T(8,128)(2,1)S(1)}, u32[]{:S(2)}, u32[]{:S(2)}) %collective-permute-start.29) | collective-permute-done | bytes 393248 | tf_op jit(solution)/shard_map/ppermute | solution.py:192
  183.4 2.3 collective-permute-done.27
  187.3 5.8 %collective-permute-done.26 = bf16[96,2048]{1,0:T(8,128)(2,1)} collective-permute-done((bf16[96,2048]{1,0:T(8,128)(2,1)S(1)}, bf16[96,2048]{1,0:T(8,128)(2,1)}, u32[]{:S(2)}, u32[]{:S(2)}) %collective-permute-start.26) | collective-permute-done | bytes 393248 | tf_op jit(solution)/shard_map/ppermute | solution.py:192
  197.8 5.7 collective-permute-done.31
  210.0 5.5 stack_blocks.1.d_ref
  215.6 9.9 %collective-permute-done.33.refs_4_ = bf16[192,2048]{1,0:T(8,128)(2,1)} collective-permute-done((bf16[192,2048]{1,0:T(8,128)(2,1)S(1)}, bf16[192,2048]{1,0:T(8,128)(2,1)}, u32[]{:S(2)}, u32[]{:S(2)}) %collective-permute-start.33) | collective-permute-done | bytes 786464 | tf_op jit(solution)/shard_map/ppermute | solution.py:192
  231.4 6.8 %collective-permute-done.42.refs_6_ = bf16[96,2048]{1,0:T(8,128)(2,1)S(1)} collective-permute-done((bf16[96,2048]{1,0:T(8,128)(2,1)S(1)}, bf16[96,2048]{1,0:T(8,128)(2,1)S(1)}, u32[]{:S(2)}, u32[]{:S(2)}) %collective-permute-start.42) | collective-permute-done | bytes 393248 | tf_op jit(solution)/shard_map/ppermute | solution.py:192
  238.2 2.2 collective-permute-done.43.refs_7_
  240.4 1.7 collective-permute-done.45.refs_9_
  243.2 3.5 all-to-all-start.2
  247.0 20.7 %feed_forward.1 = (bf16[1536,2048]{1,0:T(8,128)(2,1)}, bf16[1536,704]{1,0:T(8,128)(2,1)}, bf16[1536,704]{1,0:T(8,128)(2,1)}, bf16[1536,704]{1,0:T(8,128)(2,1)}, ...) custom-call(bf16[192,2048]{1,0:T(8,128)(2,1)} %copy-done.14, bf16[192,2048]{1,0:T(8,128)(2,1)} %copy-done.27, ...), custom_call_target="tpu_custom_call" | custom-call | flops 10000000 | bytes 20000 | tf_op jit(solution)/shard_map/feed_forward/pallas_call | solution.py:520
  267.7 9.8 %convolution_convert_fusion = bf16[704,2048]{1,0:T(8,128)(2,1)} fusion(bf16[1536,704]{1,0:T(8,128)(2,1)} %get-tuple-element.275.left_ref, bf16[1536,2048]{1,0:T(8,128)(2,1)} %stack_blocks.1.d_ref), kind=kOutput, calls=%fused_computation.3 | convolution fusion | flops 4430626816 | bytes 11337728 | tf_op jit(solution)/shard_map/dot_general | solution.py:185
  278.5 15.6 %feed_back.2 = (bf16[768,704]{1,0:T(8,128)(2,1)}, bf16[768,704]{1,0:T(8,128)(2,1)}, bf16[384,2048]{1,0:T(8,128)(2,1)}, bf16[384,2048]{1,0:T(8,128)(2,1)}) custom-call(bf16[1536,2048]{1,0:T(8,128)(2,1)} %stack_blocks.1.d_ref, bf16[1536,704]{1,0:T(8,128)(2,1)} %get-tuple-element.260.silu_ref, bf16[1536,704]{1,0:T(8,128)(2,1)} %get-tuple-element.254.slope_ref, ...), custom_call_target="tpu_custom_call" | custom-call | flops 10000000 | bytes 20000 | tf_op jit(solution)/shard_map/feed_back/pallas_call | solution.py:555
  294.7 15.8 %feed_back.3 = (bf16[768,704]{1,0:T(8,128)(2,1)}, bf16[768,704]{1,0:T(8,128)(2,1)}, bf16[384,2048]{1,0:T(8,128)(2,1)}, bf16[384,2048]{1,0:T(8,128)(2,1)}) custom-call(bf16[1536,2048]{1,0:T(8,128)(2,1)} %stack_blocks.1.d_ref, bf16[1536,704]{1,0:T(8,128)(2,1)} %get-tuple-element.260.silu_ref, bf16[1536,704]{1,0:T(8,128)(2,1)} %get-tuple-element.254.slope_ref, ...), custom_call_target="tpu_custom_call" | custom-call | flops 10000000 | bytes 20000 | tf_op jit(solution)/shard_map/feed_back/pallas_call | solution.py:555
  311.2 2.0 add_convert_fusion.3
  316.6 7.8 %collective-permute-done.49 = bf16[96,2048]{1,0:T(8,128)(2,1)S(1)} collective-permute-done((bf16[96,2048]{1,0:T(8,128)(2,1)S(1)}, bf16[96,2048]{1,0:T(8,128)(2,1)S(1)}, u32[]{:S(2)}, u32[]{:S(2)}) %collective-permute-start.49) | collective-permute-done | bytes 393248 | tf_op jit(solution)/shard_map/ppermute | solution.py:192
  330.0 15.1 %gate_up_grad.1 = bf16[4,8,2,64,704]{4,3,2,1,0:T(8,128)(2,1)} custom-call(bf16[1536,2048]{1,0:T(8,128)(2,1)} %get-tuple-element.269.x_ref, bf16[768,704]{1,0:T(8,128)(2,1)} %get-tuple-element.270.dg_low, bf16[768,704]{1,0:T(8,128)(2,1)} %get-tuple-element.271.du_low, bf16[768,704]{1,0:T(8,128)(2,1)} %get-tuple-element.272.dg_high, ...), custom_call_target="tpu_custom_call" | custom-call | flops 10000000 | bytes 20000 | tf_op jit(solution)/shard_map/gate_up_grad/pallas_call | solution.py:583
  346.9 2.5 reduce-scatter.5.cloned.1.call-done
  355.1 8.9 %pair_product.1 = (bf16[768,2048]{1,0:T(8,128)(2,1)}, bf16[768,2048]{1,0:T(8,128)(2,1)}) custom-call(bf16[1536,704]{1,0:T(8,128)(2,1)} %get-tuple-element.275.left_ref, bf16[704,2048]{1,0:T(8,128)(2,1)} %all-gather.8.cloned.1.call-done.down_ref.right_ref), custom_call_target="tpu_custom_call" | custom-call | flops 3000000000 | bytes 6000000 | tf_op jit(solution)/shard_map/pair_product/pallas_call | solution.py:607
  364.1 7.3 %collective-permute-done.55.refs_4_ = bf16[192,2048]{1,0:T(8,128)(2,1)} collective-permute-done((bf16[192,2048]{1,0:T(8,128)(2,1)}, bf16[192,2048]{1,0:T(8,128)(2,1)}, u32[]{:S(2)}, u32[]{:S(2)}) %collective-permute-start.55) | collective-permute-done | bytes 786464 | tf_op jit(solution)/shard_map/ppermute | solution.py:192
  377.3 7.9 %collective-permute-done.59.refs_6_ = bf16[96,2048]{1,0:T(8,128)(2,1)S(1)} collective-permute-done((bf16[96,2048]{1,0:T(8,128)(2,1)S(1)}, bf16[96,2048]{1,0:T(8,128)(2,1)S(1)}, u32[]{:S(2)}, u32[]{:S(2)}) %collective-permute-start.59) | collective-permute-done | bytes 393248 | tf_op jit(solution)/shard_map/ppermute | solution.py:192
  385.2 2.3 collective-permute-done.60.refs_7_
  388.0 3.3 add_convert_fusion
  394.8 9.0 %collective-permute-done.65 = bf16[96,2048]{1,0:T(8,128)(2,1)S(1)} collective-permute-done((bf16[96,2048]{1,0:T(8,128)(2,1)S(1)}, bf16[96,2048]{1,0:T(8,128)(2,1)S(1)}, u32[]{:S(2)}, u32[]{:S(2)}) %collective-permute-start.65) | collective-permute-done | bytes 393248 | tf_op jit(solution)/shard_map/ppermute | solution.py:192
  410.1 32.3 %attend_back.1 = (bf16[1536,2048]{1,0:T(8,128)(2,1)}, bf16[1536,512]{1,0:T(8,128)(2,1)}, bf16[768,1536]{1,0:T(8,128)(2,1)}, bf16[768,1536]{1,0:T(8,128)(2,1)}) custom-call(s32[1]{0:T(128)} %bitcast.1.me_ref, s32[1,1536]{1,0:T(1,128)} %reshape.187.starts_ref, f32[1536,128]{1,0:T(8,128)} %copy-done.3, f32[1536,128]{1,0:T(8,128)} %copy-done.2, ...), custom_call_target="tpu_custom_call" | custom-call | flops 10000000 | bytes 20000 | tf_op jit(solution)/shard_map/attend_back/pallas_call | solution.py:999
  442.6 4.7 collective-permute-done.70
  447.3 2.3 add_convert_fusion.2
  451.9 9.9 %attention_grads.1 = bf16[4,192,2048]{2,1,0:T(8,128)(2,1)} custom-call(bf16[1536,512]{1,0:T(8,128)(2,1)} %get-tuple-element.304.mixed_ref, bf16[1536,1024]{1,0:T(8,128)(2,1)} %get-tuple-element.334.latent_ref, bf16[1536,512]{1,0:T(8,128)(2,1)} %get-tuple-element.335.dq_ref, bf16[1536,2048]{1,0:T(8,128)(2,1)} %get-tuple-element.336.d_ref), custom_call_target="tpu_custom_call" | custom-call | flops 10000000 | bytes 20000 | tf_op jit(solution)/shard_map/attention_grads/pallas_call | solution.py:1069
  461.9 2.2 add_convert_fusion.11
  468.5 6.1 %collective-permute-done.73 = bf16[96,1536]{1,0:T(8,128)(2,1)S(1)} collective-permute-done((bf16[96,1536]{1,0:T(8,128)(2,1)}, bf16[96,1536]{1,0:T(8,128)(2,1)S(1)}, u32[]{:S(2)}, u32[]{:S(2)}) %collective-permute-start.73) | collective-permute-done | bytes 294944 | tf_op jit(solution)/shard_map/ppermute | solution.py:192
  476.2 3.4 collective-permute-done.75
  482.0 8.5 %last_products.1 = (bf16[224,1536]{1,0:T(8,128)(2,1)}, f32[192,2048]{1,0:T(8,128)}) custom-call(s32[1]{0:T(128)} %bitcast.1.me_ref, f32[192,1536]{1,0:T(8,128)} %maximum_add_fusion.3.back_ref, f32[192,1024]{1,0:T(8,128)} %get-tuple-element.342.latent_ref, f32[1,1024]{1,0:T(1,128)} %get-tuple-element.343.query_gain_ref, bf16[192,2048]{1,0:T(8,128)(2,1)} %bitcast.61, ...), custom_call_target="tpu_custom_call" | custom-call | flops 10000000 | bytes 20000 | tf_op jit(solution)/shard_map/last_products/pallas_call | solution.py:688
  492.5 14.1 %collective-permute-done.80.refs_4_ = bf16[224,1536]{1,0:T(8,128)(2,1)S(1)} collective-permute-done((bf16[224,1536]{1,0:T(8,128)(2,1)}, bf16[224,1536]{1,0:T(8,128)(2,1)S(1)}, u32[]{:S(2)}, u32[]{:S(2)}) %collective-permute-start.80) | collective-permute-done | bytes 688160 | tf_op jit(solution)/shard_map/ppermute | solution.py:192
  507.3 1.8 collective-permute-done.78.refs_2_
  509.6 5.8 %collective-permute-done.82.refs_6_ = bf16[112,1536]{1,0:T(8,128)(2,1)S(1)} collective-permute-done((bf16[112,1536]{1,0:T(8,128)(2,1)S(1)}, bf16[112,1536]{1,0:T(8,128)(2,1)S(1)}, u32[]{:S(2)}, u32[]{:S(2)}) %collective-permute-start.82) | collective-permute-done | bytes 344096 | tf_op jit(solution)/shard_map/ppermute | solution.py:192
  515.4 4.2 collective-permute-done.83.refs_7_
  523.4 5.2 first_grads.1
  528.6 4.3 all-to-all-start.3
  532.9 2.1 convert_add_fusion.1
  539.8 4.0 add_bitcast_fusion
  543.8 10.1 %all-to-all-done.3.parts_ref = bf16[8,2,64,704]{3,2,1,0:T(8,128)(2,1)} async-done(((bf16[8,2,64,704]{3,2,1,0:T(8,128)(2,1)}), bf16[8,2,64,704]{3,2,1,0:T(8,128)(2,1)}, u32[]{:S(2)}, u32[]{:S(2)}) %all-to-all-start.3) | async-done | bytes 1441824 | tf_op jit(solution)/shard_map/all_to_all | solution.py:372
  553.9 3.4 all-to-all-start.4
  557.3 2.1 slice_convert_fusion
  559.5 3.2 columns_back.1
  (369 shorter events, 131.4 us)
Async XLA Ops:
  9.6 23.2 %collective-permute-start.2 = (bf16[64,1664]{1,0:T(8,128)(2,1)S(1)}, bf16[64,1664]{1,0:T(8,128)(2,1)S(1)}, u32[]{:S(2)}, u32[]{:S(2)}) collective-permute-start(bf16[64,1664]{1,0:T(8,128)(2,1)S(1)} %fusion.6), channel_id=1, source_target_pairs={{0,3},{1,2},{2,1},{3,0},{4,7},{5,6},{6,5},{7,4},{8,11},{9,10},{10,... | collective-permute-start | bytes 638984 | tf_op jit(solution)/shard_map/ppermute | solution.py:356
  14.7 18.1 %collective-permute-start.1 = (bf16[64,1664]{1,0:T(8,128)(2,1)S(1)}, bf16[64,1664]{1,0:T(8,128)(2,1)S(1)}, u32[]{:S(2)}, u32[]{:S(2)}) collective-permute-start(bf16[64,1664]{1,0:T(8,128)(2,1)S(1)} %fusion.6), channel_id=1, source_target_pairs={{0,2},{1,3},{2,0},{3,1},{4,6},{5,7},{6,4},{7,5},{8,10},{9,11},{10,... | collective-permute-start | bytes 638984 | tf_op jit(solution)/shard_map/ppermute | solution.py:356
  14.7 13.7 %collective-permute-start = (bf16[64,1664]{1,0:T(8,128)(2,1)S(1)}, bf16[64,1664]{1,0:T(8,128)(2,1)S(1)}, u32[]{:S(2)}, u32[]{:S(2)}) collective-permute-start(bf16[64,1664]{1,0:T(8,128)(2,1)S(1)} %fusion.6), channel_id=1, source_target_pairs={{0,1},{1,0},{2,3},{3,2},{4,5},{5,4},{6,7},{7,6},{8,9},{9,8},{10,11... | collective-permute-start | bytes 638984 | tf_op jit(solution)/shard_map/ppermute | solution.py:356
  15.4 22.9 %collective-permute-start.4 = (bf16[192,2048]{1,0:T(8,128)(2,1)}, bf16[192,2048]{1,0:T(8,128)(2,1)}, u32[]{:S(2)}, u32[]{:S(2)}) collective-permute-start(bf16[192,2048]{1,0:T(8,128)(2,1)} %bitcast.62), channel_id=1, source_target_pairs={{0,16},{4,20},{8,24},{12,28},{16,0},{20,4},{24,8},{28,12},{1,17},{... | collective-permute-start | bytes 2359304 | tf_op jit(solution)/shard_map/ppermute | solution.py:192
  17.0 21.3 %collective-permute-start.3 = (bf16[192,2048]{1,0:T(8,128)(2,1)}, bf16[192,2048]{1,0:T(8,128)(2,1)}, u32[]{:S(2)}, u32[]{:S(2)}) collective-permute-start(bf16[192,2048]{1,0:T(8,128)(2,1)} %bitcast.63), channel_id=1, source_target_pairs={{0,8},{4,12},{8,0},{12,4},{16,24},{20,28},{24,16},{28,20},{1,9},{5... | collective-permute-start | bytes 2359304 | tf_op jit(solution)/shard_map/ppermute | solution.py:192
  20.2 18.1 %all-to-all-start = ((bf16[8,32,512]{2,1,0:T(8,128)(2,1)}), bf16[8,32,512]{2,1,0:T(8,128)(2,1)S(1)}, u32[]{:S(2)}, u32[]{:S(2)}) async-start(bf16[8,32,512]{2,1,0:T(8,128)(2,1)} %bitcast.53), calls=%async_computation | async-start | bytes 524288 | tf_op jit(solution)/shard_map/all_to_all | solution.py:372
  23.6 80.2 %all-gather.4.cloned.1.call-start = ((), (), s32[]{:S(2)}) async-start(), calls=%async_computation.9 | async-start | bytes 3932160 | tf_op jit(solution)/shard_map/all_gather | solution.py:346
  39.4 20.0 %collective-permute-start.6 = (bf16[256,1664]{1,0:T(8,128)(2,1)S(1)}, bf16[256,1664]{1,0:T(8,128)(2,1)S(1)}, u32[]{:S(2)}, u32[]{:S(2)}) collective-permute-start(bf16[256,1664]{1,0:T(8,128)(2,1)S(1)} %constant_dynamic-update-slice_fusion.refs_0_), channel_id=1, source_target_pairs={{0,16},{4,20},{8,24},{12,28},{16,0},{20,4},{24,8},{28,12},{1,17},{... | collective-permute-start | bytes 2555912 | tf_op jit(solution)/shard_map/ppermute | solution.py:192
  41.0 19.8 %collective-permute-start.5 = (bf16[256,1664]{1,0:T(8,128)(2,1)S(1)}, bf16[256,1664]{1,0:T(8,128)(2,1)}, u32[]{:S(2)}, u32[]{:S(2)}) collective-permute-start(bf16[256,1664]{1,0:T(8,128)(2,1)S(1)} %constant_dynamic-update-slice_fusion.refs_0_), channel_id=1, source_target_pairs={{0,8},{4,12},{8,0},{12,4},{16,24},{20,28},{24,16},{28,20},{1,9},{5... | collective-permute-start | bytes 2555912 | tf_op jit(solution)/shard_map/ppermute | solution.py:192
  74.4 25.5 %all-to-all-start.1 = ((bf16[8,2,64,704]{3,2,1,0:T(8,128)(2,1)}), bf16[8,2,64,704]{3,2,1,0:T(8,128)(2,1)}, u32[]{:S(2)}, u32[]{:S(2)}) async-start(bf16[8,2,64,704]{3,2,1,0:T(8,128)(2,1)} %copy.58), calls=%async_computation.1 | async-start | bytes 3145728 | tf_op jit(solution)/shard_map/all_to_all | solution.py:372
  78.8 147.8 %all-gather.6.cloned.1.call-start = ((), (), s32[]{:S(2)}) async-start(), calls=%async_computation.10 | async-start | bytes 7864320 | tf_op jit(solution)/shard_map/all_gather | solution.py:346
  103.9 174.6 %all-gather.8.cloned.1.call-start = ((), (), s32[]{:S(2)}) async-start(), calls=%async_computation.11 | async-start | bytes 3604480 | tf_op jit(solution)/shard_map/all_gather | solution.py:346
  104.1 15.3 %collective-permute-start.15 = (bf16[192,1536]{1,0:T(8,128)(2,1)}, bf16[192,1536]{1,0:T(8,128)(2,1)S(1)}, u32[]{:S(2)}, u32[]{:S(2)}) collective-permute-start(bf16[192,1536]{1,0:T(8,128)(2,1)} %get-tuple-element.214.refs_0_), channel_id=1, source_target_pairs={{0,16},{4,20},{8,24},{12,28},{16,0},{20,4},{24,8},{28,12},{1,17},{... | collective-permute-start | bytes 1769480 | tf_op jit(solution)/shard_map/ppermute | solution.py:192
  105.6 15.0 %collective-permute-start.14 = (bf16[192,1536]{1,0:T(8,128)(2,1)}, bf16[192,1536]{1,0:T(8,128)(2,1)S(1)}, u32[]{:S(2)}, u32[]{:S(2)}) collective-permute-start(bf16[192,1536]{1,0:T(8,128)(2,1)} %get-tuple-element.214.refs_0_), channel_id=1, source_target_pairs={{0,8},{4,12},{8,0},{12,4},{16,24},{20,28},{24,16},{28,20},{1,9},{5... | collective-permute-start | bytes 1769480 | tf_op jit(solution)/shard_map/ppermute | solution.py:192
  135.0 27.8 %collective-permute-start.23 = (bf16[96,2048]{1,0:T(8,128)(2,1)}, bf16[96,2048]{1,0:T(8,128)(2,1)S(1)}, u32[]{:S(2)}, u32[]{:S(2)}) collective-permute-start(bf16[96,2048]{1,0:T(8,128)(2,1)} %slice.197), channel_id=1, source_target_pairs={{0,8},{4,12},{8,0},{12,4},{16,24},{20,28},{24,16},{28,20},{1,9},{5... | collective-permute-start | bytes 1179656 | tf_op jit(solution)/shard_map/ppermute | solution.py:192
  135.6 27.2 %collective-permute-start.24 = (bf16[96,2048]{1,0:T(8,128)(2,1)S(1)}, bf16[96,2048]{1,0:T(8,128)(2,1)}, u32[]{:S(2)}, u32[]{:S(2)}) collective-permute-start(bf16[96,2048]{1,0:T(8,128)(2,1)S(1)} %slice.198), channel_id=1, source_target_pairs={{0,16},{4,20},{8,24},{12,28},{16,0},{20,4},{24,8},{28,12},{1,17},{... | collective-permute-start | bytes 1179656 | tf_op jit(solution)/shard_map/ppermute | solution.py:192
  172.2 11.2 %collective-permute-start.29 = (bf16[96,2048]{1,0:T(8,128)(2,1)S(1)}, bf16[96,2048]{1,0:T(8,128)(2,1)S(1)}, u32[]{:S(2)}, u32[]{:S(2)}) collective-permute-start(bf16[96,2048]{1,0:T(8,128)(2,1)S(1)} %get-tuple-element.374), channel_id=1, source_target_pairs={{0,16},{4,20},{8,24},{12,28},{16,0},{20,4},{24,8},{28,12},{1,17},{... | collective-permute-start | bytes 1179656 | tf_op jit(solution)/shard_map/ppermute | solution.py:192
  173.7 12.0 %collective-permute-start.27 = (bf16[96,2048]{1,0:T(8,128)(2,1)S(1)}, bf16[96,2048]{1,0:T(8,128)(2,1)S(1)}, u32[]{:S(2)}, u32[]{:S(2)}) collective-permute-start(bf16[96,2048]{1,0:T(8,128)(2,1)S(1)} %get-tuple-element.375), channel_id=1, source_target_pairs={{0,8},{4,12},{8,0},{12,4},{16,24},{20,28},{24,16},{28,20},{1,9},{5... | collective-permute-start | bytes 1179656 | tf_op jit(solution)/shard_map/ppermute | solution.py:192
  175.1 18.0 %collective-permute-start.26 = (bf16[96,2048]{1,0:T(8,128)(2,1)S(1)}, bf16[96,2048]{1,0:T(8,128)(2,1)}, u32[]{:S(2)}, u32[]{:S(2)}) collective-permute-start(bf16[96,2048]{1,0:T(8,128)(2,1)S(1)} %get-tuple-element.372), channel_id=1, source_target_pairs={{0,8},{4,12},{8,0},{12,4},{16,24},{20,28},{24,16},{28,20},{1,9},{5... | collective-permute-start | bytes 1179656 | tf_op jit(solution)/shard_map/ppermute | solution.py:192
  186.6 19.2 %collective-permute-start.37 = (bf16[96,2048]{1,0:T(8,128)(2,1)S(1)}, bf16[96,2048]{1,0:T(8,128)(2,1)S(1)}, u32[]{:S(2)}, u32[]{:S(2)}) collective-permute-start(bf16[96,2048]{1,0:T(8,128)(2,1)S(1)} %copy-done.39), channel_id=1, source_target_pairs={{0,4},{4,0},{8,12},{12,8},{16,20},{20,16},{24,28},{28,24},{1,5},{5... | collective-permute-start | bytes 1179656 | tf_op jit(solution)/shard_map/ppermute | solution.py:192
  186.7 20.1 %collective-permute-start.38 = (bf16[96,2048]{1,0:T(8,128)(2,1)}, bf16[96,2048]{1,0:T(8,128)(2,1)S(1)}, u32[]{:S(2)}, u32[]{:S(2)}) collective-permute-start(bf16[96,2048]{1,0:T(8,128)(2,1)} %collective-permute-done.24.refs_7_), channel_id=1, source_target_pairs={{0,4},{4,0},{8,12},{12,8},{16,20},{20,16},{24,28},{28,24},{1,5},{5... | collective-permute-start | bytes 1179656 | tf_op jit(solution)/shard_map/ppermute | solution.py:192
  187.2 21.0 %collective-permute-start.34 = (bf16[192,2048]{1,0:T(8,128)(2,1)S(1)}, bf16[192,2048]{1,0:T(8,128)(2,1)S(1)}, u32[]{:S(2)}, u32[]{:S(2)}) collective-permute-start(bf16[192,2048]{1,0:T(8,128)(2,1)S(1)} %bitcast.65), channel_id=1, source_target_pairs={{0,4},{4,0},{8,12},{12,8},{16,20},{20,16},{24,28},{28,24},{1,5},{5... | collective-permute-start | bytes 2359304 | tf_op jit(solution)/shard_map/ppermute | solution.py:192
  205.9 19.6 %collective-permute-start.33 = (bf16[192,2048]{1,0:T(8,128)(2,1)S(1)}, bf16[192,2048]{1,0:T(8,128)(2,1)}, u32[]{:S(2)}, u32[]{:S(2)}) collective-permute-start(bf16[192,2048]{1,0:T(8,128)(2,1)S(1)} %multiply_convert_fusion.refs_0_), channel_id=1, source_target_pairs={{0,16},{4,20},{8,24},{12,28},{16,0},{20,4},{24,8},{28,12},{1,17},{... | collective-permute-start | bytes 2359304 | tf_op jit(solution)/shard_map/ppermute | solution.py:192
  206.9 19.8 %collective-permute-start.32 = (bf16[192,2048]{1,0:T(8,128)(2,1)S(1)}, bf16[192,2048]{1,0:T(8,128)(2,1)}, u32[]{:S(2)}, u32[]{:S(2)}) collective-permute-start(bf16[192,2048]{1,0:T(8,128)(2,1)S(1)} %multiply_convert_fusion.refs_0_), channel_id=1, source_target_pairs={{0,8},{4,12},{8,0},{12,4},{16,24},{20,28},{24,16},{28,20},{1,9},{5... | collective-permute-start | bytes 2359304 | tf_op jit(solution)/shard_map/ppermute | solution.py:192
  227.7 10.5 %collective-permute-start.42 = (bf16[96,2048]{1,0:T(8,128)(2,1)S(1)}, bf16[96,2048]{1,0:T(8,128)(2,1)S(1)}, u32[]{:S(2)}, u32[]{:S(2)}) collective-permute-start(bf16[96,2048]{1,0:T(8,128)(2,1)S(1)} %slice.206), channel_id=1, source_target_pairs={{0,8},{4,12},{8,0},{12,4},{16,24},{20,28},{24,16},{28,20},{1,9},{5... | collective-permute-start | bytes 1179656 | tf_op jit(solution)/shard_map/ppermute | solution.py:192
  230.9 11.2 %collective-permute-start.39 = (bf16[192,2048]{1,0:T(8,128)(2,1)S(1)}, bf16[192,2048]{1,0:T(8,128)(2,1)S(1)}, u32[]{:S(2)}, u32[]{:S(2)}) collective-permute-start(bf16[192,2048]{1,0:T(8,128)(2,1)S(1)} %multiply_convert_fusion.refs_0_), channel_id=1, source_target_pairs={{0,4},{4,0},{8,12},{12,8},{16,20},{20,16},{24,28},{28,24},{1,5},{5... | collective-permute-start | bytes 2359304 | tf_op jit(solution)/shard_map/ppermute | solution.py:192
  230.9 11.3 %collective-permute-start.40 = (bf16[192,2048]{1,0:T(8,128)(2,1)}, bf16[192,2048]{1,0:T(8,128)(2,1)}, u32[]{:S(2)}, u32[]{:S(2)}) collective-permute-start(bf16[192,2048]{1,0:T(8,128)(2,1)} %collective-permute-done.32.refs_2_), channel_id=1, source_target_pairs={{0,4},{4,0},{8,12},{12,8},{16,20},{20,16},{24,28},{28,24},{1,5},{5... | collective-permute-start | bytes 2359304 | tf_op jit(solution)/shard_map/ppermute | solution.py:192
  231.4 10.8 %collective-permute-start.41 = (bf16[192,2048]{1,0:T(8,128)(2,1)}, bf16[192,2048]{1,0:T(8,128)(2,1)}, u32[]{:S(2)}, u32[]{:S(2)}) collective-permute-start(bf16[192,2048]{1,0:T(8,128)(2,1)} %collective-permute-done.33.refs_4_), channel_id=1, source_target_pairs={{0,4},{4,0},{8,12},{12,8},{16,20},{20,16},{24,28},{28,24},{1,5},{5... | collective-permute-start | bytes 2359304 | tf_op jit(solution)/shard_map/ppermute | solution.py:192
  243.2 34.3 %all-to-all-start.2 = ((bf16[8,192,256]{2,1,0:T(8,128)(2,1)}), bf16[8,192,256]{2,1,0:T(8,128)(2,1)S(1)}, u32[]{:S(2)}, u32[]{:S(2)}) async-start(bf16[8,192,256]{2,1,0:T(8,128)(2,1)} %get-tuple-element.251), calls=%async_computation.2 | async-start | bytes 1572864 | tf_op jit(solution)/shard_map/all_to_all | solution.py:372
  246.7 102.7 %reduce-scatter.5.cloned.1.call-start = ((), (), s32[]{:S(2)}) async-start(), calls=%async_computation.12 | async-start | bytes 3604480 | tf_op jit(solution)/shard_map/reduce_scatter | solution.py:362
  294.1 16.4 %collective-permute-start.46 = (bf16[384,2048]{1,0:T(8,128)(2,1)}, bf16[384,2048]{1,0:T(8,128)(2,1)}, u32[]{:S(2)}, u32[]{:S(2)}) collective-permute-start(bf16[384,2048]{1,0:T(8,128)(2,1)} %get-tuple-element.259), channel_id=1, source_target_pairs={{0,4},{4,0},{8,12},{12,8},{16,20},{20,16},{24,28},{28,24},{1,5},{5... | collective-permute-start | bytes 4718600 | tf_op jit(solution)/shard_map/ppermute | solution.py:192
  294.2 169.8 %reduce-scatter.7.cloned.1.call-start = ((), (), s32[]{:S(2)}) async-start(), calls=%async_computation.13 | async-start | bytes 7864320 | tf_op jit(solution)/shard_map/reduce_scatter | solution.py:362
  310.5 15.4 %collective-permute-start.47 = (bf16[384,2048]{1,0:T(8,128)(2,1)}, bf16[384,2048]{1,0:T(8,128)(2,1)S(1)}, u32[]{:S(2)}, u32[]{:S(2)}) collective-permute-start(bf16[384,2048]{1,0:T(8,128)(2,1)} %get-tuple-element.264), channel_id=1, source_target_pairs={{0,4},{4,0},{8,12},{12,8},{16,20},{20,16},{24,28},{28,24},{1,5},{5... | collective-permute-start | bytes 4718600 | tf_op jit(solution)/shard_map/ppermute | solution.py:192
  313.3 11.1 %collective-permute-start.49 = (bf16[96,2048]{1,0:T(8,128)(2,1)S(1)}, bf16[96,2048]{1,0:T(8,128)(2,1)S(1)}, u32[]{:S(2)}, u32[]{:S(2)}) collective-permute-start(bf16[96,2048]{1,0:T(8,128)(2,1)S(1)} %get-tuple-element.386), channel_id=1, source_target_pairs={{0,8},{4,12},{8,0},{12,4},{16,24},{20,28},{24,16},{28,20},{1,9},{5... | collective-permute-start | bytes 1179656 | tf_op jit(solution)/shard_map/ppermute | solution.py:192
  314.6 13.5 %collective-permute-start.51 = (bf16[96,2048]{1,0:T(8,128)(2,1)S(1)}, bf16[96,2048]{1,0:T(8,128)(2,1)S(1)}, u32[]{:S(2)}, u32[]{:S(2)}) collective-permute-start(bf16[96,2048]{1,0:T(8,128)(2,1)S(1)} %get-tuple-element.388), channel_id=1, source_target_pairs={{0,16},{4,20},{8,24},{12,28},{16,0},{20,4},{24,8},{28,12},{1,17},{... | collective-permute-start | bytes 1179656 | tf_op jit(solution)/shard_map/ppermute | solution.py:192
  316.1 30.3 %collective-permute-start.53 = (bf16[96,2048]{1,0:T(8,128)(2,1)S(1)}, bf16[96,2048]{1,0:T(8,128)(2,1)S(1)}, u32[]{:S(2)}, u32[]{:S(2)}) collective-permute-start(bf16[96,2048]{1,0:T(8,128)(2,1)S(1)} %get-tuple-element.387), channel_id=1, source_target_pairs={{0,16},{4,20},{8,24},{12,28},{16,0},{20,4},{24,8},{28,12},{1,17},{... | collective-permute-start | bytes 1179656 | tf_op jit(solution)/shard_map/ppermute | solution.py:192
  324.5 20.6 %collective-permute-start.50 = (bf16[96,2048]{1,0:T(8,128)(2,1)S(1)}, bf16[96,2048]{1,0:T(8,128)(2,1)S(1)}, u32[]{:S(2)}, u32[]{:S(2)}) collective-permute-start(bf16[96,2048]{1,0:T(8,128)(2,1)S(1)} %add_convert_fusion.8), channel_id=1, source_target_pairs={{0,16},{4,20},{8,24},{12,28},{16,0},{20,4},{24,8},{28,12},{1,17},{... | collective-permute-start | bytes 1179656 | tf_op jit(solution)/shard_map/ppermute | solution.py:192
  326.6 18.6 %collective-permute-start.48 = (bf16[96,2048]{1,0:T(8,128)(2,1)S(1)}, bf16[96,2048]{1,0:T(8,128)(2,1)}, u32[]{:S(2)}, u32[]{:S(2)}) collective-permute-start(bf16[96,2048]{1,0:T(8,128)(2,1)S(1)} %slice.253), channel_id=1, source_target_pairs={{0,8},{4,12},{8,0},{12,4},{16,24},{20,28},{24,16},{28,20},{1,9},{5... | collective-permute-start | bytes 1179656 | tf_op jit(solution)/shard_map/ppermute | solution.py:192
  329.0 17.4 %collective-permute-start.52 = (bf16[96,2048]{1,0:T(8,128)(2,1)}, bf16[96,2048]{1,0:T(8,128)(2,1)S(1)}, u32[]{:S(2)}, u32[]{:S(2)}) collective-permute-start(bf16[96,2048]{1,0:T(8,128)(2,1)} %add_convert_fusion.7), channel_id=1, source_target_pairs={{0,8},{4,12},{8,0},{12,4},{16,24},{20,28},{24,16},{28,20},{1,9},{5... | collective-permute-start | bytes 1179656 | tf_op jit(solution)/shard_map/ppermute | solution.py:192
  352.0 19.4 %collective-permute-start.55 = (bf16[192,2048]{1,0:T(8,128)(2,1)}, bf16[192,2048]{1,0:T(8,128)(2,1)}, u32[]{:S(2)}, u32[]{:S(2)}) collective-permute-start(bf16[192,2048]{1,0:T(8,128)(2,1)} %fusion.8.refs_0_), channel_id=1, source_target_pairs={{0,16},{4,20},{8,24},{12,28},{16,0},{20,4},{24,8},{28,12},{1,17},{... | collective-permute-start | bytes 2359304 | tf_op jit(solution)/shard_map/ppermute | solution.py:192
  353.4 19.2 %collective-permute-start.54 = (bf16[192,2048]{1,0:T(8,128)(2,1)}, bf16[192,2048]{1,0:T(8,128)(2,1)}, u32[]{:S(2)}, u32[]{:S(2)}) collective-permute-start(bf16[192,2048]{1,0:T(8,128)(2,1)} %fusion.8.refs_0_), channel_id=1, source_target_pairs={{0,8},{4,12},{8,0},{12,4},{16,24},{20,28},{24,16},{28,20},{1,9},{5... | collective-permute-start | bytes 2359304 | tf_op jit(solution)/shard_map/ppermute | solution.py:192
  354.9 173.6 %reduce-scatter.9.cloned.1.call-start = ((), (), s32[]{:S(2)}) async-start(), calls=%async_computation.14 | async-start | bytes 3932160 | tf_op jit(solution)/shard_map/reduce_scatter | solution.py:362
  372.6 14.9 %collective-permute-start.63 = (bf16[768,2048]{1,0:T(8,128)(2,1)}, bf16[768,2048]{1,0:T(8,128)(2,1)S(1)}, u32[]{:S(2)}, u32[]{:S(2)}) collective-permute-start(bf16[768,2048]{1,0:T(8,128)(2,1)} %get-tuple-element.283), channel_id=1, source_target_pairs={{0,4},{4,0},{8,12},{12,8},{16,20},{20,16},{24,28},{28,24},{1,5},{5... | collective-permute-start | bytes 9437192 | tf_op jit(solution)/shard_map/ppermute | solution.py:192
  373.6 11.6 %collective-permute-start.59 = (bf16[96,2048]{1,0:T(8,128)(2,1)S(1)}, bf16[96,2048]{1,0:T(8,128)(2,1)S(1)}, u32[]{:S(2)}, u32[]{:S(2)}) collective-permute-start(bf16[96,2048]{1,0:T(8,128)(2,1)S(1)} %slice.215), channel_id=1, source_target_pairs={{0,8},{4,12},{8,0},{12,4},{16,24},{20,28},{24,16},{28,20},{1,9},{5... | collective-permute-start | bytes 1179656 | tf_op jit(solution)/shard_map/ppermute | solution.py:192
  376.2 11.3 %collective-permute-start.60 = (bf16[96,2048]{1,0:T(8,128)(2,1)S(1)}, bf16[96,2048]{1,0:T(8,128)(2,1)S(1)}, u32[]{:S(2)}, u32[]{:S(2)}) collective-permute-start(bf16[96,2048]{1,0:T(8,128)(2,1)S(1)} %slice.216), channel_id=1, source_target_pairs={{0,16},{4,20},{8,24},{12,28},{16,0},{20,4},{24,8},{28,12},{1,17},{... | collective-permute-start | bytes 1179656 | tf_op jit(solution)/shard_map/ppermute | solution.py:192
  376.8 15.8 %collective-permute-start.57 = (bf16[192,2048]{1,0:T(8,128)(2,1)}, bf16[192,2048]{1,0:T(8,128)(2,1)S(1)}, u32[]{:S(2)}, u32[]{:S(2)}) collective-permute-start(bf16[192,2048]{1,0:T(8,128)(2,1)} %collective-permute-done.54.refs_2_), channel_id=1, source_target_pairs={{0,4},{4,0},{8,12},{12,8},{16,20},{20,16},{24,28},{28,24},{1,5},{5... | collective-permute-start | bytes 2359304 | tf_op jit(solution)/shard_map/ppermute | solution.py:192
  376.8 15.8 %collective-permute-start.58 = (bf16[192,2048]{1,0:T(8,128)(2,1)}, bf16[192,2048]{1,0:T(8,128)(2,1)S(1)}, u32[]{:S(2)}, u32[]{:S(2)}) collective-permute-start(bf16[192,2048]{1,0:T(8,128)(2,1)} %collective-permute-done.55.refs_4_), channel_id=1, source_target_pairs={{0,4},{4,0},{8,12},{12,8},{16,20},{20,16},{24,28},{28,24},{1,5},{5... | collective-permute-start | bytes 2359304 | tf_op jit(solution)/shard_map/ppermute | solution.py:192
  392.7 11.1 %collective-permute-start.65 = (bf16[96,2048]{1,0:T(8,128)(2,1)S(1)}, bf16[96,2048]{1,0:T(8,128)(2,1)S(1)}, u32[]{:S(2)}, u32[]{:S(2)}) collective-permute-start(bf16[96,2048]{1,0:T(8,128)(2,1)S(1)} %get-tuple-element.389), channel_id=1, source_target_pairs={{0,8},{4,12},{8,0},{12,4},{16,24},{20,28},{24,16},{28,20},{1,9},{5... | collective-permute-start | bytes 1179656 | tf_op jit(solution)/shard_map/ppermute | solution.py:192
  394.2 11.0 %collective-permute-start.64 = (bf16[96,2048]{1,0:T(8,128)(2,1)S(1)}, bf16[96,2048]{1,0:T(8,128)(2,1)S(1)}, u32[]{:S(2)}, u32[]{:S(2)}) collective-permute-start(bf16[96,2048]{1,0:T(8,128)(2,1)S(1)} %get-tuple-element.390), channel_id=1, source_target_pairs={{0,16},{4,20},{8,24},{12,28},{16,0},{20,4},{24,8},{28,12},{1,17},{... | collective-permute-start | bytes 1179656 | tf_op jit(solution)/shard_map/ppermute | solution.py:192
  406.1 36.4 %collective-permute-start.66 = (bf16[96,2048]{1,0:T(8,128)(2,1)S(1)}, bf16[96,2048]{1,0:T(8,128)(2,1)}, u32[]{:S(2)}, u32[]{:S(2)}) collective-permute-start(bf16[96,2048]{1,0:T(8,128)(2,1)S(1)} %slice.221), channel_id=1, source_target_pairs={{0,8},{4,12},{8,0},{12,4},{16,24},{20,28},{24,16},{28,20},{1,9},{5... | collective-permute-start | bytes 1179656 | tf_op jit(solution)/shard_map/ppermute | solution.py:192
  406.7 35.7 %collective-permute-start.67 = (bf16[96,2048]{1,0:T(8,128)(2,1)}, bf16[96,2048]{1,0:T(8,128)(2,1)}, u32[]{:S(2)}, u32[]{:S(2)}) collective-permute-start(bf16[96,2048]{1,0:T(8,128)(2,1)} %add_convert_fusion.6), channel_id=1, source_target_pairs={{0,8},{4,12},{8,0},{12,4},{16,24},{20,28},{24,16},{28,20},{1,9},{5... | collective-permute-start | bytes 1179656 | tf_op jit(solution)/shard_map/ppermute | solution.py:192
  408.1 34.4 %collective-permute-start.68 = (bf16[96,2048]{1,0:T(8,128)(2,1)S(1)}, bf16[96,2048]{1,0:T(8,128)(2,1)}, u32[]{:S(2)}, u32[]{:S(2)}) collective-permute-start(bf16[96,2048]{1,0:T(8,128)(2,1)S(1)} %slice.224), channel_id=1, source_target_pairs={{0,16},{4,20},{8,24},{12,28},{16,0},{20,4},{24,8},{28,12},{1,17},{... | collective-permute-start | bytes 1179656 | tf_op jit(solution)/shard_map/ppermute | solution.py:192
  408.8 33.7 %collective-permute-start.69 = (bf16[96,2048]{1,0:T(8,128)(2,1)}, bf16[96,2048]{1,0:T(8,128)(2,1)}, u32[]{:S(2)}, u32[]{:S(2)}) collective-permute-start(bf16[96,2048]{1,0:T(8,128)(2,1)} %add_convert_fusion.5), channel_id=1, source_target_pairs={{0,16},{4,20},{8,24},{12,28},{16,0},{20,4},{24,8},{28,12},{1,17},{... | collective-permute-start | bytes 1179656 | tf_op jit(solution)/shard_map/ppermute | solution.py:192
  450.6 11.3 %collective-permute-start.72 = (bf16[96,1536]{1,0:T(8,128)(2,1)}, bf16[96,1536]{1,0:T(8,128)(2,1)}, u32[]{:S(2)}, u32[]{:S(2)}) collective-permute-start(bf16[96,1536]{1,0:T(8,128)(2,1)} %get-tuple-element.380), channel_id=1, source_target_pairs={{0,8},{4,12},{8,0},{12,4},{16,24},{20,28},{24,16},{28,20},{1,9},{5... | collective-permute-start | bytes 884744 | tf_op jit(solution)/shard_map/ppermute | solution.py:192
  464.1 101.0 %reduce-scatter.11.cloned.1.call-start = ((), (), s32[]{:S(2)}) async-start(), calls=%async_computation.15 | async-start | bytes 1064960 | tf_op jit(solution)/shard_map/reduce_scatter | solution.py:362
  467.2 12.4 %collective-permute-start.75 = (bf16[96,1536]{1,0:T(8,128)(2,1)}, bf16[96,1536]{1,0:T(8,128)(2,1)S(1)}, u32[]{:S(2)}, u32[]{:S(2)}) collective-permute-start(bf16[96,1536]{1,0:T(8,128)(2,1)} %get-tuple-element.340), channel_id=1, source_target_pairs={{0,8},{4,12},{8,0},{12,4},{16,24},{20,28},{24,16},{28,20},{1,9},{5... | collective-permute-start | bytes 884744 | tf_op jit(solution)/shard_map/ppermute | solution.py:192
  468.0 12.8 %collective-permute-start.76 = (bf16[96,1536]{1,0:T(8,128)(2,1)S(1)}, bf16[96,1536]{1,0:T(8,128)(2,1)S(1)}, u32[]{:S(2)}, u32[]{:S(2)}) collective-permute-start(bf16[96,1536]{1,0:T(8,128)(2,1)S(1)} %get-tuple-element.341), channel_id=1, source_target_pairs={{0,16},{4,20},{8,24},{12,28},{16,0},{20,4},{24,8},{28,12},{1,17},{... | collective-permute-start | bytes 884744 | tf_op jit(solution)/shard_map/ppermute | solution.py:192
  490.5 16.1 %collective-permute-start.80 = (bf16[224,1536]{1,0:T(8,128)(2,1)}, bf16[224,1536]{1,0:T(8,128)(2,1)S(1)}, u32[]{:S(2)}, u32[]{:S(2)}) collective-permute-start(bf16[224,1536]{1,0:T(8,128)(2,1)} %get-tuple-element.346.refs_0_), channel_id=1, source_target_pairs={{0,16},{4,20},{8,24},{12,28},{16,0},{20,4},{24,8},{28,12},{1,17},{... | collective-permute-start | bytes 2064392 | tf_op jit(solution)/shard_map/ppermute | solution.py:192
  492.0 17.0 %collective-permute-start.78 = (bf16[224,1536]{1,0:T(8,128)(2,1)}, bf16[224,1536]{1,0:T(8,128)(2,1)S(1)}, u32[]{:S(2)}, u32[]{:S(2)}) collective-permute-start(bf16[224,1536]{1,0:T(8,128)(2,1)} %get-tuple-element.346.refs_0_), channel_id=1, source_target_pairs={{0,8},{4,12},{8,0},{12,4},{16,24},{20,28},{24,16},{28,20},{1,9},{5... | collective-permute-start | bytes 2064392 | tf_op jit(solution)/shard_map/ppermute | solution.py:192
  492.5 28.4 %collective-permute-start.77 = (bf16[224,1536]{1,0:T(8,128)(2,1)}, bf16[224,1536]{1,0:T(8,128)(2,1)S(1)}, u32[]{:S(2)}, u32[]{:S(2)}) collective-permute-start(bf16[224,1536]{1,0:T(8,128)(2,1)} %get-tuple-element.346.refs_0_), channel_id=1, source_target_pairs={{0,4},{4,0},{8,12},{12,8},{16,20},{20,16},{24,28},{28,24},{1,5},{5... | collective-permute-start | bytes 2064392 | tf_op jit(solution)/shard_map/ppermute | solution.py:192
  507.3 13.6 %collective-permute-start.81 = (bf16[224,1536]{1,0:T(8,128)(2,1)S(1)}, bf16[224,1536]{1,0:T(8,128)(2,1)S(1)}, u32[]{:S(2)}, u32[]{:S(2)}) collective-permute-start(bf16[224,1536]{1,0:T(8,128)(2,1)S(1)} %collective-permute-done.80.refs_4_), channel_id=1, source_target_pairs={{0,4},{4,0},{8,12},{12,8},{16,20},{20,16},{24,28},{28,24},{1,5},{5... | collective-permute-start | bytes 2064392 | tf_op jit(solution)/shard_map/ppermute | solution.py:192
  509.1 11.9 %collective-permute-start.79 = (bf16[224,1536]{1,0:T(8,128)(2,1)S(1)}, bf16[224,1536]{1,0:T(8,128)(2,1)S(1)}, u32[]{:S(2)}, u32[]{:S(2)}) collective-permute-start(bf16[224,1536]{1,0:T(8,128)(2,1)S(1)} %collective-permute-done.78.refs_2_), channel_id=1, source_target_pairs={{0,4},{4,0},{8,12},{12,8},{16,20},{20,16},{24,28},{28,24},{1,5},{5... | collective-permute-start | bytes 2064392 | tf_op jit(solution)/shard_map/ppermute | solution.py:192
  509.1 10.5 %collective-permute-start.83 = (bf16[112,1536]{1,0:T(8,128)(2,1)S(1)}, bf16[112,1536]{1,0:T(8,128)(2,1)S(1)}, u32[]{:S(2)}, u32[]{:S(2)}) collective-permute-start(bf16[112,1536]{1,0:T(8,128)(2,1)S(1)} %slice.271), channel_id=1, source_target_pairs={{0,16},{4,20},{8,24},{12,28},{16,0},{20,4},{24,8},{28,12},{1,17},{... | collective-permute-start | bytes 1032200 | tf_op jit(solution)/shard_map/ppermute | solution.py:192
  528.6 25.4 %all-to-all-start.3 = ((bf16[8,2,64,704]{3,2,1,0:T(8,128)(2,1)}), bf16[8,2,64,704]{3,2,1,0:T(8,128)(2,1)}, u32[]{:S(2)}, u32[]{:S(2)}) async-start(bf16[8,2,64,704]{3,2,1,0:T(8,128)(2,1)} %bitcast.71), calls=%async_computation.7 | async-start | bytes 3145728 | tf_op jit(solution)/shard_map/all_to_all | solution.py:372
  (96 other events, 687.8 us)
Sparse Core Ops, SparseCore 0:
  39.5 64.2 all-gather.3
  105.4 113.9 all-gather.5
  221.0 57.3 all-gather.7
  294.3 54.9 reduce-scatter.4
  355.0 108.8 reduce-scatter.6
  466.0 60.7 reduce-scatter.8
  529.1 24.1 reduce-scatter.10

commit v5 on v4

--- a/solution.py
+++ b/solution.py
@@ -80,7 +80,7 @@
     grad_gate_up_term=D_NORMED,
     result_terms=BRANCH_NEAR,
     result_sums=BRANCH_BLOCKS,
-    result_left=BRANCH_ALL,
+    result_left=BACK_TERMS,
     grad_gate_up=BACK_LEFT,
     grad_attention_term=BACK_LEFT,
     grad_attention=FIRST_SUM,
@@ -88,6 +88,9 @@
     attention_weights=PACK_NEAR,
     normed_columns=ACTIVE,
     result_hops=BACK_TERMS,
+    result_late=FIRST_TERMS,
+    layer_output=LAST_NEAR,
+    input_grad=LAST_NEAR,
 )
 BEGIN = dict(
     output=FIRST_PART,
@@ -96,7 +99,7 @@
     grad_gate_up_term=FEED_LEFT,
     result_terms=D_NORMED,
     result_left=BRANCH_NEAR,
-    result_last=FIRST_SUM,
+    result_last=BACK_LOCAL,
     grad_attention_term=BACK_SUMS,
     normed_columns=FEED_BLOCKS,
     feed_stack=HIDDEN,
@@ -297,22 +300,28 @@
     }
 
 
-def last_hops(left):
+def early_hops(left):
     if lax.axis_size("seq") != 8:
         return [flip(parts[0], 2 * k) for k, parts in left.items() if k]
-    return [flip(part, 2) for part in left[1]] + [flip(part, 4) for part in left[2]]
+    return [flip(left[1][0], 2), flip(left[2][0], 4)]
+
+
+def late_hops(left):
+    if lax.axis_size("seq") != 8:
+        return []
+    return [flip(left[1][1], 2), flip(left[2][1], 4)]
 
 
 def hops_sum(left, hops):
     own = left[0][0].astype(F32)
     if lax.axis_size("seq") != 8:
         return sum((hop.astype(F32) for hop in hops), own)
-    x_low, x_high, y_high, y_low = [hop.astype(F32) for hop in hops]
+    x_low, y_high, x_high, y_low = [hop.astype(F32) for hop in hops]
     return own + jnp.concatenate([x_low + y_low, x_high + y_high], axis=0)
 
 
 def scatter_last(left):
-    return hops_sum(left, last_hops(left))
+    return hops_sum(left, early_hops(left) + late_hops(left))
 
 
 def scatter_pairs(even, odd):
@@ -1228,16 +1237,12 @@
     )
     feed_sums = chain.stage(FEED_SUMS, feed_sums)
     feed_left = chain.stage(FEED_LEFT, scatter_relay(feed_sums))
-    chain.add(grad_gate_up_term=gate_up_grad(
-            chain.begin(grad_gate_up_term=feed),
-            (dg_low, du_low),
-            (dg_high, du_high),
-            n_dp,
-            n_seq,
-        ),
-    )
+    grad_gate_up_term = gate_up_grad(
+        chain.begin(grad_gate_up_term=feed), (dg_low, du_low), (dg_high, du_high), n_dp, n_seq
+    )
+    chain.add(grad_gate_up_term=grad_gate_up_term)
+    chain.add(grad_gate_up=scatter_dp(grad_gate_up_term.reshape(-1, hidden_units)))
     d_feed_normed = chain.stage(D_NORMED, scatter_last(feed_left))
-    chain.add(grad_gate_up=scatter_dp(chain.grad_gate_up_term.reshape(-1, hidden_units)))
 
     d_result = cotangent[0].astype(F32)
     d_hidden_norm, grad_feed_gain_term = jax.vjp(rms_norm, hidden, feed_gain_f)[1](d_feed_normed)
@@ -1250,9 +1255,7 @@
     d_branch_blocks, feed_gain_term = chain.stage(BRANCH_BLOCKS, (d_branch_blocks, grad_feed_gain_term.reshape(1, -1))
     )
     chain.add(result_left=scatter_relay(chain.begin(result_left=chain.result_sums)))
-    d_branch_blocks = chain.stage(BRANCH_ALL, d_branch_blocks)
-    result_left = chain.result_left
-    chain.add(result_hops=last_hops(result_left))
+    chain.add(result_hops=early_hops(chain.result_left))
     d_branch, d_query_low, back_even, back_odd = attend_back(
         me_array,
         starts_all,
@@ -1276,6 +1279,7 @@
     back_left = chain.stage(BACK_LEFT, scatter_relay(back_sums))
     back_local = chain.stage(BACK_LOCAL, scatter_last(back_left))
     chain.add(grad_attention=scatter_dp(chain.grad_attention_term.reshape(-1, width)))
+    chain.add(result_late=late_hops(chain.begin(result_last=chain.result_left)))
     load, d_tokens = last_products(
         me_array,
         back_local,
@@ -1289,18 +1293,20 @@
         first_blocks,
     )
     load = chain.stage(FIRST_TERMS, load)
-    near = chain.stage(LAST_NEAR, gather_near(load))
-    d_tokens = after(d_tokens, load)
+    result_left = chain.result_left
+    hops = chain.result_hops + chain.result_late
+    result = hidden + hops_sum(result_left, hops)
+    layer_output = result.astype(BF)[None]
+    chain.add(layer_output=layer_output)
     input_grad = (d_hidden + d_tokens)[None]
     chain.add(input_grad=input_grad)
+    near = chain.stage(LAST_NEAR, gather_near(load))
     loads = chain.stage(LAST_BLOCKS, gather_cores(gather_far(near)))
     first_sum = chain.stage(FIRST_SUM, first_grads(me_array, chain.normed_columns, loads, latent_width)
     )
     gate_up_rows = chain.begin(gate_up_rows=chain.grad_gate_up)
     gate_up_rows = exchange(gate_up_rows.reshape(n_seq, 2, own_rows, -1))
     grad_first = scatter_dp(first_sum).astype(F32)
-    result = hidden + hops_sum(result_left, chain.begin(result_last=chain.result_hops))
-    layer_output = result.astype(BF)[None]
 
     grad_down = chain.grad_down
     grad_attention = chain.grad_attention

time: 586 us -> 575 us (0.981)
  waiting for transfers between devices: 210 us -> 201 us
    ppermute x83, waiting for transfers between devices: 171 us -> 153 us  [flip(): return lax.ppermute(block, 'seq', [(i, i ^ bits) for i in range(n_seq)])]
    all_to_all x5, waiting for transfers between devices: 22.8 us -> 31.7 us  [exchange(): return lax.all_to_all(parts, 'seq', 0, 0)]
  transfers between devices with their start and end apart: 98 -> 98, of which waited for: 48 -> 48; matrix products, arithmetic and copies ran while one was open for 13% -> 13% of each run, Pallas kernels for 27% -> 31%
where the time goes in v5:
time: 575 us; the launch traced here: 567 us
  waiting for transfers between devices  201 us (35%)
  Pallas kernels  174 us (30%)
  starting transfers between devices  86.2 us (15%)
  other arithmetic  40.4 us (7%)
  local copies, waits for them, and re-layouts  39.4 us (7%)
  between operations  15.7 us (3%)
  matrix products  9.76 us (2%)
    ppermute x83, waiting for transfers between devices, flip(): return lax.ppermute(block, 'seq', [(i, i ^ bits) for i in range(n_seq)])  153 us
    ppermute x83, starting transfers between devices, flip(): return lax.ppermute(block, 'seq', [(i, i ^ bits) for i in range(n_seq)])  60.7 us
    pallas_call x1, Pallas kernels, attend_back(): pl.pallas_call(functools.partial(attend_back_kernel, len(blocks), heads,...  32.1 us
    all_to_all x5, waiting for transfers between devices, exchange(): return lax.all_to_all(parts, 'seq', 0, 0)  31.7 us
    pallas_call x2, Pallas kernels, feed_back(): pl.pallas_call(feed_back_kernel, grid=(count,), in_specs=[tokens, units,...  31.4 us
    pallas_call x1, Pallas kernels, attend(): pl.pallas_call(functools.partial(attend_kernel, len(packs), heads, block)...  26.5 us
    pallas_call x1, Pallas kernels, feed_forward(): pl.pallas_call(functools.partial(feed_kernel, len(blocks), block), grid=(...  20.7 us
    all_to_all x5, starting transfers between devices, exchange(): return lax.all_to_all(parts, 'seq', 0, 0)  18.5 us
  transfers between devices with their start and end apart: 98, of which 48 were waited for; matrix products, arithmetic and copies ran while one was open for 13% of the time, Pallas kernels for 31%

profile of v5, /device:TPU:0, one launch (start us, length us, event | category | flops | bytes accessed | tf_op | source)
XLA Modules:
  0.0 566.6 jit_solution(6318393885153876426)
XLA Ops:
  9.6 5.1 collective-permute-start.2
  15.4 1.7 collective-permute-start.4
  18.5 1.7 copy.65
  20.2 3.4 all-to-all-start
  23.8 4.6 collective-permute-done
  28.5 4.3 collective-permute-done.1
  32.9 5.4 all-to-all-done
  39.4 1.6 collective-permute-start.6
  42.8 1.9 reshape.184
  44.8 14.6 %collective-permute-done.6.refs_4_ = bf16[256,1664]{1,0:T(8,128)(2,1)S(1)} collective-permute-done((bf16[256,1664]{1,0:T(8,128)(2,1)S(1)}, bf16[256,1664]{1,0:T(8,128)(2,1)S(1)}, u32[]{:S(2)}, u32[]{:S(2)}) %collective-permute-start.6) | collective-permute-done | bytes 852000 | tf_op jit(solution)/shard_map/ppermute | solution.py:195
  64.3 7.4 %collective-permute-done.10.refs_6_ = bf16[128,1664]{1,0:T(8,128)(2,1)} collective-permute-done((bf16[128,1664]{1,0:T(8,128)(2,1)S(1)}, bf16[128,1664]{1,0:T(8,128)(2,1)}, u32[]{:S(2)}, u32[]{:S(2)}) %collective-permute-start.10) | collective-permute-done | bytes 426016 | tf_op jit(solution)/shard_map/ppermute | solution.py:195
  74.4 4.4 all-to-all-start.1
  81.5 2.8 multiply_sine_fusion
  87.6 6.4 %first_projections.1 = (bf16[192,1536]{1,0:T(8,128)(2,1)}, f32[192,1024]{1,0:T(8,128)}, bf16[8,192,256]{2,1,0:T(8,128)(2,1)}, f32[1,2048]{1,0:T(1,128)}, f32[1,2048]{1,0:T(1,128)}, /*index=5*/f32[1,1024]{1,0:T(1,128)}) custom-call(s32[1]{0:T(128)} %bitcast.1.me_ref, bf16[192,2048]{1,0:T(8,128)(2,1)} %bitcast.60, f32[192,128]{1,0:T(8,128)} %slice.191.cos_ref, ...), custom_call_target="tpu_custom_call" | custom-call | flops 10000000 | bytes 20000 | tf_op jit(solution)/shard_map/first_projections/pallas_call | solution.py:468
  94.0 5.8 %all-to-all-done.1 = bf16[8,2,64,704]{3,2,1,0:T(8,128)(2,1)} async-done(((bf16[8,2,64,704]{3,2,1,0:T(8,128)(2,1)}), bf16[8,2,64,704]{3,2,1,0:T(8,128)(2,1)}, u32[]{:S(2)}, u32[]{:S(2)}) %all-to-all-start.1) | async-done | bytes 1441824 | tf_op jit(solution)/shard_map/all_to_all | solution.py:381
  99.8 4.0 all-gather.4.cloned.1.call-done
  108.4 3.1 slice.243
  113.2 6.2 %collective-permute-done.15.refs_4_ = bf16[192,1536]{1,0:T(8,128)(2,1)S(1)} collective-permute-done((bf16[192,1536]{1,0:T(8,128)(2,1)}, bf16[192,1536]{1,0:T(8,128)(2,1)S(1)}, u32[]{:S(2)}, u32[]{:S(2)}) %collective-permute-start.15) | collective-permute-done | bytes 589856 | tf_op jit(solution)/shard_map/ppermute | solution.py:195
  123.3 5.0 collective-permute-done.19.refs_6_
  133.2 1.8 slice.197
  136.3 26.5 %attend.1 = (bf16[1536,1024]{1,0:T(8,128)(2,1)}, bf16[1536,256]{1,0:T(8,128)(2,1)}, bf16[1536,256]{1,0:T(8,128)(2,1)}, bf16[1536,512]{1,0:T(8,128)(2,1)}, bf16[1...) custom-call(s32[1]{0:T(128)} %bitcast.1.me_ref, ...), custom_call_target="tpu_custom_call" | custom-call | flops 10000000 | bytes 20000 | tf_op jit(solution)/shard_map/attend/pallas_call | solution.py:868
  162.9 5.9 %collective-permute-done.25 = bf16[768,2048]{1,0:T(8,128)(2,1)S(1)} collective-permute-done((bf16[768,2048]{1,0:T(8,128)(2,1)}, bf16[768,2048]{1,0:T(8,128)(2,1)S(1)}, u32[]{:S(2)}, u32[]{:S(2)}) %collective-permute-start.25) | collective-permute-done | bytes 3145760 | tf_op jit(solution)/shard_map/ppermute | solution.py:195
  168.8 3.3 add_convert_fusion.1
  175.7 7.7 %collective-permute-done.29 = bf16[96,2048]{1,0:T(8,128)(2,1)S(1)} collective-permute-done((bf16[96,2048]{1,0:T(8,128)(2,1)S(1)}, bf16[96,2048]{1,0:T(8,128)(2,1)S(1)}, u32[]{:S(2)}, u32[]{:S(2)}) %collective-permute-start.29) | collective-permute-done | bytes 393248 | tf_op jit(solution)/shard_map/ppermute | solution.py:195
  183.4 2.2 collective-permute-done.27
  187.3 5.8 %collective-permute-done.26 = bf16[96,2048]{1,0:T(8,128)(2,1)} collective-permute-done((bf16[96,2048]{1,0:T(8,128)(2,1)S(1)}, bf16[96,2048]{1,0:T(8,128)(2,1)}, u32[]{:S(2)}, u32[]{:S(2)}) %collective-permute-start.26) | collective-permute-done | bytes 393248 | tf_op jit(solution)/shard_map/ppermute | solution.py:195
  197.8 5.6 collective-permute-done.31
  210.0 5.5 stack_blocks.1.d_ref
  215.5 9.9 %collective-permute-done.33.refs_4_ = bf16[192,2048]{1,0:T(8,128)(2,1)} collective-permute-done((bf16[192,2048]{1,0:T(8,128)(2,1)S(1)}, bf16[192,2048]{1,0:T(8,128)(2,1)}, u32[]{:S(2)}, u32[]{:S(2)}) %collective-permute-start.33) | collective-permute-done | bytes 786464 | tf_op jit(solution)/shard_map/ppermute | solution.py:195
  231.4 6.8 %collective-permute-done.42.refs_6_ = bf16[96,2048]{1,0:T(8,128)(2,1)S(1)} collective-permute-done((bf16[96,2048]{1,0:T(8,128)(2,1)S(1)}, bf16[96,2048]{1,0:T(8,128)(2,1)S(1)}, u32[]{:S(2)}, u32[]{:S(2)}) %collective-permute-start.42) | collective-permute-done | bytes 393248 | tf_op jit(solution)/shard_map/ppermute | solution.py:195
  238.2 2.2 collective-permute-done.43.refs_7_
  240.4 1.7 collective-permute-done.45.refs_9_
  243.1 3.5 all-to-all-start.2
  247.0 20.7 %feed_forward.1 = (bf16[1536,2048]{1,0:T(8,128)(2,1)}, bf16[1536,704]{1,0:T(8,128)(2,1)}, bf16[1536,704]{1,0:T(8,128)(2,1)}, bf16[1536,704]{1,0:T(8,128)(2,1)}, ...) custom-call(bf16[192,2048]{1,0:T(8,128)(2,1)} %copy-done.15, bf16[192,2048]{1,0:T(8,128)(2,1)} %copy-done.33, ...), custom_call_target="tpu_custom_call" | custom-call | flops 10000000 | bytes 20000 | tf_op jit(solution)/shard_map/feed_forward/pallas_call | solution.py:529
  267.6 9.8 %convolution_convert_fusion = bf16[704,2048]{1,0:T(8,128)(2,1)} fusion(bf16[1536,704]{1,0:T(8,128)(2,1)} %get-tuple-element.268.left_ref, bf16[1536,2048]{1,0:T(8,128)(2,1)} %stack_blocks.1.d_ref), kind=kOutput, calls=%fused_computation.3 | convolution fusion | flops 4430626816 | bytes 11337728 | tf_op jit(solution)/shard_map/dot_general | solution.py:188
  278.5 15.6 %feed_back.2 = (bf16[768,704]{1,0:T(8,128)(2,1)}, bf16[768,704]{1,0:T(8,128)(2,1)}, bf16[384,2048]{1,0:T(8,128)(2,1)}, bf16[384,2048]{1,0:T(8,128)(2,1)}) custom-call(bf16[1536,2048]{1,0:T(8,128)(2,1)} %stack_blocks.1.d_ref, bf16[1536,704]{1,0:T(8,128)(2,1)} %get-tuple-element.253.silu_ref, bf16[1536,704]{1,0:T(8,128)(2,1)} %get-tuple-element.247.slope_ref, ...), custom_call_target="tpu_custom_call" | custom-call | flops 10000000 | bytes 20000 | tf_op jit(solution)/shard_map/feed_back/pallas_call | solution.py:564
  294.1 15.8 %feed_back.3 = (bf16[768,704]{1,0:T(8,128)(2,1)}, bf16[768,704]{1,0:T(8,128)(2,1)}, bf16[384,2048]{1,0:T(8,128)(2,1)}, bf16[384,2048]{1,0:T(8,128)(2,1)}) custom-call(bf16[1536,2048]{1,0:T(8,128)(2,1)} %stack_blocks.1.d_ref, bf16[1536,704]{1,0:T(8,128)(2,1)} %get-tuple-element.253.silu_ref, bf16[1536,704]{1,0:T(8,128)(2,1)} %get-tuple-element.247.slope_ref, ...), custom_call_target="tpu_custom_call" | custom-call | flops 10000000 | bytes 20000 | tf_op jit(solution)/shard_map/feed_back/pallas_call | solution.py:564
  310.4 2.0 add_convert_fusion.3
  316.1 7.6 %collective-permute-done.49 = bf16[96,2048]{1,0:T(8,128)(2,1)S(1)} collective-permute-done((bf16[96,2048]{1,0:T(8,128)(2,1)S(1)}, bf16[96,2048]{1,0:T(8,128)(2,1)S(1)}, u32[]{:S(2)}, u32[]{:S(2)}) %collective-permute-start.49) | collective-permute-done | bytes 393248 | tf_op jit(solution)/shard_map/ppermute | solution.py:195
  329.6 15.1 %gate_up_grad.1 = bf16[4,8,2,64,704]{4,3,2,1,0:T(8,128)(2,1)} custom-call(bf16[1536,2048]{1,0:T(8,128)(2,1)} %get-tuple-element.262.x_ref, bf16[768,704]{1,0:T(8,128)(2,1)} %get-tuple-element.263.dg_low, bf16[768,704]{1,0:T(8,128)(2,1)} %get-tuple-element.264.du_low, bf16[768,704]{1,0:T(8,128)(2,1)} %get-tuple-element.265.dg_high, ...), custom_call_target="tpu_custom_call" | custom-call | flops 10000000 | bytes 20000 | tf_op jit(solution)/shard_map/gate_up_grad/pallas_call | solution.py:592
  351.6 8.9 %pair_product.1 = (bf16[768,2048]{1,0:T(8,128)(2,1)}, bf16[768,2048]{1,0:T(8,128)(2,1)}) custom-call(bf16[1536,704]{1,0:T(8,128)(2,1)} %get-tuple-element.268.left_ref, bf16[704,2048]{1,0:T(8,128)(2,1)} %all-gather.8.cloned.1.call-done.down_ref.right_ref), custom_call_target="tpu_custom_call" | custom-call | flops 3000000000 | bytes 6000000 | tf_op jit(solution)/shard_map/pair_product/pallas_call | solution.py:616
  360.5 8.2 %collective-permute-done.55.refs_4_ = bf16[192,2048]{1,0:T(8,128)(2,1)} collective-permute-done((bf16[192,2048]{1,0:T(8,128)(2,1)}, bf16[192,2048]{1,0:T(8,128)(2,1)}, u32[]{:S(2)}, u32[]{:S(2)}) %collective-permute-start.55) | collective-permute-done | bytes 786464 | tf_op jit(solution)/shard_map/ppermute | solution.py:195
  373.8 7.8 %collective-permute-done.59.refs_6_ = bf16[96,2048]{1,0:T(8,128)(2,1)S(1)} collective-permute-done((bf16[96,2048]{1,0:T(8,128)(2,1)S(1)}, bf16[96,2048]{1,0:T(8,128)(2,1)S(1)}, u32[]{:S(2)}, u32[]{:S(2)}) %collective-permute-start.59) | collective-permute-done | bytes 393248 | tf_op jit(solution)/shard_map/ppermute | solution.py:195
  383.6 3.2 add_convert_fusion
  393.6 32.1 %attend_back.1 = (bf16[1536,2048]{1,0:T(8,128)(2,1)}, bf16[1536,512]{1,0:T(8,128)(2,1)}, bf16[768,1536]{1,0:T(8,128)(2,1)}, bf16[768,1536]{1,0:T(8,128)(2,1)}) custom-call(s32[1]{0:T(128)} %bitcast.1.me_ref, s32[1,1536]{1,0:T(1,128)} %reshape.187.starts_ref, f32[1536,128]{1,0:T(8,128)} %copy-done.3, f32[1536,128]{1,0:T(8,128)} %copy-done.2, ...), custom_call_target="tpu_custom_call" | custom-call | flops 10000000 | bytes 20000 | tf_op jit(solution)/shard_map/attend_back/pallas_call | solution.py:1008
  425.7 2.1 add_convert_fusion.5
  427.9 2.0 add_convert_fusion.6
  429.8 4.7 collective-permute-done.68
  439.0 10.1 %attention_grads.1 = bf16[4,192,2048]{2,1,0:T(8,128)(2,1)} custom-call(bf16[1536,512]{1,0:T(8,128)(2,1)} %get-tuple-element.216.mixed_ref, bf16[1536,1024]{1,0:T(8,128)(2,1)} %get-tuple-element.303.latent_ref, bf16[1536,512]{1,0:T(8,128)(2,1)} %get-tuple-element.304.dq_ref, bf16[1536,2048]{1,0:T(8,128)(2,1)} %get-tuple-element.305.d_ref), custom_call_target="tpu_custom_call" | custom-call | flops 10000000 | bytes 20000 | tf_op jit(solution)/shard_map/attention_grads/pallas_call | solution.py:1078
  449.1 2.2 add_convert_fusion.11
  451.3 1.9 reduce-scatter.7.cloned.1.call-done
  457.3 6.0 %collective-permute-done.71 = bf16[96,1536]{1,0:T(8,128)(2,1)S(1)} collective-permute-done((bf16[96,1536]{1,0:T(8,128)(2,1)}, bf16[96,1536]{1,0:T(8,128)(2,1)S(1)}, u32[]{:S(2)}, u32[]{:S(2)}) %collective-permute-start.71) | collective-permute-done | bytes 294944 | tf_op jit(solution)/shard_map/ppermute | solution.py:195
  464.9 3.7 collective-permute-done.73
  473.1 8.5 %last_products.1 = (bf16[224,1536]{1,0:T(8,128)(2,1)}, f32[192,2048]{1,0:T(8,128)}) custom-call(s32[1]{0:T(128)} %bitcast.1.me_ref, f32[192,1536]{1,0:T(8,128)} %maximum_add_fusion.3.back_ref, f32[192,1024]{1,0:T(8,128)} %get-tuple-element.311.latent_ref, f32[1,1024]{1,0:T(1,128)} %get-tuple-element.312.query_gain_ref, bf16[192,2048]{1,0:T(8,128)(2,1)} %bitcast.61, ...), custom_call_target="tpu_custom_call" | custom-call | flops 10000000 | bytes 20000 | tf_op jit(solution)/shard_map/last_products/pallas_call | solution.py:697
  486.7 2.4 add_bitcast_fusion
  489.1 8.4 %collective-permute-done.78.refs_4_ = bf16[224,1536]{1,0:T(8,128)(2,1)S(1)} collective-permute-done((bf16[224,1536]{1,0:T(8,128)(2,1)}, bf16[224,1536]{1,0:T(8,128)(2,1)S(1)}, u32[]{:S(2)}, u32[]{:S(2)}) %collective-permute-start.78) | collective-permute-done | bytes 688160 | tf_op jit(solution)/shard_map/ppermute | solution.py:195
  501.5 7.9 %collective-permute-done.82.refs_6_ = bf16[112,1536]{1,0:T(8,128)(2,1)S(1)} collective-permute-done((bf16[112,1536]{1,0:T(8,128)(2,1)S(1)}, bf16[112,1536]{1,0:T(8,128)(2,1)S(1)}, u32[]{:S(2)}, u32[]{:S(2)}) %collective-permute-start.82) | collective-permute-done | bytes 344096 | tf_op jit(solution)/shard_map/ppermute | solution.py:195
  513.0 5.2 first_grads.1
  518.2 3.7 all-to-all-start.3
  524.9 18.0 %all-to-all-done.3.parts_ref = bf16[8,2,64,704]{3,2,1,0:T(8,128)(2,1)S(1)} async-done(((bf16[8,2,64,704]{3,2,1,0:T(8,128)(2,1)}), bf16[8,2,64,704]{3,2,1,0:T(8,128)(2,1)S(1)}, u32[]{:S(2)}, u32[]{:S(2)}) %all-to-all-start.3) | async-done | bytes 1441824 | tf_op jit(solution)/shard_map/all_to_all | solution.py:381
  542.9 3.4 all-to-all-start.4
  547.4 3.2 columns_back.1
  550.7 2.5 all-to-all-done.4
  557.9 1.6 slice.271
  (390 shorter events, 128.6 us)
Async XLA Ops:
  9.6 23.2 %collective-permute-start.2 = (bf16[64,1664]{1,0:T(8,128)(2,1)S(1)}, bf16[64,1664]{1,0:T(8,128)(2,1)S(1)}, u32[]{:S(2)}, u32[]{:S(2)}) collective-permute-start(bf16[64,1664]{1,0:T(8,128)(2,1)S(1)} %fusion.6), channel_id=1, source_target_pairs={{0,3},{1,2},{2,1},{3,0},{4,7},{5,6},{6,5},{7,4},{8,11},{9,10},{10,... | collective-permute-start | bytes 638984 | tf_op jit(solution)/shard_map/ppermute | solution.py:365
  14.7 18.1 %collective-permute-start.1 = (bf16[64,1664]{1,0:T(8,128)(2,1)S(1)}, bf16[64,1664]{1,0:T(8,128)(2,1)S(1)}, u32[]{:S(2)}, u32[]{:S(2)}) collective-permute-start(bf16[64,1664]{1,0:T(8,128)(2,1)S(1)} %fusion.6), channel_id=1, source_target_pairs={{0,2},{1,3},{2,0},{3,1},{4,6},{5,7},{6,4},{7,5},{8,10},{9,11},{10,... | collective-permute-start | bytes 638984 | tf_op jit(solution)/shard_map/ppermute | solution.py:365
  14.7 13.7 %collective-permute-start = (bf16[64,1664]{1,0:T(8,128)(2,1)S(1)}, bf16[64,1664]{1,0:T(8,128)(2,1)S(1)}, u32[]{:S(2)}, u32[]{:S(2)}) collective-permute-start(bf16[64,1664]{1,0:T(8,128)(2,1)S(1)} %fusion.6), channel_id=1, source_target_pairs={{0,1},{1,0},{2,3},{3,2},{4,5},{5,4},{6,7},{7,6},{8,9},{9,8},{10,11... | collective-permute-start | bytes 638984 | tf_op jit(solution)/shard_map/ppermute | solution.py:365
  15.4 22.9 %collective-permute-start.4 = (bf16[192,2048]{1,0:T(8,128)(2,1)}, bf16[192,2048]{1,0:T(8,128)(2,1)}, u32[]{:S(2)}, u32[]{:S(2)}) collective-permute-start(bf16[192,2048]{1,0:T(8,128)(2,1)} %bitcast.62), channel_id=1, source_target_pairs={{0,16},{4,20},{8,24},{12,28},{16,0},{20,4},{24,8},{28,12},{1,17},{... | collective-permute-start | bytes 2359304 | tf_op jit(solution)/shard_map/ppermute | solution.py:195
  17.0 21.3 %collective-permute-start.3 = (bf16[192,2048]{1,0:T(8,128)(2,1)}, bf16[192,2048]{1,0:T(8,128)(2,1)}, u32[]{:S(2)}, u32[]{:S(2)}) collective-permute-start(bf16[192,2048]{1,0:T(8,128)(2,1)} %bitcast.63), channel_id=1, source_target_pairs={{0,8},{4,12},{8,0},{12,4},{16,24},{20,28},{24,16},{28,20},{1,9},{5... | collective-permute-start | bytes 2359304 | tf_op jit(solution)/shard_map/ppermute | solution.py:195
  20.2 18.1 %all-to-all-start = ((bf16[8,32,512]{2,1,0:T(8,128)(2,1)}), bf16[8,32,512]{2,1,0:T(8,128)(2,1)S(1)}, u32[]{:S(2)}, u32[]{:S(2)}) async-start(bf16[8,32,512]{2,1,0:T(8,128)(2,1)} %bitcast.53), calls=%async_computation | async-start | bytes 524288 | tf_op jit(solution)/shard_map/all_to_all | solution.py:381
  23.6 80.2 %all-gather.4.cloned.1.call-start = ((), (), s32[]{:S(2)}) async-start(), calls=%async_computation.9 | async-start | bytes 3932160 | tf_op jit(solution)/shard_map/all_gather | solution.py:355
  39.4 20.0 %collective-permute-start.6 = (bf16[256,1664]{1,0:T(8,128)(2,1)S(1)}, bf16[256,1664]{1,0:T(8,128)(2,1)S(1)}, u32[]{:S(2)}, u32[]{:S(2)}) collective-permute-start(bf16[256,1664]{1,0:T(8,128)(2,1)S(1)} %constant_dynamic-update-slice_fusion.refs_0_), channel_id=1, source_target_pairs={{0,16},{4,20},{8,24},{12,28},{16,0},{20,4},{24,8},{28,12},{1,17},{... | collective-permute-start | bytes 2555912 | tf_op jit(solution)/shard_map/ppermute | solution.py:195
  41.0 19.8 %collective-permute-start.5 = (bf16[256,1664]{1,0:T(8,128)(2,1)S(1)}, bf16[256,1664]{1,0:T(8,128)(2,1)}, u32[]{:S(2)}, u32[]{:S(2)}) collective-permute-start(bf16[256,1664]{1,0:T(8,128)(2,1)S(1)} %constant_dynamic-update-slice_fusion.refs_0_), channel_id=1, source_target_pairs={{0,8},{4,12},{8,0},{12,4},{16,24},{20,28},{24,16},{28,20},{1,9},{5... | collective-permute-start | bytes 2555912 | tf_op jit(solution)/shard_map/ppermute | solution.py:195
  74.4 25.5 %all-to-all-start.1 = ((bf16[8,2,64,704]{3,2,1,0:T(8,128)(2,1)}), bf16[8,2,64,704]{3,2,1,0:T(8,128)(2,1)}, u32[]{:S(2)}, u32[]{:S(2)}) async-start(bf16[8,2,64,704]{3,2,1,0:T(8,128)(2,1)} %copy.58), calls=%async_computation.1 | async-start | bytes 3145728 | tf_op jit(solution)/shard_map/all_to_all | solution.py:381
  78.8 147.8 %all-gather.6.cloned.1.call-start = ((), (), s32[]{:S(2)}) async-start(), calls=%async_computation.10 | async-start | bytes 7864320 | tf_op jit(solution)/shard_map/all_gather | solution.py:355
  103.9 174.6 %all-gather.8.cloned.1.call-start = ((), (), s32[]{:S(2)}) async-start(), calls=%async_computation.11 | async-start | bytes 3604480 | tf_op jit(solution)/shard_map/all_gather | solution.py:355
  104.1 15.3 %collective-permute-start.15 = (bf16[192,1536]{1,0:T(8,128)(2,1)}, bf16[192,1536]{1,0:T(8,128)(2,1)S(1)}, u32[]{:S(2)}, u32[]{:S(2)}) collective-permute-start(bf16[192,1536]{1,0:T(8,128)(2,1)} %get-tuple-element.202.refs_0_), channel_id=1, source_target_pairs={{0,16},{4,20},{8,24},{12,28},{16,0},{20,4},{24,8},{28,12},{1,17},{... | collective-permute-start | bytes 1769480 | tf_op jit(solution)/shard_map/ppermute | solution.py:195
  105.6 15.0 %collective-permute-start.14 = (bf16[192,1536]{1,0:T(8,128)(2,1)}, bf16[192,1536]{1,0:T(8,128)(2,1)S(1)}, u32[]{:S(2)}, u32[]{:S(2)}) collective-permute-start(bf16[192,1536]{1,0:T(8,128)(2,1)} %get-tuple-element.202.refs_0_), channel_id=1, source_target_pairs={{0,8},{4,12},{8,0},{12,4},{16,24},{20,28},{24,16},{28,20},{1,9},{5... | collective-permute-start | bytes 1769480 | tf_op jit(solution)/shard_map/ppermute | solution.py:195
  135.0 27.8 %collective-permute-start.23 = (bf16[96,2048]{1,0:T(8,128)(2,1)}, bf16[96,2048]{1,0:T(8,128)(2,1)S(1)}, u32[]{:S(2)}, u32[]{:S(2)}) collective-permute-start(bf16[96,2048]{1,0:T(8,128)(2,1)} %slice.197), channel_id=1, source_target_pairs={{0,8},{4,12},{8,0},{12,4},{16,24},{20,28},{24,16},{28,20},{1,9},{5... | collective-permute-start | bytes 1179656 | tf_op jit(solution)/shard_map/ppermute | solution.py:195
  135.6 27.2 %collective-permute-start.24 = (bf16[96,2048]{1,0:T(8,128)(2,1)S(1)}, bf16[96,2048]{1,0:T(8,128)(2,1)}, u32[]{:S(2)}, u32[]{:S(2)}) collective-permute-start(bf16[96,2048]{1,0:T(8,128)(2,1)S(1)} %slice.198), channel_id=1, source_target_pairs={{0,16},{4,20},{8,24},{12,28},{16,0},{20,4},{24,8},{28,12},{1,17},{... | collective-permute-start | bytes 1179656 | tf_op jit(solution)/shard_map/ppermute | solution.py:195
  172.2 11.2 %collective-permute-start.29 = (bf16[96,2048]{1,0:T(8,128)(2,1)S(1)}, bf16[96,2048]{1,0:T(8,128)(2,1)S(1)}, u32[]{:S(2)}, u32[]{:S(2)}) collective-permute-start(bf16[96,2048]{1,0:T(8,128)(2,1)S(1)} %get-tuple-element.350), channel_id=1, source_target_pairs={{0,16},{4,20},{8,24},{12,28},{16,0},{20,4},{24,8},{28,12},{1,17},{... | collective-permute-start | bytes 1179656 | tf_op jit(solution)/shard_map/ppermute | solution.py:195
  173.7 12.0 %collective-permute-start.27 = (bf16[96,2048]{1,0:T(8,128)(2,1)S(1)}, bf16[96,2048]{1,0:T(8,128)(2,1)S(1)}, u32[]{:S(2)}, u32[]{:S(2)}) collective-permute-start(bf16[96,2048]{1,0:T(8,128)(2,1)S(1)} %get-tuple-element.351), channel_id=1, source_target_pairs={{0,8},{4,12},{8,0},{12,4},{16,24},{20,28},{24,16},{28,20},{1,9},{5... | collective-permute-start | bytes 1179656 | tf_op jit(solution)/shard_map/ppermute | solution.py:195
  175.1 18.0 %collective-permute-start.26 = (bf16[96,2048]{1,0:T(8,128)(2,1)S(1)}, bf16[96,2048]{1,0:T(8,128)(2,1)}, u32[]{:S(2)}, u32[]{:S(2)}) collective-permute-start(bf16[96,2048]{1,0:T(8,128)(2,1)S(1)} %get-tuple-element.348), channel_id=1, source_target_pairs={{0,8},{4,12},{8,0},{12,4},{16,24},{20,28},{24,16},{28,20},{1,9},{5... | collective-permute-start | bytes 1179656 | tf_op jit(solution)/shard_map/ppermute | solution.py:195
  186.7 19.2 %collective-permute-start.37 = (bf16[96,2048]{1,0:T(8,128)(2,1)S(1)}, bf16[96,2048]{1,0:T(8,128)(2,1)S(1)}, u32[]{:S(2)}, u32[]{:S(2)}) collective-permute-start(bf16[96,2048]{1,0:T(8,128)(2,1)S(1)} %copy-done.46), channel_id=1, source_target_pairs={{0,4},{4,0},{8,12},{12,8},{16,20},{20,16},{24,28},{28,24},{1,5},{5... | collective-permute-start | bytes 1179656 | tf_op jit(solution)/shard_map/ppermute | solution.py:195
  186.7 20.1 %collective-permute-start.38 = (bf16[96,2048]{1,0:T(8,128)(2,1)}, bf16[96,2048]{1,0:T(8,128)(2,1)S(1)}, u32[]{:S(2)}, u32[]{:S(2)}) collective-permute-start(bf16[96,2048]{1,0:T(8,128)(2,1)} %collective-permute-done.24.refs_7_), channel_id=1, source_target_pairs={{0,4},{4,0},{8,12},{12,8},{16,20},{20,16},{24,28},{28,24},{1,5},{5... | collective-permute-start | bytes 1179656 | tf_op jit(solution)/shard_map/ppermute | solution.py:195
  187.2 21.0 %collective-permute-start.34 = (bf16[192,2048]{1,0:T(8,128)(2,1)S(1)}, bf16[192,2048]{1,0:T(8,128)(2,1)S(1)}, u32[]{:S(2)}, u32[]{:S(2)}) collective-permute-start(bf16[192,2048]{1,0:T(8,128)(2,1)S(1)} %bitcast.65), channel_id=1, source_target_pairs={{0,4},{4,0},{8,12},{12,8},{16,20},{20,16},{24,28},{28,24},{1,5},{5... | collective-permute-start | bytes 2359304 | tf_op jit(solution)/shard_map/ppermute | solution.py:195
  205.9 19.6 %collective-permute-start.33 = (bf16[192,2048]{1,0:T(8,128)(2,1)S(1)}, bf16[192,2048]{1,0:T(8,128)(2,1)}, u32[]{:S(2)}, u32[]{:S(2)}) collective-permute-start(bf16[192,2048]{1,0:T(8,128)(2,1)S(1)} %multiply_convert_fusion.refs_0_), channel_id=1, source_target_pairs={{0,16},{4,20},{8,24},{12,28},{16,0},{20,4},{24,8},{28,12},{1,17},{... | collective-permute-start | bytes 2359304 | tf_op jit(solution)/shard_map/ppermute | solution.py:195
  206.8 19.8 %collective-permute-start.32 = (bf16[192,2048]{1,0:T(8,128)(2,1)S(1)}, bf16[192,2048]{1,0:T(8,128)(2,1)}, u32[]{:S(2)}, u32[]{:S(2)}) collective-permute-start(bf16[192,2048]{1,0:T(8,128)(2,1)S(1)} %multiply_convert_fusion.refs_0_), channel_id=1, source_target_pairs={{0,8},{4,12},{8,0},{12,4},{16,24},{20,28},{24,16},{28,20},{1,9},{5... | collective-permute-start | bytes 2359304 | tf_op jit(solution)/shard_map/ppermute | solution.py:195
  227.7 10.5 %collective-permute-start.42 = (bf16[96,2048]{1,0:T(8,128)(2,1)S(1)}, bf16[96,2048]{1,0:T(8,128)(2,1)S(1)}, u32[]{:S(2)}, u32[]{:S(2)}) collective-permute-start(bf16[96,2048]{1,0:T(8,128)(2,1)S(1)} %slice.206), channel_id=1, source_target_pairs={{0,8},{4,12},{8,0},{12,4},{16,24},{20,28},{24,16},{28,20},{1,9},{5... | collective-permute-start | bytes 1179656 | tf_op jit(solution)/shard_map/ppermute | solution.py:195
  230.9 11.2 %collective-permute-start.39 = (bf16[192,2048]{1,0:T(8,128)(2,1)S(1)}, bf16[192,2048]{1,0:T(8,128)(2,1)S(1)}, u32[]{:S(2)}, u32[]{:S(2)}) collective-permute-start(bf16[192,2048]{1,0:T(8,128)(2,1)S(1)} %multiply_convert_fusion.refs_0_), channel_id=1, source_target_pairs={{0,4},{4,0},{8,12},{12,8},{16,20},{20,16},{24,28},{28,24},{1,5},{5... | collective-permute-start | bytes 2359304 | tf_op jit(solution)/shard_map/ppermute | solution.py:195
  230.9 11.3 %collective-permute-start.40 = (bf16[192,2048]{1,0:T(8,128)(2,1)}, bf16[192,2048]{1,0:T(8,128)(2,1)}, u32[]{:S(2)}, u32[]{:S(2)}) collective-permute-start(bf16[192,2048]{1,0:T(8,128)(2,1)} %collective-permute-done.32.refs_2_), channel_id=1, source_target_pairs={{0,4},{4,0},{8,12},{12,8},{16,20},{20,16},{24,28},{28,24},{1,5},{5... | collective-permute-start | bytes 2359304 | tf_op jit(solution)/shard_map/ppermute | solution.py:195
  231.4 10.8 %collective-permute-start.41 = (bf16[192,2048]{1,0:T(8,128)(2,1)}, bf16[192,2048]{1,0:T(8,128)(2,1)}, u32[]{:S(2)}, u32[]{:S(2)}) collective-permute-start(bf16[192,2048]{1,0:T(8,128)(2,1)} %collective-permute-done.33.refs_4_), channel_id=1, source_target_pairs={{0,4},{4,0},{8,12},{12,8},{16,20},{20,16},{24,28},{28,24},{1,5},{5... | collective-permute-start | bytes 2359304 | tf_op jit(solution)/shard_map/ppermute | solution.py:195
  243.1 34.3 %all-to-all-start.2 = ((bf16[8,192,256]{2,1,0:T(8,128)(2,1)}), bf16[8,192,256]{2,1,0:T(8,128)(2,1)S(1)}, u32[]{:S(2)}, u32[]{:S(2)}) async-start(bf16[8,192,256]{2,1,0:T(8,128)(2,1)} %get-tuple-element.244), calls=%async_computation.2 | async-start | bytes 1572864 | tf_op jit(solution)/shard_map/all_to_all | solution.py:381
  246.7 100.9 %reduce-scatter.5.cloned.1.call-start = ((), (), s32[]{:S(2)}) async-start(), calls=%async_computation.12 | async-start | bytes 3604480 | tf_op jit(solution)/shard_map/reduce_scatter | solution.py:371
  277.4 175.7 %reduce-scatter.7.cloned.1.call-start = ((), (), s32[]{:S(2)}) async-start(), calls=%async_computation.13 | async-start | bytes 7864320 | tf_op jit(solution)/shard_map/reduce_scatter | solution.py:371
  294.1 15.9 %collective-permute-start.46 = (bf16[384,2048]{1,0:T(8,128)(2,1)}, bf16[384,2048]{1,0:T(8,128)(2,1)}, u32[]{:S(2)}, u32[]{:S(2)}) collective-permute-start(bf16[384,2048]{1,0:T(8,128)(2,1)} %get-tuple-element.252), channel_id=1, source_target_pairs={{0,4},{4,0},{8,12},{12,8},{16,20},{20,16},{24,28},{28,24},{1,5},{5... | collective-permute-start | bytes 4718600 | tf_op jit(solution)/shard_map/ppermute | solution.py:195
  310.0 15.4 %collective-permute-start.47 = (bf16[384,2048]{1,0:T(8,128)(2,1)}, bf16[384,2048]{1,0:T(8,128)(2,1)S(1)}, u32[]{:S(2)}, u32[]{:S(2)}) collective-permute-start(bf16[384,2048]{1,0:T(8,128)(2,1)} %get-tuple-element.257), channel_id=1, source_target_pairs={{0,4},{4,0},{8,12},{12,8},{16,20},{20,16},{24,28},{28,24},{1,5},{5... | collective-permute-start | bytes 4718600 | tf_op jit(solution)/shard_map/ppermute | solution.py:195
  312.5 11.2 %collective-permute-start.49 = (bf16[96,2048]{1,0:T(8,128)(2,1)S(1)}, bf16[96,2048]{1,0:T(8,128)(2,1)S(1)}, u32[]{:S(2)}, u32[]{:S(2)}) collective-permute-start(bf16[96,2048]{1,0:T(8,128)(2,1)S(1)} %get-tuple-element.362), channel_id=1, source_target_pairs={{0,8},{4,12},{8,0},{12,4},{16,24},{20,28},{24,16},{28,20},{1,9},{5... | collective-permute-start | bytes 1179656 | tf_op jit(solution)/shard_map/ppermute | solution.py:195
  314.1 13.6 %collective-permute-start.51 = (bf16[96,2048]{1,0:T(8,128)(2,1)S(1)}, bf16[96,2048]{1,0:T(8,128)(2,1)S(1)}, u32[]{:S(2)}, u32[]{:S(2)}) collective-permute-start(bf16[96,2048]{1,0:T(8,128)(2,1)S(1)} %get-tuple-element.364), channel_id=1, source_target_pairs={{0,16},{4,20},{8,24},{12,28},{16,0},{20,4},{24,8},{28,12},{1,17},{... | collective-permute-start | bytes 1179656 | tf_op jit(solution)/shard_map/ppermute | solution.py:195
  315.5 30.7 %collective-permute-start.53 = (bf16[96,2048]{1,0:T(8,128)(2,1)S(1)}, bf16[96,2048]{1,0:T(8,128)(2,1)S(1)}, u32[]{:S(2)}, u32[]{:S(2)}) collective-permute-start(bf16[96,2048]{1,0:T(8,128)(2,1)S(1)} %get-tuple-element.363), channel_id=1, source_target_pairs={{0,16},{4,20},{8,24},{12,28},{16,0},{20,4},{24,8},{28,12},{1,17},{... | collective-permute-start | bytes 1179656 | tf_op jit(solution)/shard_map/ppermute | solution.py:195
  323.8 21.1 %collective-permute-start.50 = (bf16[96,2048]{1,0:T(8,128)(2,1)S(1)}, bf16[96,2048]{1,0:T(8,128)(2,1)S(1)}, u32[]{:S(2)}, u32[]{:S(2)}) collective-permute-start(bf16[96,2048]{1,0:T(8,128)(2,1)S(1)} %add_convert_fusion.8), channel_id=1, source_target_pairs={{0,16},{4,20},{8,24},{12,28},{16,0},{20,4},{24,8},{28,12},{1,17},{... | collective-permute-start | bytes 1179656 | tf_op jit(solution)/shard_map/ppermute | solution.py:195
  326.1 18.9 %collective-permute-start.48 = (bf16[96,2048]{1,0:T(8,128)(2,1)S(1)}, bf16[96,2048]{1,0:T(8,128)(2,1)}, u32[]{:S(2)}, u32[]{:S(2)}) collective-permute-start(bf16[96,2048]{1,0:T(8,128)(2,1)S(1)} %slice.253), channel_id=1, source_target_pairs={{0,8},{4,12},{8,0},{12,4},{16,24},{20,28},{24,16},{28,20},{1,9},{5... | collective-permute-start | bytes 1179656 | tf_op jit(solution)/shard_map/ppermute | solution.py:195
  328.5 17.7 %collective-permute-start.52 = (bf16[96,2048]{1,0:T(8,128)(2,1)}, bf16[96,2048]{1,0:T(8,128)(2,1)}, u32[]{:S(2)}, u32[]{:S(2)}) collective-permute-start(bf16[96,2048]{1,0:T(8,128)(2,1)} %add_convert_fusion.7), channel_id=1, source_target_pairs={{0,8},{4,12},{8,0},{12,4},{16,24},{20,28},{24,16},{28,20},{1,9},{5... | collective-permute-start | bytes 1179656 | tf_op jit(solution)/shard_map/ppermute | solution.py:195
  344.7 173.5 %reduce-scatter.9.cloned.1.call-start = ((), (), s32[]{:S(2)}) async-start(), calls=%async_computation.14 | async-start | bytes 3932160 | tf_op jit(solution)/shard_map/reduce_scatter | solution.py:371
  350.4 18.3 %collective-permute-start.55 = (bf16[192,2048]{1,0:T(8,128)(2,1)}, bf16[192,2048]{1,0:T(8,128)(2,1)}, u32[]{:S(2)}, u32[]{:S(2)}) collective-permute-start(bf16[192,2048]{1,0:T(8,128)(2,1)} %fusion.8.refs_0_), channel_id=1, source_target_pairs={{0,16},{4,20},{8,24},{12,28},{16,0},{20,4},{24,8},{28,12},{1,17},{... | collective-permute-start | bytes 2359304 | tf_op jit(solution)/shard_map/ppermute | solution.py:195
  350.7 18.3 %collective-permute-start.54 = (bf16[192,2048]{1,0:T(8,128)(2,1)}, bf16[192,2048]{1,0:T(8,128)(2,1)}, u32[]{:S(2)}, u32[]{:S(2)}) collective-permute-start(bf16[192,2048]{1,0:T(8,128)(2,1)} %fusion.8.refs_0_), channel_id=1, source_target_pairs={{0,8},{4,12},{8,0},{12,4},{16,24},{20,28},{24,16},{28,20},{1,9},{5... | collective-permute-start | bytes 2359304 | tf_op jit(solution)/shard_map/ppermute | solution.py:195
  369.0 14.1 %collective-permute-start.63 = (bf16[768,2048]{1,0:T(8,128)(2,1)}, bf16[768,2048]{1,0:T(8,128)(2,1)S(1)}, u32[]{:S(2)}, u32[]{:S(2)}) collective-permute-start(bf16[768,2048]{1,0:T(8,128)(2,1)} %get-tuple-element.276), channel_id=1, source_target_pairs={{0,4},{4,0},{8,12},{12,8},{16,20},{20,16},{24,28},{28,24},{1,5},{5... | collective-permute-start | bytes 9437192 | tf_op jit(solution)/shard_map/ppermute | solution.py:195
  370.0 11.6 %collective-permute-start.59 = (bf16[96,2048]{1,0:T(8,128)(2,1)S(1)}, bf16[96,2048]{1,0:T(8,128)(2,1)S(1)}, u32[]{:S(2)}, u32[]{:S(2)}) collective-permute-start(bf16[96,2048]{1,0:T(8,128)(2,1)S(1)} %slice.215), channel_id=1, source_target_pairs={{0,8},{4,12},{8,0},{12,4},{16,24},{20,28},{24,16},{28,20},{1,9},{5... | collective-permute-start | bytes 1179656 | tf_op jit(solution)/shard_map/ppermute | solution.py:195
  371.8 11.3 %collective-permute-start.60 = (bf16[96,2048]{1,0:T(8,128)(2,1)S(1)}, bf16[96,2048]{1,0:T(8,128)(2,1)S(1)}, u32[]{:S(2)}, u32[]{:S(2)}) collective-permute-start(bf16[96,2048]{1,0:T(8,128)(2,1)S(1)} %slice.216), channel_id=1, source_target_pairs={{0,16},{4,20},{8,24},{12,28},{16,0},{20,4},{24,8},{28,12},{1,17},{... | collective-permute-start | bytes 1179656 | tf_op jit(solution)/shard_map/ppermute | solution.py:195
  373.3 14.9 %collective-permute-start.57 = (bf16[192,2048]{1,0:T(8,128)(2,1)}, bf16[192,2048]{1,0:T(8,128)(2,1)S(1)}, u32[]{:S(2)}, u32[]{:S(2)}) collective-permute-start(bf16[192,2048]{1,0:T(8,128)(2,1)} %collective-permute-done.54.refs_2_), channel_id=1, source_target_pairs={{0,4},{4,0},{8,12},{12,8},{16,20},{20,16},{24,28},{28,24},{1,5},{5... | collective-permute-start | bytes 2359304 | tf_op jit(solution)/shard_map/ppermute | solution.py:195
  373.3 14.9 %collective-permute-start.58 = (bf16[192,2048]{1,0:T(8,128)(2,1)}, bf16[192,2048]{1,0:T(8,128)(2,1)S(1)}, u32[]{:S(2)}, u32[]{:S(2)}) collective-permute-start(bf16[192,2048]{1,0:T(8,128)(2,1)} %collective-permute-done.55.refs_4_), channel_id=1, source_target_pairs={{0,4},{4,0},{8,12},{12,8},{16,20},{20,16},{24,28},{28,24},{1,5},{5... | collective-permute-start | bytes 2359304 | tf_op jit(solution)/shard_map/ppermute | solution.py:195
  389.3 36.4 %collective-permute-start.65 = (bf16[96,2048]{1,0:T(8,128)(2,1)}, bf16[96,2048]{1,0:T(8,128)(2,1)}, u32[]{:S(2)}, u32[]{:S(2)}) collective-permute-start(bf16[96,2048]{1,0:T(8,128)(2,1)} %get-tuple-element.365), channel_id=1, source_target_pairs={{0,8},{4,12},{8,0},{12,4},{16,24},{20,28},{24,16},{28,20},{1,9},{5... | collective-permute-start | bytes 1179656 | tf_op jit(solution)/shard_map/ppermute | solution.py:195
  390.7 39.1 %collective-permute-start.67 = (bf16[96,2048]{1,0:T(8,128)(2,1)S(1)}, bf16[96,2048]{1,0:T(8,128)(2,1)}, u32[]{:S(2)}, u32[]{:S(2)}) collective-permute-start(bf16[96,2048]{1,0:T(8,128)(2,1)S(1)} %slice.224), channel_id=1, source_target_pairs={{0,16},{4,20},{8,24},{12,28},{16,0},{20,4},{24,8},{28,12},{1,17},{... | collective-permute-start | bytes 1179656 | tf_op jit(solution)/shard_map/ppermute | solution.py:195
  392.3 37.6 %collective-permute-start.66 = (bf16[96,2048]{1,0:T(8,128)(2,1)S(1)}, bf16[96,2048]{1,0:T(8,128)(2,1)}, u32[]{:S(2)}, u32[]{:S(2)}) collective-permute-start(bf16[96,2048]{1,0:T(8,128)(2,1)S(1)} %slice.221), channel_id=1, source_target_pairs={{0,8},{4,12},{8,0},{12,4},{16,24},{20,28},{24,16},{28,20},{1,9},{5... | collective-permute-start | bytes 1179656 | tf_op jit(solution)/shard_map/ppermute | solution.py:195
  393.0 34.8 %collective-permute-start.64 = (bf16[96,2048]{1,0:T(8,128)(2,1)}, bf16[96,2048]{1,0:T(8,128)(2,1)}, u32[]{:S(2)}, u32[]{:S(2)}) collective-permute-start(bf16[96,2048]{1,0:T(8,128)(2,1)} %get-tuple-element.366), channel_id=1, source_target_pairs={{0,16},{4,20},{8,24},{12,28},{16,0},{20,4},{24,8},{28,12},{1,17},{... | collective-permute-start | bytes 1179656 | tf_op jit(solution)/shard_map/ppermute | solution.py:195
  436.2 12.9 %collective-permute-start.70 = (bf16[96,1536]{1,0:T(8,128)(2,1)}, bf16[96,1536]{1,0:T(8,128)(2,1)}, u32[]{:S(2)}, u32[]{:S(2)}) collective-permute-start(bf16[96,1536]{1,0:T(8,128)(2,1)} %get-tuple-element.356), channel_id=1, source_target_pairs={{0,8},{4,12},{8,0},{12,4},{16,24},{20,28},{24,16},{28,20},{1,9},{5... | collective-permute-start | bytes 884744 | tf_op jit(solution)/shard_map/ppermute | solution.py:195
  437.5 11.6 %collective-permute-start.69 = (bf16[96,1536]{1,0:T(8,128)(2,1)S(1)}, bf16[96,1536]{1,0:T(8,128)(2,1)}, u32[]{:S(2)}, u32[]{:S(2)}) collective-permute-start(bf16[96,1536]{1,0:T(8,128)(2,1)S(1)} %get-tuple-element.358), channel_id=1, source_target_pairs={{0,16},{4,20},{8,24},{12,28},{16,0},{20,4},{24,8},{28,12},{1,17},{... | collective-permute-start | bytes 884744 | tf_op jit(solution)/shard_map/ppermute | solution.py:195
  456.2 12.4 %collective-permute-start.73 = (bf16[96,1536]{1,0:T(8,128)(2,1)}, bf16[96,1536]{1,0:T(8,128)(2,1)S(1)}, u32[]{:S(2)}, u32[]{:S(2)}) collective-permute-start(bf16[96,1536]{1,0:T(8,128)(2,1)} %get-tuple-element.309), channel_id=1, source_target_pairs={{0,8},{4,12},{8,0},{12,4},{16,24},{20,28},{24,16},{28,20},{1,9},{5... | collective-permute-start | bytes 884744 | tf_op jit(solution)/shard_map/ppermute | solution.py:195
  456.8 13.0 %collective-permute-start.74 = (bf16[96,1536]{1,0:T(8,128)(2,1)S(1)}, bf16[96,1536]{1,0:T(8,128)(2,1)S(1)}, u32[]{:S(2)}, u32[]{:S(2)}) collective-permute-start(bf16[96,1536]{1,0:T(8,128)(2,1)S(1)} %get-tuple-element.310), channel_id=1, source_target_pairs={{0,16},{4,20},{8,24},{12,28},{16,0},{20,4},{24,8},{28,12},{1,17},{... | collective-permute-start | bytes 884744 | tf_op jit(solution)/shard_map/ppermute | solution.py:195
  471.0 10.5 %collective-permute-start.75 = (bf16[96,2048]{1,0:T(8,128)(2,1)S(1)}, bf16[96,2048]{1,0:T(8,128)(2,1)}, u32[]{:S(2)}, u32[]{:S(2)}) collective-permute-start(bf16[96,2048]{1,0:T(8,128)(2,1)S(1)} %copy-done.54), channel_id=1, source_target_pairs={{0,8},{4,12},{8,0},{12,4},{16,24},{20,28},{24,16},{28,20},{1,9},{5... | collective-permute-start | bytes 1179656 | tf_op jit(solution)/shard_map/ppermute | solution.py:195
  481.6 15.9 %collective-permute-start.78 = (bf16[224,1536]{1,0:T(8,128)(2,1)}, bf16[224,1536]{1,0:T(8,128)(2,1)S(1)}, u32[]{:S(2)}, u32[]{:S(2)}) collective-permute-start(bf16[224,1536]{1,0:T(8,128)(2,1)} %get-tuple-element.326.refs_0_), channel_id=1, source_target_pairs={{0,16},{4,20},{8,24},{12,28},{16,0},{20,4},{24,8},{28,12},{1,17},{... | collective-permute-start | bytes 2064392 | tf_op jit(solution)/shard_map/ppermute | solution.py:195
  482.8 15.0 %collective-permute-start.77 = (bf16[224,1536]{1,0:T(8,128)(2,1)}, bf16[224,1536]{1,0:T(8,128)(2,1)S(1)}, u32[]{:S(2)}, u32[]{:S(2)}) collective-permute-start(bf16[224,1536]{1,0:T(8,128)(2,1)} %get-tuple-element.326.refs_0_), channel_id=1, source_target_pairs={{0,8},{4,12},{8,0},{12,4},{16,24},{20,28},{24,16},{28,20},{1,9},{5... | collective-permute-start | bytes 2064392 | tf_op jit(solution)/shard_map/ppermute | solution.py:195
  498.4 12.3 %collective-permute-start.81 = (bf16[224,1536]{1,0:T(8,128)(2,1)S(1)}, bf16[224,1536]{1,0:T(8,128)(2,1)S(1)}, u32[]{:S(2)}, u32[]{:S(2)}) collective-permute-start(bf16[224,1536]{1,0:T(8,128)(2,1)S(1)} %collective-permute-done.78.refs_4_), channel_id=1, source_target_pairs={{0,4},{4,0},{8,12},{12,8},{16,20},{20,16},{24,28},{28,24},{1,5},{5... | collective-permute-start | bytes 2064392 | tf_op jit(solution)/shard_map/ppermute | solution.py:195
  498.4 12.2 %collective-permute-start.79 = (bf16[224,1536]{1,0:T(8,128)(2,1)S(1)}, bf16[224,1536]{1,0:T(8,128)(2,1)S(1)}, u32[]{:S(2)}, u32[]{:S(2)}) collective-permute-start(bf16[224,1536]{1,0:T(8,128)(2,1)S(1)} %copy-done.37), channel_id=1, source_target_pairs={{0,4},{4,0},{8,12},{12,8},{16,20},{20,16},{24,28},{28,24},{1,5},{5... | collective-permute-start | bytes 2064392 | tf_op jit(solution)/shard_map/ppermute | solution.py:195
  498.9 11.8 %collective-permute-start.80 = (bf16[224,1536]{1,0:T(8,128)(2,1)S(1)}, bf16[224,1536]{1,0:T(8,128)(2,1)S(1)}, u32[]{:S(2)}, u32[]{:S(2)}) collective-permute-start(bf16[224,1536]{1,0:T(8,128)(2,1)S(1)} %collective-permute-done.77.refs_2_), channel_id=1, source_target_pairs={{0,4},{4,0},{8,12},{12,8},{16,20},{20,16},{24,28},{28,24},{1,5},{5... | collective-permute-start | bytes 2064392 | tf_op jit(solution)/shard_map/ppermute | solution.py:195
  498.9 10.5 %collective-permute-start.82 = (bf16[112,1536]{1,0:T(8,128)(2,1)S(1)}, bf16[112,1536]{1,0:T(8,128)(2,1)S(1)}, u32[]{:S(2)}, u32[]{:S(2)}) collective-permute-start(bf16[112,1536]{1,0:T(8,128)(2,1)S(1)} %slice.234), channel_id=1, source_target_pairs={{0,8},{4,12},{8,0},{12,4},{16,24},{20,28},{24,16},{28,20},{1,9},{5... | collective-permute-start | bytes 1032200 | tf_op jit(solution)/shard_map/ppermute | solution.py:195
  518.2 24.7 %all-to-all-start.3 = ((bf16[8,2,64,704]{3,2,1,0:T(8,128)(2,1)}), bf16[8,2,64,704]{3,2,1,0:T(8,128)(2,1)S(1)}, u32[]{:S(2)}, u32[]{:S(2)}) async-start(bf16[8,2,64,704]{3,2,1,0:T(8,128)(2,1)} %bitcast.28), calls=%async_computation.7 | async-start | bytes 3145728 | tf_op jit(solution)/shard_map/all_to_all | solution.py:381
  522.0 32.1 %reduce-scatter.11.cloned.1.call-start = ((), (), s32[]{:S(2)}) async-start(), calls=%async_computation.15 | async-start | bytes 1064960 | tf_op jit(solution)/shard_map/reduce_scatter | solution.py:371
  (107 other events, 721.5 us)
Sparse Core Ops, SparseCore 0:
  39.5 64.2 all-gather.3
  105.4 113.9 all-gather.5
  221.0 57.3 all-gather.7
  280.6 54.8 reduce-scatter.4
  344.9 108.2 reduce-scatter.6
  455.3 60.7 reduce-scatter.8
  525.1 25.1 reduce-scatter.10

commit v6 on v5

--- a/solution.py
+++ b/solution.py
@@ -16,7 +16,7 @@
 NEGATIVE = -1e30
 BF = jnp.bfloat16
 F32 = jnp.float32
-KERNEL_VMEM = 60 * 2**20
+KERNEL_VMEM = 50 * 2**20
 
 
 KERNEL_COST = dict(
@@ -103,7 +103,7 @@
     grad_attention_term=BACK_SUMS,
     normed_columns=FEED_BLOCKS,
     feed_stack=HIDDEN,
-    gate_up_rows=FIRST_SUM,
+    gate_up_rows=LAST_BLOCKS,
 )
 
 

time: 575 us -> 572 us (level)
  local copies, waits for them, and re-layouts: 39.4 us -> 61.7 us
  Pallas kernels: 174 us -> 159 us
  waiting for transfers between devices: 201 us -> 194 us
    unnamed x142 -> x158, local copies, waits for them, and re-layouts: 6.03 us -> 26.1 us
    all_to_all x5, waiting for transfers between devices: 31.7 us -> 24.3 us  [exchange(): return lax.all_to_all(parts, 'seq', 0, 0)]
    reduce_scatter x4, waiting for transfers between devices: 1.88 us -> 8.72 us  [scatter_dp(): return lax.psum_scatter(terms, 'dp', scatter_dimension=0, tiled=True)]
  transfers between devices with their start and end apart: 98 -> 98, of which waited for: 48 -> 50; matrix products, arithmetic and copies ran while one was open for 13% -> 13% of each run, Pallas kernels for 31% -> 28%
where the time goes in v6:
time: 572 us; the launch traced here: 563 us
  waiting for transfers between devices  194 us (34%)
  Pallas kernels  159 us (28%)
  starting transfers between devices  87.4 us (15%)
  local copies, waits for them, and re-layouts  61.7 us (11%)
  other arithmetic  37.6 us (7%)
  between operations  15.8 us (3%)
  matrix products  7.69 us (1%)
    ppermute x83, waiting for transfers between devices, flip(): return lax.ppermute(block, 'seq', [(i, i ^ bits) for i in range(n_seq)])  149 us
    ppermute x83, starting transfers between devices, flip(): return lax.ppermute(block, 'seq', [(i, i ^ bits) for i in range(n_seq)])  61.4 us
    pallas_call x1, Pallas kernels, attend_back(): pl.pallas_call(functools.partial(attend_back_kernel, len(blocks), heads,...  30.9 us
    pallas_call x2, Pallas kernels, feed_back(): pl.pallas_call(feed_back_kernel, grid=(count,), in_specs=[tokens, units,...  30.8 us
    unnamed x158, local copies, waits for them, and re-layouts  26.1 us
    pallas_call x1, Pallas kernels, attend(): pl.pallas_call(functools.partial(attend_kernel, len(packs), heads, block)...  25.3 us
    all_to_all x5, waiting for transfers between devices, exchange(): return lax.all_to_all(parts, 'seq', 0, 0)  24.3 us
    all_to_all x5, starting transfers between devices, exchange(): return lax.all_to_all(parts, 'seq', 0, 0)  19.1 us
  transfers between devices with their start and end apart: 98, of which 50 were waited for; matrix products, arithmetic and copies ran while one was open for 13% of the time, Pallas kernels for 28%

profile of v6, /device:TPU:0, one launch (start us, length us, event | category | flops | bytes accessed | tf_op | source)
XLA Modules:
  0.0 563.4 jit_solution(977213622091495297)
XLA Ops:
  9.6 5.1 collective-permute-start.2
  18.5 1.7 copy.65
  20.2 3.4 all-to-all-start
  25.3 3.1 collective-permute-done
  29.1 3.7 collective-permute-done.1
  33.5 1.7 constant_dynamic-update-slice_fusion.refs_0_
  35.2 3.1 all-to-all-done
  42.9 1.9 reshape.184
  44.9 14.9 %collective-permute-done.6.refs_4_ = bf16[256,1664]{1,0:T(8,128)(2,1)} collective-permute-done((bf16[256,1664]{1,0:T(8,128)(2,1)}, bf16[256,1664]{1,0:T(8,128)(2,1)}, u32[]{:S(2)}, u32[]{:S(2)}) %collective-permute-start.6) | collective-permute-done | bytes 852000 | tf_op jit(solution)/shard_map/ppermute | solution.py:195
  65.5 7.3 %collective-permute-done.10.refs_6_ = bf16[128,1664]{1,0:T(8,128)(2,1)S(1)} collective-permute-done((bf16[128,1664]{1,0:T(8,128)(2,1)S(1)}, bf16[128,1664]{1,0:T(8,128)(2,1)S(1)}, u32[]{:S(2)}, u32[]{:S(2)}) %collective-permute-start.10) | collective-permute-done | bytes 426016 | tf_op jit(solution)/shard_map/ppermute | solution.py:195
  75.2 4.4 all-to-all-start.1
  81.8 2.8 multiply_sine_fusion
  86.5 4.7 first_projections.1
  95.5 5.2 all-to-all-done.1
  100.7 3.2 all-gather.4.cloned.1.call-done
  108.7 3.2 slice.243
  113.3 2.4 copy.59
  115.7 3.9 collective-permute-done.15.refs_4_
  124.4 5.0 collective-permute-done.19.refs_6_
  133.6 25.3 %attend.1 = (bf16[1536,1024]{1,0:T(8,128)(2,1)}, bf16[1536,256]{1,0:T(8,128)(2,1)}, bf16[1536,256]{1,0:T(8,128)(2,1)}, bf16[1536,512]{1,0:T(8,128)(2,1)}, bf16[1...) custom-call(s32[1]{0:T(128)} %bitcast.1.me_ref, ...), custom_call_target="tpu_custom_call" | custom-call | flops 10000000 | bytes 20000 | tf_op jit(solution)/shard_map/attend/pallas_call | solution.py:868
  159.0 5.9 %collective-permute-done.25 = bf16[768,2048]{1,0:T(8,128)(2,1)S(1)} collective-permute-done((bf16[768,2048]{1,0:T(8,128)(2,1)}, bf16[768,2048]{1,0:T(8,128)(2,1)S(1)}, u32[]{:S(2)}, u32[]{:S(2)}) %collective-permute-start.25) | collective-permute-done | bytes 3145760 | tf_op jit(solution)/shard_map/ppermute | solution.py:195
  164.9 3.2 add_convert_fusion.1
  172.6 7.7 %collective-permute-done.29 = bf16[96,2048]{1,0:T(8,128)(2,1)S(1)} collective-permute-done((bf16[96,2048]{1,0:T(8,128)(2,1)S(1)}, bf16[96,2048]{1,0:T(8,128)(2,1)S(1)}, u32[]{:S(2)}, u32[]{:S(2)}) %collective-permute-start.29) | collective-permute-done | bytes 393248 | tf_op jit(solution)/shard_map/ppermute | solution.py:195
  180.3 2.3 collective-permute-done.27
  184.9 5.1 collective-permute-done.26
  190.5 2.9 collective-permute-done.28
  196.1 5.0 collective-permute-done.31
  207.3 3.8 stack_blocks.1.d_ref
  211.1 12.3 %collective-permute-done.33.refs_4_ = bf16[192,2048]{1,0:T(8,128)(2,1)S(1)} collective-permute-done((bf16[192,2048]{1,0:T(8,128)(2,1)S(1)}, bf16[192,2048]{1,0:T(8,128)(2,1)S(1)}, u32[]{:S(2)}, u32[]{:S(2)}) %collective-permute-start.33) | collective-permute-done | bytes 786464 | tf_op jit(solution)/shard_map/ppermute | solution.py:195
  228.3 7.8 %collective-permute-done.42.refs_6_ = bf16[96,2048]{1,0:T(8,128)(2,1)S(1)} collective-permute-done((bf16[96,2048]{1,0:T(8,128)(2,1)S(1)}, bf16[96,2048]{1,0:T(8,128)(2,1)S(1)}, u32[]{:S(2)}, u32[]{:S(2)}) %collective-permute-start.42) | collective-permute-done | bytes 393248 | tf_op jit(solution)/shard_map/ppermute | solution.py:195
  241.6 4.2 all-to-all-start.2
  249.9 18.5 %feed_forward.1 = (bf16[1536,2048]{1,0:T(8,128)(2,1)}, bf16[1536,704]{1,0:T(8,128)(2,1)}, bf16[1536,704]{1,0:T(8,128)(2,1)}, bf16[1536,704]{1,0:T(8,128)(2,1)}, ...) custom-call(bf16[192,2048]{1,0:T(8,128)(2,1)S(1)} %multiply_convert_fusion.refs_0_, ...), custom_call_target="tpu_custom_call" | custom-call | flops 10000000 | bytes 20000 | tf_op jit(solution)/shard_map/feed_forward/pallas_call | solution.py:529
  268.4 7.7 %convolution_convert_fusion = bf16[704,2048]{1,0:T(8,128)(2,1)} fusion(bf16[1536,704]{1,0:T(8,128)(2,1)} %get-tuple-element.268.left_ref, bf16[1536,2048]{1,0:T(8,128)(2,1)S(1)} %copy-done.43), kind=kOutput, calls=%fused_computation.3 | convolution fusion | flops 4430626816 | bytes 11337728 | tf_op jit(solution)/shard_map/dot_general | solution.py:188
  276.4 2.1 all-gather.8.cloned.1.call-done.down_ref.right_ref
  278.5 15.4 %feed_back.2 = (bf16[768,704]{1,0:T(8,128)(2,1)S(1)}, bf16[768,704]{1,0:T(8,128)(2,1)S(1)}, bf16[384,2048]{1,0:T(8,128)(2,1)S(1)}, bf16[384,2048]{1,0:T(8,128)(2,1)}) custom-call(bf16[1536,2048]{1,0:T(8,128)(2,1)} %stack_blocks.1.d_ref, bf16[1536,704]{1,0:T(8,128)(2,1)} %get-tuple-element.253.silu_ref, bf16[1536,704]{1,0:T(8,128)(2,1)} %get-tuple-element.247.slope_ref, ...), custom_call_target="tpu_custom_call" | custom-call | flops 10000000 | bytes 20000 | tf_op jit(solution)/shard_map/feed_back/pallas_call | solution.py:564
  294.9 15.4 %feed_back.3 = (bf16[768,704]{1,0:T(8,128)(2,1)S(1)}, bf16[768,704]{1,0:T(8,128)(2,1)S(1)}, bf16[384,2048]{1,0:T(8,128)(2,1)S(1)}, bf16[384,2048]{1,0:T(8,128)(2,1)}) custom-call(bf16[1536,2048]{1,0:T(8,128)(2,1)} %stack_blocks.1.d_ref, bf16[1536,704]{1,0:T(8,128)(2,1)} %get-tuple-element.253.silu_ref, bf16[1536,704]{1,0:T(8,128)(2,1)} %get-tuple-element.247.slope_ref, ...), custom_call_target="tpu_custom_call" | custom-call | flops 10000000 | bytes 20000 | tf_op jit(solution)/shard_map/feed_back/pallas_call | solution.py:564
  315.1 7.5 %collective-permute-done.49 = bf16[96,2048]{1,0:T(8,128)(2,1)S(1)} collective-permute-done((bf16[96,2048]{1,0:T(8,128)(2,1)S(1)}, bf16[96,2048]{1,0:T(8,128)(2,1)S(1)}, u32[]{:S(2)}, u32[]{:S(2)}) %collective-permute-start.49) | collective-permute-done | bytes 393248 | tf_op jit(solution)/shard_map/ppermute | solution.py:195
  329.3 13.9 %gate_up_grad.1 = bf16[4,8,2,64,704]{4,3,2,1,0:T(8,128)(2,1)} custom-call(bf16[1536,2048]{1,0:T(8,128)(2,1)} %get-tuple-element.262.x_ref, bf16[768,704]{1,0:T(8,128)(2,1)S(1)} %get-tuple-element.263.dg_low, bf16[768,704]{1,0:T(8,128)(2,1)S(1)} %get-tuple-element.264.du_low, bf16[768,704]{1,0:T(8,128)(2,1)S(1)} %get-tuple-element.265.dg_high, ...), custom_call_target="tpu_custom_call" | custom-call | flops 10000000 | bytes 20000 | tf_op jit(solution)/shard_map/gate_up_grad/pallas_call | solution.py:592
  347.6 2.7 multiply_reduce_fusion
  354.1 8.5 %pair_product.1 = (bf16[768,2048]{1,0:T(8,128)(2,1)}, bf16[768,2048]{1,0:T(8,128)(2,1)}) custom-call(bf16[1536,704]{1,0:T(8,128)(2,1)S(1)} %copy-done.42, bf16[704,2048]{1,0:T(8,128)(2,1)} %all-gather.8.cloned.1.call-done.down_ref.right_ref), custom_call_target="tpu_custom_call" | custom-call | flops 3000000000 | bytes 6000000 | tf_op jit(solution)/shard_map/pair_product/pallas_call | solution.py:616
  362.6 7.0 %collective-permute-done.55.refs_4_ = bf16[192,2048]{1,0:T(8,128)(2,1)S(1)} collective-permute-done((bf16[192,2048]{1,0:T(8,128)(2,1)S(1)}, bf16[192,2048]{1,0:T(8,128)(2,1)S(1)}, u32[]{:S(2)}, u32[]{:S(2)}) %collective-permute-start.55) | collective-permute-done | bytes 786464 | tf_op jit(solution)/shard_map/ppermute | solution.py:195
  372.2 1.7 collective-permute-start.60
  374.4 7.0 %collective-permute-done.59.refs_6_ = bf16[96,2048]{1,0:T(8,128)(2,1)S(1)} collective-permute-done((bf16[96,2048]{1,0:T(8,128)(2,1)S(1)}, bf16[96,2048]{1,0:T(8,128)(2,1)S(1)}, u32[]{:S(2)}, u32[]{:S(2)}) %collective-permute-start.59) | collective-permute-done | bytes 393248 | tf_op jit(solution)/shard_map/ppermute | solution.py:195
  381.4 2.1 collective-permute-done.60.refs_7_
  384.0 3.2 add_convert_fusion
  390.0 1.7 collective-permute-start.67
  393.0 30.9 %attend_back.1 = (bf16[1536,2048]{1,0:T(8,128)(2,1)}, bf16[1536,512]{1,0:T(8,128)(2,1)}, bf16[768,1536]{1,0:T(8,128)(2,1)}, bf16[768,1536]{1,0:T(8,128)(2,1)}) custom-call(s32[1]{0:T(128)} %bitcast.1.me_ref, s32[1,1536]{1,0:T(1,128)S(1)} %reshape.187.starts_ref, f32[1536,128]{1,0:T(8,128)S(1)} %copy-done.3, f32[1536,128]{1,0:T(8,128)S(1)} %copy-done.1, ...), custom_call_target="tpu_custom_call" | custom-call | flops 10000000 | bytes 20000 | tf_op jit(solution)/shard_map/attend_back/pallas_call | solution.py:1008
  425.0 4.0 collective-permute-done.68
  433.1 9.2 %attention_grads.1 = bf16[4,192,2048]{2,1,0:T(8,128)(2,1)} custom-call(bf16[1536,512]{1,0:T(8,128)(2,1)S(1)} %copy-done.5, bf16[1536,1024]{1,0:T(8,128)(2,1)} %get-tuple-element.303.latent_ref, bf16[1536,512]{1,0:T(8,128)(2,1)S(1)} %copy-done.14, bf16[1536,2048]{1,0:T(8,128)(2,1)} %get-tuple-element.305.d_ref), custom_call_target="tpu_custom_call" | custom-call | flops 10000000 | bytes 20000 | tf_op jit(solution)/shard_map/attention_grads/pallas_call | solution.py:1078
  443.2 8.7 %reduce-scatter.7.cloned.1.call-done = bf16[1024,704]{1,0:T(8,128)(2,1)} async-done(((bf16[4096,704]{1,0:T(8,128)(2,1)}), bf16[1024,704]{1,0:T(8,128)(2,1)}) %reduce-scatter.7.cloned.1.call-update) | async-done | bytes 1441808 | tf_op jit(solution)/shard_map/reduce_scatter | solution.py:371
  456.1 5.8 %collective-permute-done.71 = bf16[96,1536]{1,0:T(8,128)(2,1)S(1)} collective-permute-done((bf16[96,1536]{1,0:T(8,128)(2,1)S(1)}, bf16[96,1536]{1,0:T(8,128)(2,1)S(1)}, u32[]{:S(2)}, u32[]{:S(2)}) %collective-permute-start.71) | collective-permute-done | bytes 294944 | tf_op jit(solution)/shard_map/ppermute | solution.py:195
  463.5 3.7 collective-permute-done.73
  471.7 7.6 %last_products.1 = (bf16[224,1536]{1,0:T(8,128)(2,1)S(1)}, f32[192,2048]{1,0:T(8,128)}) custom-call(s32[1]{0:T(128)} %bitcast.1.me_ref, f32[192,1536]{1,0:T(8,128)} %maximum_add_fusion.3.back_ref, f32[192,1024]{1,0:T(8,128)S(1)} %copy-done.18, f32[1,1024]{1,0:T(1,128)S(1)} %get-tuple-element.312.query_gain_ref, bf16[192,2048]{1,0:T(8,128)(2,1)} %bitcast.70, ...), custom_call_target="tpu_custom_call" | custom-call | flops 10000000 | bytes 20000 | tf_op jit(solution)/shard_map/last_products/pallas_call | solution.py:697
  482.9 3.8 add_bitcast_fusion
  486.8 8.3 %collective-permute-done.78.refs_4_ = bf16[224,1536]{1,0:T(8,128)(2,1)S(1)} collective-permute-done((bf16[224,1536]{1,0:T(8,128)(2,1)S(1)}, bf16[224,1536]{1,0:T(8,128)(2,1)S(1)}, u32[]{:S(2)}, u32[]{:S(2)}) %collective-permute-start.78) | collective-permute-done | bytes 688160 | tf_op jit(solution)/shard_map/ppermute | solution.py:195
  499.0 7.9 %collective-permute-done.82.refs_6_ = bf16[112,1536]{1,0:T(8,128)(2,1)S(1)} collective-permute-done((bf16[112,1536]{1,0:T(8,128)(2,1)S(1)}, bf16[112,1536]{1,0:T(8,128)(2,1)S(1)}, u32[]{:S(2)}, u32[]{:S(2)}) %collective-permute-start.82) | collective-permute-done | bytes 344096 | tf_op jit(solution)/shard_map/ppermute | solution.py:195
  506.9 1.8 collective-permute-done.83.refs_7_
  512.2 3.6 all-to-all-start.3
  519.9 4.2 first_grads.1
  524.1 2.4 convert_element_type.296
  526.4 10.3 %all-to-all-done.3.parts_ref = bf16[8,2,64,704]{3,2,1,0:T(8,128)(2,1)S(1)} async-done(((bf16[8,2,64,704]{3,2,1,0:T(8,128)(2,1)}), bf16[8,2,64,704]{3,2,1,0:T(8,128)(2,1)S(1)}, u32[]{:S(2)}, u32[]{:S(2)}) %all-to-all-start.3) | async-done | bytes 1441824 | tf_op jit(solution)/shard_map/all_to_all | solution.py:381
  536.7 1.8 columns_back.1
  539.5 3.4 all-to-all-start.4
  544.0 5.8 %all-to-all-done.4 = bf16[8,32,512]{2,1,0:T(8,128)(2,1)S(1)} async-done(((bf16[8,32,512]{2,1,0:T(8,128)(2,1)}), bf16[8,32,512]{2,1,0:T(8,128)(2,1)S(1)}, u32[]{:S(2)}, u32[]{:S(2)}) %all-to-all-start.4) | async-done | bytes 262176 | tf_op jit(solution)/shard_map/all_to_all | solution.py:381
  (406 shorter events, 143.9 us)
Async XLA Ops:
  9.6 23.9 %collective-permute-start.2 = (bf16[64,1664]{1,0:T(8,128)(2,1)S(1)}, bf16[64,1664]{1,0:T(8,128)(2,1)}, u32[]{:S(2)}, u32[]{:S(2)}) collective-permute-start(bf16[64,1664]{1,0:T(8,128)(2,1)S(1)} %fusion.6), channel_id=1, source_target_pairs={{0,3},{1,2},{2,1},{3,0},{4,7},{5,6},{6,5},{7,4},{8,11},{9,10},{10,... | collective-permute-start | bytes 638984 | tf_op jit(solution)/shard_map/ppermute | solution.py:365
  14.7 18.1 %collective-permute-start.1 = (bf16[64,1664]{1,0:T(8,128)(2,1)S(1)}, bf16[64,1664]{1,0:T(8,128)(2,1)S(1)}, u32[]{:S(2)}, u32[]{:S(2)}) collective-permute-start(bf16[64,1664]{1,0:T(8,128)(2,1)S(1)} %fusion.6), channel_id=1, source_target_pairs={{0,2},{1,3},{2,0},{3,1},{4,6},{5,7},{6,4},{7,5},{8,10},{9,11},{10,... | collective-permute-start | bytes 638984 | tf_op jit(solution)/shard_map/ppermute | solution.py:365
  14.7 13.7 %collective-permute-start = (bf16[64,1664]{1,0:T(8,128)(2,1)S(1)}, bf16[64,1664]{1,0:T(8,128)(2,1)S(1)}, u32[]{:S(2)}, u32[]{:S(2)}) collective-permute-start(bf16[64,1664]{1,0:T(8,128)(2,1)S(1)} %fusion.6), channel_id=1, source_target_pairs={{0,1},{1,0},{2,3},{3,2},{4,5},{5,4},{6,7},{7,6},{8,9},{9,8},{10,11... | collective-permute-start | bytes 638984 | tf_op jit(solution)/shard_map/ppermute | solution.py:365
  15.4 22.9 %collective-permute-start.4 = (bf16[192,2048]{1,0:T(8,128)(2,1)}, bf16[192,2048]{1,0:T(8,128)(2,1)S(1)}, u32[]{:S(2)}, u32[]{:S(2)}) collective-permute-start(bf16[192,2048]{1,0:T(8,128)(2,1)} %bitcast.54), channel_id=1, source_target_pairs={{0,16},{4,20},{8,24},{12,28},{16,0},{20,4},{24,8},{28,12},{1,17},{... | collective-permute-start | bytes 2359304 | tf_op jit(solution)/shard_map/ppermute | solution.py:195
  17.0 21.3 %collective-permute-start.3 = (bf16[192,2048]{1,0:T(8,128)(2,1)}, bf16[192,2048]{1,0:T(8,128)(2,1)S(1)}, u32[]{:S(2)}, u32[]{:S(2)}) collective-permute-start(bf16[192,2048]{1,0:T(8,128)(2,1)} %bitcast.55), channel_id=1, source_target_pairs={{0,8},{4,12},{8,0},{12,4},{16,24},{20,28},{24,16},{28,20},{1,9},{5... | collective-permute-start | bytes 2359304 | tf_op jit(solution)/shard_map/ppermute | solution.py:195
  20.2 18.1 %all-to-all-start = ((bf16[8,32,512]{2,1,0:T(8,128)(2,1)}), bf16[8,32,512]{2,1,0:T(8,128)(2,1)S(1)}, u32[]{:S(2)}, u32[]{:S(2)}) async-start(bf16[8,32,512]{2,1,0:T(8,128)(2,1)} %bitcast.53), calls=%async_computation | async-start | bytes 524288 | tf_op jit(solution)/shard_map/all_to_all | solution.py:381
  23.6 80.2 %all-gather.4.cloned.1.call-start = ((), (), s32[]{:S(2)}) async-start(), calls=%async_computation.9 | async-start | bytes 3932160 | tf_op jit(solution)/shard_map/all_gather | solution.py:355
  39.4 20.4 %collective-permute-start.6 = (bf16[256,1664]{1,0:T(8,128)(2,1)}, bf16[256,1664]{1,0:T(8,128)(2,1)}, u32[]{:S(2)}, u32[]{:S(2)}) collective-permute-start(bf16[256,1664]{1,0:T(8,128)(2,1)} %constant_dynamic-update-slice_fusion.refs_0_), channel_id=1, source_target_pairs={{0,16},{4,20},{8,24},{12,28},{16,0},{20,4},{24,8},{28,12},{1,17},{... | collective-permute-start | bytes 2555912 | tf_op jit(solution)/shard_map/ppermute | solution.py:195
  41.1 20.0 %collective-permute-start.5 = (bf16[256,1664]{1,0:T(8,128)(2,1)}, bf16[256,1664]{1,0:T(8,128)(2,1)}, u32[]{:S(2)}, u32[]{:S(2)}) collective-permute-start(bf16[256,1664]{1,0:T(8,128)(2,1)} %constant_dynamic-update-slice_fusion.refs_0_), channel_id=1, source_target_pairs={{0,8},{4,12},{8,0},{12,4},{16,24},{20,28},{24,16},{28,20},{1,9},{5... | collective-permute-start | bytes 2555912 | tf_op jit(solution)/shard_map/ppermute | solution.py:195
  75.2 25.5 %all-to-all-start.1 = ((bf16[8,2,64,704]{3,2,1,0:T(8,128)(2,1)}), bf16[8,2,64,704]{3,2,1,0:T(8,128)(2,1)}, u32[]{:S(2)}, u32[]{:S(2)}) async-start(bf16[8,2,64,704]{3,2,1,0:T(8,128)(2,1)} %copy.58), calls=%async_computation.1 | async-start | bytes 3145728 | tf_op jit(solution)/shard_map/all_to_all | solution.py:381
  79.7 144.6 %all-gather.6.cloned.1.call-start = ((), (), s32[]{:S(2)}) async-start(), calls=%async_computation.10 | async-start | bytes 7864320 | tf_op jit(solution)/shard_map/all_gather | solution.py:355
  103.9 174.6 %all-gather.8.cloned.1.call-start = ((), (), s32[]{:S(2)}) async-start(), calls=%async_computation.11 | async-start | bytes 3604480 | tf_op jit(solution)/shard_map/all_gather | solution.py:355
  104.4 15.2 %collective-permute-start.15 = (bf16[192,1536]{1,0:T(8,128)(2,1)S(1)}, bf16[192,1536]{1,0:T(8,128)(2,1)}, u32[]{:S(2)}, u32[]{:S(2)}) collective-permute-start(bf16[192,1536]{1,0:T(8,128)(2,1)S(1)} %copy-done.23), channel_id=1, source_target_pairs={{0,16},{4,20},{8,24},{12,28},{16,0},{20,4},{24,8},{28,12},{1,17},{... | collective-permute-start | bytes 1769480 | tf_op jit(solution)/shard_map/ppermute | solution.py:195
  106.0 14.7 %collective-permute-start.14 = (bf16[192,1536]{1,0:T(8,128)(2,1)S(1)}, bf16[192,1536]{1,0:T(8,128)(2,1)S(1)}, u32[]{:S(2)}, u32[]{:S(2)}) collective-permute-start(bf16[192,1536]{1,0:T(8,128)(2,1)S(1)} %copy-done.23), channel_id=1, source_target_pairs={{0,8},{4,12},{8,0},{12,4},{16,24},{20,28},{24,16},{28,20},{1,9},{5... | collective-permute-start | bytes 1769480 | tf_op jit(solution)/shard_map/ppermute | solution.py:195
  132.3 26.6 %collective-permute-start.23 = (bf16[96,2048]{1,0:T(8,128)(2,1)S(1)}, bf16[96,2048]{1,0:T(8,128)(2,1)S(1)}, u32[]{:S(2)}, u32[]{:S(2)}) collective-permute-start(bf16[96,2048]{1,0:T(8,128)(2,1)S(1)} %slice.197), channel_id=1, source_target_pairs={{0,8},{4,12},{8,0},{12,4},{16,24},{20,28},{24,16},{28,20},{1,9},{5... | collective-permute-start | bytes 1179656 | tf_op jit(solution)/shard_map/ppermute | solution.py:195
  133.0 25.9 %collective-permute-start.24 = (bf16[96,2048]{1,0:T(8,128)(2,1)S(1)}, bf16[96,2048]{1,0:T(8,128)(2,1)S(1)}, u32[]{:S(2)}, u32[]{:S(2)}) collective-permute-start(bf16[96,2048]{1,0:T(8,128)(2,1)S(1)} %slice.198), channel_id=1, source_target_pairs={{0,16},{4,20},{8,24},{12,28},{16,0},{20,4},{24,8},{28,12},{1,17},{... | collective-permute-start | bytes 1179656 | tf_op jit(solution)/shard_map/ppermute | solution.py:195
  169.1 11.2 %collective-permute-start.29 = (bf16[96,2048]{1,0:T(8,128)(2,1)S(1)}, bf16[96,2048]{1,0:T(8,128)(2,1)S(1)}, u32[]{:S(2)}, u32[]{:S(2)}) collective-permute-start(bf16[96,2048]{1,0:T(8,128)(2,1)S(1)} %get-tuple-element.350), channel_id=1, source_target_pairs={{0,16},{4,20},{8,24},{12,28},{16,0},{20,4},{24,8},{28,12},{1,17},{... | collective-permute-start | bytes 1179656 | tf_op jit(solution)/shard_map/ppermute | solution.py:195
  170.6 12.0 %collective-permute-start.27 = (bf16[96,2048]{1,0:T(8,128)(2,1)S(1)}, bf16[96,2048]{1,0:T(8,128)(2,1)S(1)}, u32[]{:S(2)}, u32[]{:S(2)}) collective-permute-start(bf16[96,2048]{1,0:T(8,128)(2,1)S(1)} %get-tuple-element.351), channel_id=1, source_target_pairs={{0,8},{4,12},{8,0},{12,4},{16,24},{20,28},{24,16},{28,20},{1,9},{5... | collective-permute-start | bytes 1179656 | tf_op jit(solution)/shard_map/ppermute | solution.py:195
  172.0 18.0 %collective-permute-start.26 = (bf16[96,2048]{1,0:T(8,128)(2,1)S(1)}, bf16[96,2048]{1,0:T(8,128)(2,1)}, u32[]{:S(2)}, u32[]{:S(2)}) collective-permute-start(bf16[96,2048]{1,0:T(8,128)(2,1)S(1)} %get-tuple-element.348), channel_id=1, source_target_pairs={{0,8},{4,12},{8,0},{12,4},{16,24},{20,28},{24,16},{28,20},{1,9},{5... | collective-permute-start | bytes 1179656 | tf_op jit(solution)/shard_map/ppermute | solution.py:195
  184.2 19.2 %collective-permute-start.37 = (bf16[96,2048]{1,0:T(8,128)(2,1)S(1)}, bf16[96,2048]{1,0:T(8,128)(2,1)S(1)}, u32[]{:S(2)}, u32[]{:S(2)}) collective-permute-start(bf16[96,2048]{1,0:T(8,128)(2,1)S(1)} %collective-permute-done.23.refs_6_), channel_id=1, source_target_pairs={{0,4},{4,0},{8,12},{12,8},{16,20},{20,16},{24,28},{28,24},{1,5},{5... | collective-permute-start | bytes 1179656 | tf_op jit(solution)/shard_map/ppermute | solution.py:195
  184.3 19.8 %collective-permute-start.38 = (bf16[96,2048]{1,0:T(8,128)(2,1)S(1)}, bf16[96,2048]{1,0:T(8,128)(2,1)S(1)}, u32[]{:S(2)}, u32[]{:S(2)}) collective-permute-start(bf16[96,2048]{1,0:T(8,128)(2,1)S(1)} %collective-permute-done.24.refs_7_), channel_id=1, source_target_pairs={{0,4},{4,0},{8,12},{12,8},{16,20},{20,16},{24,28},{28,24},{1,5},{5... | collective-permute-start | bytes 1179656 | tf_op jit(solution)/shard_map/ppermute | solution.py:195
  184.8 20.7 %collective-permute-start.34 = (bf16[192,2048]{1,0:T(8,128)(2,1)S(1)}, bf16[192,2048]{1,0:T(8,128)(2,1)S(1)}, u32[]{:S(2)}, u32[]{:S(2)}) collective-permute-start(bf16[192,2048]{1,0:T(8,128)(2,1)S(1)} %bitcast.56), channel_id=1, source_target_pairs={{0,4},{4,0},{8,12},{12,8},{16,20},{20,16},{24,28},{28,24},{1,5},{5... | collective-permute-start | bytes 2359304 | tf_op jit(solution)/shard_map/ppermute | solution.py:195
  190.0 11.0 %collective-permute-start.31 = (bf16[96,2048]{1,0:T(8,128)(2,1)}, bf16[96,2048]{1,0:T(8,128)(2,1)S(1)}, u32[]{:S(2)}, u32[]{:S(2)}) collective-permute-start(bf16[96,2048]{1,0:T(8,128)(2,1)} %get-tuple-element.349), channel_id=1, source_target_pairs={{0,16},{4,20},{8,24},{12,28},{16,0},{20,4},{24,8},{28,12},{1,17},{... | collective-permute-start | bytes 1179656 | tf_op jit(solution)/shard_map/ppermute | solution.py:195
  203.4 19.9 %collective-permute-start.33 = (bf16[192,2048]{1,0:T(8,128)(2,1)S(1)}, bf16[192,2048]{1,0:T(8,128)(2,1)S(1)}, u32[]{:S(2)}, u32[]{:S(2)}) collective-permute-start(bf16[192,2048]{1,0:T(8,128)(2,1)S(1)} %multiply_convert_fusion.refs_0_), channel_id=1, source_target_pairs={{0,16},{4,20},{8,24},{12,28},{16,0},{20,4},{24,8},{28,12},{1,17},{... | collective-permute-start | bytes 2359304 | tf_op jit(solution)/shard_map/ppermute | solution.py:195
  204.1 20.2 %collective-permute-start.32 = (bf16[192,2048]{1,0:T(8,128)(2,1)S(1)}, bf16[192,2048]{1,0:T(8,128)(2,1)S(1)}, u32[]{:S(2)}, u32[]{:S(2)}) collective-permute-start(bf16[192,2048]{1,0:T(8,128)(2,1)S(1)} %multiply_convert_fusion.refs_0_), channel_id=1, source_target_pairs={{0,8},{4,12},{8,0},{12,4},{16,24},{20,28},{24,16},{28,20},{1,9},{5... | collective-permute-start | bytes 2359304 | tf_op jit(solution)/shard_map/ppermute | solution.py:195
  225.4 10.7 %collective-permute-start.42 = (bf16[96,2048]{1,0:T(8,128)(2,1)S(1)}, bf16[96,2048]{1,0:T(8,128)(2,1)S(1)}, u32[]{:S(2)}, u32[]{:S(2)}) collective-permute-start(bf16[96,2048]{1,0:T(8,128)(2,1)S(1)} %slice.206), channel_id=1, source_target_pairs={{0,8},{4,12},{8,0},{12,4},{16,24},{20,28},{24,16},{28,20},{1,9},{5... | collective-permute-start | bytes 1179656 | tf_op jit(solution)/shard_map/ppermute | solution.py:195
  227.8 12.0 %collective-permute-start.39 = (bf16[192,2048]{1,0:T(8,128)(2,1)S(1)}, bf16[192,2048]{1,0:T(8,128)(2,1)S(1)}, u32[]{:S(2)}, u32[]{:S(2)}) collective-permute-start(bf16[192,2048]{1,0:T(8,128)(2,1)S(1)} %multiply_convert_fusion.refs_0_), channel_id=1, source_target_pairs={{0,4},{4,0},{8,12},{12,8},{16,20},{20,16},{24,28},{28,24},{1,5},{5... | collective-permute-start | bytes 2359304 | tf_op jit(solution)/shard_map/ppermute | solution.py:195
  227.8 12.0 %collective-permute-start.40 = (bf16[192,2048]{1,0:T(8,128)(2,1)S(1)}, bf16[192,2048]{1,0:T(8,128)(2,1)S(1)}, u32[]{:S(2)}, u32[]{:S(2)}) collective-permute-start(bf16[192,2048]{1,0:T(8,128)(2,1)S(1)} %collective-permute-done.32.refs_2_), channel_id=1, source_target_pairs={{0,4},{4,0},{8,12},{12,8},{16,20},{20,16},{24,28},{28,24},{1,5},{5... | collective-permute-start | bytes 2359304 | tf_op jit(solution)/shard_map/ppermute | solution.py:195
  228.3 11.5 %collective-permute-start.41 = (bf16[192,2048]{1,0:T(8,128)(2,1)S(1)}, bf16[192,2048]{1,0:T(8,128)(2,1)S(1)}, u32[]{:S(2)}, u32[]{:S(2)}) collective-permute-start(bf16[192,2048]{1,0:T(8,128)(2,1)S(1)} %copy-done.59), channel_id=1, source_target_pairs={{0,4},{4,0},{8,12},{12,8},{16,20},{20,16},{24,28},{28,24},{1,5},{5... | collective-permute-start | bytes 2359304 | tf_op jit(solution)/shard_map/ppermute | solution.py:195
  241.6 34.5 %all-to-all-start.2 = ((bf16[8,192,256]{2,1,0:T(8,128)(2,1)}), bf16[8,192,256]{2,1,0:T(8,128)(2,1)}, u32[]{:S(2)}, u32[]{:S(2)}) async-start(bf16[8,192,256]{2,1,0:T(8,128)(2,1)} %copy-done.19), calls=%async_computation.2 | async-start | bytes 1572864 | tf_op jit(solution)/shard_map/all_to_all | solution.py:381
  245.8 101.7 %reduce-scatter.5.cloned.1.call-start = ((), (), s32[]{:S(2)}) async-start(), calls=%async_computation.12 | async-start | bytes 3604480 | tf_op jit(solution)/shard_map/reduce_scatter | solution.py:371
  276.1 175.8 %reduce-scatter.7.cloned.1.call-start = ((), (), s32[]{:S(2)}) async-start(), calls=%async_computation.13 | async-start | bytes 7864320 | tf_op jit(solution)/shard_map/reduce_scatter | solution.py:371
  294.9 15.4 %collective-permute-start.46 = (bf16[384,2048]{1,0:T(8,128)(2,1)}, bf16[384,2048]{1,0:T(8,128)(2,1)S(1)}, u32[]{:S(2)}, u32[]{:S(2)}) collective-permute-start(bf16[384,2048]{1,0:T(8,128)(2,1)} %get-tuple-element.252), channel_id=1, source_target_pairs={{0,4},{4,0},{8,12},{12,8},{16,20},{20,16},{24,28},{28,24},{1,5},{5... | collective-permute-start | bytes 4718600 | tf_op jit(solution)/shard_map/ppermute | solution.py:195
  310.3 14.7 %collective-permute-start.47 = (bf16[384,2048]{1,0:T(8,128)(2,1)}, bf16[384,2048]{1,0:T(8,128)(2,1)S(1)}, u32[]{:S(2)}, u32[]{:S(2)}) collective-permute-start(bf16[384,2048]{1,0:T(8,128)(2,1)} %get-tuple-element.257), channel_id=1, source_target_pairs={{0,4},{4,0},{8,12},{12,8},{16,20},{20,16},{24,28},{28,24},{1,5},{5... | collective-permute-start | bytes 4718600 | tf_op jit(solution)/shard_map/ppermute | solution.py:195
  311.5 11.1 %collective-permute-start.49 = (bf16[96,2048]{1,0:T(8,128)(2,1)S(1)}, bf16[96,2048]{1,0:T(8,128)(2,1)S(1)}, u32[]{:S(2)}, u32[]{:S(2)}) collective-permute-start(bf16[96,2048]{1,0:T(8,128)(2,1)S(1)} %get-tuple-element.362), channel_id=1, source_target_pairs={{0,8},{4,12},{8,0},{12,4},{16,24},{20,28},{24,16},{28,20},{1,9},{5... | collective-permute-start | bytes 1179656 | tf_op jit(solution)/shard_map/ppermute | solution.py:195
  313.1 14.8 %collective-permute-start.51 = (bf16[96,2048]{1,0:T(8,128)(2,1)S(1)}, bf16[96,2048]{1,0:T(8,128)(2,1)S(1)}, u32[]{:S(2)}, u32[]{:S(2)}) collective-permute-start(bf16[96,2048]{1,0:T(8,128)(2,1)S(1)} %get-tuple-element.364), channel_id=1, source_target_pairs={{0,16},{4,20},{8,24},{12,28},{16,0},{20,4},{24,8},{28,12},{1,17},{... | collective-permute-start | bytes 1179656 | tf_op jit(solution)/shard_map/ppermute | solution.py:195
  314.5 30.2 %collective-permute-start.53 = (bf16[96,2048]{1,0:T(8,128)(2,1)S(1)}, bf16[96,2048]{1,0:T(8,128)(2,1)}, u32[]{:S(2)}, u32[]{:S(2)}) collective-permute-start(bf16[96,2048]{1,0:T(8,128)(2,1)S(1)} %get-tuple-element.363), channel_id=1, source_target_pairs={{0,16},{4,20},{8,24},{12,28},{16,0},{20,4},{24,8},{28,12},{1,17},{... | collective-permute-start | bytes 1179656 | tf_op jit(solution)/shard_map/ppermute | solution.py:195
  323.5 20.0 %collective-permute-start.50 = (bf16[96,2048]{1,0:T(8,128)(2,1)}, bf16[96,2048]{1,0:T(8,128)(2,1)}, u32[]{:S(2)}, u32[]{:S(2)}) collective-permute-start(bf16[96,2048]{1,0:T(8,128)(2,1)} %add_convert_fusion.8), channel_id=1, source_target_pairs={{0,16},{4,20},{8,24},{12,28},{16,0},{20,4},{24,8},{28,12},{1,17},{... | collective-permute-start | bytes 1179656 | tf_op jit(solution)/shard_map/ppermute | solution.py:195
  326.4 17.1 %collective-permute-start.48 = (bf16[96,2048]{1,0:T(8,128)(2,1)}, bf16[96,2048]{1,0:T(8,128)(2,1)}, u32[]{:S(2)}, u32[]{:S(2)}) collective-permute-start(bf16[96,2048]{1,0:T(8,128)(2,1)} %slice.253), channel_id=1, source_target_pairs={{0,8},{4,12},{8,0},{12,4},{16,24},{20,28},{24,16},{28,20},{1,9},{5... | collective-permute-start | bytes 1179656 | tf_op jit(solution)/shard_map/ppermute | solution.py:195
  328.7 16.3 %collective-permute-start.52 = (bf16[96,2048]{1,0:T(8,128)(2,1)}, bf16[96,2048]{1,0:T(8,128)(2,1)S(1)}, u32[]{:S(2)}, u32[]{:S(2)}) collective-permute-start(bf16[96,2048]{1,0:T(8,128)(2,1)} %add_convert_fusion.7), channel_id=1, source_target_pairs={{0,8},{4,12},{8,0},{12,4},{16,24},{20,28},{24,16},{28,20},{1,9},{5... | collective-permute-start | bytes 1179656 | tf_op jit(solution)/shard_map/ppermute | solution.py:195
  343.2 180.8 %reduce-scatter.9.cloned.1.call-start = ((), (), s32[]{:S(2)}) async-start(), calls=%async_computation.14 | async-start | bytes 3932160 | tf_op jit(solution)/shard_map/reduce_scatter | solution.py:371
  351.3 18.3 %collective-permute-start.55 = (bf16[192,2048]{1,0:T(8,128)(2,1)S(1)}, bf16[192,2048]{1,0:T(8,128)(2,1)S(1)}, u32[]{:S(2)}, u32[]{:S(2)}) collective-permute-start(bf16[192,2048]{1,0:T(8,128)(2,1)S(1)} %fusion.8.refs_0_), channel_id=1, source_target_pairs={{0,16},{4,20},{8,24},{12,28},{16,0},{20,4},{24,8},{28,12},{1,17},{... | collective-permute-start | bytes 2359304 | tf_op jit(solution)/shard_map/ppermute | solution.py:195
  352.6 17.2 %collective-permute-start.54 = (bf16[192,2048]{1,0:T(8,128)(2,1)S(1)}, bf16[192,2048]{1,0:T(8,128)(2,1)}, u32[]{:S(2)}, u32[]{:S(2)}) collective-permute-start(bf16[192,2048]{1,0:T(8,128)(2,1)S(1)} %fusion.8.refs_0_), channel_id=1, source_target_pairs={{0,8},{4,12},{8,0},{12,4},{16,24},{20,28},{24,16},{28,20},{1,9},{5... | collective-permute-start | bytes 2359304 | tf_op jit(solution)/shard_map/ppermute | solution.py:195
  369.8 13.7 %collective-permute-start.63 = (bf16[768,2048]{1,0:T(8,128)(2,1)}, bf16[768,2048]{1,0:T(8,128)(2,1)S(1)}, u32[]{:S(2)}, u32[]{:S(2)}) collective-permute-start(bf16[768,2048]{1,0:T(8,128)(2,1)} %get-tuple-element.276), channel_id=1, source_target_pairs={{0,4},{4,0},{8,12},{12,8},{16,20},{20,16},{24,28},{28,24},{1,5},{5... | collective-permute-start | bytes 9437192 | tf_op jit(solution)/shard_map/ppermute | solution.py:195
  369.8 11.6 %collective-permute-start.59 = (bf16[96,2048]{1,0:T(8,128)(2,1)S(1)}, bf16[96,2048]{1,0:T(8,128)(2,1)S(1)}, u32[]{:S(2)}, u32[]{:S(2)}) collective-permute-start(bf16[96,2048]{1,0:T(8,128)(2,1)S(1)} %slice.215), channel_id=1, source_target_pairs={{0,8},{4,12},{8,0},{12,4},{16,24},{20,28},{24,16},{28,20},{1,9},{5... | collective-permute-start | bytes 1179656 | tf_op jit(solution)/shard_map/ppermute | solution.py:195
  372.2 11.3 %collective-permute-start.60 = (bf16[96,2048]{1,0:T(8,128)(2,1)S(1)}, bf16[96,2048]{1,0:T(8,128)(2,1)S(1)}, u32[]{:S(2)}, u32[]{:S(2)}) collective-permute-start(bf16[96,2048]{1,0:T(8,128)(2,1)S(1)} %slice.216), channel_id=1, source_target_pairs={{0,16},{4,20},{8,24},{12,28},{16,0},{20,4},{24,8},{28,12},{1,17},{... | collective-permute-start | bytes 1179656 | tf_op jit(solution)/shard_map/ppermute | solution.py:195
  373.9 14.6 %collective-permute-start.57 = (bf16[192,2048]{1,0:T(8,128)(2,1)}, bf16[192,2048]{1,0:T(8,128)(2,1)S(1)}, u32[]{:S(2)}, u32[]{:S(2)}) collective-permute-start(bf16[192,2048]{1,0:T(8,128)(2,1)} %collective-permute-done.54.refs_2_), channel_id=1, source_target_pairs={{0,4},{4,0},{8,12},{12,8},{16,20},{20,16},{24,28},{28,24},{1,5},{5... | collective-permute-start | bytes 2359304 | tf_op jit(solution)/shard_map/ppermute | solution.py:195
  373.9 14.6 %collective-permute-start.58 = (bf16[192,2048]{1,0:T(8,128)(2,1)S(1)}, bf16[192,2048]{1,0:T(8,128)(2,1)S(1)}, u32[]{:S(2)}, u32[]{:S(2)}) collective-permute-start(bf16[192,2048]{1,0:T(8,128)(2,1)S(1)} %collective-permute-done.55.refs_4_), channel_id=1, source_target_pairs={{0,4},{4,0},{8,12},{12,8},{16,20},{20,16},{24,28},{28,24},{1,5},{5... | collective-permute-start | bytes 2359304 | tf_op jit(solution)/shard_map/ppermute | solution.py:195
  388.7 35.2 %collective-permute-start.65 = (bf16[96,2048]{1,0:T(8,128)(2,1)S(1)}, bf16[96,2048]{1,0:T(8,128)(2,1)S(1)}, u32[]{:S(2)}, u32[]{:S(2)}) collective-permute-start(bf16[96,2048]{1,0:T(8,128)(2,1)S(1)} %get-tuple-element.365), channel_id=1, source_target_pairs={{0,8},{4,12},{8,0},{12,4},{16,24},{20,28},{24,16},{28,20},{1,9},{5... | collective-permute-start | bytes 1179656 | tf_op jit(solution)/shard_map/ppermute | solution.py:195
  390.0 34.1 %collective-permute-start.67 = (bf16[96,2048]{1,0:T(8,128)(2,1)S(1)}, bf16[96,2048]{1,0:T(8,128)(2,1)S(1)}, u32[]{:S(2)}, u32[]{:S(2)}) collective-permute-start(bf16[96,2048]{1,0:T(8,128)(2,1)S(1)} %slice.224), channel_id=1, source_target_pairs={{0,16},{4,20},{8,24},{12,28},{16,0},{20,4},{24,8},{28,12},{1,17},{... | collective-permute-start | bytes 1179656 | tf_op jit(solution)/shard_map/ppermute | solution.py:195
  391.6 32.5 %collective-permute-start.66 = (bf16[96,2048]{1,0:T(8,128)(2,1)S(1)}, bf16[96,2048]{1,0:T(8,128)(2,1)S(1)}, u32[]{:S(2)}, u32[]{:S(2)}) collective-permute-start(bf16[96,2048]{1,0:T(8,128)(2,1)S(1)} %slice.221), channel_id=1, source_target_pairs={{0,8},{4,12},{8,0},{12,4},{16,24},{20,28},{24,16},{28,20},{1,9},{5... | collective-permute-start | bytes 1179656 | tf_op jit(solution)/shard_map/ppermute | solution.py:195
  392.6 31.4 %collective-permute-start.64 = (bf16[96,2048]{1,0:T(8,128)(2,1)S(1)}, bf16[96,2048]{1,0:T(8,128)(2,1)S(1)}, u32[]{:S(2)}, u32[]{:S(2)}) collective-permute-start(bf16[96,2048]{1,0:T(8,128)(2,1)S(1)} %get-tuple-element.366), channel_id=1, source_target_pairs={{0,16},{4,20},{8,24},{12,28},{16,0},{20,4},{24,8},{28,12},{1,17},{... | collective-permute-start | bytes 1179656 | tf_op jit(solution)/shard_map/ppermute | solution.py:195
  430.4 11.9 %collective-permute-start.70 = (bf16[96,1536]{1,0:T(8,128)(2,1)S(1)}, bf16[96,1536]{1,0:T(8,128)(2,1)S(1)}, u32[]{:S(2)}, u32[]{:S(2)}) collective-permute-start(bf16[96,1536]{1,0:T(8,128)(2,1)S(1)} %get-tuple-element.356), channel_id=1, source_target_pairs={{0,8},{4,12},{8,0},{12,4},{16,24},{20,28},{24,16},{28,20},{1,9},{5... | collective-permute-start | bytes 884744 | tf_op jit(solution)/shard_map/ppermute | solution.py:195
  431.5 10.9 %collective-permute-start.69 = (bf16[96,1536]{1,0:T(8,128)(2,1)S(1)}, bf16[96,1536]{1,0:T(8,128)(2,1)S(1)}, u32[]{:S(2)}, u32[]{:S(2)}) collective-permute-start(bf16[96,1536]{1,0:T(8,128)(2,1)S(1)} %get-tuple-element.358), channel_id=1, source_target_pairs={{0,16},{4,20},{8,24},{12,28},{16,0},{20,4},{24,8},{28,12},{1,17},{... | collective-permute-start | bytes 884744 | tf_op jit(solution)/shard_map/ppermute | solution.py:195
  455.0 12.2 %collective-permute-start.73 = (bf16[96,1536]{1,0:T(8,128)(2,1)}, bf16[96,1536]{1,0:T(8,128)(2,1)S(1)}, u32[]{:S(2)}, u32[]{:S(2)}) collective-permute-start(bf16[96,1536]{1,0:T(8,128)(2,1)} %get-tuple-element.309), channel_id=1, source_target_pairs={{0,8},{4,12},{8,0},{12,4},{16,24},{20,28},{24,16},{28,20},{1,9},{5... | collective-permute-start | bytes 884744 | tf_op jit(solution)/shard_map/ppermute | solution.py:195
  455.5 12.8 %collective-permute-start.74 = (bf16[96,1536]{1,0:T(8,128)(2,1)}, bf16[96,1536]{1,0:T(8,128)(2,1)S(1)}, u32[]{:S(2)}, u32[]{:S(2)}) collective-permute-start(bf16[96,1536]{1,0:T(8,128)(2,1)} %get-tuple-element.310), channel_id=1, source_target_pairs={{0,16},{4,20},{8,24},{12,28},{16,0},{20,4},{24,8},{28,12},{1,17},{... | collective-permute-start | bytes 884744 | tf_op jit(solution)/shard_map/ppermute | solution.py:195
  479.8 15.3 %collective-permute-start.78 = (bf16[224,1536]{1,0:T(8,128)(2,1)S(1)}, bf16[224,1536]{1,0:T(8,128)(2,1)S(1)}, u32[]{:S(2)}, u32[]{:S(2)}) collective-permute-start(bf16[224,1536]{1,0:T(8,128)(2,1)S(1)} %get-tuple-element.326.refs_0_), channel_id=1, source_target_pairs={{0,16},{4,20},{8,24},{12,28},{16,0},{20,4},{24,8},{28,12},{1,17},{... | collective-permute-start | bytes 2064392 | tf_op jit(solution)/shard_map/ppermute | solution.py:195
  481.3 14.8 %collective-permute-start.77 = (bf16[224,1536]{1,0:T(8,128)(2,1)S(1)}, bf16[224,1536]{1,0:T(8,128)(2,1)S(1)}, u32[]{:S(2)}, u32[]{:S(2)}) collective-permute-start(bf16[224,1536]{1,0:T(8,128)(2,1)S(1)} %get-tuple-element.326.refs_0_), channel_id=1, source_target_pairs={{0,8},{4,12},{8,0},{12,4},{16,24},{20,28},{24,16},{28,20},{1,9},{5... | collective-permute-start | bytes 2064392 | tf_op jit(solution)/shard_map/ppermute | solution.py:195
  496.2 14.1 %collective-permute-start.80 = (bf16[224,1536]{1,0:T(8,128)(2,1)S(1)}, bf16[224,1536]{1,0:T(8,128)(2,1)S(1)}, u32[]{:S(2)}, u32[]{:S(2)}) collective-permute-start(bf16[224,1536]{1,0:T(8,128)(2,1)S(1)} %collective-permute-done.77.refs_2_), channel_id=1, source_target_pairs={{0,4},{4,0},{8,12},{12,8},{16,20},{20,16},{24,28},{28,24},{1,5},{5... | collective-permute-start | bytes 2064392 | tf_op jit(solution)/shard_map/ppermute | solution.py:195
  496.3 13.1 %collective-permute-start.79 = (bf16[224,1536]{1,0:T(8,128)(2,1)S(1)}, bf16[224,1536]{1,0:T(8,128)(2,1)S(1)}, u32[]{:S(2)}, u32[]{:S(2)}) collective-permute-start(bf16[224,1536]{1,0:T(8,128)(2,1)S(1)} %get-tuple-element.326.refs_0_), channel_id=1, source_target_pairs={{0,4},{4,0},{8,12},{12,8},{16,20},{20,16},{24,28},{28,24},{1,5},{5... | collective-permute-start | bytes 2064392 | tf_op jit(solution)/shard_map/ppermute | solution.py:195
  498.2 12.1 %collective-permute-start.81 = (bf16[224,1536]{1,0:T(8,128)(2,1)S(1)}, bf16[224,1536]{1,0:T(8,128)(2,1)S(1)}, u32[]{:S(2)}, u32[]{:S(2)}) collective-permute-start(bf16[224,1536]{1,0:T(8,128)(2,1)S(1)} %collective-permute-done.78.refs_4_), channel_id=1, source_target_pairs={{0,4},{4,0},{8,12},{12,8},{16,20},{20,16},{24,28},{28,24},{1,5},{5... | collective-permute-start | bytes 2064392 | tf_op jit(solution)/shard_map/ppermute | solution.py:195
  498.2 10.5 %collective-permute-start.83 = (bf16[112,1536]{1,0:T(8,128)(2,1)S(1)}, bf16[112,1536]{1,0:T(8,128)(2,1)S(1)}, u32[]{:S(2)}, u32[]{:S(2)}) collective-permute-start(bf16[112,1536]{1,0:T(8,128)(2,1)S(1)} %slice.235), channel_id=1, source_target_pairs={{0,16},{4,20},{8,24},{12,28},{16,0},{20,4},{24,8},{28,12},{1,17},{... | collective-permute-start | bytes 1032200 | tf_op jit(solution)/shard_map/ppermute | solution.py:195
  512.2 24.6 %all-to-all-start.3 = ((bf16[8,2,64,704]{3,2,1,0:T(8,128)(2,1)}), bf16[8,2,64,704]{3,2,1,0:T(8,128)(2,1)S(1)}, u32[]{:S(2)}, u32[]{:S(2)}) async-start(bf16[8,2,64,704]{3,2,1,0:T(8,128)(2,1)} %bitcast.76), calls=%async_computation.7 | async-start | bytes 3145728 | tf_op jit(solution)/shard_map/all_to_all | solution.py:381
  515.8 34.9 %reduce-scatter.11.cloned.1.call-start = ((), (), s32[]{:S(2)}) async-start(), calls=%async_computation.15 | async-start | bytes 1064960 | tf_op jit(solution)/shard_map/reduce_scatter | solution.py:371
  (115 other events, 683.9 us)
Sparse Core Ops, SparseCore 0:
  39.6 64.2 all-gather.3
  105.4 113.9 all-gather.5
  221.0 57.3 all-gather.7
  280.6 54.8 reduce-scatter.4
  343.3 108.5 reduce-scatter.6
  454.1 60.7 reduce-scatter.8
  524.2 25.0 reduce-scatter.10

commit v7 on v6

--- a/solution.py
+++ b/solution.py
@@ -1313,7 +1313,7 @@
     grad_output_weight = grad_attention[:out_rows].astype(F32)
     grad_query_up = grad_attention[out_rows:].reshape(fold, -1, heads * HEAD_DIM)
     grad_query_up = grad_query_up.transpose(1, 0, 2).reshape(n_seq, query_rows, -1)
-    grad_query_up = exchange(after(grad_query_up, gate_up_rows))
+    grad_query_up = exchange(grad_query_up)
     grad_query_up = grad_query_up.transpose(1, 0, 2).reshape(query_rows, -1).astype(F32)
 
     grad_gate, grad_up = columns_back(gate_up_rows)

time: 572 us -> 572 us (level)
  no operation moved by 1% of the time
where the time goes in v7:
time: 572 us; the launch traced here: 563 us
  waiting for transfers between devices  194 us (34%)
  Pallas kernels  159 us (28%)
  starting transfers between devices  87.4 us (15%)
  local copies, waits for them, and re-layouts  61.7 us (11%)
  other arithmetic  37.6 us (7%)
  between operations  15.8 us (3%)
  matrix products  7.69 us (1%)
    ppermute x83, waiting for transfers between devices, flip(): return lax.ppermute(block, 'seq', [(i, i ^ bits) for i in range(n_seq)])  149 us
    ppermute x83, starting transfers between devices, flip(): return lax.ppermute(block, 'seq', [(i, i ^ bits) for i in range(n_seq)])  61.4 us
    pallas_call x1, Pallas kernels, attend_back(): pl.pallas_call(functools.partial(attend_back_kernel, len(blocks), heads,...  30.9 us
    pallas_call x2, Pallas kernels, feed_back(): pl.pallas_call(feed_back_kernel, grid=(count,), in_specs=[tokens, units,...  30.8 us
    unnamed x158, local copies, waits for them, and re-layouts  26.1 us
    pallas_call x1, Pallas kernels, attend(): pl.pallas_call(functools.partial(attend_kernel, len(packs), heads, block)...  25.3 us
    all_to_all x5, waiting for transfers between devices, exchange(): return lax.all_to_all(parts, 'seq', 0, 0)  24.3 us
    all_to_all x5, starting transfers between devices, exchange(): return lax.all_to_all(parts, 'seq', 0, 0)  19.1 us
  transfers between devices with their start and end apart: 98, of which 50 were waited for; matrix products, arithmetic and copies ran while one was open for 13% of the time, Pallas kernels for 28%

profile of v7, /device:TPU:0, one launch (start us, length us, event | category | flops | bytes accessed | tf_op | source)
XLA Modules:
  0.0 563.4 jit_solution(977213622091495297)
XLA Ops:
  9.6 5.1 collective-permute-start.2
  18.5 1.7 copy.65
  20.2 3.4 all-to-all-start
  25.3 3.1 collective-permute-done
  29.1 3.7 collective-permute-done.1
  33.5 1.7 constant_dynamic-update-slice_fusion.refs_0_
  35.2 3.1 all-to-all-done
  42.9 1.9 reshape.184
  44.9 14.9 %collective-permute-done.6.refs_4_ = bf16[256,1664]{1,0:T(8,128)(2,1)} collective-permute-done((bf16[256,1664]{1,0:T(8,128)(2,1)}, bf16[256,1664]{1,0:T(8,128)(2,1)}, u32[]{:S(2)}, u32[]{:S(2)}) %collective-permute-start.6) | collective-permute-done | bytes 852000 | tf_op jit(solution)/shard_map/ppermute | solution.py:195
  65.5 7.3 %collective-permute-done.10.refs_6_ = bf16[128,1664]{1,0:T(8,128)(2,1)S(1)} collective-permute-done((bf16[128,1664]{1,0:T(8,128)(2,1)S(1)}, bf16[128,1664]{1,0:T(8,128)(2,1)S(1)}, u32[]{:S(2)}, u32[]{:S(2)}) %collective-permute-start.10) | collective-permute-done | bytes 426016 | tf_op jit(solution)/shard_map/ppermute | solution.py:195
  75.2 4.4 all-to-all-start.1
  81.8 2.8 multiply_sine_fusion
  86.5 4.7 first_projections.1
  95.5 5.2 all-to-all-done.1
  100.7 3.2 all-gather.4.cloned.1.call-done
  108.7 3.2 slice.243
  113.3 2.4 copy.59
  115.7 3.9 collective-permute-done.15.refs_4_
  124.4 5.0 collective-permute-done.19.refs_6_
  133.6 25.3 %attend.1 = (bf16[1536,1024]{1,0:T(8,128)(2,1)}, bf16[1536,256]{1,0:T(8,128)(2,1)}, bf16[1536,256]{1,0:T(8,128)(2,1)}, bf16[1536,512]{1,0:T(8,128)(2,1)}, bf16[1...) custom-call(s32[1]{0:T(128)} %bitcast.1.me_ref, ...), custom_call_target="tpu_custom_call" | custom-call | flops 10000000 | bytes 20000 | tf_op jit(solution)/shard_map/attend/pallas_call | solution.py:868
  159.0 5.9 %collective-permute-done.25 = bf16[768,2048]{1,0:T(8,128)(2,1)S(1)} collective-permute-done((bf16[768,2048]{1,0:T(8,128)(2,1)}, bf16[768,2048]{1,0:T(8,128)(2,1)S(1)}, u32[]{:S(2)}, u32[]{:S(2)}) %collective-permute-start.25) | collective-permute-done | bytes 3145760 | tf_op jit(solution)/shard_map/ppermute | solution.py:195
  164.9 3.2 add_convert_fusion.1
  172.6 7.7 %collective-permute-done.29 = bf16[96,2048]{1,0:T(8,128)(2,1)S(1)} collective-permute-done((bf16[96,2048]{1,0:T(8,128)(2,1)S(1)}, bf16[96,2048]{1,0:T(8,128)(2,1)S(1)}, u32[]{:S(2)}, u32[]{:S(2)}) %collective-permute-start.29) | collective-permute-done | bytes 393248 | tf_op jit(solution)/shard_map/ppermute | solution.py:195
  180.3 2.3 collective-permute-done.27
  184.9 5.1 collective-permute-done.26
  190.5 2.9 collective-permute-done.28
  196.1 5.0 collective-permute-done.31
  207.3 3.8 stack_blocks.1.d_ref
  211.1 12.3 %collective-permute-done.33.refs_4_ = bf16[192,2048]{1,0:T(8,128)(2,1)S(1)} collective-permute-done((bf16[192,2048]{1,0:T(8,128)(2,1)S(1)}, bf16[192,2048]{1,0:T(8,128)(2,1)S(1)}, u32[]{:S(2)}, u32[]{:S(2)}) %collective-permute-start.33) | collective-permute-done | bytes 786464 | tf_op jit(solution)/shard_map/ppermute | solution.py:195
  228.3 7.8 %collective-permute-done.42.refs_6_ = bf16[96,2048]{1,0:T(8,128)(2,1)S(1)} collective-permute-done((bf16[96,2048]{1,0:T(8,128)(2,1)S(1)}, bf16[96,2048]{1,0:T(8,128)(2,1)S(1)}, u32[]{:S(2)}, u32[]{:S(2)}) %collective-permute-start.42) | collective-permute-done | bytes 393248 | tf_op jit(solution)/shard_map/ppermute | solution.py:195
  241.6 4.2 all-to-all-start.2
  249.9 18.5 %feed_forward.1 = (bf16[1536,2048]{1,0:T(8,128)(2,1)}, bf16[1536,704]{1,0:T(8,128)(2,1)}, bf16[1536,704]{1,0:T(8,128)(2,1)}, bf16[1536,704]{1,0:T(8,128)(2,1)}, ...) custom-call(bf16[192,2048]{1,0:T(8,128)(2,1)S(1)} %multiply_convert_fusion.refs_0_, ...), custom_call_target="tpu_custom_call" | custom-call | flops 10000000 | bytes 20000 | tf_op jit(solution)/shard_map/feed_forward/pallas_call | solution.py:529
  268.4 7.7 %convolution_convert_fusion = bf16[704,2048]{1,0:T(8,128)(2,1)} fusion(bf16[1536,704]{1,0:T(8,128)(2,1)} %get-tuple-element.267.left_ref, bf16[1536,2048]{1,0:T(8,128)(2,1)S(1)} %copy-done.43), kind=kOutput, calls=%fused_computation.3 | convolution fusion | flops 4430626816 | bytes 11337728 | tf_op jit(solution)/shard_map/dot_general | solution.py:188
  276.4 2.1 all-gather.8.cloned.1.call-done.down_ref.right_ref
  278.5 15.4 %feed_back.2 = (bf16[768,704]{1,0:T(8,128)(2,1)S(1)}, bf16[768,704]{1,0:T(8,128)(2,1)S(1)}, bf16[384,2048]{1,0:T(8,128)(2,1)S(1)}, bf16[384,2048]{1,0:T(8,128)(2,1)}) custom-call(bf16[1536,2048]{1,0:T(8,128)(2,1)} %stack_blocks.1.d_ref, bf16[1536,704]{1,0:T(8,128)(2,1)} %get-tuple-element.252.silu_ref, bf16[1536,704]{1,0:T(8,128)(2,1)} %get-tuple-element.246.slope_ref, ...), custom_call_target="tpu_custom_call" | custom-call | flops 10000000 | bytes 20000 | tf_op jit(solution)/shard_map/feed_back/pallas_call | solution.py:564
  294.9 15.4 %feed_back.3 = (bf16[768,704]{1,0:T(8,128)(2,1)S(1)}, bf16[768,704]{1,0:T(8,128)(2,1)S(1)}, bf16[384,2048]{1,0:T(8,128)(2,1)S(1)}, bf16[384,2048]{1,0:T(8,128)(2,1)}) custom-call(bf16[1536,2048]{1,0:T(8,128)(2,1)} %stack_blocks.1.d_ref, bf16[1536,704]{1,0:T(8,128)(2,1)} %get-tuple-element.252.silu_ref, bf16[1536,704]{1,0:T(8,128)(2,1)} %get-tuple-element.246.slope_ref, ...), custom_call_target="tpu_custom_call" | custom-call | flops 10000000 | bytes 20000 | tf_op jit(solution)/shard_map/feed_back/pallas_call | solution.py:564
  315.1 7.5 %collective-permute-done.49 = bf16[96,2048]{1,0:T(8,128)(2,1)S(1)} collective-permute-done((bf16[96,2048]{1,0:T(8,128)(2,1)S(1)}, bf16[96,2048]{1,0:T(8,128)(2,1)S(1)}, u32[]{:S(2)}, u32[]{:S(2)}) %collective-permute-start.49) | collective-permute-done | bytes 393248 | tf_op jit(solution)/shard_map/ppermute | solution.py:195
  329.3 13.9 %gate_up_grad.1 = bf16[4,8,2,64,704]{4,3,2,1,0:T(8,128)(2,1)} custom-call(bf16[1536,2048]{1,0:T(8,128)(2,1)} %get-tuple-element.261.x_ref, bf16[768,704]{1,0:T(8,128)(2,1)S(1)} %get-tuple-element.262.dg_low, bf16[768,704]{1,0:T(8,128)(2,1)S(1)} %get-tuple-element.263.du_low, bf16[768,704]{1,0:T(8,128)(2,1)S(1)} %get-tuple-element.264.dg_high, ...), custom_call_target="tpu_custom_call" | custom-call | flops 10000000 | bytes 20000 | tf_op jit(solution)/shard_map/gate_up_grad/pallas_call | solution.py:592
  347.6 2.7 multiply_reduce_fusion
  354.1 8.5 %pair_product.1 = (bf16[768,2048]{1,0:T(8,128)(2,1)}, bf16[768,2048]{1,0:T(8,128)(2,1)}) custom-call(bf16[1536,704]{1,0:T(8,128)(2,1)S(1)} %copy-done.42, bf16[704,2048]{1,0:T(8,128)(2,1)} %all-gather.8.cloned.1.call-done.down_ref.right_ref), custom_call_target="tpu_custom_call" | custom-call | flops 3000000000 | bytes 6000000 | tf_op jit(solution)/shard_map/pair_product/pallas_call | solution.py:616
  362.6 7.0 %collective-permute-done.55.refs_4_ = bf16[192,2048]{1,0:T(8,128)(2,1)S(1)} collective-permute-done((bf16[192,2048]{1,0:T(8,128)(2,1)S(1)}, bf16[192,2048]{1,0:T(8,128)(2,1)S(1)}, u32[]{:S(2)}, u32[]{:S(2)}) %collective-permute-start.55) | collective-permute-done | bytes 786464 | tf_op jit(solution)/shard_map/ppermute | solution.py:195
  372.2 1.7 collective-permute-start.60
  374.4 7.0 %collective-permute-done.59.refs_6_ = bf16[96,2048]{1,0:T(8,128)(2,1)S(1)} collective-permute-done((bf16[96,2048]{1,0:T(8,128)(2,1)S(1)}, bf16[96,2048]{1,0:T(8,128)(2,1)S(1)}, u32[]{:S(2)}, u32[]{:S(2)}) %collective-permute-start.59) | collective-permute-done | bytes 393248 | tf_op jit(solution)/shard_map/ppermute | solution.py:195
  381.4 2.1 collective-permute-done.60.refs_7_
  384.0 3.2 add_convert_fusion
  390.0 1.7 collective-permute-start.67
  393.0 30.9 %attend_back.1 = (bf16[1536,2048]{1,0:T(8,128)(2,1)}, bf16[1536,512]{1,0:T(8,128)(2,1)}, bf16[768,1536]{1,0:T(8,128)(2,1)}, bf16[768,1536]{1,0:T(8,128)(2,1)}) custom-call(s32[1]{0:T(128)} %bitcast.1.me_ref, s32[1,1536]{1,0:T(1,128)S(1)} %reshape.187.starts_ref, f32[1536,128]{1,0:T(8,128)S(1)} %copy-done.3, f32[1536,128]{1,0:T(8,128)S(1)} %copy-done.1, ...), custom_call_target="tpu_custom_call" | custom-call | flops 10000000 | bytes 20000 | tf_op jit(solution)/shard_map/attend_back/pallas_call | solution.py:1008
  425.0 4.0 collective-permute-done.68
  433.1 9.2 %attention_grads.1 = bf16[4,192,2048]{2,1,0:T(8,128)(2,1)} custom-call(bf16[1536,512]{1,0:T(8,128)(2,1)S(1)} %copy-done.5, bf16[1536,1024]{1,0:T(8,128)(2,1)} %get-tuple-element.302.latent_ref, bf16[1536,512]{1,0:T(8,128)(2,1)S(1)} %copy-done.14, bf16[1536,2048]{1,0:T(8,128)(2,1)} %get-tuple-element.304.d_ref), custom_call_target="tpu_custom_call" | custom-call | flops 10000000 | bytes 20000 | tf_op jit(solution)/shard_map/attention_grads/pallas_call | solution.py:1078
  443.2 8.7 %reduce-scatter.7.cloned.1.call-done = bf16[1024,704]{1,0:T(8,128)(2,1)} async-done(((bf16[4096,704]{1,0:T(8,128)(2,1)}), bf16[1024,704]{1,0:T(8,128)(2,1)}) %reduce-scatter.7.cloned.1.call-update) | async-done | bytes 1441808 | tf_op jit(solution)/shard_map/reduce_scatter | solution.py:371
  456.1 5.8 %collective-permute-done.71 = bf16[96,1536]{1,0:T(8,128)(2,1)S(1)} collective-permute-done((bf16[96,1536]{1,0:T(8,128)(2,1)S(1)}, bf16[96,1536]{1,0:T(8,128)(2,1)S(1)}, u32[]{:S(2)}, u32[]{:S(2)}) %collective-permute-start.71) | collective-permute-done | bytes 294944 | tf_op jit(solution)/shard_map/ppermute | solution.py:195
  463.5 3.7 collective-permute-done.73
  471.7 7.6 %last_products.1 = (bf16[224,1536]{1,0:T(8,128)(2,1)S(1)}, f32[192,2048]{1,0:T(8,128)}) custom-call(s32[1]{0:T(128)} %bitcast.1.me_ref, f32[192,1536]{1,0:T(8,128)} %maximum_add_fusion.3.back_ref, f32[192,1024]{1,0:T(8,128)S(1)} %copy-done.18, f32[1,1024]{1,0:T(1,128)S(1)} %get-tuple-element.311.query_gain_ref, bf16[192,2048]{1,0:T(8,128)(2,1)} %bitcast.70, ...), custom_call_target="tpu_custom_call" | custom-call | flops 10000000 | bytes 20000 | tf_op jit(solution)/shard_map/last_products/pallas_call | solution.py:697
  482.9 3.8 add_bitcast_fusion
  486.8 8.3 %collective-permute-done.78.refs_4_ = bf16[224,1536]{1,0:T(8,128)(2,1)S(1)} collective-permute-done((bf16[224,1536]{1,0:T(8,128)(2,1)S(1)}, bf16[224,1536]{1,0:T(8,128)(2,1)S(1)}, u32[]{:S(2)}, u32[]{:S(2)}) %collective-permute-start.78) | collective-permute-done | bytes 688160 | tf_op jit(solution)/shard_map/ppermute | solution.py:195
  499.0 7.9 %collective-permute-done.82.refs_6_ = bf16[112,1536]{1,0:T(8,128)(2,1)S(1)} collective-permute-done((bf16[112,1536]{1,0:T(8,128)(2,1)S(1)}, bf16[112,1536]{1,0:T(8,128)(2,1)S(1)}, u32[]{:S(2)}, u32[]{:S(2)}) %collective-permute-start.82) | collective-permute-done | bytes 344096 | tf_op jit(solution)/shard_map/ppermute | solution.py:195
  506.9 1.8 collective-permute-done.83.refs_7_
  512.2 3.6 all-to-all-start.4
  519.9 4.2 first_grads.1
  524.1 2.4 convert_element_type.296
  526.4 10.3 %all-to-all-done.4.parts_ref = bf16[8,2,64,704]{3,2,1,0:T(8,128)(2,1)S(1)} async-done(((bf16[8,2,64,704]{3,2,1,0:T(8,128)(2,1)}), bf16[8,2,64,704]{3,2,1,0:T(8,128)(2,1)S(1)}, u32[]{:S(2)}, u32[]{:S(2)}) %all-to-all-start.4) | async-done | bytes 1441824 | tf_op jit(solution)/shard_map/all_to_all | solution.py:381
  536.7 1.8 columns_back.1
  539.5 3.4 all-to-all-start.3
  544.0 5.8 %all-to-all-done.3 = bf16[8,32,512]{2,1,0:T(8,128)(2,1)S(1)} async-done(((bf16[8,32,512]{2,1,0:T(8,128)(2,1)}), bf16[8,32,512]{2,1,0:T(8,128)(2,1)S(1)}, u32[]{:S(2)}, u32[]{:S(2)}) %all-to-all-start.3) | async-done | bytes 262176 | tf_op jit(solution)/shard_map/all_to_all | solution.py:381
  (406 shorter events, 143.9 us)
Async XLA Ops:
  9.6 23.9 %collective-permute-start.2 = (bf16[64,1664]{1,0:T(8,128)(2,1)S(1)}, bf16[64,1664]{1,0:T(8,128)(2,1)}, u32[]{:S(2)}, u32[]{:S(2)}) collective-permute-start(bf16[64,1664]{1,0:T(8,128)(2,1)S(1)} %fusion.6), channel_id=1, source_target_pairs={{0,3},{1,2},{2,1},{3,0},{4,7},{5,6},{6,5},{7,4},{8,11},{9,10},{10,... | collective-permute-start | bytes 638984 | tf_op jit(solution)/shard_map/ppermute | solution.py:365
  14.7 18.1 %collective-permute-start.1 = (bf16[64,1664]{1,0:T(8,128)(2,1)S(1)}, bf16[64,1664]{1,0:T(8,128)(2,1)S(1)}, u32[]{:S(2)}, u32[]{:S(2)}) collective-permute-start(bf16[64,1664]{1,0:T(8,128)(2,1)S(1)} %fusion.6), channel_id=1, source_target_pairs={{0,2},{1,3},{2,0},{3,1},{4,6},{5,7},{6,4},{7,5},{8,10},{9,11},{10,... | collective-permute-start | bytes 638984 | tf_op jit(solution)/shard_map/ppermute | solution.py:365
  14.7 13.7 %collective-permute-start = (bf16[64,1664]{1,0:T(8,128)(2,1)S(1)}, bf16[64,1664]{1,0:T(8,128)(2,1)S(1)}, u32[]{:S(2)}, u32[]{:S(2)}) collective-permute-start(bf16[64,1664]{1,0:T(8,128)(2,1)S(1)} %fusion.6), channel_id=1, source_target_pairs={{0,1},{1,0},{2,3},{3,2},{4,5},{5,4},{6,7},{7,6},{8,9},{9,8},{10,11... | collective-permute-start | bytes 638984 | tf_op jit(solution)/shard_map/ppermute | solution.py:365
  15.4 22.9 %collective-permute-start.4 = (bf16[192,2048]{1,0:T(8,128)(2,1)}, bf16[192,2048]{1,0:T(8,128)(2,1)S(1)}, u32[]{:S(2)}, u32[]{:S(2)}) collective-permute-start(bf16[192,2048]{1,0:T(8,128)(2,1)} %bitcast.54), channel_id=1, source_target_pairs={{0,16},{4,20},{8,24},{12,28},{16,0},{20,4},{24,8},{28,12},{1,17},{... | collective-permute-start | bytes 2359304 | tf_op jit(solution)/shard_map/ppermute | solution.py:195
  17.0 21.3 %collective-permute-start.3 = (bf16[192,2048]{1,0:T(8,128)(2,1)}, bf16[192,2048]{1,0:T(8,128)(2,1)S(1)}, u32[]{:S(2)}, u32[]{:S(2)}) collective-permute-start(bf16[192,2048]{1,0:T(8,128)(2,1)} %bitcast.55), channel_id=1, source_target_pairs={{0,8},{4,12},{8,0},{12,4},{16,24},{20,28},{24,16},{28,20},{1,9},{5... | collective-permute-start | bytes 2359304 | tf_op jit(solution)/shard_map/ppermute | solution.py:195
  20.2 18.1 %all-to-all-start = ((bf16[8,32,512]{2,1,0:T(8,128)(2,1)}), bf16[8,32,512]{2,1,0:T(8,128)(2,1)S(1)}, u32[]{:S(2)}, u32[]{:S(2)}) async-start(bf16[8,32,512]{2,1,0:T(8,128)(2,1)} %bitcast.53), calls=%async_computation | async-start | bytes 524288 | tf_op jit(solution)/shard_map/all_to_all | solution.py:381
  23.6 80.2 %all-gather.4.cloned.1.call-start = ((), (), s32[]{:S(2)}) async-start(), calls=%async_computation.9 | async-start | bytes 3932160 | tf_op jit(solution)/shard_map/all_gather | solution.py:355
  39.4 20.4 %collective-permute-start.6 = (bf16[256,1664]{1,0:T(8,128)(2,1)}, bf16[256,1664]{1,0:T(8,128)(2,1)}, u32[]{:S(2)}, u32[]{:S(2)}) collective-permute-start(bf16[256,1664]{1,0:T(8,128)(2,1)} %constant_dynamic-update-slice_fusion.refs_0_), channel_id=1, source_target_pairs={{0,16},{4,20},{8,24},{12,28},{16,0},{20,4},{24,8},{28,12},{1,17},{... | collective-permute-start | bytes 2555912 | tf_op jit(solution)/shard_map/ppermute | solution.py:195
  41.1 20.0 %collective-permute-start.5 = (bf16[256,1664]{1,0:T(8,128)(2,1)}, bf16[256,1664]{1,0:T(8,128)(2,1)}, u32[]{:S(2)}, u32[]{:S(2)}) collective-permute-start(bf16[256,1664]{1,0:T(8,128)(2,1)} %constant_dynamic-update-slice_fusion.refs_0_), channel_id=1, source_target_pairs={{0,8},{4,12},{8,0},{12,4},{16,24},{20,28},{24,16},{28,20},{1,9},{5... | collective-permute-start | bytes 2555912 | tf_op jit(solution)/shard_map/ppermute | solution.py:195
  75.2 25.5 %all-to-all-start.1 = ((bf16[8,2,64,704]{3,2,1,0:T(8,128)(2,1)}), bf16[8,2,64,704]{3,2,1,0:T(8,128)(2,1)}, u32[]{:S(2)}, u32[]{:S(2)}) async-start(bf16[8,2,64,704]{3,2,1,0:T(8,128)(2,1)} %copy.58), calls=%async_computation.1 | async-start | bytes 3145728 | tf_op jit(solution)/shard_map/all_to_all | solution.py:381
  79.7 144.6 %all-gather.6.cloned.1.call-start = ((), (), s32[]{:S(2)}) async-start(), calls=%async_computation.10 | async-start | bytes 7864320 | tf_op jit(solution)/shard_map/all_gather | solution.py:355
  103.9 174.6 %all-gather.8.cloned.1.call-start = ((), (), s32[]{:S(2)}) async-start(), calls=%async_computation.11 | async-start | bytes 3604480 | tf_op jit(solution)/shard_map/all_gather | solution.py:355
  104.4 15.2 %collective-permute-start.15 = (bf16[192,1536]{1,0:T(8,128)(2,1)S(1)}, bf16[192,1536]{1,0:T(8,128)(2,1)}, u32[]{:S(2)}, u32[]{:S(2)}) collective-permute-start(bf16[192,1536]{1,0:T(8,128)(2,1)S(1)} %copy-done.23), channel_id=1, source_target_pairs={{0,16},{4,20},{8,24},{12,28},{16,0},{20,4},{24,8},{28,12},{1,17},{... | collective-permute-start | bytes 1769480 | tf_op jit(solution)/shard_map/ppermute | solution.py:195
  106.0 14.7 %collective-permute-start.14 = (bf16[192,1536]{1,0:T(8,128)(2,1)S(1)}, bf16[192,1536]{1,0:T(8,128)(2,1)S(1)}, u32[]{:S(2)}, u32[]{:S(2)}) collective-permute-start(bf16[192,1536]{1,0:T(8,128)(2,1)S(1)} %copy-done.23), channel_id=1, source_target_pairs={{0,8},{4,12},{8,0},{12,4},{16,24},{20,28},{24,16},{28,20},{1,9},{5... | collective-permute-start | bytes 1769480 | tf_op jit(solution)/shard_map/ppermute | solution.py:195
  132.3 26.6 %collective-permute-start.23 = (bf16[96,2048]{1,0:T(8,128)(2,1)S(1)}, bf16[96,2048]{1,0:T(8,128)(2,1)S(1)}, u32[]{:S(2)}, u32[]{:S(2)}) collective-permute-start(bf16[96,2048]{1,0:T(8,128)(2,1)S(1)} %slice.197), channel_id=1, source_target_pairs={{0,8},{4,12},{8,0},{12,4},{16,24},{20,28},{24,16},{28,20},{1,9},{5... | collective-permute-start | bytes 1179656 | tf_op jit(solution)/shard_map/ppermute | solution.py:195
  133.0 25.9 %collective-permute-start.24 = (bf16[96,2048]{1,0:T(8,128)(2,1)S(1)}, bf16[96,2048]{1,0:T(8,128)(2,1)S(1)}, u32[]{:S(2)}, u32[]{:S(2)}) collective-permute-start(bf16[96,2048]{1,0:T(8,128)(2,1)S(1)} %slice.198), channel_id=1, source_target_pairs={{0,16},{4,20},{8,24},{12,28},{16,0},{20,4},{24,8},{28,12},{1,17},{... | collective-permute-start | bytes 1179656 | tf_op jit(solution)/shard_map/ppermute | solution.py:195
  169.1 11.2 %collective-permute-start.29 = (bf16[96,2048]{1,0:T(8,128)(2,1)S(1)}, bf16[96,2048]{1,0:T(8,128)(2,1)S(1)}, u32[]{:S(2)}, u32[]{:S(2)}) collective-permute-start(bf16[96,2048]{1,0:T(8,128)(2,1)S(1)} %get-tuple-element.348), channel_id=1, source_target_pairs={{0,16},{4,20},{8,24},{12,28},{16,0},{20,4},{24,8},{28,12},{1,17},{... | collective-permute-start | bytes 1179656 | tf_op jit(solution)/shard_map/ppermute | solution.py:195
  170.6 12.0 %collective-permute-start.27 = (bf16[96,2048]{1,0:T(8,128)(2,1)S(1)}, bf16[96,2048]{1,0:T(8,128)(2,1)S(1)}, u32[]{:S(2)}, u32[]{:S(2)}) collective-permute-start(bf16[96,2048]{1,0:T(8,128)(2,1)S(1)} %get-tuple-element.349), channel_id=1, source_target_pairs={{0,8},{4,12},{8,0},{12,4},{16,24},{20,28},{24,16},{28,20},{1,9},{5... | collective-permute-start | bytes 1179656 | tf_op jit(solution)/shard_map/ppermute | solution.py:195
  172.0 18.0 %collective-permute-start.26 = (bf16[96,2048]{1,0:T(8,128)(2,1)S(1)}, bf16[96,2048]{1,0:T(8,128)(2,1)}, u32[]{:S(2)}, u32[]{:S(2)}) collective-permute-start(bf16[96,2048]{1,0:T(8,128)(2,1)S(1)} %get-tuple-element.346), channel_id=1, source_target_pairs={{0,8},{4,12},{8,0},{12,4},{16,24},{20,28},{24,16},{28,20},{1,9},{5... | collective-permute-start | bytes 1179656 | tf_op jit(solution)/shard_map/ppermute | solution.py:195
  184.2 19.2 %collective-permute-start.37 = (bf16[96,2048]{1,0:T(8,128)(2,1)S(1)}, bf16[96,2048]{1,0:T(8,128)(2,1)S(1)}, u32[]{:S(2)}, u32[]{:S(2)}) collective-permute-start(bf16[96,2048]{1,0:T(8,128)(2,1)S(1)} %collective-permute-done.23.refs_6_), channel_id=1, source_target_pairs={{0,4},{4,0},{8,12},{12,8},{16,20},{20,16},{24,28},{28,24},{1,5},{5... | collective-permute-start | bytes 1179656 | tf_op jit(solution)/shard_map/ppermute | solution.py:195
  184.3 19.8 %collective-permute-start.38 = (bf16[96,2048]{1,0:T(8,128)(2,1)S(1)}, bf16[96,2048]{1,0:T(8,128)(2,1)S(1)}, u32[]{:S(2)}, u32[]{:S(2)}) collective-permute-start(bf16[96,2048]{1,0:T(8,128)(2,1)S(1)} %collective-permute-done.24.refs_7_), channel_id=1, source_target_pairs={{0,4},{4,0},{8,12},{12,8},{16,20},{20,16},{24,28},{28,24},{1,5},{5... | collective-permute-start | bytes 1179656 | tf_op jit(solution)/shard_map/ppermute | solution.py:195
  184.8 20.7 %collective-permute-start.34 = (bf16[192,2048]{1,0:T(8,128)(2,1)S(1)}, bf16[192,2048]{1,0:T(8,128)(2,1)S(1)}, u32[]{:S(2)}, u32[]{:S(2)}) collective-permute-start(bf16[192,2048]{1,0:T(8,128)(2,1)S(1)} %bitcast.56), channel_id=1, source_target_pairs={{0,4},{4,0},{8,12},{12,8},{16,20},{20,16},{24,28},{28,24},{1,5},{5... | collective-permute-start | bytes 2359304 | tf_op jit(solution)/shard_map/ppermute | solution.py:195
  190.0 11.0 %collective-permute-start.31 = (bf16[96,2048]{1,0:T(8,128)(2,1)}, bf16[96,2048]{1,0:T(8,128)(2,1)S(1)}, u32[]{:S(2)}, u32[]{:S(2)}) collective-permute-start(bf16[96,2048]{1,0:T(8,128)(2,1)} %get-tuple-element.347), channel_id=1, source_target_pairs={{0,16},{4,20},{8,24},{12,28},{16,0},{20,4},{24,8},{28,12},{1,17},{... | collective-permute-start | bytes 1179656 | tf_op jit(solution)/shard_map/ppermute | solution.py:195
  203.4 19.9 %collective-permute-start.33 = (bf16[192,2048]{1,0:T(8,128)(2,1)S(1)}, bf16[192,2048]{1,0:T(8,128)(2,1)S(1)}, u32[]{:S(2)}, u32[]{:S(2)}) collective-permute-start(bf16[192,2048]{1,0:T(8,128)(2,1)S(1)} %multiply_convert_fusion.refs_0_), channel_id=1, source_target_pairs={{0,16},{4,20},{8,24},{12,28},{16,0},{20,4},{24,8},{28,12},{1,17},{... | collective-permute-start | bytes 2359304 | tf_op jit(solution)/shard_map/ppermute | solution.py:195
  204.1 20.2 %collective-permute-start.32 = (bf16[192,2048]{1,0:T(8,128)(2,1)S(1)}, bf16[192,2048]{1,0:T(8,128)(2,1)S(1)}, u32[]{:S(2)}, u32[]{:S(2)}) collective-permute-start(bf16[192,2048]{1,0:T(8,128)(2,1)S(1)} %multiply_convert_fusion.refs_0_), channel_id=1, source_target_pairs={{0,8},{4,12},{8,0},{12,4},{16,24},{20,28},{24,16},{28,20},{1,9},{5... | collective-permute-start | bytes 2359304 | tf_op jit(solution)/shard_map/ppermute | solution.py:195
  225.4 10.7 %collective-permute-start.42 = (bf16[96,2048]{1,0:T(8,128)(2,1)S(1)}, bf16[96,2048]{1,0:T(8,128)(2,1)S(1)}, u32[]{:S(2)}, u32[]{:S(2)}) collective-permute-start(bf16[96,2048]{1,0:T(8,128)(2,1)S(1)} %slice.206), channel_id=1, source_target_pairs={{0,8},{4,12},{8,0},{12,4},{16,24},{20,28},{24,16},{28,20},{1,9},{5... | collective-permute-start | bytes 1179656 | tf_op jit(solution)/shard_map/ppermute | solution.py:195
  227.8 12.0 %collective-permute-start.39 = (bf16[192,2048]{1,0:T(8,128)(2,1)S(1)}, bf16[192,2048]{1,0:T(8,128)(2,1)S(1)}, u32[]{:S(2)}, u32[]{:S(2)}) collective-permute-start(bf16[192,2048]{1,0:T(8,128)(2,1)S(1)} %multiply_convert_fusion.refs_0_), channel_id=1, source_target_pairs={{0,4},{4,0},{8,12},{12,8},{16,20},{20,16},{24,28},{28,24},{1,5},{5... | collective-permute-start | bytes 2359304 | tf_op jit(solution)/shard_map/ppermute | solution.py:195
  227.8 12.0 %collective-permute-start.40 = (bf16[192,2048]{1,0:T(8,128)(2,1)S(1)}, bf16[192,2048]{1,0:T(8,128)(2,1)S(1)}, u32[]{:S(2)}, u32[]{:S(2)}) collective-permute-start(bf16[192,2048]{1,0:T(8,128)(2,1)S(1)} %collective-permute-done.32.refs_2_), channel_id=1, source_target_pairs={{0,4},{4,0},{8,12},{12,8},{16,20},{20,16},{24,28},{28,24},{1,5},{5... | collective-permute-start | bytes 2359304 | tf_op jit(solution)/shard_map/ppermute | solution.py:195
  228.3 11.5 %collective-permute-start.41 = (bf16[192,2048]{1,0:T(8,128)(2,1)S(1)}, bf16[192,2048]{1,0:T(8,128)(2,1)S(1)}, u32[]{:S(2)}, u32[]{:S(2)}) collective-permute-start(bf16[192,2048]{1,0:T(8,128)(2,1)S(1)} %copy-done.59), channel_id=1, source_target_pairs={{0,4},{4,0},{8,12},{12,8},{16,20},{20,16},{24,28},{28,24},{1,5},{5... | collective-permute-start | bytes 2359304 | tf_op jit(solution)/shard_map/ppermute | solution.py:195
  241.6 34.5 %all-to-all-start.2 = ((bf16[8,192,256]{2,1,0:T(8,128)(2,1)}), bf16[8,192,256]{2,1,0:T(8,128)(2,1)}, u32[]{:S(2)}, u32[]{:S(2)}) async-start(bf16[8,192,256]{2,1,0:T(8,128)(2,1)} %copy-done.19), calls=%async_computation.2 | async-start | bytes 1572864 | tf_op jit(solution)/shard_map/all_to_all | solution.py:381
  245.8 101.7 %reduce-scatter.5.cloned.1.call-start = ((), (), s32[]{:S(2)}) async-start(), calls=%async_computation.12 | async-start | bytes 3604480 | tf_op jit(solution)/shard_map/reduce_scatter | solution.py:371
  276.1 175.8 %reduce-scatter.7.cloned.1.call-start = ((), (), s32[]{:S(2)}) async-start(), calls=%async_computation.13 | async-start | bytes 7864320 | tf_op jit(solution)/shard_map/reduce_scatter | solution.py:371
  294.9 15.4 %collective-permute-start.46 = (bf16[384,2048]{1,0:T(8,128)(2,1)}, bf16[384,2048]{1,0:T(8,128)(2,1)S(1)}, u32[]{:S(2)}, u32[]{:S(2)}) collective-permute-start(bf16[384,2048]{1,0:T(8,128)(2,1)} %get-tuple-element.251), channel_id=1, source_target_pairs={{0,4},{4,0},{8,12},{12,8},{16,20},{20,16},{24,28},{28,24},{1,5},{5... | collective-permute-start | bytes 4718600 | tf_op jit(solution)/shard_map/ppermute | solution.py:195
  310.3 14.7 %collective-permute-start.47 = (bf16[384,2048]{1,0:T(8,128)(2,1)}, bf16[384,2048]{1,0:T(8,128)(2,1)S(1)}, u32[]{:S(2)}, u32[]{:S(2)}) collective-permute-start(bf16[384,2048]{1,0:T(8,128)(2,1)} %get-tuple-element.256), channel_id=1, source_target_pairs={{0,4},{4,0},{8,12},{12,8},{16,20},{20,16},{24,28},{28,24},{1,5},{5... | collective-permute-start | bytes 4718600 | tf_op jit(solution)/shard_map/ppermute | solution.py:195
  311.5 11.1 %collective-permute-start.49 = (bf16[96,2048]{1,0:T(8,128)(2,1)S(1)}, bf16[96,2048]{1,0:T(8,128)(2,1)S(1)}, u32[]{:S(2)}, u32[]{:S(2)}) collective-permute-start(bf16[96,2048]{1,0:T(8,128)(2,1)S(1)} %get-tuple-element.360), channel_id=1, source_target_pairs={{0,8},{4,12},{8,0},{12,4},{16,24},{20,28},{24,16},{28,20},{1,9},{5... | collective-permute-start | bytes 1179656 | tf_op jit(solution)/shard_map/ppermute | solution.py:195
  313.1 14.8 %collective-permute-start.51 = (bf16[96,2048]{1,0:T(8,128)(2,1)S(1)}, bf16[96,2048]{1,0:T(8,128)(2,1)S(1)}, u32[]{:S(2)}, u32[]{:S(2)}) collective-permute-start(bf16[96,2048]{1,0:T(8,128)(2,1)S(1)} %get-tuple-element.362), channel_id=1, source_target_pairs={{0,16},{4,20},{8,24},{12,28},{16,0},{20,4},{24,8},{28,12},{1,17},{... | collective-permute-start | bytes 1179656 | tf_op jit(solution)/shard_map/ppermute | solution.py:195
  314.5 30.2 %collective-permute-start.53 = (bf16[96,2048]{1,0:T(8,128)(2,1)S(1)}, bf16[96,2048]{1,0:T(8,128)(2,1)}, u32[]{:S(2)}, u32[]{:S(2)}) collective-permute-start(bf16[96,2048]{1,0:T(8,128)(2,1)S(1)} %get-tuple-element.361), channel_id=1, source_target_pairs={{0,16},{4,20},{8,24},{12,28},{16,0},{20,4},{24,8},{28,12},{1,17},{... | collective-permute-start | bytes 1179656 | tf_op jit(solution)/shard_map/ppermute | solution.py:195
  323.5 20.0 %collective-permute-start.50 = (bf16[96,2048]{1,0:T(8,128)(2,1)}, bf16[96,2048]{1,0:T(8,128)(2,1)}, u32[]{:S(2)}, u32[]{:S(2)}) collective-permute-start(bf16[96,2048]{1,0:T(8,128)(2,1)} %add_convert_fusion.8), channel_id=1, source_target_pairs={{0,16},{4,20},{8,24},{12,28},{16,0},{20,4},{24,8},{28,12},{1,17},{... | collective-permute-start | bytes 1179656 | tf_op jit(solution)/shard_map/ppermute | solution.py:195
  326.4 17.1 %collective-permute-start.48 = (bf16[96,2048]{1,0:T(8,128)(2,1)}, bf16[96,2048]{1,0:T(8,128)(2,1)}, u32[]{:S(2)}, u32[]{:S(2)}) collective-permute-start(bf16[96,2048]{1,0:T(8,128)(2,1)} %slice.253), channel_id=1, source_target_pairs={{0,8},{4,12},{8,0},{12,4},{16,24},{20,28},{24,16},{28,20},{1,9},{5... | collective-permute-start | bytes 1179656 | tf_op jit(solution)/shard_map/ppermute | solution.py:195
  328.7 16.3 %collective-permute-start.52 = (bf16[96,2048]{1,0:T(8,128)(2,1)}, bf16[96,2048]{1,0:T(8,128)(2,1)S(1)}, u32[]{:S(2)}, u32[]{:S(2)}) collective-permute-start(bf16[96,2048]{1,0:T(8,128)(2,1)} %add_convert_fusion.7), channel_id=1, source_target_pairs={{0,8},{4,12},{8,0},{12,4},{16,24},{20,28},{24,16},{28,20},{1,9},{5... | collective-permute-start | bytes 1179656 | tf_op jit(solution)/shard_map/ppermute | solution.py:195
  343.2 180.8 %reduce-scatter.9.cloned.1.call-start = ((), (), s32[]{:S(2)}) async-start(), calls=%async_computation.14 | async-start | bytes 3932160 | tf_op jit(solution)/shard_map/reduce_scatter | solution.py:371
  351.3 18.3 %collective-permute-start.55 = (bf16[192,2048]{1,0:T(8,128)(2,1)S(1)}, bf16[192,2048]{1,0:T(8,128)(2,1)S(1)}, u32[]{:S(2)}, u32[]{:S(2)}) collective-permute-start(bf16[192,2048]{1,0:T(8,128)(2,1)S(1)} %fusion.8.refs_0_), channel_id=1, source_target_pairs={{0,16},{4,20},{8,24},{12,28},{16,0},{20,4},{24,8},{28,12},{1,17},{... | collective-permute-start | bytes 2359304 | tf_op jit(solution)/shard_map/ppermute | solution.py:195
  352.6 17.2 %collective-permute-start.54 = (bf16[192,2048]{1,0:T(8,128)(2,1)S(1)}, bf16[192,2048]{1,0:T(8,128)(2,1)}, u32[]{:S(2)}, u32[]{:S(2)}) collective-permute-start(bf16[192,2048]{1,0:T(8,128)(2,1)S(1)} %fusion.8.refs_0_), channel_id=1, source_target_pairs={{0,8},{4,12},{8,0},{12,4},{16,24},{20,28},{24,16},{28,20},{1,9},{5... | collective-permute-start | bytes 2359304 | tf_op jit(solution)/shard_map/ppermute | solution.py:195
  369.8 13.7 %collective-permute-start.63 = (bf16[768,2048]{1,0:T(8,128)(2,1)}, bf16[768,2048]{1,0:T(8,128)(2,1)S(1)}, u32[]{:S(2)}, u32[]{:S(2)}) collective-permute-start(bf16[768,2048]{1,0:T(8,128)(2,1)} %get-tuple-element.275), channel_id=1, source_target_pairs={{0,4},{4,0},{8,12},{12,8},{16,20},{20,16},{24,28},{28,24},{1,5},{5... | collective-permute-start | bytes 9437192 | tf_op jit(solution)/shard_map/ppermute | solution.py:195
  369.8 11.6 %collective-permute-start.59 = (bf16[96,2048]{1,0:T(8,128)(2,1)S(1)}, bf16[96,2048]{1,0:T(8,128)(2,1)S(1)}, u32[]{:S(2)}, u32[]{:S(2)}) collective-permute-start(bf16[96,2048]{1,0:T(8,128)(2,1)S(1)} %slice.215), channel_id=1, source_target_pairs={{0,8},{4,12},{8,0},{12,4},{16,24},{20,28},{24,16},{28,20},{1,9},{5... | collective-permute-start | bytes 1179656 | tf_op jit(solution)/shard_map/ppermute | solution.py:195
  372.2 11.3 %collective-permute-start.60 = (bf16[96,2048]{1,0:T(8,128)(2,1)S(1)}, bf16[96,2048]{1,0:T(8,128)(2,1)S(1)}, u32[]{:S(2)}, u32[]{:S(2)}) collective-permute-start(bf16[96,2048]{1,0:T(8,128)(2,1)S(1)} %slice.216), channel_id=1, source_target_pairs={{0,16},{4,20},{8,24},{12,28},{16,0},{20,4},{24,8},{28,12},{1,17},{... | collective-permute-start | bytes 1179656 | tf_op jit(solution)/shard_map/ppermute | solution.py:195
  373.9 14.6 %collective-permute-start.57 = (bf16[192,2048]{1,0:T(8,128)(2,1)}, bf16[192,2048]{1,0:T(8,128)(2,1)S(1)}, u32[]{:S(2)}, u32[]{:S(2)}) collective-permute-start(bf16[192,2048]{1,0:T(8,128)(2,1)} %collective-permute-done.54.refs_2_), channel_id=1, source_target_pairs={{0,4},{4,0},{8,12},{12,8},{16,20},{20,16},{24,28},{28,24},{1,5},{5... | collective-permute-start | bytes 2359304 | tf_op jit(solution)/shard_map/ppermute | solution.py:195
  373.9 14.6 %collective-permute-start.58 = (bf16[192,2048]{1,0:T(8,128)(2,1)S(1)}, bf16[192,2048]{1,0:T(8,128)(2,1)S(1)}, u32[]{:S(2)}, u32[]{:S(2)}) collective-permute-start(bf16[192,2048]{1,0:T(8,128)(2,1)S(1)} %collective-permute-done.55.refs_4_), channel_id=1, source_target_pairs={{0,4},{4,0},{8,12},{12,8},{16,20},{20,16},{24,28},{28,24},{1,5},{5... | collective-permute-start | bytes 2359304 | tf_op jit(solution)/shard_map/ppermute | solution.py:195
  388.7 35.2 %collective-permute-start.65 = (bf16[96,2048]{1,0:T(8,128)(2,1)S(1)}, bf16[96,2048]{1,0:T(8,128)(2,1)S(1)}, u32[]{:S(2)}, u32[]{:S(2)}) collective-permute-start(bf16[96,2048]{1,0:T(8,128)(2,1)S(1)} %get-tuple-element.363), channel_id=1, source_target_pairs={{0,8},{4,12},{8,0},{12,4},{16,24},{20,28},{24,16},{28,20},{1,9},{5... | collective-permute-start | bytes 1179656 | tf_op jit(solution)/shard_map/ppermute | solution.py:195
  390.0 34.1 %collective-permute-start.67 = (bf16[96,2048]{1,0:T(8,128)(2,1)S(1)}, bf16[96,2048]{1,0:T(8,128)(2,1)S(1)}, u32[]{:S(2)}, u32[]{:S(2)}) collective-permute-start(bf16[96,2048]{1,0:T(8,128)(2,1)S(1)} %slice.224), channel_id=1, source_target_pairs={{0,16},{4,20},{8,24},{12,28},{16,0},{20,4},{24,8},{28,12},{1,17},{... | collective-permute-start | bytes 1179656 | tf_op jit(solution)/shard_map/ppermute | solution.py:195
  391.6 32.5 %collective-permute-start.66 = (bf16[96,2048]{1,0:T(8,128)(2,1)S(1)}, bf16[96,2048]{1,0:T(8,128)(2,1)S(1)}, u32[]{:S(2)}, u32[]{:S(2)}) collective-permute-start(bf16[96,2048]{1,0:T(8,128)(2,1)S(1)} %slice.221), channel_id=1, source_target_pairs={{0,8},{4,12},{8,0},{12,4},{16,24},{20,28},{24,16},{28,20},{1,9},{5... | collective-permute-start | bytes 1179656 | tf_op jit(solution)/shard_map/ppermute | solution.py:195
  392.6 31.4 %collective-permute-start.64 = (bf16[96,2048]{1,0:T(8,128)(2,1)S(1)}, bf16[96,2048]{1,0:T(8,128)(2,1)S(1)}, u32[]{:S(2)}, u32[]{:S(2)}) collective-permute-start(bf16[96,2048]{1,0:T(8,128)(2,1)S(1)} %get-tuple-element.364), channel_id=1, source_target_pairs={{0,16},{4,20},{8,24},{12,28},{16,0},{20,4},{24,8},{28,12},{1,17},{... | collective-permute-start | bytes 1179656 | tf_op jit(solution)/shard_map/ppermute | solution.py:195
  430.4 11.9 %collective-permute-start.70 = (bf16[96,1536]{1,0:T(8,128)(2,1)S(1)}, bf16[96,1536]{1,0:T(8,128)(2,1)S(1)}, u32[]{:S(2)}, u32[]{:S(2)}) collective-permute-start(bf16[96,1536]{1,0:T(8,128)(2,1)S(1)} %get-tuple-element.354), channel_id=1, source_target_pairs={{0,8},{4,12},{8,0},{12,4},{16,24},{20,28},{24,16},{28,20},{1,9},{5... | collective-permute-start | bytes 884744 | tf_op jit(solution)/shard_map/ppermute | solution.py:195
  431.5 10.9 %collective-permute-start.69 = (bf16[96,1536]{1,0:T(8,128)(2,1)S(1)}, bf16[96,1536]{1,0:T(8,128)(2,1)S(1)}, u32[]{:S(2)}, u32[]{:S(2)}) collective-permute-start(bf16[96,1536]{1,0:T(8,128)(2,1)S(1)} %get-tuple-element.356), channel_id=1, source_target_pairs={{0,16},{4,20},{8,24},{12,28},{16,0},{20,4},{24,8},{28,12},{1,17},{... | collective-permute-start | bytes 884744 | tf_op jit(solution)/shard_map/ppermute | solution.py:195
  455.0 12.2 %collective-permute-start.73 = (bf16[96,1536]{1,0:T(8,128)(2,1)}, bf16[96,1536]{1,0:T(8,128)(2,1)S(1)}, u32[]{:S(2)}, u32[]{:S(2)}) collective-permute-start(bf16[96,1536]{1,0:T(8,128)(2,1)} %get-tuple-element.308), channel_id=1, source_target_pairs={{0,8},{4,12},{8,0},{12,4},{16,24},{20,28},{24,16},{28,20},{1,9},{5... | collective-permute-start | bytes 884744 | tf_op jit(solution)/shard_map/ppermute | solution.py:195
  455.5 12.8 %collective-permute-start.74 = (bf16[96,1536]{1,0:T(8,128)(2,1)}, bf16[96,1536]{1,0:T(8,128)(2,1)S(1)}, u32[]{:S(2)}, u32[]{:S(2)}) collective-permute-start(bf16[96,1536]{1,0:T(8,128)(2,1)} %get-tuple-element.309), channel_id=1, source_target_pairs={{0,16},{4,20},{8,24},{12,28},{16,0},{20,4},{24,8},{28,12},{1,17},{... | collective-permute-start | bytes 884744 | tf_op jit(solution)/shard_map/ppermute | solution.py:195
  479.8 15.3 %collective-permute-start.78 = (bf16[224,1536]{1,0:T(8,128)(2,1)S(1)}, bf16[224,1536]{1,0:T(8,128)(2,1)S(1)}, u32[]{:S(2)}, u32[]{:S(2)}) collective-permute-start(bf16[224,1536]{1,0:T(8,128)(2,1)S(1)} %get-tuple-element.325.refs_0_), channel_id=1, source_target_pairs={{0,16},{4,20},{8,24},{12,28},{16,0},{20,4},{24,8},{28,12},{1,17},{... | collective-permute-start | bytes 2064392 | tf_op jit(solution)/shard_map/ppermute | solution.py:195
  481.3 14.8 %collective-permute-start.77 = (bf16[224,1536]{1,0:T(8,128)(2,1)S(1)}, bf16[224,1536]{1,0:T(8,128)(2,1)S(1)}, u32[]{:S(2)}, u32[]{:S(2)}) collective-permute-start(bf16[224,1536]{1,0:T(8,128)(2,1)S(1)} %get-tuple-element.325.refs_0_), channel_id=1, source_target_pairs={{0,8},{4,12},{8,0},{12,4},{16,24},{20,28},{24,16},{28,20},{1,9},{5... | collective-permute-start | bytes 2064392 | tf_op jit(solution)/shard_map/ppermute | solution.py:195
  496.2 14.1 %collective-permute-start.80 = (bf16[224,1536]{1,0:T(8,128)(2,1)S(1)}, bf16[224,1536]{1,0:T(8,128)(2,1)S(1)}, u32[]{:S(2)}, u32[]{:S(2)}) collective-permute-start(bf16[224,1536]{1,0:T(8,128)(2,1)S(1)} %collective-permute-done.77.refs_2_), channel_id=1, source_target_pairs={{0,4},{4,0},{8,12},{12,8},{16,20},{20,16},{24,28},{28,24},{1,5},{5... | collective-permute-start | bytes 2064392 | tf_op jit(solution)/shard_map/ppermute | solution.py:195
  496.3 13.1 %collective-permute-start.79 = (bf16[224,1536]{1,0:T(8,128)(2,1)S(1)}, bf16[224,1536]{1,0:T(8,128)(2,1)S(1)}, u32[]{:S(2)}, u32[]{:S(2)}) collective-permute-start(bf16[224,1536]{1,0:T(8,128)(2,1)S(1)} %get-tuple-element.325.refs_0_), channel_id=1, source_target_pairs={{0,4},{4,0},{8,12},{12,8},{16,20},{20,16},{24,28},{28,24},{1,5},{5... | collective-permute-start | bytes 2064392 | tf_op jit(solution)/shard_map/ppermute | solution.py:195
  498.2 12.1 %collective-permute-start.81 = (bf16[224,1536]{1,0:T(8,128)(2,1)S(1)}, bf16[224,1536]{1,0:T(8,128)(2,1)S(1)}, u32[]{:S(2)}, u32[]{:S(2)}) collective-permute-start(bf16[224,1536]{1,0:T(8,128)(2,1)S(1)} %collective-permute-done.78.refs_4_), channel_id=1, source_target_pairs={{0,4},{4,0},{8,12},{12,8},{16,20},{20,16},{24,28},{28,24},{1,5},{5... | collective-permute-start | bytes 2064392 | tf_op jit(solution)/shard_map/ppermute | solution.py:195
  498.2 10.5 %collective-permute-start.83 = (bf16[112,1536]{1,0:T(8,128)(2,1)S(1)}, bf16[112,1536]{1,0:T(8,128)(2,1)S(1)}, u32[]{:S(2)}, u32[]{:S(2)}) collective-permute-start(bf16[112,1536]{1,0:T(8,128)(2,1)S(1)} %slice.235), channel_id=1, source_target_pairs={{0,16},{4,20},{8,24},{12,28},{16,0},{20,4},{24,8},{28,12},{1,17},{... | collective-permute-start | bytes 1032200 | tf_op jit(solution)/shard_map/ppermute | solution.py:195
  512.2 24.6 %all-to-all-start.4 = ((bf16[8,2,64,704]{3,2,1,0:T(8,128)(2,1)}), bf16[8,2,64,704]{3,2,1,0:T(8,128)(2,1)S(1)}, u32[]{:S(2)}, u32[]{:S(2)}) async-start(bf16[8,2,64,704]{3,2,1,0:T(8,128)(2,1)} %bitcast.76), calls=%async_computation.8 | async-start | bytes 3145728 | tf_op jit(solution)/shard_map/all_to_all | solution.py:381
  515.8 34.9 %reduce-scatter.11.cloned.1.call-start = ((), (), s32[]{:S(2)}) async-start(), calls=%async_computation.15 | async-start | bytes 1064960 | tf_op jit(solution)/shard_map/reduce_scatter | solution.py:371
  (115 other events, 683.9 us)
Sparse Core Ops, SparseCore 0:
  39.6 64.2 all-gather.3
  105.4 113.9 all-gather.5
  221.0 57.3 all-gather.7
  280.6 54.8 reduce-scatter.4
  343.3 108.5 reduce-scatter.6
  454.1 60.7 reduce-scatter.8
  524.2 25.0 reduce-scatter.10
